TPU v7x, 32 devices: a whole 2x2x4 slice. The times are simulated.
32 devices in a mesh: rec: 8 (over z, y), tile: 4 (over x, core).
Axes of the slice: x: 2, y: 2, z: 4, core: 2. Of those that a mesh axis runs over, the one named last changes fastest.
Arguments:
- prior_flux: bfloat16 [240, 128, 512], P(None, 'rec', 'tile'), may hold values from -6 to 6
- flux_scale: bfloat16 [240, 128, 512], P(None, 'rec', 'tile'), may hold values from 0.5 to 2
- control: float32 [240, 128, 512], P(None, 'rec', 'tile'), may hold values from -6 to 6
- footprint: bfloat16 [1024, 8, 24, 128], P(('rec', 'tile')), may hold values from 0 to 0.019897461
- slot_count: int32 [1024], P(('rec', 'tile')), may hold values from 0 to 8, as said below
- start_hour: int32 [1024, 8], P(('rec', 'tile')), may hold values from 0 to 216
- grid_row: int32 [1024, 8], P(('rec', 'tile')), may hold values from 0 to 15
- receptor_slot: int32 [1024, 8], P(('rec', 'tile')), may hold values from 0 to 63
- observed: float32 [512], P('rec'), may hold values from -32 to 32
- obs_error: float32 [512], P('rec'), may hold values from 0.1 to 0.4
Outputs:
- model_co2: float32 [512], P('rec')
- flux_gradient: float32 [240, 128, 512], P(None, 'rec', 'tile')
Inputs may be any that keep to these rules, and one draw needn't show every extreme that they name: `slot_count`: A source device sends at most 8 blocks to one flux owner; some source reaches it, and in every draw one owner receives 8 blocks from every source.
All inputs are finite; a program needn't handle non-finite values.
Results may differ from a plain program's by a relative error of at most 0.0003.
Values may be sent and summed in bfloat16 or wider, within the bound.
No kernel may reach another device: no remote copies, remote signals or barrier semaphores. Data moves between devices by JAX's collectives and lax.ppermute only.
A program may use at most 128 MiB of HBM per device.

v0:
```python
import jax
import jax.numpy as jnp
from jax import lax
from jax.sharding import PartitionSpec as P

RAD = 4
TAPS = 12


def padded_2(block, sides, width):
    for axis, dim in sides:
        count = lax.axis_size(axis)
        forward = [(i, i + 1) for i in range(count - 1)]
        backward = [(target, source) for source, target in forward]
        low = lax.ppermute(
            lax.slice_in_dim(block, block.shape[dim] - width, None, axis=dim), axis, forward
        )
        high = lax.ppermute(lax.slice_in_dim(block, 0, width, axis=dim), axis, backward)
        block = jnp.concatenate([low, block, high], axis=dim)
    return block


def space_kernel():
    offsets = jnp.arange(-RAD, RAD + 1).astype(jnp.float32)
    values = jnp.exp(-2.0 * offsets * offsets / (RAD * RAD))
    return values / jnp.sqrt(jnp.sum(values * values))


def time_matrix(length):
    offsets = jnp.arange(-TAPS, TAPS + 1).astype(jnp.float32)
    values = jnp.exp(-2.0 * jnp.abs(offsets) / TAPS)
    norm_total = jnp.sqrt(jnp.sum(values * values))
    target = jnp.arange(length)[:, None]
    source = jnp.arange(length)[None, :]
    distance = jnp.abs(source - target).astype(jnp.float32)
    inside = jnp.abs(source - target) <= TAPS
    return jnp.where(inside, jnp.exp(-2.0 * distance / TAPS), 0.0) / norm_total


def correlate(field):
    padded = padded_2(field, (("rec", 1), ("tile", 2)), RAD)
    spatial = space_kernel()
    height = field.shape[1]
    breadth = field.shape[2]
    by_rows = spatial[0] * padded[:, 0:height, :]
    for offset in range(1, 2 * RAD + 1):
        by_rows = by_rows + spatial[offset] * padded[:, offset : offset + height, :]
    by_cols = spatial[0] * by_rows[:, :, 0:breadth]
    for offset in range(1, 2 * RAD + 1):
        by_cols = by_cols + spatial[offset] * by_rows[:, :, offset : offset + breadth]
    matrix = time_matrix(field.shape[0])
    flat_field = by_cols.reshape(field.shape[0], height * breadth)
    result = jnp.dot(
        matrix, flat_field, precision=lax.Precision.HIGHEST, preferred_element_type=jnp.float32
    )
    return result.reshape(field.shape)


def block_scalars(numbers):
    return lax.all_to_all(numbers, ("rec", "tile"), split_axis=0, concat_axis=0, tiled=True)


def per_device(
    prior_flux,
    flux_scale,
    control,
    footprint,
    slot_count,
    start_hour,
    grid_row,
    receptor_slot,
    observed,
    obs_error,
):
    slot_total = footprint.shape[1]
    arrived = (
        lax.all_to_all(footprint, ("rec", "tile"), split_axis=0, concat_axis=0, tiled=True),
        lax.all_to_all(start_hour, ("rec", "tile"), split_axis=0, concat_axis=0, tiled=True),
        lax.all_to_all(grid_row, ("rec", "tile"), split_axis=0, concat_axis=0, tiled=True),
        lax.all_to_all(slot_count, ("rec", "tile"), split_axis=0, concat_axis=0, tiled=True),
    )
    got_foot, got_start, got_row, got_count = arrived
    flux_field = prior_flux.astype(jnp.float32) + flux_scale.astype(jnp.float32) * correlate(
        control
    )
    rows_here = flux_field.shape[1]
    breadth = flux_field.shape[2]
    heights = footprint.shape[2]
    flux_rows = flux_field.reshape(-1, breadth)
    hour_steps = jnp.arange(heights)
    flat_index = (
        (got_start[:, :, None] + hour_steps[None, None, :]) * rows_here + got_row[:, :, None]
    ).reshape(-1)
    windows = flux_rows[flat_index].reshape(got_foot.shape)
    slot_ids = jnp.arange(slot_total)[None, :]
    arrived_valid = slot_ids < got_count[:, None]
    block_value = jnp.where(
        arrived_valid, jnp.sum(got_foot.astype(jnp.float32) * windows, axis=(2, 3)), 0.0
    )
    returned = block_scalars(block_value)
    receptor_ids = jnp.arange(observed.shape[0])[None, None, :]
    chosen = receptor_slot[:, :, None] == receptor_ids
    partial_co2 = jnp.sum(jnp.where(chosen, returned[:, :, None], 0.0), axis=(0, 1))
    model_co2 = lax.psum(partial_co2, "tile")
    weight = (model_co2 - observed) / (obs_error * obs_error)
    own_valid = slot_ids < slot_count[:, None]
    block_weight = jnp.where(
        own_valid, jnp.sum(jnp.where(chosen, weight[None, None, :], 0.0), axis=2), 0.0
    )
    at_owner = block_scalars(block_weight)
    contrib = got_foot.astype(jnp.float32) * at_owner[:, :, None, None]
    adjoint_rows = (
        jnp.zeros(flux_rows.shape, jnp.float32).at[flat_index].add(contrib.reshape(-1, breadth))
    )
    adjoint_field = adjoint_rows.reshape(flux_field.shape)
    flux_gradient = correlate(flux_scale.astype(jnp.float32) * adjoint_field)
    return (model_co2, flux_gradient)


def solution(mesh):
    return jax.shard_map(
        per_device,
        mesh=mesh,
        in_specs=(
            P(None, "rec", "tile"),
            P(None, "rec", "tile"),
            P(None, "rec", "tile"),
            P(("rec", "tile"), None, None, None),
            P(("rec", "tile")),
            P(("rec", "tile"), None),
            P(("rec", "tile"), None),
            P(("rec", "tile"), None),
            P("rec"),
            P("rec"),
        ),
        out_specs=(P("rec"), P(None, "rec", "tile")),
        check_vma=False,
    )
```

profile of v0, /device:TPU:5, one launch (start us, length us, event | category | flops | bytes accessed | tf_op | source)
XLA Modules:
  0.0 271.3 jit_solution(7677658504469761763)
XLA Ops:
  0.7 1.7 fusion.68
  2.4 3.1 %collective-permute-start = (f32[240,4,128]{2,0,1:T(8,128)S(1)}, f32[240,4,128]{2,0,1:T(8,128)}, u32[]{:S(2)}, u32[]{:S(2)}) collective-permute-start(f32[240,4,128]{2,0,1:T(8,128)S(1)} %copy.131), channel_id=1, source_target_pairs={{0,4},{4,8},{8,12},{12,16},{16,20},{20,24},{24,28},{1,5},{5,9},{9,... | collective-permute-start | bytes 1474568 | tf_op jit(solution)/shard_map/ppermute | solution.py:15
  5.6 2.9 %collective-permute-start.1 = (f32[240,4,128]{2,0,1:T(8,128)S(1)}, f32[240,4,128]{2,0,1:T(8,128)}, u32[]{:S(2)}, u32[]{:S(2)}) collective-permute-start(f32[240,4,128]{2,0,1:T(8,128)S(1)} %copy.132), channel_id=1, source_target_pairs={{4,0},{8,4},{12,8},{16,12},{20,16},{24,20},{28,24},{5,1},{9,5},{13... | collective-permute-start | bytes 1474568 | tf_op jit(solution)/shard_map/ppermute | solution.py:18
  8.5 0.7 copy.85
  9.2 7.0 %all-to-all-start = ((s32[32,1,1]{2,1,0:T(1,128)}), s32[32,1,1]{2,1,0:T(1,128)S(1)}, u32[]{:S(2)}, u32[]{:S(2)}) async-start(s32[32,1,1]{2,1,0:T(1,128)} %copy.85), calls=%async_computation | async-start | bytes 32768 | tf_op jit(solution)/shard_map/all_to_all | solution.py:80
  16.2 0.6 multiply_reduce_fusion
  17.5 0.7 copy.98
  18.2 10.1 %all-to-all-done = s32[32,1,1]{2,1,0:T(1,128)S(1)} async-done(((s32[32,1,1]{2,1,0:T(1,128)}), s32[32,1,1]{2,1,0:T(1,128)S(1)}, u32[]{:S(2)}, u32[]{:S(2)}) %all-to-all-start) | async-done | bytes 160 | tf_op jit(solution)/shard_map/all_to_all | solution.py:80
  28.3 6.1 %all-to-all-start.2 = ((s32[32,1,8]{2,1,0:T(1,128)}), s32[32,1,8]{2,1,0:T(1,128)S(1)}, u32[]{:S(2)}, u32[]{:S(2)}) async-start(s32[32,1,8]{2,1,0:T(1,128)} %bitcast.13), calls=%async_computation.2 | async-start | bytes 32768 | tf_op jit(solution)/shard_map/all_to_all | solution.py:78
  34.4 0.7 copy.99
  35.1 4.9 %all-to-all-done.2 = s32[32,1,8]{2,1,0:T(1,128)S(1)} async-done(((s32[32,1,8]{2,1,0:T(1,128)}), s32[32,1,8]{2,1,0:T(1,128)S(1)}, u32[]{:S(2)}, u32[]{:S(2)}) %all-to-all-start.2) | async-done | bytes 1056 | tf_op jit(solution)/shard_map/all_to_all | solution.py:78
  40.0 4.0 %all-to-all-start.3 = ((s32[32,1,8]{2,1,0:T(1,128)}), s32[32,1,8]{2,1,0:T(1,128)S(1)}, u32[]{:S(2)}, u32[]{:S(2)}) async-start(s32[32,1,8]{2,1,0:T(1,128)} %bitcast.15), calls=%async_computation.3 | async-start | bytes 32768 | tf_op jit(solution)/shard_map/all_to_all | solution.py:79
  44.0 0.7 fusion.69
  44.7 0.6 multiply_reduce_fusion.1
  46.0 0.7 reduce
  46.6 3.0 %all-to-all-done.3 = s32[32,1,8]{2,1,0:T(1,128)S(1)} async-done(((s32[32,1,8]{2,1,0:T(1,128)}), s32[32,1,8]{2,1,0:T(1,128)S(1)}, u32[]{:S(2)}, u32[]{:S(2)}) %all-to-all-start.3) | async-done | bytes 1056 | tf_op jit(solution)/shard_map/all_to_all | solution.py:79
  49.6 4.8 %all-to-all-start.1 = ((bf16[32,8,24,128]{3,2,1,0:T(8,128)(2,1)}), bf16[32,8,24,128]{3,2,1,0:T(8,128)(2,1)}, u32[]{:S(2)}, u32[]{:S(2)}) async-start(bf16[32,8,24,128]{3,2,1,0:T(8,128)(2,1)} %param.13), calls=%async_computation.1 | async-start | bytes 3145728 | tf_op jit(solution)/shard_map/all_to_all | solution.py:77
  54.4 0.1 multiply_add_fusion
  54.6 0.1 add.195
  54.8 1.1 constant_dynamic-update-slice_fusion.2
  55.8 2.1 constant_dynamic-update-slice_fusion.1
  58.0 1.1 constant_dynamic-update-slice_fusion
  59.0 3.5 %fusion.66 = (f32[240,24,4]{2,0,1:T(8,128)}, f32[240,24,4]{2,0,1:T(8,128)}) fusion(f32[240,24,128]{2,0,1:T(8,128)S(1)} %constant_dynamic-update-slice_fusion), kind=kLoop, calls=%fused_computation.131 | loop fusion | bytes 368640 | tf_op jit(solution)/shard_map/slice | solution.py:16
  62.5 2.7 %copy.91 = f32[240,24,4]{0,1,2:T(8,128)S(1)} copy(f32[240,24,4]{2,0,1:T(8,128)} %get-tuple-element.14) | data formatting | bytes 184320 | tf_op jit(solution)/shard_map/slice | solution.py:16
  65.2 3.4 %collective-permute-start.2 = (f32[240,24,4]{0,1,2:T(8,128)S(1)}, f32[240,24,4]{0,1,2:T(8,128)S(1)}, u32[]{:S(2)}, u32[]{:S(2)}) collective-permute-start(f32[240,24,4]{0,1,2:T(8,128)S(1)} %copy.91), channel_id=1, source_target_pairs={{0,1},{1,2},{2,3},{4,5},{5,6},{6,7},{8,9},{9,10},{10,11},{12,13},{... | collective-permute-start | bytes 276488 | tf_op jit(solution)/shard_map/ppermute | solution.py:15
  68.6 2.7 %copy.92 = f32[240,24,4]{0,1,2:T(8,128)S(1)} copy(f32[240,24,4]{2,0,1:T(8,128)} %get-tuple-element.15) | data formatting | bytes 184320 | tf_op jit(solution)/shard_map/slice | solution.py:18
  71.3 1.9 collective-permute-start.3
  73.3 2.5 copy.93
  75.8 2.1 collective-permute-done.3
  77.9 2.5 copy.94
  80.4 5.1 %pad_maximum_fusion = f32[240,24,136]{2,0,1:T(8,128)S(1)} fusion(f32[240,24,4]{2,0,1:T(8,128)} %copy.94, f32[240,24,128]{2,0,1:T(8,128)S(1)} %constant_dynamic-update-slice_fusion, f32[240,24,4]{2,0,1:T(8,128)} %copy.93), kind=kLoop, calls=%fused_computation.2 | loop fusion | flops 1566720 | bytes 6266880 | tf_op jit(solution)/shard_map/concatenate | solution.py:19
  85.5 9.9 %fusion.8 = f32[240,16,136]{2,0,1:T(8,128)S(1)} fusion(f32[240,24,136]{2,0,1:T(8,128)S(1)} %pad_maximum_fusion, f32[]{:T(128)} %bitcast.10, f32[]{:T(128)} %bitcast.9, f32[]{:T(128)} %bitcast.8, f32[]{:T(128)} %bitcast.7, f32[]{:T(128)} %bitcast.6, f32[]{:T(128)} %bitcast.5, f32[]{:T(128)} %bitcast.4, f32[]{:T(128)} %bitcast.3, f32[]{:T(128)} %bitcast.2), kind=kLoop, calls=%fused_computation.22 | loop fusion | flops 8878080 | bytes 20889636 | tf_op jit(solution)/shard_map/add | solution.py:47
  95.4 11.6 %fusion.17 = f32[240,16,128]{2,0,1:T(8,128)S(1)} fusion(bf16[240,16,128]{2,1,0:T(8,128)(2,1)S(1)} %copy-done.8, bf16[240,16,128]{2,1,0:T(8,128)(2,1)S(1)} %copy-done, f32[]{:T(128)S(6)} %sqrt.8, f32[240,16,136]{2,0,1:T(8,128)S(1)} %fusion.8, f32[]{:T(128)} %bitcast.10, f32[]{:T(128)} %bitcast.9, f32[]{:T(128)} %bitcast.8, f32[]{:T(128)} %bitcast.7, ...), kind=kOutput, calls=%fused_computation.44 | convolution fusion | flops 1426302720 | bytes 21626920 | tf_op jit(solution)/shard_map/dot_general | solution.py:53
  107.1 0.6 copy.97
  107.7 21.0 %gather_fusion = f32[6144,128]{1,0:T(8,128)} fusion(f32[3840,128]{1,0:T(8,128)S(1)} %bitcast.68, s32[6144]{0:T(1024)S(1)} %broadcast_clamp_fusion), kind=kCustom, calls=%fused_computation | custom fusion | bytes 6316032 | tf_op jit(solution)/shard_map/gather | solution.py:94
  128.8 3.1 %fusion.16 = f32[32,8]{1,0:T(8,128)S(1)} fusion(f32[32,8,24,128]{3,2,1,0:T(8,128)} %bitcast.69, bf16[32,8,24,128]{3,2,1,0:T(8,128)(2,1)} %all-to-all-done.1), kind=kLoop, calls=%fused_computation.40 | loop fusion | flops 2359040 | bytes 4719616 | tf_op jit(solution)/shard_map/reduce_sum | solution.py:98
  131.9 0.7 bitcast_select_fusion.1
  132.6 5.1 %all-to-all-start.4 = ((f32[32,1,8]{2,1,0:T(1,128)}), f32[32,1,8]{2,1,0:T(1,128)S(1)}, u32[]{:S(2)}, u32[]{:S(2)}) async-start(f32[32,1,8]{2,1,0:T(1,128)} %bitcast.20), calls=%async_computation.4 | async-start | bytes 32768 | tf_op jit(solution)/shard_map/all_to_all | solution.py:60
  137.7 0.1 copy.84
  137.8 5.4 %all-to-all-done.4 = f32[32,1,8]{2,1,0:T(1,128)S(1)} async-done(((f32[32,1,8]{2,1,0:T(1,128)}), f32[32,1,8]{2,1,0:T(1,128)S(1)}, u32[]{:S(2)}, u32[]{:S(2)}) %all-to-all-start.4) | async-done | bytes 1056 | tf_op jit(solution)/shard_map/all_to_all | solution.py:60
  143.2 0.1 select_reduce_fusion.1
  143.3 5.7 %psum.7 = f32[64]{0:T(128)S(1)} all-reduce(f32[64]{0:T(128)S(1)} %select_reduce_fusion.1), channel_id=1, replica_groups=mesh['rec'=8,'tile'=4] {'tile'}, use_global_device_ids=true, to_apply=%region_4.5 | all-reduce | flops 64 | bytes 512 | tf_op jit(solution)/shard_map/psum | solution.py:104
  149.1 0.2 select_reduce_fusion
  149.3 0.1 bitcast_select_fusion
  149.4 9.0 %all_to_all.44 = f32[32,1,8]{2,1,0:T(1,128)S(1)} all-to-all(f32[32,1,8]{2,1,0:T(1,128)S(1)} %bitcast.78), channel_id=1, replica_groups=mesh['rec'=8,'tile'=4] {'rec','tile'}, dimensions={0} | all-to-all | bytes 2048 | tf_op jit(solution)/shard_map/all_to_all | solution.py:60
  158.4 1.7 convert_multiply_fusion
  160.1 34.6 %scatter_custom_fusion = f32[3840,128]{1,0:T(8,128)} fusion(s32[6144]{0:T(1024)S(1)} %bitcast.73, f32[6144,128]{1,0:T(8,128)S(1)} %bitcast.71, f32[]{:T(128)} %constant.12.clone.1), kind=kCustom, calls=%fused_computation.89 | custom fusion | flops 786432 | bytes 1966084 | tf_op jit(solution)/shard_map/scatter-add | solution.py:113
  194.7 2.6 convert_multiply_fusion.2
  197.3 3.0 %collective-permute-start.4 = (f32[240,4,128]{2,0,1:T(8,128)S(1)}, f32[240,4,128]{2,0,1:T(8,128)S(1)}, u32[]{:S(2)}, u32[]{:S(2)}) collective-permute-start(f32[240,4,128]{2,0,1:T(8,128)S(1)} %get-tuple-element.16), channel_id=1, source_target_pairs={{0,4},{4,8},{8,12},{12,16},{16,20},{20,24},{24,28},{1,5},{5,9},{9,... | collective-permute-start | bytes 1474568 | tf_op jit(solution)/shard_map/ppermute | solution.py:15
  200.4 2.3 collective-permute-start.5
  202.7 19.2 %collective-permute-done.4 = f32[240,4,128]{2,0,1:T(8,128)S(1)} collective-permute-done((f32[240,4,128]{2,0,1:T(8,128)S(1)}, f32[240,4,128]{2,0,1:T(8,128)S(1)}, u32[]{:S(2)}, u32[]{:S(2)}) %collective-permute-start.4) | collective-permute-done | bytes 491552 | tf_op jit(solution)/shard_map/ppermute | solution.py:15
  221.9 0.2 pad_maximum_fusion.2
  222.1 3.5 %fusion.65 = (f32[240,24,4]{2,0,1:T(8,128)}, f32[240,24,4]{2,0,1:T(8,128)}) fusion(f32[240,24,128]{2,0,1:T(8,128)S(1)} %pad_maximum_fusion.2), kind=kLoop, calls=%fused_computation.130 | loop fusion | bytes 368640 | tf_op jit(solution)/shard_map/slice | solution.py:16
  225.5 2.7 %copy.103 = f32[240,24,4]{0,1,2:T(8,128)S(1)} copy(f32[240,24,4]{2,0,1:T(8,128)} %get-tuple-element.12) | data formatting | bytes 184320 | tf_op jit(solution)/shard_map/slice | solution.py:16
  228.2 3.6 %collective-permute-start.6 = (f32[240,24,4]{0,1,2:T(8,128)S(1)}, f32[240,24,4]{0,1,2:T(8,128)S(1)}, u32[]{:S(2)}, u32[]{:S(2)}) collective-permute-start(f32[240,24,4]{0,1,2:T(8,128)S(1)} %copy.103), channel_id=1, source_target_pairs={{0,1},{1,2},{2,3},{4,5},{5,6},{6,7},{8,9},{9,10},{10,11},{12,13},{... | collective-permute-start | bytes 276488 | tf_op jit(solution)/shard_map/ppermute | solution.py:15
  231.9 2.7 %copy.104 = f32[240,24,4]{0,1,2:T(8,128)S(1)} copy(f32[240,24,4]{2,0,1:T(8,128)} %get-tuple-element.13) | data formatting | bytes 184320 | tf_op jit(solution)/shard_map/slice | solution.py:18
  234.6 1.9 collective-permute-start.7
  236.6 2.5 copy.105
  239.1 1.5 collective-permute-done.7
  240.6 2.5 copy.106
  243.1 5.4 %pad_maximum_fusion.1 = f32[240,24,136]{2,0,1:T(8,128)S(1)} fusion(f32[240,24,4]{2,0,1:T(8,128)} %copy.106, f32[240,4,128]{2,0,1:T(8,128)S(1)} %collective-permute-done.5, f32[240,16,128]{2,0,1:T(8,128)S(1)} %convert_multiply_fusion.2, f32[240,4,128]{2,0,1:T(8,128)S(1)} %collective-permute-done.4, f32[240,24,4]{2,0,1:T(8,128)} %copy.105), kind=kLoop, calls=%fused_computation.3 | loop fusion | flops 3133440 | bytes 6266880 | tf_op jit(solution)/shard_map/concatenate | solution.py:19
  248.5 9.6 %fusion = f32[240,16,136]{2,0,1:T(8,128)S(1)} fusion(f32[240,24,136]{2,0,1:T(8,128)S(1)} %pad_maximum_fusion.1, f32[]{:T(128)} %bitcast.10, f32[]{:T(128)} %bitcast.9, f32[]{:T(128)} %bitcast.8, f32[]{:T(128)} %bitcast.7, f32[]{:T(128)} %bitcast.6, f32[]{:T(128)} %bitcast.5, f32[]{:T(128)} %bitcast.4, f32[]{:T(128)} %bitcast.3, f32[]{:T(128)} %bitcast.2), kind=kLoop, calls=%fused_computation.5 | loop fusion | flops 8878080 | bytes 20889636 | tf_op jit(solution)/shard_map/add | solution.py:47
  258.1 11.3 %fusion.18 = f32[240,16,128]{2,0,1:T(8,128)S(1)} fusion(f32[]{:T(128)S(6)} %sqrt.8, f32[240,16,136]{2,0,1:T(8,128)S(1)} %fusion, f32[]{:T(128)} %bitcast.10, f32[]{:T(128)} %bitcast.9, f32[]{:T(128)} %bitcast.8, f32[]{:T(128)} %bitcast.7, f32[]{:T(128)} %bitcast.6, f32[]{:T(128)} %bitcast.5, f32[]{:T(128)} %bitcast.4, f32[]{:T(128)} %bitcast.3, f32[]{:T(128)} %bitcast.2), kind=kOutput, calls=%fused_computation.47 | convolution fusion | flops 1424336640 | bytes 19660840 | tf_op jit(solution)/shard_map/dot_general | solution.py:53
  269.5 1.9 copy.109
  (31 shorter events, 0.2 us)
Async XLA Ops:
  0.6 7.9 %copy-start.4 = (s32[32]{0:T(128)S(1)}, s32[32]{0:T(128)}, u32[]{:S(2)}) copy-start(s32[32]{0:T(128)} %param.14) | copy-start | bytes 388
  0.6 16.9 %copy-start.1 = (s32[32,8]{0,1:T(8,128)S(1)}, s32[32,8]{0,1:T(8,128)}, u32[]{:S(2)}) copy-start(s32[32,8]{0,1:T(8,128)} %param.15) | copy-start | bytes 3076
  0.7 33.8 %copy-start.2 = (s32[32,8]{0,1:T(8,128)S(1)}, s32[32,8]{0,1:T(8,128)}, u32[]{:S(2)}) copy-start(s32[32,8]{0,1:T(8,128)} %param.16) | copy-start | bytes 3076
  2.4 52.4 %collective-permute-start = (f32[240,4,128]{2,0,1:T(8,128)S(1)}, f32[240,4,128]{2,0,1:T(8,128)}, u32[]{:S(2)}, u32[]{:S(2)}) collective-permute-start(f32[240,4,128]{2,0,1:T(8,128)S(1)} %copy.131), channel_id=1, source_target_pairs={{0,4},{4,8},{8,12},{12,16},{16,20},{20,24},{24,28},{1,5},{5,9},{9,... | collective-permute-start | bytes 1474568 | tf_op jit(solution)/shard_map/ppermute | solution.py:15
  5.6 52.4 %collective-permute-start.1 = (f32[240,4,128]{2,0,1:T(8,128)S(1)}, f32[240,4,128]{2,0,1:T(8,128)}, u32[]{:S(2)}, u32[]{:S(2)}) collective-permute-start(f32[240,4,128]{2,0,1:T(8,128)S(1)} %copy.132), channel_id=1, source_target_pairs={{4,0},{8,4},{12,8},{16,12},{20,16},{24,20},{28,24},{5,1},{9,5},{13... | collective-permute-start | bytes 1474568 | tf_op jit(solution)/shard_map/ppermute | solution.py:18
  9.2 19.1 %all-to-all-start = ((s32[32,1,1]{2,1,0:T(1,128)}), s32[32,1,1]{2,1,0:T(1,128)S(1)}, u32[]{:S(2)}, u32[]{:S(2)}) async-start(s32[32,1,1]{2,1,0:T(1,128)} %copy.85), calls=%async_computation | async-start | bytes 32768 | tf_op jit(solution)/shard_map/all_to_all | solution.py:80
  28.3 11.7 %all-to-all-start.2 = ((s32[32,1,8]{2,1,0:T(1,128)}), s32[32,1,8]{2,1,0:T(1,128)S(1)}, u32[]{:S(2)}, u32[]{:S(2)}) async-start(s32[32,1,8]{2,1,0:T(1,128)} %bitcast.13), calls=%async_computation.2 | async-start | bytes 32768 | tf_op jit(solution)/shard_map/all_to_all | solution.py:78
  40.0 9.6 %all-to-all-start.3 = ((s32[32,1,8]{2,1,0:T(1,128)}), s32[32,1,8]{2,1,0:T(1,128)S(1)}, u32[]{:S(2)}, u32[]{:S(2)}) async-start(s32[32,1,8]{2,1,0:T(1,128)} %bitcast.15), calls=%async_computation.3 | async-start | bytes 32768 | tf_op jit(solution)/shard_map/all_to_all | solution.py:79
  49.6 79.1 %all-to-all-start.1 = ((bf16[32,8,24,128]{3,2,1,0:T(8,128)(2,1)}), bf16[32,8,24,128]{3,2,1,0:T(8,128)(2,1)}, u32[]{:S(2)}, u32[]{:S(2)}) async-start(bf16[32,8,24,128]{3,2,1,0:T(8,128)(2,1)} %param.13), calls=%async_computation.1 | async-start | bytes 3145728 | tf_op jit(solution)/shard_map/all_to_all | solution.py:77
  65.2 8.1 %collective-permute-start.2 = (f32[240,24,4]{0,1,2:T(8,128)S(1)}, f32[240,24,4]{0,1,2:T(8,128)S(1)}, u32[]{:S(2)}, u32[]{:S(2)}) collective-permute-start(f32[240,24,4]{0,1,2:T(8,128)S(1)} %copy.91), channel_id=1, source_target_pairs={{0,1},{1,2},{2,3},{4,5},{5,6},{6,7},{8,9},{9,10},{10,11},{12,13},{... | collective-permute-start | bytes 276488 | tf_op jit(solution)/shard_map/ppermute | solution.py:15
  71.3 6.6 %collective-permute-start.3 = (f32[240,24,4]{0,1,2:T(8,128)S(1)}, f32[240,24,4]{0,1,2:T(8,128)S(1)}, u32[]{:S(2)}, u32[]{:S(2)}) collective-permute-start(f32[240,24,4]{0,1,2:T(8,128)S(1)} %copy.92), channel_id=1, source_target_pairs={{1,0},{2,1},{3,2},{5,4},{6,5},{7,6},{9,8},{10,9},{11,10},{13,12},{... | collective-permute-start | bytes 276488 | tf_op jit(solution)/shard_map/ppermute | solution.py:18
  85.5 10.0 %copy-start = (bf16[240,16,128]{2,1,0:T(8,128)(2,1)S(1)}, bf16[240,16,128]{2,1,0:T(8,128)(2,1)}, u32[]{:S(2)}) copy-start(bf16[240,16,128]{2,1,0:T(8,128)(2,1)} %param.11) | copy-start | bytes 2949124
  85.5 9.9 %copy-start.8 = (bf16[240,16,128]{2,1,0:T(8,128)(2,1)S(1)}, bf16[240,16,128]{2,1,0:T(8,128)(2,1)}, u32[]{:S(2)}) copy-start(bf16[240,16,128]{2,1,0:T(8,128)(2,1)} %param.10) | copy-start | bytes 2949124
  128.8 8.9 %copy-start.3 = (s32[32,8]{0,1:T(8,128)S(1)}, s32[32,8]{0,1:T(8,128)}, u32[]{:S(2)}) copy-start(s32[32,8]{0,1:T(8,128)} %param.17) | copy-start | bytes 3076
  128.8 20.3 %copy-start.5 = (f32[64]{0:T(128)S(1)}, f32[64]{0:T(128)}, u32[]{:S(2)}) copy-start(f32[64]{0:T(128)} %param.19) | copy-start | bytes 772
  128.8 20.3 %copy-start.6 = (f32[64]{0:T(128)S(1)}, f32[64]{0:T(128)}, u32[]{:S(2)}) copy-start(f32[64]{0:T(128)} %param.18) | copy-start | bytes 772
  132.6 10.6 %all-to-all-start.4 = ((f32[32,1,8]{2,1,0:T(1,128)}), f32[32,1,8]{2,1,0:T(1,128)S(1)}, u32[]{:S(2)}, u32[]{:S(2)}) async-start(f32[32,1,8]{2,1,0:T(1,128)} %bitcast.20), calls=%async_computation.4 | async-start | bytes 32768 | tf_op jit(solution)/shard_map/all_to_all | solution.py:60
  149.1 45.6 %copy-start.7 = (f32[64]{0:T(128)}, f32[64]{0:T(128)S(1)}, u32[]{:S(2)}) copy-start(f32[64]{0:T(128)S(1)} %psum.7) | copy-start | bytes 772
  197.3 24.5 %collective-permute-start.4 = (f32[240,4,128]{2,0,1:T(8,128)S(1)}, f32[240,4,128]{2,0,1:T(8,128)S(1)}, u32[]{:S(2)}, u32[]{:S(2)}) collective-permute-start(f32[240,4,128]{2,0,1:T(8,128)S(1)} %get-tuple-element.16), channel_id=1, source_target_pairs={{0,4},{4,8},{8,12},{12,16},{16,20},{20,24},{24,28},{1,5},{5,9},{9,... | collective-permute-start | bytes 1474568 | tf_op jit(solution)/shard_map/ppermute | solution.py:15
  200.4 21.5 %collective-permute-start.5 = (f32[240,4,128]{2,0,1:T(8,128)S(1)}, f32[240,4,128]{2,0,1:T(8,128)S(1)}, u32[]{:S(2)}, u32[]{:S(2)}) collective-permute-start(f32[240,4,128]{2,0,1:T(8,128)S(1)} %get-tuple-element.17), channel_id=1, source_target_pairs={{4,0},{8,4},{12,8},{16,12},{20,16},{24,20},{28,24},{5,1},{9,5},{13... | collective-permute-start | bytes 1474568 | tf_op jit(solution)/shard_map/ppermute | solution.py:18
  228.2 8.3 %collective-permute-start.6 = (f32[240,24,4]{0,1,2:T(8,128)S(1)}, f32[240,24,4]{0,1,2:T(8,128)S(1)}, u32[]{:S(2)}, u32[]{:S(2)}) collective-permute-start(f32[240,24,4]{0,1,2:T(8,128)S(1)} %copy.103), channel_id=1, source_target_pairs={{0,1},{1,2},{2,3},{4,5},{5,6},{6,7},{8,9},{9,10},{10,11},{12,13},{... | collective-permute-start | bytes 276488 | tf_op jit(solution)/shard_map/ppermute | solution.py:15
  234.6 5.9 %collective-permute-start.7 = (f32[240,24,4]{0,1,2:T(8,128)S(1)}, f32[240,24,4]{0,1,2:T(8,128)S(1)}, u32[]{:S(2)}, u32[]{:S(2)}) collective-permute-start(f32[240,24,4]{0,1,2:T(8,128)S(1)} %copy.104), channel_id=1, source_target_pairs={{1,0},{2,1},{3,2},{5,4},{6,5},{7,6},{9,8},{10,9},{11,10},{13,12},{... | collective-permute-start | bytes 276488 | tf_op jit(solution)/shard_map/ppermute | solution.py:18
where the time goes:
time: 273 us; the launch traced here: 271 us
  other arithmetic  75.4 us (28%)
  local copies, waits for them, and re-layouts  60.5 us (22%)
  starting transfers between devices  49.1 us (18%)
  waiting for transfers between devices  46.2 us (17%)
  matrix products  23 us (8%)
  blocking collectives  14.7 us (5%)
    scatter-add x1, other arithmetic, per_device(): jnp.zeros(flux_rows.shape, jnp.float32).at[flat_index]  34.6 us
    dot_general x2, matrix products, correlate(): jnp.dot(matrix, flat_field, precision=lax.Precision.HIGHEST, preferred_el...  23 us
    gather x1, local copies, waits for them, and re-layouts, per_device(): windows = flux_rows[flat_index].reshape(got_foot.shape)  21 us
    add x2, other arithmetic, correlate(): by_rows = by_rows + spatial[offset] * padded[:, offset:offset + height, :]  19.5 us
    ppermute x4, waiting for transfers between devices, padded_2(): lax.ppermute(lax.slice_in_dim(block, block.shape[dim] - width, None, axis...  19.2 us
    ppermute x4, starting transfers between devices, padded_2(): lax.ppermute(lax.slice_in_dim(block, block.shape[dim] - width, None, axis...  13.2 us
    slice x5, local copies, waits for them, and re-layouts, padded_2(): lax.slice_in_dim(block, block.shape[dim] - width, None, axis=dim)  12.5 us
    concatenate x3, other arithmetic, padded_2(): block = jnp.concatenate([low, block, high], axis=dim)  10.7 us
  transfers between devices with their start and end apart: 13, of which 7 were waited for; matrix products, arithmetic and copies ran while one was open for 28% of the time, Pallas kernels for 0%

commit v1 on v0

v1 whole, which is shorter than its diff:
```python
import numpy as np
import jax
import jax.numpy as jnp
from jax import lax
from jax.experimental import pallas as pl
from jax.experimental.pallas import tpu as pltpu
from jax.sharding import PartitionSpec as P

RAD = 4
TAPS = 12
AXES = ("rec", "tile")
LANES = 128
SUB = 8
VMEM_LIMIT = 56 * 1024 * 1024
F32 = jnp.float32
BF16 = jnp.bfloat16


def space_taps():
    offsets = np.arange(-RAD, RAD + 1).astype(np.float64)
    values = np.exp(-2.0 * offsets * offsets / (RAD * RAD))
    return values / np.sqrt(np.sum(values * values))


def time_taps():
    offsets = np.arange(-TAPS, TAPS + 1).astype(np.float64)
    values = np.exp(-2.0 * np.abs(offsets) / TAPS)
    return values / np.sqrt(np.sum(values * values))


def banded(distance, taps, reach):
    inside = np.abs(distance) <= reach
    return np.where(inside, taps[np.clip(distance, -reach, reach) + reach], 0.0)


def two_parts(matrix):
    high = matrix.astype(np.float32).astype(jnp.bfloat16)
    low = (matrix - high.astype(np.float64)).astype(np.float32).astype(jnp.bfloat16)
    return high, low


def constants(hours, rows, cols):
    space = space_taps()
    hour = np.arange(hours)
    time_high, time_low = two_parts(banded(hour[:, None] - hour[None, :], time_taps(), TAPS))
    col = np.arange(cols)
    col_high, col_low = two_parts(banded(col[:, None] - col[None, :], space, RAD))
    halo_col = np.concatenate([np.arange(-RAD, 0), np.arange(cols, cols + RAD)])
    edge = banded(halo_col[:, None] - col[None, :], space, RAD)
    edge_high, edge_low = two_parts(np.tile(edge, (rows, 1)))
    row_of, halo_of = [], []
    for side in range(2):
        for row in range(rows):
            row_of += [row] * RAD
            halo_of += [side * RAD + j for j in range(RAD)]
    for row_side in range(2):
        for side in range(2):
            for row in range(RAD):
                row_of += [row - RAD if row_side == 0 else rows + row] * RAD
                halo_of += [side * RAD + j for j in range(RAD)]
    row_of, halo_of = np.array(row_of), np.array(halo_of)
    target = np.arange(rows * 2 * RAD)
    gather = banded(row_of[:, None] - (target // (2 * RAD))[None, :], space, RAD)
    gather = np.where(halo_of[:, None] == (target % (2 * RAD))[None, :], gather, 0.0)
    return {
        "time": (time_high, time_low),
        "col": (col_high, col_low),
        "edge": (edge_high, edge_low),
        "gather": gather.astype(np.float32),
    }


def split(value):
    high = value.astype(BF16)
    low = (value - high.astype(F32)).astype(BF16)
    return high, low


def dot(a, b):
    return jnp.dot(a, b, preferred_element_type=F32)


def pack_strips(row_value, parity, rows, strips):
    cols = row_value(0).shape[1]
    lane = lax.broadcasted_iota(jnp.int32, (2 * RAD, cols), 1)
    which = lax.broadcasted_iota(jnp.int32, (2 * RAD, cols), 0)
    first = which < RAD
    j = jnp.where(first, which, which - RAD)
    high_end = jnp.logical_xor(first, parity == 1)
    pick = jnp.where(lane == jnp.where(high_end, cols - RAD + j, j), 1.0, 0.0).astype(BF16)
    pick = jnp.concatenate([pick, pick], axis=1)
    for row in range(rows):
        high, low = split(row_value(row))
        both = jnp.concatenate([high, low], axis=1)
        strips[row] = lax.dot_general(
            pick, both, (((1,), (1,)), ((), ())), preferred_element_type=F32
        )


def write_halos(par_ref, row_value, rows, strips, rows_e, rows_o, cols_e, cols_o, corners):
    rec_parity, tile_parity = par_ref[0], par_ref[1]
    pack_strips(row_value, tile_parity, rows, strips)
    for row in range(rows):
        cols_e[row] = strips[row, 0:RAD, :]
        cols_o[row] = strips[row, RAD : 2 * RAD, :]
    top = rows - RAD

    def send(even_ref, odd_ref, first, last):
        for row in range(RAD):
            rows_e[row] = row_value(first + row)
            rows_o[row] = row_value(last + row)
            for which, source in ((0, first), (1, last)):
                corners[2 * which][row] = strips[source + row, 0:RAD, :]
                corners[2 * which + 1][row] = strips[source + row, RAD : 2 * RAD, :]

    @pl.when(rec_parity == 0)
    def _():
        send(rows_e, rows_o, top, 0)

    @pl.when(rec_parity == 1)
    def _():
        send(rows_e, rows_o, 0, top)


def pack_kernel(par_ref, field_ref, rows_e, rows_o, cols_e, cols_o, c0, c1, c2, c3, strips):
    rows = field_ref.shape[1]
    write_halos(
        par_ref, lambda r: field_ref[:, r, :], rows, strips, rows_e, rows_o, cols_e, cols_o, (c0, c1, c2, c3)
    )


def halo_shapes(hours, rows, cols):
    block = jax.ShapeDtypeStruct((RAD, hours, cols), F32)
    strip = jax.ShapeDtypeStruct((rows, RAD, hours), F32)
    corner = jax.ShapeDtypeStruct((RAD, RAD, hours), F32)
    return [block, block, strip, strip, corner, corner, corner, corner]


def column_halo(par_ref, cols_e, cols_o, corners, gather_ref, strips):
    rec_parity, tile_parity = par_ref[0], par_ref[1]
    rows, _, hours = cols_e.shape
    strips[...] = jnp.zeros_like(strips)
    for row in range(rows):
        even, odd = cols_e[row], cols_o[row]
        strips[row * RAD : (row + 1) * RAD, 0:hours] = jnp.where(tile_parity == 0, odd, even)
        base = (rows + row) * RAD
        strips[base : base + RAD, 0:hours] = jnp.where(tile_parity == 0, even, odd)
    for row in range(RAD):
        by_tile = []
        for a in range(2):
            even, odd = corners[2 * a][row], corners[2 * a + 1][row]
            by_tile.append(
                (jnp.where(tile_parity == 0, odd, even), jnp.where(tile_parity == 0, even, odd))
            )
        for side in range(2):
            prev_rec = jnp.where(rec_parity == 0, by_tile[1][side], by_tile[0][side])
            next_rec = jnp.where(rec_parity == 0, by_tile[0][side], by_tile[1][side])
            base = (2 * rows + side * RAD + row) * RAD
            strips[base : base + RAD, 0:hours] = prev_rec
            base = (2 * rows + (2 + side) * RAD + row) * RAD
            strips[base : base + RAD, 0:hours] = next_rec
    turned = jnp.transpose(strips[...])[0:hours, 0 : gather_ref.shape[0]]
    return jnp.dot(turned, gather_ref[...], precision=lax.Precision.HIGHEST, preferred_element_type=F32)


def edge_weights(row, edge_ref):
    group = lax.broadcasted_iota(jnp.int32, edge_ref.shape, 0) // (2 * RAD)
    return jnp.where(group == row, edge_ref[...].astype(F32), 0.0).astype(BF16)


def column_sums(value, halo_parts, row, col_high, col_low, edge_high, edge_low):
    high, low = split(value)
    out = dot(high, col_high) + dot(low, col_high) + dot(high, col_low)
    if halo_parts is not None:
        halo_high, halo_low = halo_parts
        weights_high, weights_low = edge_weights(row, edge_high), edge_weights(row, edge_low)
        out = out + (dot(halo_high, weights_high) + dot(halo_low, weights_high) + dot(halo_high, weights_low))
    return out


def time_sums(value, time_high, time_low):
    high, low = split(value)
    return dot(time_high, high) + dot(time_high, low) + dot(time_low, high)


def row_sums(get, row, low, high, taps):
    total = None
    for distance in range(RAD + 1):
        here = [get(r) for r in sorted({row - distance, row + distance}) if low <= r < high]
        if not here:
            continue
        part = here[0] if len(here) == 1 else here[0] + here[1]
        part = float(taps[RAD + distance]) * part
        total = part if total is None else total + part
    return total


def flux_kernel(
    par_ref, control_ref, prior_ref, scale_ref, rows_e, rows_o, cols_e, cols_o, c0, c1, c2, c3,
    gather_ref, time_high, time_low, col_high, col_low, edge_high, edge_low,
    flux_ref, scale_out, padded, strips, wide,
):
    hours, rows, cols = control_ref.shape
    taps = space_taps()
    rec_parity = par_ref[0]
    for row in range(RAD):
        even, odd = rows_e[row], rows_o[row]
        padded[row] = jnp.where(rec_parity == 0, odd, even)
        padded[RAD + rows + row] = jnp.where(rec_parity == 0, even, odd)
    for row in range(rows):
        padded[RAD + row] = control_ref[:, row, :]
    halo = split(column_halo(par_ref, cols_e, cols_o, (c0, c1, c2, c3), gather_ref, strips))
    wide[...] = scale_ref[...].astype(F32)
    for row in range(rows):
        scale_out[row] = wide[:, row, :].astype(BF16)
    wide[...] = prior_ref[...].astype(F32)
    for row in range(0, rows, 2):
        pair = []
        for r in (row, row + 1):
            summed = row_sums(lambda i: padded[i], RAD + r, 0, rows + 2 * RAD, taps)
            pair.append(
                column_sums(summed, halo, r, col_high[...], col_low[...], edge_high, edge_low)
            )
        both = time_sums(jnp.concatenate(pair, axis=1), time_high[...], time_low[...])
        for k, r in enumerate((row, row + 1)):
            part = both[:, k * cols : (k + 1) * cols]
            flux_ref[r] = wide[:, r, :] + scale_out[r].astype(F32) * part


def forward_kernel(me_ref, offset_ref, receptor_ref, foot_ref, flux_ref, own_ref, out_ref, sums, *, shift):
    sources, slots, heights, cols = foot_ref.shape
    me = me_ref[0]

    def body(j, carry):
        source = jnp.bitwise_xor(me, j)
        parts = []
        for c in range(slots):
            offset = offset_ref[j * slots + c]
            row = lax.shift_right_logical(offset, shift)
            start = jnp.bitwise_and(offset, (1 << shift) - 1)
            window = flux_ref[row, pl.ds(start, heights), :]
            product = foot_ref[source, c].astype(F32) * window
            parts.append(jnp.sum(product, axis=0, keepdims=True))
        sums[pl.ds(pl.multiple_of(j * slots, slots), slots), :] = jnp.concatenate(parts, axis=0)
        return carry

    lax.fori_loop(0, sources, body, 0)
    value = jnp.sum(sums[...], axis=1, keepdims=True)
    receptor = receptor_ref[...]
    lane = lax.broadcasted_iota(jnp.int32, (sources * slots, LANES), 1)
    groups = out_ref.shape[1] - 1
    for q in range(groups):
        hit = receptor == lane + q * LANES
        total = jnp.sum(jnp.where(hit, value, 0.0), axis=0, keepdims=True)
        out_ref[:, q : q + 1, :] = jnp.broadcast_to(total[None], (sources, 1, LANES))
    out_ref[:, groups : groups + 1, :] = jnp.broadcast_to(own_ref[...][None], (sources, 1, LANES))


def adjoint_kernel(
    me_ref, par_ref, offset_ref, receptor_ref, got_ref, foot_ref, scale_ref,
    model_ref, field_ref, rows_e, rows_o, cols_e, cols_o, c0, c1, c2, c3,
    weight_vmem, weight_smem, strips, sem, *, shift, tiles, per,
):
    sources, slots, heights, cols = foot_ref.shape
    groups = model_ref.shape[0]
    rows = field_ref.shape[0]
    me = me_ref[0]
    model = jnp.sum(got_ref[:, 0:groups, :], axis=0)
    model_ref[...] = model
    packed = LANES // per
    lane = lax.broadcasted_iota(jnp.int32, (1, LANES), 1)
    weight_vmem[...] = jnp.zeros_like(weight_vmem)
    for q in range(groups):
        observed, error = jnp.zeros((1, LANES), F32), jnp.ones((1, LANES), F32)
        for k in range(packed):
            line = got_ref[(q * packed + k) * tiles, groups : groups + 1, :]
            here = (lane >= k * per) & (lane < (k + 1) * per)
            observed = jnp.where(here, line if k == 0 else pltpu.roll(line, k * per, 1), observed)
            turn = (k * per - per) % LANES
            error = jnp.where(here, line if turn == 0 else pltpu.roll(line, turn, 1), error)
        weight_vmem[q : q + 1, :] = (model[q : q + 1, :] - observed) / (error * error)
    copy = pltpu.make_async_copy(weight_vmem, weight_smem, sem)
    copy.start()
    field_ref[...] = jnp.zeros_like(field_ref)
    copy.wait()

    def body(j, carry):
        source = jnp.bitwise_xor(me, j)
        for c in range(slots):
            offset = offset_ref[j * slots + c]
            receptor = receptor_ref[j * slots + c]
            row = lax.shift_right_logical(offset, shift)
            start = jnp.bitwise_and(offset, (1 << shift) - 1)
            weight = weight_smem[lax.shift_right_logical(receptor, 7), jnp.bitwise_and(receptor, LANES - 1)]
            field_ref[row, pl.ds(start, heights), :] += foot_ref[source, c].astype(F32) * weight
        return carry

    lax.fori_loop(0, sources, body, 0)
    for row in range(rows):
        field_ref[row] = field_ref[row] * scale_ref[row].astype(F32)
    write_halos(
        par_ref, lambda r: field_ref[r], rows, strips, rows_e, rows_o, cols_e, cols_o, (c0, c1, c2, c3)
    )


def local_kernel(
    par_ref, field_ref, cols_e, cols_o, c0, c1, c2, c3,
    gather_ref, time_high, time_low, col_high, col_low, edge_high, edge_low, out_ref, strips,
):
    rows, hours, cols = field_ref.shape
    taps = space_taps()
    halo = split(column_halo(par_ref, cols_e, cols_o, (c0, c1, c2, c3), gather_ref, strips))
    for row in range(0, rows, 2):
        pair = []
        for r in (row, row + 1):
            summed = row_sums(lambda i: field_ref[i], r, 0, rows, taps)
            pair.append(
                column_sums(summed, halo, r, col_high[...], col_low[...], edge_high, edge_low)
            )
        both = time_sums(jnp.concatenate(pair, axis=1), time_high[...], time_low[...])
        for k, r in enumerate((row, row + 1)):
            out_ref[r] = both[:, k * cols : (k + 1) * cols]


def finish_kernel(
    par_ref, local_ref, rows_e, rows_o, time_high, time_low, col_high, col_low, out_ref, halo,
):
    rows, hours, cols = local_ref.shape
    taps = space_taps()
    rec_parity = par_ref[0]
    for row in range(RAD):
        even, odd = rows_e[row], rows_o[row]
        halo[row] = jnp.where(rec_parity == 0, odd, even)
        halo[RAD + row] = jnp.where(rec_parity == 0, even, odd)
    edge = list(range(RAD)) + list(range(rows - RAD, rows))
    for row in range(RAD, rows - RAD):
        out_ref[:, row, :] = local_ref[row]
    for first in range(0, 2 * RAD, 2):
        pair = []
        for r in edge[first : first + 2]:
            if r < RAD:
                summed = row_sums(lambda i: halo[i + RAD], r, -RAD, 0, taps)
            else:
                summed = row_sums(lambda i: halo[RAD + i - rows], r, rows, rows + RAD, taps)
            pair.append(column_sums(summed, None, r, col_high[...], col_low[...], None, None))
        both = time_sums(jnp.concatenate(pair, axis=1), time_high[...], time_low[...])
        for k, r in enumerate(edge[first : first + 2]):
            out_ref[:, r, :] = local_ref[r] + both[:, k * cols : (k + 1) * cols]


def swap_pairs(count, odd):
    pairs = []
    for i in range(1 if odd else 0, count - 1, 2):
        pairs += [(i, i + 1), (i + 1, i)]
    return pairs


def swap_halos(parts, n_rec, n_tile):
    rows_e, rows_o, cols_e, cols_o, c0, c1, c2, c3 = parts
    out = [
        lax.ppermute(rows_e, "rec", swap_pairs(n_rec, False)),
        lax.ppermute(rows_o, "rec", swap_pairs(n_rec, True)),
        lax.ppermute(cols_e, "tile", swap_pairs(n_tile, False)),
        lax.ppermute(cols_o, "tile", swap_pairs(n_tile, True)),
    ]
    corner = (c0, c1, c2, c3)
    for a in range(2):
        for b in range(2):
            pairs = [
                (r0 * n_tile + t0, r1 * n_tile + t1)
                for r0, r1 in swap_pairs(n_rec, a == 1)
                for t0, t1 in swap_pairs(n_tile, b == 1)
            ]
            out.append(lax.ppermute(corner[2 * a + b], AXES, pairs))
    return out


def call(kernel, out_shape, in_specs, scratch, name):
    return pl.pallas_call(
        kernel,
        out_shape=out_shape,
        in_specs=in_specs,
        out_specs=jax.tree.map(lambda _: VM, out_shape),
        scratch_shapes=scratch,
        compiler_params=pltpu.CompilerParams(vmem_limit_bytes=VMEM_LIMIT),
        name=name,
    )


SM = pl.BlockSpec(memory_space=pltpu.SMEM)
VM = pl.BlockSpec(memory_space=pltpu.VMEM)


def per_device(
    prior_flux,
    flux_scale,
    control,
    footprint,
    slot_count,
    start_hour,
    grid_row,
    receptor_slot,
    observed,
    obs_error,
):
    hours, rows, cols = control.shape
    n_rec, n_tile = lax.axis_size("rec"), lax.axis_size("tile")
    devices = n_rec * n_tile
    slots = footprint.shape[1]
    per = observed.shape[0]
    receptors = per * n_rec
    groups = receptors // LANES
    shift = (hours - 1).bit_length()
    rec, tile = lax.axis_index("rec"), lax.axis_index("tile")
    me = (rec * n_tile + tile).astype(jnp.int32)
    me_arr = me[None]
    par = jnp.stack([rec % 2, tile % 2]).astype(jnp.int32)
    const = constants(hours, rows, cols)
    time_parts = [jnp.asarray(c) for c in const["time"]]
    col_parts = [jnp.asarray(c) for c in const["col"]]
    edge_parts = [jnp.asarray(c) for c in const["edge"]]
    gather = jnp.asarray(const["gather"])
    n_strips = gather.shape[0]
    strip_scratch = pltpu.VMEM((rows, 2 * RAD, hours), F32)
    turn_scratch = pltpu.VMEM((-(-n_strips // LANES) * LANES, -(-hours // LANES) * LANES), F32)

    foot = lax.all_to_all(footprint, AXES, split_axis=0, concat_axis=0, tiled=True)

    halos = call(
        pack_kernel, halo_shapes(hours, rows, cols), [SM, VM], [strip_scratch], "pack_control"
    )(par, control)
    got = swap_halos(halos, n_rec, n_tile)

    valid = jnp.arange(slots)[None, :] < slot_count[:, None]
    receptor = jnp.where(valid, rec * per + receptor_slot, receptors).astype(jnp.int32)
    offset = (grid_row << shift) + start_hour
    info = jnp.concatenate([offset, receptor], axis=1)[None]
    step = 1
    while step < devices:
        other = lax.ppermute(info, AXES, [(i, i ^ step) for i in range(devices)])
        info = jnp.concatenate([info, other], axis=0)
        step *= 2
    info = lax.dynamic_index_in_dim(info, me, axis=1, keepdims=False)
    offset = info[:, :slots].reshape(-1)
    receptor = info[:, slots:].reshape(-1)

    flux, scale = call(
        flux_kernel,
        [jax.ShapeDtypeStruct((rows, hours, cols), F32), jax.ShapeDtypeStruct((rows, hours, cols), BF16)],
        [SM] + [VM] * 18,
        [pltpu.VMEM((rows + 2 * RAD, hours, cols), F32), turn_scratch, pltpu.VMEM((hours, rows, cols), F32)],
        "flux_field",
    )(par, control, prior_flux, flux_scale, *got, gather, *time_parts, *col_parts, *edge_parts)

    own = jnp.concatenate(
        [observed, obs_error, jnp.zeros((LANES - 2 * per,), F32)]
    )[None]

    def forward(*args):
        return forward_kernel(*args, shift=shift)

    partial = call(
        forward,
        jax.ShapeDtypeStruct((devices, groups + 1, LANES), F32),
        [SM, SM, VM, VM, VM, VM],
        [pltpu.VMEM((devices * slots, LANES), F32)],
        "block_values",
    )(me_arr, offset, receptor[:, None], foot, flux, own)
    everyone = lax.all_to_all(partial, AXES, split_axis=0, concat_axis=0, tiled=True)

    def adjoint(*args):
        return adjoint_kernel(*args, shift=shift, tiles=n_tile, per=per)

    weight_rows = -(-(groups + 1) // SUB) * SUB
    model, field, *halos = call(
        adjoint,
        [jax.ShapeDtypeStruct((groups, LANES), F32), jax.ShapeDtypeStruct((rows, hours, cols), F32)]
        + halo_shapes(hours, rows, cols),
        [SM, SM, SM, SM, VM, VM, VM],
        [
            pltpu.VMEM((weight_rows, LANES), F32),
            pltpu.SMEM((weight_rows, LANES), F32),
            strip_scratch,
            pltpu.SemaphoreType.DMA,
        ],
        "adjoint_field",
    )(me_arr, par, offset, receptor, everyone, foot, scale)
    got = swap_halos(halos, n_rec, n_tile)
    model_co2 = lax.dynamic_slice_in_dim(model.reshape(-1), rec * per, per)

    local = call(
        local_kernel,
        jax.ShapeDtypeStruct((rows, hours, cols), F32),
        [SM] + [VM] * 14,
        [turn_scratch],
        "correlate_local",
    )(par, field, *got[2:], gather, *time_parts, *col_parts, *edge_parts)
    gradient = call(
        finish_kernel,
        jax.ShapeDtypeStruct((hours, rows, cols), F32),
        [SM] + [VM] * 7,
        [pltpu.VMEM((2 * RAD, hours, cols), F32)],
        "correlate_edges",
    )(par, local, got[0], got[1], *time_parts, *col_parts)
    return (model_co2, gradient)


def solution(mesh):
    return jax.shard_map(
        per_device,
        mesh=mesh,
        in_specs=(
            P(None, "rec", "tile"),
            P(None, "rec", "tile"),
            P(None, "rec", "tile"),
            P(("rec", "tile"), None, None, None),
            P(("rec", "tile")),
            P(("rec", "tile"), None),
            P(("rec", "tile"), None),
            P(("rec", "tile"), None),
            P("rec"),
            P("rec"),
        ),
        out_specs=(P("rec"), P(None, "rec", "tile")),
        check_vma=False,
    )
```

time: 273 us -> 180 us (0.66)
  other arithmetic: 75.4 us -> 1.26 us
  local copies, waits for them, and re-layouts: 60.5 us -> 9.52 us
  Pallas kernels: 0 us -> 50.6 us
  matrix products: 23 us -> 0 us
  waiting for transfers between devices: 46.2 us -> 65.5 us
  blocking collectives: 14.7 us -> 0 us
    pallas_call x0 -> x6, Pallas kernels: none -> 50.6 us  [the longest x1 14.7 us: per_device(): call(flux_kernel, [jax.ShapeDtypeStruct((rows, hours, cols), F32), jax.Sh...]
    ppermute x8 -> x21, waiting for transfers between devices: 22.7 us -> 59.3 us  [the longest x5 31 us: per_device(): other = lax.ppermute(info, AXES, [(i, i ^ step) for i in range(devices)])]
    scatter-add x1 -> x0, other arithmetic: 34.6 us -> none  [per_device(): jnp.zeros(flux_rows.shape, jnp.float32).at[flat_index]]
    dot_general x2 -> x0, matrix products: 23 us -> none  [correlate(): jnp.dot(matrix, flat_field, precision=lax.Precision.HIGHEST, preferred_el...]
    gather x1 -> x0, local copies, waits for them, and re-layouts: 21 us -> none  [per_device(): windows = flux_rows[flat_index].reshape(got_foot.shape)]
    slice x9 -> x3, local copies, waits for them, and re-layouts: 20.3 us -> 0.15 us  [the longest x2 0.08 us: per_device(): receptor = info[:, slots:].reshape(-1)]
    add x3 -> x0, other arithmetic: 19.6 us -> none  [the longest x2 19.5 us: correlate(): by_rows = by_rows + spatial[offset] * padded[:, offset:offset + height, :]]
    all_to_all x5 -> x2, waiting for transfers between devices: 23.5 us -> 6.17 us  [the longest x1 6.17 us: per_device(): lax.all_to_all(partial, AXES, split_axis=0, concat_axis=0, tiled=True)]
  transfers between devices with their start and end apart: 13 -> 23, of which waited for: 7 -> 10; matrix products, arithmetic and copies ran while one was open for 28% -> 3% of each run, Pallas kernels for 0% -> 19%
where the time goes in v1:
time: 180 us; the launch traced here: 179 us
  waiting for transfers between devices  65.5 us (36%)
  starting transfers between devices  51.2 us (28%)
  Pallas kernels  50.6 us (28%)
  local copies, waits for them, and re-layouts  9.52 us (5%)
    ppermute x5, waiting for transfers between devices, per_device(): other = lax.ppermute(info, AXES, [(i, i ^ step) for i in range(devices)])  31 us
    ppermute x8, waiting for transfers between devices, swap_halos(): out.append(lax.ppermute(corner[2 * a + b], AXES, pairs))  27.9 us
    ppermute x8, starting transfers between devices, swap_halos(): out.append(lax.ppermute(corner[2 * a + b], AXES, pairs))  17.9 us
    pallas_call x1, Pallas kernels, per_device(): call(flux_kernel, [jax.ShapeDtypeStruct((rows, hours, cols), F32), jax.Sh...  14.7 us
    pallas_call x1, Pallas kernels, per_device(): call(pack_kernel, halo_shapes(hours, rows, cols), [SM, VM], [strip_scratc...  10.1 us
    pallas_call x1, Pallas kernels, per_device(): call(local_kernel, jax.ShapeDtypeStruct((rows, hours, cols), F32), [SM] +...  9.48 us
    ppermute x2, starting transfers between devices, swap_halos(): lax.ppermute(cols_o, 'tile', swap_pairs(n_tile, True))  7.06 us
    all_to_all x1, starting transfers between devices, per_device(): lax.all_to_all(footprint, AXES, split_axis=0, concat_axis=0, tiled=True)  6.42 us
  transfers between devices with their start and end apart: 23, of which 10 were waited for; matrix products, arithmetic and copies ran while one was open for 3% of the time, Pallas kernels for 19%

profile of v1, /device:TPU:5, one launch (start us, length us, event | category | flops | bytes accessed | tf_op | source)
XLA Modules:
  0.0 179.1 jit_solution(13354574436508617735)
XLA Ops:
  0.7 6.4 %all-to-all-start = ((bf16[32,8,24,128]{3,2,1,0:T(8,128)(2,1)}), bf16[32,8,24,128]{3,2,1,0:T(8,128)(2,1)S(1)}, u32[]{:S(2)}, u32[]{:S(2)}) async-start(bf16[32,8,24,128]{3,2,1,0:T(8,128)(2,1)} %param.20), calls=%async_computation | async-start | bytes 3145728 | tf_op jit(solution)/shard_map/all_to_all | solution.py:427
  7.1 0.0 copy-start.22
  7.1 0.0 copy-start.23
  7.2 0.4 collective-permute-start
  7.6 0.6 pad_add_fusion.3.par_ref.args_1_
  8.2 10.1 %pack_control.1 = (f32[4,240,128]{2,1,0:T(8,128)}, f32[4,240,128]{2,1,0:T(8,128)}, f32[16,4,240]{2,1,0:T(4,128)}, f32[16,4,240]{2,1,0:T(4,128)}, f32[4,4,240]{2,...) custom-call(s32[2]{0:T(128)} %pad_add_fusion.3.par_ref.args_1_, ...), custom_call_target="tpu_custom_call" | custom-call | tf_op jit(solution)/shard_map/pack_control/pallas_call | solution.py:429
  18.3 0.1 collective-permute-start.9
  18.4 4.4 %collective-permute-start.10 = (f32[4,4,240]{2,1,0:T(4,128)}, f32[4,4,240]{2,1,0:T(4,128)S(1)}, u32[]{:S(2)}, u32[]{:S(2)}) collective-permute-start(f32[4,4,240]{2,1,0:T(4,128)} %get-tuple-element.27), channel_id=1, source_target_pairs={{1,6},{2,5},{5,2},{6,1},{9,14},{10,13},{13,10},{14,9},{17,22},{18,... | collective-permute-start | bytes 46088 | tf_op jit(solution)/shard_map/ppermute | solution.py:374
  22.8 0.3 collective-permute-start.5
  23.1 4.0 %collective-permute-start.6 = (f32[4,240,128]{2,1,0:T(8,128)}, f32[4,240,128]{2,1,0:T(8,128)S(1)}, u32[]{:S(2)}, u32[]{:S(2)}) collective-permute-start(f32[4,240,128]{2,1,0:T(8,128)} %get-tuple-element.23), channel_id=1, source_target_pairs={{4,8},{8,4},{12,16},{16,12},{20,24},{24,20},{5,9},{9,5},{13,17},{1... | collective-permute-start | bytes 1474568 | tf_op jit(solution)/shard_map/ppermute | solution.py:362
  27.2 0.0 collective-permute-done
  27.2 0.1 collective-permute-start.1
  27.3 3.0 %collective-permute-done.1 = s32[2,32,16]{1,2,0:T(8,128)S(1)} collective-permute-done((s32[2,32,16]{1,2,0:T(8,128)S(1)}, s32[2,32,16]{1,2,0:T(8,128)S(1)}, u32[]{:S(2)}, u32[]{:S(2)}) %collective-permute-start.1) | collective-permute-done | bytes 4128 | tf_op jit(solution)/shard_map/ppermute | solution.py:440
  30.3 20.3 %collective-permute-done.2 = s32[4,32,16]{1,2,0:T(8,128)S(1)} collective-permute-done((s32[4,32,16]{1,2,0:T(8,128)S(1)}, s32[4,32,16]{1,2,0:T(8,128)S(1)}, u32[]{:S(2)}, u32[]{:S(2)}) %collective-permute-start.2) | collective-permute-done | bytes 8224 | tf_op jit(solution)/shard_map/ppermute | solution.py:440
  50.6 1.9 %collective-permute-start.3 = (s32[8,32,16]{1,2,0:T(8,128)S(1)}, s32[8,32,16]{1,2,0:T(8,128)S(1)}, u32[]{:S(2)}, u32[]{:S(2)}) collective-permute-start(s32[8,32,16]{1,2,0:T(8,128)S(1)} %pad_add_fusion), channel_id=1, source_target_pairs={{0,8},{1,9},{2,10},{3,11},{4,12},{5,13},{6,14},{7,15},{8,0},{9,1},... | collective-permute-start | bytes 49160 | tf_op jit(solution)/shard_map/ppermute | solution.py:440
  52.5 1.9 %collective-permute-done.3 = s32[8,32,16]{1,2,0:T(8,128)S(1)} collective-permute-done((s32[8,32,16]{1,2,0:T(8,128)S(1)}, s32[8,32,16]{1,2,0:T(8,128)S(1)}, u32[]{:S(2)}, u32[]{:S(2)}) %collective-permute-start.3) | collective-permute-done | bytes 16416 | tf_op jit(solution)/shard_map/ppermute | solution.py:440
  54.5 2.1 %collective-permute-start.4 = (s32[16,32,16]{1,2,0:T(8,128)S(1)}, s32[16,32,16]{1,2,0:T(8,128)S(1)}, u32[]{:S(2)}, u32[]{:S(2)}) collective-permute-start(s32[16,32,16]{1,2,0:T(8,128)S(1)} %get-tuple-element.42), channel_id=1, source_target_pairs={{0,16},{1,17},{2,18},{3,19},{4,20},{5,21},{6,22},{7,23},{8,24},{9,... | collective-permute-start | bytes 98312 | tf_op jit(solution)/shard_map/ppermute | solution.py:440
  56.6 0.7 maximum_bitcast_fusion.args_5_
  57.2 5.8 %collective-permute-done.4 = s32[16,32,16]{1,2,0:T(8,128)S(1)} collective-permute-done((s32[16,32,16]{1,2,0:T(8,128)S(1)}, s32[16,32,16]{1,2,0:T(8,128)S(1)}, u32[]{:S(2)}, u32[]{:S(2)}) %collective-permute-start.4) | collective-permute-done | bytes 32800 | tf_op jit(solution)/shard_map/ppermute | solution.py:440
  63.0 4.2 %collective-permute-start.11 = (f32[4,4,240]{2,1,0:T(4,128)}, f32[4,4,240]{2,1,0:T(4,128)S(1)}, u32[]{:S(2)}, u32[]{:S(2)}) collective-permute-start(f32[4,4,240]{2,1,0:T(4,128)} %get-tuple-element.28), channel_id=1, source_target_pairs={{4,9},{5,8},{6,11},{7,10},{8,5},{9,4},{10,7},{11,6},{12,17},{13,16... | collective-permute-start | bytes 46088 | tf_op jit(solution)/shard_map/ppermute | solution.py:374
  67.2 0.1 constant_dynamic-slice_fusion
  67.3 0.2 copy.26
  67.5 0.0 collective-permute-done.9.c0
  67.5 1.9 %collective-permute-start.12 = (f32[4,4,240]{2,1,0:T(4,128)}, f32[4,4,240]{2,1,0:T(4,128)S(1)}, u32[]{:S(2)}, u32[]{:S(2)}) collective-permute-start(f32[4,4,240]{2,1,0:T(4,128)} %get-tuple-element.29), channel_id=1, source_target_pairs={{5,10},{6,9},{9,6},{10,5},{13,18},{14,17},{17,14},{18,13},{21,26},... | collective-permute-start | bytes 46088 | tf_op jit(solution)/shard_map/ppermute | solution.py:374
  69.4 0.1 collective-permute-start.7
  69.5 4.7 %collective-permute-start.8 = (f32[16,4,240]{2,1,0:T(4,128)}, f32[16,4,240]{2,1,0:T(4,128)S(1)}, u32[]{:S(2)}, u32[]{:S(2)}) collective-permute-start(f32[16,4,240]{2,1,0:T(4,128)} %get-tuple-element.25), channel_id=1, source_target_pairs={{1,2},{2,1},{5,6},{6,5},{9,10},{10,9},{13,14},{14,13},{17,18},{18,... | collective-permute-start | bytes 184328 | tf_op jit(solution)/shard_map/ppermute | solution.py:364
  74.3 0.1 copy.28
  74.4 0.1 copy.27
  74.4 0.7 reshape.14.args_1_.args_2_
  75.1 0.7 broadcast_in_dim_reshape.4.args_2_
  75.9 0.4 collective-permute-done.8.cols_o
  76.3 0.2 copy-done.14
  76.5 0.0 copy-done.8
  76.5 0.4 copy-done.9
  76.9 0.2 copy-done.2
  77.0 0.8 copy-done.3
  77.8 14.7 %flux_field.1 = (f32[16,240,128]{2,1,0:T(8,128)}, bf16[16,240,128]{2,1,0:T(8,128)(2,1)}) custom-call(s32[2]{0:T(128)} %pad_add_fusion.3.par_ref.args_1_, f32[240,16,128]{2,1,0:T(8,128)} %control_ref.1, bf16[240,16,128]{2,1,0:T(8,128)(2,1)} %prior_ref.1, bf16[240,16,128]{2,1,0:T(8,128)(2,1)} %scale_ref.1, f32[4,240,128]{2,1,0:T(8,128)} %copy-done.2, ...), custom_call_target="tpu_custom_call" | custom-call | tf_op jit(solution)/shard_map/flux_field/pallas_call | solution.py:447
  92.5 1.2 copy-done
  93.7 3.9 %block_values.1 = f32[32,5,128]{2,1,0:T(8,128)} custom-call(s32[1]{0:T(128)} %bitcast.args_0_, s32[256]{0:T(256)} %reshape.14.args_1_.args_2_, s32[256,1]{1,0:T(8,128)} %broadcast_in_dim_reshape.4.args_2_, bf16[32,8,24,128]{3,2,1,0:T(8,128)(2,1)} %copy-done, f32[16,240,128]{2,1,0:T(8,128)} %get-tuple-element.30.args_4_, f32[1,128]{1,0:T(1,128)} %maximum_bitcast_fusion.args_5_), custom_call_target="tpu_custom_call" | custom-call | tf_op jit(solution)/shard_map/block_values/pallas_call | solution.py:462
  97.6 6.2 %all-to-all-start.1 = ((f32[32,5,128]{2,1,0:T(8,128)}), f32[32,5,128]{2,1,0:T(8,128)S(1)}, u32[]{:S(2)}, u32[]{:S(2)}) async-start(f32[32,5,128]{2,1,0:T(8,128)} %block_values.1), calls=%async_computation.1 | async-start | bytes 262144 | tf_op jit(solution)/shard_map/all_to_all | solution.py:469
  103.7 0.7 reshape.15.args_3_
  104.4 6.2 %all-to-all-done.1.args_4_ = f32[32,5,128]{2,1,0:T(8,128)S(1)} async-done(((f32[32,5,128]{2,1,0:T(8,128)}), f32[32,5,128]{2,1,0:T(8,128)S(1)}, u32[]{:S(2)}, u32[]{:S(2)}) %all-to-all-start.1) | async-done | bytes 81952 | tf_op jit(solution)/shard_map/all_to_all | solution.py:469
  110.6 0.7 copy-done.1
  111.3 6.3 %adjoint_field.1 = (f32[4,128]{1,0:T(4,128)}, f32[16,240,128]{2,1,0:T(8,128)}, f32[4,240,128]{2,1,0:T(8,128)}, f32[4,240,128]{2,1,0:T(8,128)}, f32[16,4,240]{2,1...) custom-call(s32[1]{0:T(128)} %bitcast.args_0_, ...), custom_call_target="tpu_custom_call" | custom-call | tf_op jit(solution)/shard_map/adjoint_field/pallas_call | solution.py:475
  117.5 1.4 collective-permute-start.19
  119.0 2.2 %collective-permute-start.20 = (f32[4,240,128]{2,1,0:T(8,128)}, f32[4,240,128]{2,1,0:T(8,128)S(1)}, u32[]{:S(2)}, u32[]{:S(2)}) collective-permute-start(f32[4,240,128]{2,1,0:T(8,128)} %get-tuple-element.41), channel_id=1, source_target_pairs={{4,8},{8,4},{12,16},{16,12},{20,24},{24,20},{5,9},{9,5},{13,17},{1... | collective-permute-start | bytes 1474568 | tf_op jit(solution)/shard_map/ppermute | solution.py:362
  121.1 0.1 collective-permute-start.15
  121.2 1.2 collective-permute-start.13
  122.4 2.3 %collective-permute-start.14 = (f32[16,4,240]{2,1,0:T(4,128)}, f32[16,4,240]{2,1,0:T(4,128)S(1)}, u32[]{:S(2)}, u32[]{:S(2)}) collective-permute-start(f32[16,4,240]{2,1,0:T(4,128)} %get-tuple-element.35), channel_id=1, source_target_pairs={{1,2},{2,1},{5,6},{6,5},{9,10},{10,9},{13,14},{14,13},{17,18},{18,... | collective-permute-start | bytes 184328 | tf_op jit(solution)/shard_map/ppermute | solution.py:364
  124.7 17.0 %collective-permute-done.15.c0 = f32[4,4,240]{2,1,0:T(4,128)S(1)} collective-permute-done((f32[4,4,240]{2,1,0:T(4,128)}, f32[4,4,240]{2,1,0:T(4,128)S(1)}, u32[]{:S(2)}, u32[]{:S(2)}) %collective-permute-start.15) | collective-permute-done | bytes 15392 | tf_op jit(solution)/shard_map/ppermute | solution.py:374
  141.8 1.9 %collective-permute-start.16 = (f32[4,4,240]{2,1,0:T(4,128)}, f32[4,4,240]{2,1,0:T(4,128)S(1)}, u32[]{:S(2)}, u32[]{:S(2)}) collective-permute-start(f32[4,4,240]{2,1,0:T(4,128)} %get-tuple-element.37), channel_id=1, source_target_pairs={{1,6},{2,5},{5,2},{6,1},{9,14},{10,13},{13,10},{14,9},{17,22},{18,... | collective-permute-start | bytes 46088 | tf_op jit(solution)/shard_map/ppermute | solution.py:374
  143.7 4.2 %collective-permute-done.16.c1 = f32[4,4,240]{2,1,0:T(4,128)S(1)} collective-permute-done((f32[4,4,240]{2,1,0:T(4,128)}, f32[4,4,240]{2,1,0:T(4,128)S(1)}, u32[]{:S(2)}, u32[]{:S(2)}) %collective-permute-start.16) | collective-permute-done | bytes 15392 | tf_op jit(solution)/shard_map/ppermute | solution.py:374
  147.9 1.9 %collective-permute-start.17 = (f32[4,4,240]{2,1,0:T(4,128)}, f32[4,4,240]{2,1,0:T(4,128)S(1)}, u32[]{:S(2)}, u32[]{:S(2)}) collective-permute-start(f32[4,4,240]{2,1,0:T(4,128)} %get-tuple-element.38), channel_id=1, source_target_pairs={{4,9},{5,8},{6,11},{7,10},{8,5},{9,4},{10,7},{11,6},{12,17},{13,16... | collective-permute-start | bytes 46088 | tf_op jit(solution)/shard_map/ppermute | solution.py:374
  149.8 4.2 %collective-permute-done.17.c2 = f32[4,4,240]{2,1,0:T(4,128)S(1)} collective-permute-done((f32[4,4,240]{2,1,0:T(4,128)}, f32[4,4,240]{2,1,0:T(4,128)S(1)}, u32[]{:S(2)}, u32[]{:S(2)}) %collective-permute-start.17) | collective-permute-done | bytes 15392 | tf_op jit(solution)/shard_map/ppermute | solution.py:374
  154.1 3.4 %collective-permute-start.18 = (f32[4,4,240]{2,1,0:T(4,128)}, f32[4,4,240]{2,1,0:T(4,128)S(1)}, u32[]{:S(2)}, u32[]{:S(2)}) collective-permute-start(f32[4,4,240]{2,1,0:T(4,128)} %get-tuple-element.39), channel_id=1, source_target_pairs={{5,10},{6,9},{9,6},{10,5},{13,18},{14,17},{17,14},{18,13},{21,26},... | collective-permute-start | bytes 46088 | tf_op jit(solution)/shard_map/ppermute | solution.py:374
  157.4 1.3 dynamic_slice.8
  158.7 2.4 %collective-permute-done.18.c3 = f32[4,4,240]{2,1,0:T(4,128)S(1)} collective-permute-done((f32[4,4,240]{2,1,0:T(4,128)}, f32[4,4,240]{2,1,0:T(4,128)S(1)}, u32[]{:S(2)}, u32[]{:S(2)}) %collective-permute-start.18) | collective-permute-done | bytes 15392 | tf_op jit(solution)/shard_map/ppermute | solution.py:374
  161.2 0.5 copy-done.17
  161.7 0.0 copy-done.6
  161.8 0.0 copy-done.7
  161.8 9.5 %correlate_local.1.local_ref = f32[16,240,128]{2,1,0:T(8,128)} custom-call(s32[2]{0:T(128)} %pad_add_fusion.3.par_ref.args_1_, f32[16,240,128]{2,1,0:T(8,128)} %get-tuple-element.33.field_ref, f32[16,4,240]{2,1,0:T(4,128)} %copy-done.6, f32[16,4,240]{2,1,0:T(4,128)} %copy-done.7, f32[4,4,240]{2,1,0:T(4,128)} %copy-done.13, f32[4,4,240]{2,1,0:T(4,128)} %copy-done.15, ...), custom_call_target="tpu_custom_call" | custom-call | tf_op jit(solution)/shard_map/correlate_local/pallas_call | solution.py:491
  171.3 0.8 copy-done.4
  172.1 0.8 copy-done.5
  172.9 6.2 %correlate_edges.1 = f32[240,16,128]{2,1,0:T(8,128)} custom-call(s32[2]{0:T(128)} %pad_add_fusion.3.par_ref.args_1_, f32[16,240,128]{2,1,0:T(8,128)} %correlate_local.1.local_ref, f32[4,240,128]{2,1,0:T(8,128)} %copy-done.4, f32[4,240,128]{2,1,0:T(8,128)} %copy-done.5, bf16[240,240]{1,0:T(8,128)(2,1)} %constant.54.clone.time_high, ...), custom_call_target="tpu_custom_call" | custom-call | tf_op jit(solution)/shard_map/correlate_edges/pallas_call | solution.py:498
  (58 shorter events, 0.2 us)
Async XLA Ops:
  0.6 6.5 %copy-start.18 = (s32[32,8]{0,1:T(8,128)S(1)}, s32[32,8]{0,1:T(8,128)}, u32[]{:S(2)}) copy-start(s32[32,8]{0,1:T(8,128)} %param.24) | copy-start | bytes 3076
  0.6 6.5 %copy-start.20 = (s32[32,8]{0,1:T(8,128)S(1)}, s32[32,8]{0,1:T(8,128)}, u32[]{:S(2)}) copy-start(s32[32,8]{0,1:T(8,128)} %param.23) | copy-start | bytes 3076
  0.7 6.5 %copy-start.19 = (s32[32,8]{0,1:T(8,128)S(1)}, s32[32,8]{0,1:T(8,128)}, u32[]{:S(2)}) copy-start(s32[32,8]{0,1:T(8,128)} %param.22) | copy-start | bytes 3076
  0.7 6.5 %copy-start.21 = (s32[32]{0:T(128)S(1)}, s32[32]{0:T(128)}, u32[]{:S(2)}) copy-start(s32[32]{0:T(128)} %param.21) | copy-start | bytes 388
  0.7 91.8 %all-to-all-start = ((bf16[32,8,24,128]{3,2,1,0:T(8,128)(2,1)}), bf16[32,8,24,128]{3,2,1,0:T(8,128)(2,1)S(1)}, u32[]{:S(2)}, u32[]{:S(2)}) async-start(bf16[32,8,24,128]{3,2,1,0:T(8,128)(2,1)} %param.20), calls=%async_computation | async-start | bytes 3145728 | tf_op jit(solution)/shard_map/all_to_all | solution.py:427
  7.1 49.5 %copy-start.22 = (f32[64]{0:T(128)S(1)}, f32[64]{0:T(128)}, u32[]{:S(2)}) copy-start(f32[64]{0:T(128)} %param.26) | copy-start | bytes 772
  7.1 49.4 %copy-start.23 = (f32[64]{0:T(128)S(1)}, f32[64]{0:T(128)}, u32[]{:S(2)}) copy-start(f32[64]{0:T(128)} %param.25) | copy-start | bytes 772
  7.2 20.0 %collective-permute-start = (s32[1,32,16]{1,2,0:T(8,128)S(1)}, s32[1,32,16]{1,2,0:T(8,128)S(1)}, u32[]{:S(2)}, u32[]{:S(2)}) collective-permute-start(s32[1,32,16]{1,2,0:T(8,128)S(1)} %add_bitcast_fusion), channel_id=1, source_target_pairs={{0,1},{1,0},{2,3},{3,2},{4,5},{5,4},{6,7},{7,6},{8,9},{9,8},{10,11... | collective-permute-start | bytes 6152 | tf_op jit(solution)/shard_map/ppermute | solution.py:440
  18.3 49.2 %collective-permute-start.9 = (f32[4,4,240]{2,1,0:T(4,128)}, f32[4,4,240]{2,1,0:T(4,128)S(1)}, u32[]{:S(2)}, u32[]{:S(2)}) collective-permute-start(f32[4,4,240]{2,1,0:T(4,128)} %get-tuple-element.26), channel_id=1, source_target_pairs={{0,5},{1,4},{2,7},{3,6},{4,1},{5,0},{6,3},{7,2},{8,13},{9,12},{10,... | collective-permute-start | bytes 46088 | tf_op jit(solution)/shard_map/ppermute | solution.py:374
  18.4 51.1 %collective-permute-start.10 = (f32[4,4,240]{2,1,0:T(4,128)}, f32[4,4,240]{2,1,0:T(4,128)S(1)}, u32[]{:S(2)}, u32[]{:S(2)}) collective-permute-start(f32[4,4,240]{2,1,0:T(4,128)} %get-tuple-element.27), channel_id=1, source_target_pairs={{1,6},{2,5},{5,2},{6,1},{9,14},{10,13},{13,10},{14,9},{17,22},{18,... | collective-permute-start | bytes 46088 | tf_op jit(solution)/shard_map/ppermute | solution.py:374
  22.8 53.4 %collective-permute-start.5 = (f32[4,240,128]{2,1,0:T(8,128)}, f32[4,240,128]{2,1,0:T(8,128)S(1)}, u32[]{:S(2)}, u32[]{:S(2)}) collective-permute-start(f32[4,240,128]{2,1,0:T(8,128)} %get-tuple-element.22), channel_id=1, source_target_pairs={{0,4},{4,0},{8,12},{12,8},{16,20},{20,16},{24,28},{28,24},{1,5},{5... | collective-permute-start | bytes 1474568 | tf_op jit(solution)/shard_map/ppermute | solution.py:361
  23.1 53.1 %collective-permute-start.6 = (f32[4,240,128]{2,1,0:T(8,128)}, f32[4,240,128]{2,1,0:T(8,128)S(1)}, u32[]{:S(2)}, u32[]{:S(2)}) collective-permute-start(f32[4,240,128]{2,1,0:T(8,128)} %get-tuple-element.23), channel_id=1, source_target_pairs={{4,8},{8,4},{12,16},{16,12},{20,24},{24,20},{5,9},{9,5},{13,17},{1... | collective-permute-start | bytes 1474568 | tf_op jit(solution)/shard_map/ppermute | solution.py:362
  27.2 3.1 %collective-permute-start.1 = (s32[2,32,16]{1,2,0:T(8,128)S(1)}, s32[2,32,16]{1,2,0:T(8,128)S(1)}, u32[]{:S(2)}, u32[]{:S(2)}) collective-permute-start(s32[2,32,16]{1,2,0:T(8,128)S(1)} %pad_add_fusion.2), channel_id=1, source_target_pairs={{0,2},{1,3},{2,0},{3,1},{4,6},{5,7},{6,4},{7,5},{8,10},{9,11},{10,... | collective-permute-start | bytes 12296 | tf_op jit(solution)/shard_map/ppermute | solution.py:440
  30.3 20.3 %collective-permute-start.2 = (s32[4,32,16]{1,2,0:T(8,128)S(1)}, s32[4,32,16]{1,2,0:T(8,128)S(1)}, u32[]{:S(2)}, u32[]{:S(2)}) collective-permute-start(s32[4,32,16]{1,2,0:T(8,128)S(1)} %pad_add_fusion.1), channel_id=1, source_target_pairs={{0,4},{1,5},{2,6},{3,7},{4,0},{5,1},{6,2},{7,3},{8,12},{9,13},{10,... | collective-permute-start | bytes 24584 | tf_op jit(solution)/shard_map/ppermute | solution.py:440
  50.6 3.9 %collective-permute-start.3 = (s32[8,32,16]{1,2,0:T(8,128)S(1)}, s32[8,32,16]{1,2,0:T(8,128)S(1)}, u32[]{:S(2)}, u32[]{:S(2)}) collective-permute-start(s32[8,32,16]{1,2,0:T(8,128)S(1)} %pad_add_fusion), channel_id=1, source_target_pairs={{0,8},{1,9},{2,10},{3,11},{4,12},{5,13},{6,14},{7,15},{8,0},{9,1},... | collective-permute-start | bytes 49160 | tf_op jit(solution)/shard_map/ppermute | solution.py:440
  54.5 8.5 %collective-permute-start.4 = (s32[16,32,16]{1,2,0:T(8,128)S(1)}, s32[16,32,16]{1,2,0:T(8,128)S(1)}, u32[]{:S(2)}, u32[]{:S(2)}) collective-permute-start(s32[16,32,16]{1,2,0:T(8,128)S(1)} %get-tuple-element.42), channel_id=1, source_target_pairs={{0,16},{1,17},{2,18},{3,19},{4,20},{5,21},{6,22},{7,23},{8,24},{9,... | collective-permute-start | bytes 98312 | tf_op jit(solution)/shard_map/ppermute | solution.py:440
  63.0 6.6 %collective-permute-start.11 = (f32[4,4,240]{2,1,0:T(4,128)}, f32[4,4,240]{2,1,0:T(4,128)S(1)}, u32[]{:S(2)}, u32[]{:S(2)}) collective-permute-start(f32[4,4,240]{2,1,0:T(4,128)} %get-tuple-element.28), channel_id=1, source_target_pairs={{4,9},{5,8},{6,11},{7,10},{8,5},{9,4},{10,7},{11,6},{12,17},{13,16... | collective-permute-start | bytes 46088 | tf_op jit(solution)/shard_map/ppermute | solution.py:374
  67.5 8.7 %copy-start.10 = (f32[4,4,240]{2,1,0:T(4,128)}, f32[4,4,240]{2,1,0:T(4,128)S(1)}, u32[]{:S(2)}) copy-start(f32[4,4,240]{2,1,0:T(4,128)S(1)} %collective-permute-done.9.c0) | copy-start | bytes 46084
  67.5 8.3 %collective-permute-start.12 = (f32[4,4,240]{2,1,0:T(4,128)}, f32[4,4,240]{2,1,0:T(4,128)S(1)}, u32[]{:S(2)}, u32[]{:S(2)}) collective-permute-start(f32[4,4,240]{2,1,0:T(4,128)} %get-tuple-element.29), channel_id=1, source_target_pairs={{5,10},{6,9},{9,6},{10,5},{13,18},{14,17},{17,14},{18,13},{21,26},... | collective-permute-start | bytes 46088 | tf_op jit(solution)/shard_map/ppermute | solution.py:374
  69.4 6.8 %copy-start.11 = (f32[4,4,240]{2,1,0:T(4,128)}, f32[4,4,240]{2,1,0:T(4,128)S(1)}, u32[]{:S(2)}) copy-start(f32[4,4,240]{2,1,0:T(4,128)S(1)} %collective-permute-done.10.c1) | copy-start | bytes 46084
  69.4 6.4 %collective-permute-start.7 = (f32[16,4,240]{2,1,0:T(4,128)}, f32[16,4,240]{2,1,0:T(4,128)S(1)}, u32[]{:S(2)}, u32[]{:S(2)}) collective-permute-start(f32[16,4,240]{2,1,0:T(4,128)} %get-tuple-element.24), channel_id=1, source_target_pairs={{0,1},{1,0},{2,3},{3,2},{4,5},{5,4},{6,7},{7,6},{8,9},{9,8},{10,11... | collective-permute-start | bytes 184328 | tf_op jit(solution)/shard_map/ppermute | solution.py:363
  69.5 6.7 %copy-start.12 = (f32[4,4,240]{2,1,0:T(4,128)}, f32[4,4,240]{2,1,0:T(4,128)S(1)}, u32[]{:S(2)}) copy-start(f32[4,4,240]{2,1,0:T(4,128)S(1)} %collective-permute-done.11.c2) | copy-start | bytes 46084
  69.5 6.7 %collective-permute-start.8 = (f32[16,4,240]{2,1,0:T(4,128)}, f32[16,4,240]{2,1,0:T(4,128)S(1)}, u32[]{:S(2)}, u32[]{:S(2)}) collective-permute-start(f32[16,4,240]{2,1,0:T(4,128)} %get-tuple-element.25), channel_id=1, source_target_pairs={{1,2},{2,1},{5,6},{6,5},{9,10},{10,9},{13,14},{14,13},{17,18},{18,... | collective-permute-start | bytes 184328 | tf_op jit(solution)/shard_map/ppermute | solution.py:364
  75.9 0.6 copy-start.14
  75.9 0.6 copy-start.8
  76.2 0.6 copy-start.9
  76.2 0.8 copy-start.2
  77.0 0.8 copy-start.3
  92.5 1.2 copy-start
  97.6 13.0 %all-to-all-start.1 = ((f32[32,5,128]{2,1,0:T(8,128)}), f32[32,5,128]{2,1,0:T(8,128)S(1)}, u32[]{:S(2)}, u32[]{:S(2)}) async-start(f32[32,5,128]{2,1,0:T(8,128)} %block_values.1), calls=%async_computation.1 | async-start | bytes 262144 | tf_op jit(solution)/shard_map/all_to_all | solution.py:469
  110.6 0.7 copy-start.1
  117.5 53.8 %collective-permute-start.19 = (f32[4,240,128]{2,1,0:T(8,128)}, f32[4,240,128]{2,1,0:T(8,128)S(1)}, u32[]{:S(2)}, u32[]{:S(2)}) collective-permute-start(f32[4,240,128]{2,1,0:T(8,128)} %get-tuple-element.40), channel_id=1, source_target_pairs={{0,4},{4,0},{8,12},{12,8},{16,20},{20,16},{24,28},{28,24},{1,5},{5... | collective-permute-start | bytes 1474568 | tf_op jit(solution)/shard_map/ppermute | solution.py:361
  119.0 52.3 %collective-permute-start.20 = (f32[4,240,128]{2,1,0:T(8,128)}, f32[4,240,128]{2,1,0:T(8,128)S(1)}, u32[]{:S(2)}, u32[]{:S(2)}) collective-permute-start(f32[4,240,128]{2,1,0:T(8,128)} %get-tuple-element.41), channel_id=1, source_target_pairs={{4,8},{8,4},{12,16},{16,12},{20,24},{24,20},{5,9},{9,5},{13,17},{1... | collective-permute-start | bytes 1474568 | tf_op jit(solution)/shard_map/ppermute | solution.py:362
  121.1 20.6 %collective-permute-start.15 = (f32[4,4,240]{2,1,0:T(4,128)}, f32[4,4,240]{2,1,0:T(4,128)S(1)}, u32[]{:S(2)}, u32[]{:S(2)}) collective-permute-start(f32[4,4,240]{2,1,0:T(4,128)} %get-tuple-element.36), channel_id=1, source_target_pairs={{0,5},{1,4},{2,7},{3,6},{4,1},{5,0},{6,3},{7,2},{8,13},{9,12},{10,... | collective-permute-start | bytes 46088 | tf_op jit(solution)/shard_map/ppermute | solution.py:374
  121.2 39.9 %collective-permute-start.13 = (f32[16,4,240]{2,1,0:T(4,128)}, f32[16,4,240]{2,1,0:T(4,128)S(1)}, u32[]{:S(2)}, u32[]{:S(2)}) collective-permute-start(f32[16,4,240]{2,1,0:T(4,128)} %get-tuple-element.34), channel_id=1, source_target_pairs={{0,1},{1,0},{2,3},{3,2},{4,5},{5,4},{6,7},{7,6},{8,9},{9,8},{10,11... | collective-permute-start | bytes 184328 | tf_op jit(solution)/shard_map/ppermute | solution.py:363
  122.4 38.7 %collective-permute-start.14 = (f32[16,4,240]{2,1,0:T(4,128)}, f32[16,4,240]{2,1,0:T(4,128)S(1)}, u32[]{:S(2)}, u32[]{:S(2)}) collective-permute-start(f32[16,4,240]{2,1,0:T(4,128)} %get-tuple-element.35), channel_id=1, source_target_pairs={{1,2},{2,1},{5,6},{6,5},{9,10},{10,9},{13,14},{14,13},{17,18},{18,... | collective-permute-start | bytes 184328 | tf_op jit(solution)/shard_map/ppermute | solution.py:364
  141.8 19.4 %copy-start.13 = (f32[4,4,240]{2,1,0:T(4,128)}, f32[4,4,240]{2,1,0:T(4,128)S(1)}, u32[]{:S(2)}) copy-start(f32[4,4,240]{2,1,0:T(4,128)S(1)} %collective-permute-done.15.c0) | copy-start | bytes 46084
  141.8 6.2 %collective-permute-start.16 = (f32[4,4,240]{2,1,0:T(4,128)}, f32[4,4,240]{2,1,0:T(4,128)S(1)}, u32[]{:S(2)}, u32[]{:S(2)}) collective-permute-start(f32[4,4,240]{2,1,0:T(4,128)} %get-tuple-element.37), channel_id=1, source_target_pairs={{1,6},{2,5},{5,2},{6,1},{9,14},{10,13},{13,10},{14,9},{17,22},{18,... | collective-permute-start | bytes 46088 | tf_op jit(solution)/shard_map/ppermute | solution.py:374
  147.9 13.3 %copy-start.15 = (f32[4,4,240]{2,1,0:T(4,128)}, f32[4,4,240]{2,1,0:T(4,128)S(1)}, u32[]{:S(2)}) copy-start(f32[4,4,240]{2,1,0:T(4,128)S(1)} %collective-permute-done.16.c1) | copy-start | bytes 46084
  147.9 6.2 %collective-permute-start.17 = (f32[4,4,240]{2,1,0:T(4,128)}, f32[4,4,240]{2,1,0:T(4,128)S(1)}, u32[]{:S(2)}, u32[]{:S(2)}) collective-permute-start(f32[4,4,240]{2,1,0:T(4,128)} %get-tuple-element.38), channel_id=1, source_target_pairs={{4,9},{5,8},{6,11},{7,10},{8,5},{9,4},{10,7},{11,6},{12,17},{13,16... | collective-permute-start | bytes 46088 | tf_op jit(solution)/shard_map/ppermute | solution.py:374
  154.1 7.1 %copy-start.16 = (f32[4,4,240]{2,1,0:T(4,128)}, f32[4,4,240]{2,1,0:T(4,128)S(1)}, u32[]{:S(2)}) copy-start(f32[4,4,240]{2,1,0:T(4,128)S(1)} %collective-permute-done.17.c2) | copy-start | bytes 46084
  154.1 7.1 %collective-permute-start.18 = (f32[4,4,240]{2,1,0:T(4,128)}, f32[4,4,240]{2,1,0:T(4,128)S(1)}, u32[]{:S(2)}, u32[]{:S(2)}) collective-permute-start(f32[4,4,240]{2,1,0:T(4,128)} %get-tuple-element.39), channel_id=1, source_target_pairs={{5,10},{6,9},{9,6},{10,5},{13,18},{14,17},{17,14},{18,13},{21,26},... | collective-permute-start | bytes 46088 | tf_op jit(solution)/shard_map/ppermute | solution.py:374
  161.1 0.6 copy-start.17
  161.1 0.6 copy-start.6
  161.1 0.7 copy-start.7
  171.3 0.8 copy-start.4
  172.1 0.8 copy-start.5

commit v2 on v0

v2 whole, which is shorter than its diff:
```python
import numpy as np
import jax
import jax.numpy as jnp
from jax import lax
from jax.experimental import pallas as pl
from jax.experimental.pallas import tpu as pltpu
from jax.sharding import PartitionSpec as P

RAD = 4
TAPS = 12
AXES = ("rec", "tile")
LANES = 128
SUB = 8
FOOT_MAX = 0.02
SCALE_MAX = 2.0
HALF_TOP = 32768.0
F16 = jnp.float16
VMEM_LIMIT = 12 * 1024 * 1024
F32 = jnp.float32
BF16 = jnp.bfloat16


def space_taps():
    offsets = np.arange(-RAD, RAD + 1).astype(np.float64)
    values = np.exp(-2.0 * offsets * offsets / (RAD * RAD))
    return values / np.sqrt(np.sum(values * values))


def time_taps():
    offsets = np.arange(-TAPS, TAPS + 1).astype(np.float64)
    values = np.exp(-2.0 * np.abs(offsets) / TAPS)
    return values / np.sqrt(np.sum(values * values))


def banded(distance, taps, reach):
    inside = np.abs(distance) <= reach
    return np.where(inside, taps[np.clip(distance, -reach, reach) + reach], 0.0)


def two_parts(matrix):
    high = matrix.astype(np.float32).astype(jnp.bfloat16)
    low = (matrix - high.astype(np.float64)).astype(np.float32).astype(jnp.bfloat16)
    return high, low


def constants(hours, rows, cols):
    space = space_taps()
    hour = np.arange(hours)
    time_high, time_low = two_parts(banded(hour[:, None] - hour[None, :], time_taps(), TAPS))
    col = np.arange(cols)
    col_high, col_low = two_parts(banded(col[:, None] - col[None, :], space, RAD))
    col_both = np.block([[col_high, col_low], [col_high, np.zeros_like(col_high)]])
    halo_col = np.concatenate([np.arange(-RAD, 0), np.arange(cols, cols + RAD)])
    edge = banded(halo_col[:, None] - col[None, :], space, RAD)

    def strips(row_of, halo_of, targets):
        by_row = banded(np.array(row_of)[:, None] - np.array(targets)[None, :], space, RAD)
        both = by_row[:, :, None] * edge[np.array(halo_of)][:, None, :]
        return two_parts(both.reshape(len(row_of), -1))

    own = [(row, side * RAD + j) for side in range(2) for row in range(rows) for j in range(RAD)]
    corner = [
        (row, side * RAD + j)
        for first in (-RAD, rows)
        for side in range(2)
        for row in range(first, first + RAD)
        for j in range(RAD)
    ]
    corner += [(-100, 0)] * (LANES - len(corner))
    edge_rows = list(range(RAD)) + list(range(rows - RAD, rows))
    own_parts = strips(*zip(*own), np.arange(rows))
    corner_parts = strips(*zip(*corner), np.array(edge_rows))
    return (time_high, time_low, col_both), own_parts, corner_parts


def split(value):
    high = value.astype(BF16)
    low = (value - high.astype(F32)).astype(BF16)
    return high, low


def dot(a, b):
    return jnp.dot(a, b, preferred_element_type=F32)


def lane_ids(shape):
    return lax.broadcasted_iota(jnp.int32, shape, 1)


def choose(flag, yes, no):
    return jnp.where(flag, yes, no)


def pack_strips(row_value, parity, rows):
    cols = row_value(0).shape[1]
    half = rows * RAD
    source = lax.broadcasted_iota(jnp.int32, (cols, 2 * half), 0)
    lane = lax.broadcasted_iota(jnp.int32, (cols, 2 * half), 1)
    first = lane < half
    j = lane & (RAD - 1)
    high_end = jnp.logical_xor(first, parity == 1)
    wanted = jnp.where(high_end, cols - RAD + j, j)
    lane_row = jnp.where(first, lane, lane - half) // RAD
    total = None
    for row in range(rows):
        high, low = split(row_value(row))
        pick = jnp.where((source == wanted) & (lane_row == row), 1.0, 0.0).astype(BF16)
        part = dot(jnp.concatenate([high, low], axis=1), jnp.concatenate([pick, pick], axis=0))
        total = part if total is None else total + part
    return total


def fold_hours(value, hours, strip_e, strip_o):
    fold = strip_e.shape[0]
    half = LANES // 2
    early = value[0:fold]
    late = jnp.concatenate([value[fold:hours], jnp.zeros((2 * fold - hours, LANES), F32)], axis=0)
    left = lane_ids((fold, LANES)) < half
    strip_e[...] = choose(left, early, pltpu.roll(late, half, 1))
    strip_o[...] = choose(left, pltpu.roll(early, half, 1), late)


def write_rows(parity, row_value, rows, rows_e, rows_o):
    top = rows - RAD

    def send(first, last):
        for row in range(RAD):
            rows_e[row] = row_value(first + row)
            rows_o[row] = row_value(last + row)

    @pl.when(parity == 0)
    def _():
        send(top, 0)

    @pl.when(parity == 1)
    def _():
        send(0, top)


def pack_kernel(par_ref, control_ref, field_ref, rows_e, rows_o, strip_e, strip_o):
    hours, rows, _ = control_ref.shape
    for row in range(rows):
        field_ref[row] = control_ref[:, row, :]
    write_rows(par_ref[0], lambda r: field_ref[r], rows, rows_e, rows_o)
    fold_hours(pack_strips(lambda r: field_ref[r], par_ref[1], rows), hours, strip_e, strip_o)


def corner_kernel(par_ref, strip_e, strip_o, halo_ref, corner_e, corner_o):
    fold = strip_e.shape[0]
    quarter = corner_e.shape[0]
    half = LANES // 2
    part = RAD * RAD
    even, odd = strip_e[...], strip_o[...]
    is_even = par_ref[1] == 0
    prev, following = choose(is_even, odd, even), choose(is_even, even, odd)
    left = lane_ids((fold, LANES)) < half
    halo_ref[0:fold] = choose(left, prev, pltpu.roll(following, half, 1))
    halo_ref[fold : 2 * fold] = choose(left, pltpu.roll(prev, half, 1), following)
    lane = lane_ids((quarter, LANES))
    low = high = jnp.zeros((quarter, LANES), F32)
    for q in range(LANES // (2 * part)):
        piece = halo_ref[q * quarter : (q + 1) * quarter]
        base = q * 2 * part
        for side in range(2):
            here = (lane >= base + side * part) & (lane < base + (side + 1) * part)
            to = base + side * part
            low = choose(here, pltpu.roll(piece, (to - side * half) % LANES, 1), low)
            high = choose(here, pltpu.roll(piece, (to - side * half - (half - part)) % LANES, 1), high)
    rec_even = par_ref[0] == 0
    corner_e[...] = choose(rec_even, high, low)
    corner_o[...] = choose(rec_even, low, high)


def corner_strips(is_even, corner_e, corner_o):
    part = 2 * RAD * RAD
    prev = choose(is_even, corner_o[...], corner_e[...])
    following = choose(is_even, corner_e[...], corner_o[...])
    lane = lane_ids(prev.shape)
    pieces = []
    for q in range(LANES // part):
        a = prev if q == 0 else pltpu.roll(prev, LANES - q * part, 1)
        turn = (part - q * part) % LANES
        b = following if turn == 0 else pltpu.roll(following, turn, 1)
        pieces.append(choose(lane < part, a, choose(lane < 2 * part, b, 0.0)))
    return jnp.concatenate(pieces, axis=0)


def halo_sums(parts, high_ref, low_ref, first, width):
    high, both = parts
    weights = high_ref[:, first : first + width]
    return dot(both, jnp.concatenate([weights, weights], axis=0)) + dot(high, low_ref[:, first : first + width])


def halo_parts(value):
    high, low = split(value)
    return high, jnp.concatenate([high, low], axis=1)


def column_sums(value, col_both):
    cols = value.shape[1]
    high, low = split(value)
    out = dot(jnp.concatenate([high, low], axis=1), col_both)
    return out[:, :cols] + out[:, cols:]


def time_sums(value, time_high, time_low):
    high, low = split(value)
    return dot(time_high, high) + dot(time_high, low) + dot(time_low, high)


def row_sums(get, row, low, high, taps):
    total = None
    for distance in range(RAD + 1):
        here = [get(r) for r in sorted({row - distance, row + distance}) if low <= r < high]
        if not here:
            continue
        part = here[0] if len(here) == 1 else here[0] + here[1]
        part = float(taps[RAD + distance]) * part
        total = part if total is None else total + part
    return total


def local_kernel(field_ref, halo_ref, time_high, time_low, col_both, own_high, own_low, out_ref, *, by_hour):
    rows, hours, cols = field_ref.shape
    taps = space_taps()
    halo = halo_parts(halo_ref[0:hours, :])
    for row in range(0, rows, 2):
        pair = [
            column_sums(row_sums(lambda i: field_ref[i], r, 0, rows, taps), col_both[...])
            for r in (row, row + 1)
        ]
        value = jnp.concatenate(pair, axis=1) + halo_sums(halo, own_high, own_low, row * cols, 2 * cols)
        both = time_sums(value, time_high[...], time_low[...])
        for k, r in enumerate((row, row + 1)):
            part = both[:, k * cols : (k + 1) * cols]
            if by_hour:
                out_ref[:, r, :] = part
            else:
                out_ref[r] = part


def edge_parts(is_even, rows, got_e, got_o, corner_e, corner_o, consts, halo, factor):
    time_high, time_low, col_both, corner_high, corner_low = consts
    hours, cols = halo.shape[1:]
    taps = space_taps()
    for row in range(RAD):
        even, odd = got_e[row].astype(F32), got_o[row].astype(F32)
        if factor is not None:
            even, odd = even * factor, odd * factor
        halo[row] = choose(is_even, odd, even)
        halo[RAD + row] = choose(is_even, even, odd)
    corner = halo_parts(corner_strips(is_even, corner_e, corner_o)[0:hours])
    edge = list(range(RAD)) + list(range(rows - RAD, rows))
    for first in range(0, 2 * RAD, 2):
        pair = []
        for r in edge[first : first + 2]:
            if r < RAD:
                summed = row_sums(lambda i: halo[i + RAD], r, -RAD, 0, taps)
            else:
                summed = row_sums(lambda i: halo[RAD + i - rows], r, rows, rows + RAD, taps)
            pair.append(column_sums(summed, col_both[...]))
        value = jnp.concatenate(pair, axis=1)
        value = value + halo_sums(corner, corner_high, corner_low, first * cols, 2 * cols)
        both = time_sums(value, time_high[...], time_low[...])
        for k, r in enumerate(edge[first : first + 2]):
            yield r, both[:, k * cols : (k + 1) * cols]


def flux_kernel(
    par_ref, local_ref, prior_ref, scale_ref, got_e, got_o, corner_e, corner_o,
    time_high, time_low, col_both, corner_high, corner_low, flux_ref, scale_out, halo, wide,
):
    rows, hours, cols = local_ref.shape
    consts = (time_high, time_low, col_both, corner_high, corner_low)
    wide[...] = scale_ref[...].astype(F32)
    for row in range(rows):
        scale_out[row] = wide[:, row, :]
    wide[...] = prior_ref[...].astype(F32)
    for row in range(RAD, rows - RAD):
        flux_ref[row] = wide[:, row, :] + scale_out[row] * local_ref[row]
    parts = edge_parts(par_ref[0] == 0, rows, got_e, got_o, corner_e, corner_o, consts, halo, None)
    for row, part in parts:
        flux_ref[row] = wide[:, row, :] + scale_out[row] * (local_ref[row] + part)


def finish_kernel(
    par_ref, local_ref, factor_ref, got_e, got_o, corner_e, corner_o,
    time_high, time_low, col_both, corner_high, corner_low, out_ref, halo,
):
    hours, rows, cols = local_ref.shape
    consts = (time_high, time_low, col_both, corner_high, corner_low)
    out_ref[...] = local_ref[...]
    factor = factor_ref[1:2, :]
    parts = edge_parts(par_ref[0] == 0, rows, got_e, got_o, corner_e, corner_o, consts, halo, factor)
    for row, part in parts:
        out_ref[:, row, :] = out_ref[:, row, :] + part


def blocks_of(foot_ref, source, heights, slots):
    for c in range(0, slots, 2):
        both = foot_ref[source, c * heights : (c + 2) * heights, :].astype(F32)
        yield c, both[0:heights]
        yield c + 1, both[heights : 2 * heights]


def forward_kernel(
    foot_ref, flux_ref, own_ref, out_ref, table_ref, sums, table_smem, sem,
    *, shift, slots, heights, tiles, per,
):
    sources = foot_ref.shape[0]
    groups = out_ref.shape[1] - 1
    base = slots * heights
    lane = lane_ids((sources, LANES))
    notes = foot_ref[:, base : base + SUB, :].astype(F32)[:, 0, :].astype(jnp.int32)
    start = notes * 16 + pltpu.roll(notes, LANES - slots, 1)
    offset = start + pltpu.roll(notes, LANES - 2 * slots, 1) * (1 << shift)
    source_rec = lax.broadcasted_iota(jnp.int32, (sources, LANES), 0) // tiles
    receptor = jnp.where(notes < per, source_rec * per + notes, groups * LANES)
    table = jnp.where(lane < slots, offset, receptor)
    table_ref[...] = table
    copy = pltpu.make_async_copy(table_ref, table_smem, sem)
    copy.start()
    copy.wait()

    def body(source, carry):
        for c, block in blocks_of(foot_ref, source, heights, slots):
            offset = table_smem[source, c]
            row = lax.shift_right_logical(offset, shift)
            begin = jnp.bitwise_and(offset, (1 << shift) - 1)
            product = flux_ref[row, pl.ds(begin, heights), :] * block
            sums[c, pl.ds(source, 1), :] = jnp.sum(product, axis=0, keepdims=True)
        return carry

    lax.fori_loop(0, sources, body, 0)
    totals = [jnp.zeros((sources, LANES), F32) for _ in range(groups)]
    for c in range(slots):
        value = jnp.sum(sums[c], axis=1, keepdims=True)
        which = table[:, 3 * slots + c : 3 * slots + c + 1]
        for q in range(groups):
            totals[q] = totals[q] + jnp.where(which == lane + q * LANES, value, 0.0)
    for q in range(groups):
        total = jnp.sum(totals[q], axis=0, keepdims=True)
        out_ref[:, q : q + 1, :] = jnp.broadcast_to(total[None], (sources, 1, LANES))
    out_ref[:, groups : groups + 1, :] = jnp.broadcast_to(own_ref[...][None], (sources, 1, LANES))


def adjoint_kernel(
    par_ref, table_ref, got_ref, foot_ref, scale_ref,
    model_ref, factor_ref, field_ref, rows_e, rows_o, strip_e, strip_o,
    weight_vmem, weight_smem, sem, *, shift, slots, heights, tiles, per,
):
    sources = foot_ref.shape[0]
    groups = model_ref.shape[0]
    rows, hours, _ = field_ref.shape
    model = jnp.sum(got_ref[:, 0:groups, :], axis=0)
    model_ref[...] = model
    packed = LANES // per
    lane = lane_ids((1, LANES))
    weight_vmem[...] = jnp.zeros_like(weight_vmem)
    for q in range(groups):
        observed, error = jnp.zeros((1, LANES), F32), jnp.ones((1, LANES), F32)
        for k in range(packed):
            line = got_ref[(q * packed + k) * tiles, groups : groups + 1, :]
            here = (lane >= k * per) & (lane < (k + 1) * per)
            observed = jnp.where(here, line if k == 0 else pltpu.roll(line, k * per, 1), observed)
            turn = (k * per - per) % LANES
            error = jnp.where(here, line if turn == 0 else pltpu.roll(line, turn, 1), error)
        weight_vmem[q : q + 1, :] = (model[q : q + 1, :] - observed) / (error * error)
    copy = pltpu.make_async_copy(weight_vmem, weight_smem, sem)
    copy.start()
    field_ref[...] = jnp.zeros_like(field_ref)
    top = jnp.max(jnp.abs(weight_vmem[...]), keepdims=True) * (FOOT_MAX * SCALE_MAX * sources * slots)
    top = jnp.maximum(top, 1e-25)
    factor_ref[0:1, :] = jnp.broadcast_to(HALF_TOP / top, (1, LANES))
    factor_ref[1:2, :] = jnp.broadcast_to(top * (1.0 / HALF_TOP), (1, LANES))
    copy.wait()

    def body(source, carry):
        for c, block in blocks_of(foot_ref, source, heights, slots):
            offset = table_ref[source, c]
            receptor = table_ref[source, 3 * slots + c]
            row = lax.shift_right_logical(offset, shift)
            begin = jnp.bitwise_and(offset, (1 << shift) - 1)
            weight = weight_smem[lax.shift_right_logical(receptor, 7), jnp.bitwise_and(receptor, LANES - 1)]
            field_ref[row, pl.ds(begin, heights), :] += block * weight
        return carry

    lax.fori_loop(0, sources, body, 0)
    for row in range(rows):
        field_ref[row] = field_ref[row] * scale_ref[row]
    factor = factor_ref[0:1, :]
    write_rows(par_ref[0], lambda r: field_ref[r] * factor, rows, rows_e, rows_o)
    fold_hours(pack_strips(lambda r: field_ref[r], par_ref[1], rows), hours, strip_e, strip_o)


def swap_pairs(count, odd):
    pairs = []
    for i in range(1 if odd else 0, count - 1, 2):
        pairs += [(i, i + 1), (i + 1, i)]
    return pairs


def swap(axis, even, odd):
    count = lax.axis_size(axis)
    return (
        lax.ppermute(even, axis, swap_pairs(count, False)),
        lax.ppermute(odd, axis, swap_pairs(count, True)),
    )


SM = pl.BlockSpec(memory_space=pltpu.SMEM)
VM = pl.BlockSpec(memory_space=pltpu.VMEM)


def call(kernel, out_shape, in_specs, scratch, name):
    return pl.pallas_call(
        kernel,
        out_shape=out_shape,
        in_specs=in_specs,
        out_specs=jax.tree.map(lambda _: VM, out_shape),
        scratch_shapes=scratch,
        compiler_params=pltpu.CompilerParams(vmem_limit_bytes=VMEM_LIMIT),
        name=name,
    )


def array(*shape):
    return jax.ShapeDtypeStruct(shape, F32)


def per_device(
    prior_flux,
    flux_scale,
    control,
    footprint,
    slot_count,
    start_hour,
    grid_row,
    receptor_slot,
    observed,
    obs_error,
):
    hours, rows, cols = control.shape
    n_rec, n_tile = lax.axis_size("rec"), lax.axis_size("tile")
    devices = n_rec * n_tile
    slots, heights = footprint.shape[1], footprint.shape[2]
    per = observed.shape[0]
    groups = per * n_rec // LANES
    shift = (hours - 1).bit_length()
    rec, tile = lax.axis_index("rec"), lax.axis_index("tile")
    par = jnp.stack([rec % 2, tile % 2]).astype(jnp.int32)
    base, own_parts, corner_parts = constants(hours, rows, cols)
    base = [jnp.asarray(c) for c in base]
    own_parts = [jnp.asarray(c) for c in own_parts]
    corner_parts = [jnp.asarray(c) for c in corner_parts]
    fold = -(-hours // (2 * 64)) * 64
    strip, corner = array(fold, LANES), array(fold // 2, LANES)
    block = array(RAD, hours, cols)
    field_shape = array(rows, hours, cols)
    halo_scratch = pltpu.VMEM((2 * RAD, hours, cols), F32)

    valid = jnp.arange(slots)[None, :] < slot_count[:, None]
    notes = jnp.concatenate(
        [start_hour >> 4, start_hour & 15, grid_row, jnp.where(valid, receptor_slot, per)], axis=1
    ).astype(BF16)
    notes = jnp.pad(notes, ((0, 0), (0, LANES - 4 * slots)))[:, None, :]
    notes = jnp.pad(notes, ((0, 0), (0, SUB - 1), (0, 0)))
    sent = jnp.concatenate([footprint.reshape(devices, slots * heights, cols), notes], axis=1)
    foot = lax.all_to_all(sent, AXES, split_axis=0, concat_axis=0, tiled=True)

    field, rows_e, rows_o, strip_e, strip_o = call(
        pack_kernel, [field_shape, block, block, strip, strip], [SM, VM], [], "pack_control"
    )(par, control)

    def neighbours(rows_e, rows_o, strip_e, strip_o):
        got_rows = swap("rec", rows_e, rows_o)
        got_strips = swap("tile", strip_e, strip_o)
        halo, corner_e, corner_o = call(
            corner_kernel, [array(2 * fold, LANES), corner, corner], [SM, VM, VM], [], "corners"
        )(par, *got_strips)
        return got_rows, halo, swap("rec", corner_e, corner_o)

    def local_sums(field, halo, by_hour, name):
        def kernel(*refs):
            local_kernel(*refs, by_hour=by_hour)

        shape = array(hours, rows, cols) if by_hour else field_shape
        return call(kernel, shape, [VM] * 7, [], name)(field, halo, *base, *own_parts)

    got_rows, halo, got_corners = neighbours(rows_e, rows_o, strip_e, strip_o)
    local = local_sums(field, halo, False, "control_local")
    flux, scale = call(
        flux_kernel,
        [field_shape, field_shape],
        [SM] + [VM] * 12,
        [halo_scratch, pltpu.VMEM((hours, rows, cols), F32)],
        "flux_field",
    )(par, local, prior_flux, flux_scale, *got_rows, *got_corners, *base, *corner_parts)

    own = jnp.concatenate([observed, obs_error, jnp.zeros((LANES - 2 * per,), F32)])[None]
    sizes = dict(shift=shift, slots=slots, heights=heights, tiles=n_tile, per=per)

    def forward(*refs):
        forward_kernel(*refs, **sizes)

    partial, table = call(
        forward,
        [array(devices, groups + 1, LANES), jax.ShapeDtypeStruct((devices, LANES), jnp.int32)],
        [VM, VM, VM],
        [
            pltpu.VMEM((slots, devices, LANES), F32),
            pltpu.SMEM((devices, LANES), jnp.int32),
            pltpu.SemaphoreType.DMA,
        ],
        "block_values",
    )(foot, flux, own)
    everyone = lax.all_to_all(partial, AXES, split_axis=0, concat_axis=0, tiled=True)

    def adjoint(*refs):
        adjoint_kernel(*refs, **sizes)

    weight_rows = -(-(groups + 1) // SUB) * SUB
    model, factor, field, rows_e, rows_o, strip_e, strip_o = call(
        adjoint,
        [array(groups, LANES), array(2, LANES), field_shape, block, block, strip, strip],
        [SM, SM, VM, VM, VM],
        [
            pltpu.VMEM((weight_rows, LANES), F32),
            pltpu.SMEM((weight_rows, LANES), F32),
            pltpu.SemaphoreType.DMA,
        ],
        "adjoint_field",
    )(par, table, everyone, foot, scale)
    got_rows, halo, got_corners = neighbours(rows_e.astype(F16), rows_o.astype(F16), strip_e, strip_o)
    got_rows = [r.astype(F32) for r in got_rows]
    local = local_sums(field, halo, True, "gradient_local")
    gradient = call(
        finish_kernel, array(hours, rows, cols), [SM] + [VM] * 11, [halo_scratch], "gradient"
    )(par, local, factor, *got_rows, *got_corners, *base, *corner_parts)
    model_co2 = lax.dynamic_slice_in_dim(model.reshape(-1), rec * per, per)
    return (model_co2, gradient)


def solution(mesh):
    return jax.shard_map(
        per_device,
        mesh=mesh,
        in_specs=(
            P(None, "rec", "tile"),
            P(None, "rec", "tile"),
            P(None, "rec", "tile"),
            P(("rec", "tile"), None, None, None),
            P(("rec", "tile")),
            P(("rec", "tile"), None),
            P(("rec", "tile"), None),
            P(("rec", "tile"), None),
            P("rec"),
            P("rec"),
        ),
        out_specs=(P("rec"), P(None, "rec", "tile")),
        check_vma=False,
    )
```

time: 273 us -> 116 us (0.42)
  other arithmetic: 75.4 us -> 4.39 us
  local copies, waits for them, and re-layouts: 60.5 us -> 9.36 us
  Pallas kernels: 0 us -> 28.3 us
  matrix products: 23 us -> 0 us
  starting transfers between devices: 49.1 us -> 28.1 us
  waiting for transfers between devices: 46.2 us -> 25.4 us
  blocking collectives: 14.7 us -> 18.9 us
    scatter-add x1 -> x0, other arithmetic: 34.6 us -> none  [per_device(): jnp.zeros(flux_rows.shape, jnp.float32).at[flat_index]]
    pallas_call x0 -> x9, Pallas kernels: none -> 28.3 us  [the longest x2 8.53 us: local_sums(): call(kernel, shape, [VM] * 7, [], name)(field, halo, *base, *own_parts)]
    all_to_all x5 -> x1, waiting for transfers between devices: 23.5 us -> 0.01 us  [per_device(): foot = lax.all_to_all(sent, AXES, split_axis=0, concat_axis=0, tiled=True)]
    dot_general x2 -> x0, matrix products: 23 us -> none  [correlate(): jnp.dot(matrix, flat_field, precision=lax.Precision.HIGHEST, preferred_el...]
    gather x1 -> x0, local copies, waits for them, and re-layouts: 21 us -> none  [per_device(): windows = flux_rows[flat_index].reshape(got_foot.shape)]
    all_to_all x5 -> x1, starting transfers between devices: 26.9 us -> 6.42 us  [per_device(): foot = lax.all_to_all(sent, AXES, split_axis=0, concat_axis=0, tiled=True)]
    slice x9 -> x0, local copies, waits for them, and re-layouts: 20.3 us -> none  [the longest x5 12.5 us: padded_2(): lax.slice_in_dim(block, block.shape[dim] - width, None, axis=dim)]
    add x3 -> x0, other arithmetic: 19.6 us -> none  [the longest x2 19.5 us: correlate(): by_rows = by_rows + spatial[offset] * padded[:, offset:offset + height, :]]
  transfers between devices with their start and end apart: 13 -> 13, of which waited for: 7 -> 3; matrix products, arithmetic and copies ran while one was open for 28% -> 1% of each run, Pallas kernels for 0% -> 15%
where the time goes in v2:
time: 116 us; the launch traced here: 115 us
  Pallas kernels  28.3 us (24%)
  starting transfers between devices  28.1 us (24%)
  waiting for transfers between devices  25.4 us (22%)
  blocking collectives  18.9 us (16%)
  local copies, waits for them, and re-layouts  9.36 us (8%)
  other arithmetic  4.39 us (4%)
    all_to_all x1, blocking collectives, per_device(): lax.all_to_all(partial, AXES, split_axis=0, concat_axis=0, tiled=True)  18.9 us
    ppermute x6, starting transfers between devices, swap(): lax.ppermute(odd, axis, swap_pairs(count, True))  17.7 us
    ppermute x6, waiting for transfers between devices, swap(): lax.ppermute(even, axis, swap_pairs(count, False))  16.7 us
    unnamed x38, local copies, waits for them, and re-layouts  8.68 us
    ppermute x6, waiting for transfers between devices, swap(): lax.ppermute(odd, axis, swap_pairs(count, True))  8.63 us
    pallas_call x2, Pallas kernels, local_sums(): call(kernel, shape, [VM] * 7, [], name)(field, halo, *base, *own_parts)  8.53 us
    all_to_all x1, starting transfers between devices, per_device(): foot = lax.all_to_all(sent, AXES, split_axis=0, concat_axis=0, tiled=True)  6.42 us
    pallas_call x1, Pallas kernels, per_device(): call(flux_kernel, [field_shape, field_shape], [SM] + [VM] * 12, [halo_scr...  4.96 us
  transfers between devices with their start and end apart: 13, of which 3 were waited for; matrix products, arithmetic and copies ran while one was open for 1% of the time, Pallas kernels for 15%

profile of v2, /device:TPU:5, one launch (start us, length us, event | category | flops | bytes accessed | tf_op | source)
XLA Modules:
  0.0 115.4 jit_solution(6568220101014926423)
XLA Ops:
  0.6 0.7 convert.14
  1.3 0.7 shift-right-arithmetic_convert_fusion
  2.0 0.1 copy.29
  2.1 2.7 %fusion.1 = bf16[32,200,128]{2,1,0:T(8,128)(2,1)} fusion(bf16[32,1,128]{2,1,0:T(2,128)(2,1)S(1)} %copy.29, bf16[32,192,128]{2,1,0:T(8,128)(2,1)} %bitcast.9), kind=kLoop, calls=%fused_computation.2 | loop fusion | flops 4915200 | bytes 3219456 | tf_op jit(solution)/shard_map/concatenate | solution.py:468
  4.8 0.0 copy-start.2
  4.9 0.0 copy-start.6
  4.9 0.0 copy-start.7
  4.9 6.4 %all-to-all-start = ((bf16[32,200,128]{2,1,0:T(8,128)(2,1)}), bf16[32,200,128]{2,1,0:T(8,128)(2,1)S(1)}, u32[]{:S(2)}, u32[]{:S(2)}) async-start(bf16[32,200,128]{2,1,0:T(8,128)(2,1)} %fusion.1), calls=%async_computation | async-start | bytes 3276800 | tf_op jit(solution)/shard_map/all_to_all | solution.py:469
  11.3 0.1 pad_add_fusion.par_ref.refs_0_
  11.4 1.5 %copy-done.3 = f32[240,16,128]{2,1,0:T(8,128)S(1)} copy-done((f32[240,16,128]{2,1,0:T(8,128)S(1)}, f32[240,16,128]{2,1,0:T(8,128)}, u32[]{:S(2)}) %copy-start.3) | copy-done | bytes 1966104
  12.9 2.4 %pack_control.1 = (f32[16,240,128]{2,1,0:T(8,128)S(1)}, f32[4,240,128]{2,1,0:T(8,128)S(1)}, f32[4,240,128]{2,1,0:T(8,128)S(1)}, f32[128,128]{1,0:T(8,128)S(1)}, f32[128,128]{1,0:T(8,128)S(1)}) custom-call(s32[2]{0:T(128)S(1)} %pad_add_fusion.par_ref.refs_0_, f32[240,16,128]{2,1,0:T(8,128)S(1)} %copy-done.3), custom_call_target="tpu_custom_call" | custom-call | tf_op jit(solution)/shard_map/pack_control/pallas_call | solution.py:471
  15.3 0.1 collective-permute-start.2
  15.5 4.2 %collective-permute-start.3 = (f32[4,240,128]{2,1,0:T(8,128)S(1)}, f32[4,240,128]{2,1,0:T(8,128)S(1)}, u32[]{:S(2)}, u32[]{:S(2)}) collective-permute-start(f32[4,240,128]{2,1,0:T(8,128)S(1)} %get-tuple-element.29), channel_id=1, source_target_pairs={{4,8},{8,4},{12,16},{16,12},{20,24},{24,20},{5,9},{9,5},{13,17},{1... | collective-permute-start | bytes 1474568 | tf_op jit(solution)/shard_map/ppermute | solution.py:407
  19.7 1.0 collective-permute-start
  20.6 3.0 %collective-permute-start.1 = (f32[128,128]{1,0:T(8,128)S(1)}, f32[128,128]{1,0:T(8,128)S(1)}, u32[]{:S(2)}, u32[]{:S(2)}) collective-permute-start(f32[128,128]{1,0:T(8,128)S(1)} %get-tuple-element.26), channel_id=1, source_target_pairs={{1,2},{2,1},{5,6},{6,5},{9,10},{10,9},{13,14},{14,13},{17,18},{18,... | collective-permute-start | bytes 196616 | tf_op jit(solution)/shard_map/ppermute | solution.py:407
  23.6 0.0 collective-permute-done.strip_e
  23.7 5.1 %collective-permute-done.1.strip_o = f32[128,128]{1,0:T(8,128)S(1)} collective-permute-done((f32[128,128]{1,0:T(8,128)S(1)}, f32[128,128]{1,0:T(8,128)S(1)}, u32[]{:S(2)}, u32[]{:S(2)}) %collective-permute-start.1) | collective-permute-done | bytes 65568 | tf_op jit(solution)/shard_map/ppermute | solution.py:407
  28.8 0.8 corners.2
  29.5 0.1 collective-permute-start.4
  29.6 2.1 %collective-permute-start.5 = (f32[64,128]{1,0:T(8,128)S(1)}, f32[64,128]{1,0:T(8,128)S(1)}, u32[]{:S(2)}, u32[]{:S(2)}) collective-permute-start(f32[64,128]{1,0:T(8,128)S(1)} %get-tuple-element.31), channel_id=1, source_target_pairs={{4,8},{8,4},{12,16},{16,12},{20,24},{24,20},{5,9},{9,5},{13,17},{1... | collective-permute-start | bytes 98312 | tf_op jit(solution)/shard_map/ppermute | solution.py:407
  31.7 0.0 copy-done.17
  31.7 0.0 copy-done.18
  31.7 0.1 maximum_bitcast_fusion.refs_2_
  31.8 0.0 copy-done
  31.8 0.0 copy-done.1
  31.8 0.0 copy-done.2
  31.8 0.0 copy-done.6
  31.8 0.0 copy-done.7
  31.8 0.0 copy-start.12
  31.9 0.0 copy-start.13
  31.9 0.0 copy-start.15
  31.9 0.0 copy-start.16
  31.9 3.8 %control_local.1.local_ref = f32[16,240,128]{2,1,0:T(8,128)S(1)} custom-call(f32[16,240,128]{2,1,0:T(8,128)S(1)} %get-tuple-element.24.refs_0_, f32[256,128]{1,0:T(8,128)S(1)} %get-tuple-element.27.refs_1_, bf16[240,240]{1,0:T(8,128)(2,1)S(1)} %copy-done.6, bf16[240,240]{1,0:T(8,128)(2,1)S(1)} %copy-done.7, bf16[256,256]{1,0:T(8,128)(2,1)S(1)} %copy-done, ...), custom_call_target="tpu_custom_call" | custom-call | tf_op jit(solution)/shard_map/control_local/pallas_call | solution.py:488
  35.7 16.7 %collective-permute-done.4.corner_e = f32[64,128]{1,0:T(8,128)S(1)} collective-permute-done((f32[64,128]{1,0:T(8,128)S(1)}, f32[64,128]{1,0:T(8,128)S(1)}, u32[]{:S(2)}, u32[]{:S(2)}) %collective-permute-start.4) | collective-permute-done | bytes 32800 | tf_op jit(solution)/shard_map/ppermute | solution.py:406
  52.5 0.0 collective-permute-done.5.corner_o
  52.5 0.0 collective-permute-done.2.got_e
  52.5 0.0 collective-permute-done.3.got_o
  52.5 5.0 %flux_field.1 = (f32[16,240,128]{2,1,0:T(8,128)S(1)}, f32[16,240,128]{2,1,0:T(8,128)S(1)}) custom-call(s32[2]{0:T(128)S(1)} %pad_add_fusion.par_ref.refs_0_, f32[16,240,128]{2,1,0:T(8,128)S(1)} %control_local.1.local_ref, bf16[240,16,128]{2,1,0:T(8,128)(2,1)S(1)} %copy-done.15, bf16[240,16,128]{2,1,0:T(8,128)(2,1)S(1)} %copy-done.16, ...), custom_call_target="tpu_custom_call" | custom-call | tf_op jit(solution)/shard_map/flux_field/pallas_call | solution.py:492
  57.5 1.3 %copy-done.4 = f32[16,240,128]{2,1,0:T(8,128)} copy-done((f32[16,240,128]{2,1,0:T(8,128)}, f32[16,240,128]{2,1,0:T(8,128)S(1)}, u32[]{:S(2)}) %copy-start.4) | copy-done | bytes 1966104
  58.8 1.3 %copy-done.8 = f32[16,240,128]{2,1,0:T(8,128)} copy-done((f32[16,240,128]{2,1,0:T(8,128)}, f32[16,240,128]{2,1,0:T(8,128)S(1)}, u32[]{:S(2)}) %copy-start.8) | copy-done | bytes 1966104
  60.1 0.0 all-to-all-done.refs_0_.refs_3_
  60.1 1.7 %copy-done.9 = f32[16,240,128]{2,1,0:T(8,128)S(1)} copy-done((f32[16,240,128]{2,1,0:T(8,128)S(1)}, f32[16,240,128]{2,1,0:T(8,128)}, u32[]{:S(2)}) %copy-start.9) | copy-done | bytes 1966104
  61.8 2.2 %block_values.1 = (f32[32,5,128]{2,1,0:T(8,128)S(1)}, s32[32,128]{1,0:T(8,128)S(1)}) custom-call(bf16[32,200,128]{2,1,0:T(8,128)(2,1)S(1)} %all-to-all-done.refs_0_.refs_3_, f32[16,240,128]{2,1,0:T(8,128)S(1)} %copy-done.9, f32[1,128]{1,0:T(1,128)S(1)} %maximum_bitcast_fusion.refs_2_), custom_call_target="tpu_custom_call" | custom-call | tf_op jit(solution)/shard_map/block_values/pallas_call | solution.py:506
  64.0 18.9 %all_to_all.10.refs_2_ = f32[32,5,128]{2,1,0:T(8,128)S(1)} all-to-all(f32[32,5,128]{2,1,0:T(8,128)S(1)} %get-tuple-element.34), channel_id=1, replica_groups=mesh['rec'=8,'tile'=4] {'rec','tile'}, dimensions={0} | all-to-all | bytes 163840 | tf_op jit(solution)/shard_map/all_to_all | solution.py:517
  82.9 4.1 %adjoint_field.1 = (f32[4,128]{1,0:T(4,128)S(1)}, f32[2,128]{1,0:T(2,128)S(1)}, f32[16,240,128]{2,1,0:T(8,128)S(1)}, f32[4,240,128]{2,1,0:T(8,128)S(1)}, f32[4,2...) custom-call(s32[2]{0:T(128)S(1)} %pad_add_fusion.par_ref.refs_0_, ...), custom_call_target="tpu_custom_call" | custom-call | tf_op jit(solution)/shard_map/adjoint_field/pallas_call | solution.py:523
  86.9 0.0 copy-start.10
  86.9 1.3 %copy-done.10 = f32[16,240,128]{2,1,0:T(8,128)} copy-done((f32[16,240,128]{2,1,0:T(8,128)}, f32[16,240,128]{2,1,0:T(8,128)S(1)}, u32[]{:S(2)}) %copy-start.10) | copy-done | bytes 1966104
  88.2 1.5 %collective-permute-start.8 = (f16[4,240,128]{2,1,0:T(8,128)(2,1)S(1)}, f16[4,240,128]{2,1,0:T(8,128)(2,1)S(1)}, u32[]{:S(2)}, u32[]{:S(2)}) collective-permute-start(f16[4,240,128]{2,1,0:T(8,128)(2,1)S(1)} %convert_element_type.17), channel_id=1, source_target_pairs={{0,4},{4,0},{8,12},{12,8},{16,20},{20,16},{24,28},{28,24},{1,5},{5... | collective-permute-start | bytes 737288 | tf_op jit(solution)/shard_map/ppermute | solution.py:406
  89.8 2.3 %collective-permute-start.9 = (f16[4,240,128]{2,1,0:T(8,128)(2,1)S(1)}, f16[4,240,128]{2,1,0:T(8,128)(2,1)S(1)}, u32[]{:S(2)}, u32[]{:S(2)}) collective-permute-start(f16[4,240,128]{2,1,0:T(8,128)(2,1)S(1)} %convert_element_type.19), channel_id=1, source_target_pairs={{4,8},{8,4},{12,16},{16,12},{20,24},{24,20},{5,9},{9,5},{13,17},{1... | collective-permute-start | bytes 737288 | tf_op jit(solution)/shard_map/ppermute | solution.py:407
  92.1 1.2 %collective-permute-start.6 = (f32[128,128]{1,0:T(8,128)S(1)}, f32[128,128]{1,0:T(8,128)S(1)}, u32[]{:S(2)}, u32[]{:S(2)}) collective-permute-start(f32[128,128]{1,0:T(8,128)S(1)} %get-tuple-element.38), channel_id=1, source_target_pairs={{0,1},{1,0},{2,3},{3,2},{4,5},{5,4},{6,7},{7,6},{8,9},{9,8},{10,11... | collective-permute-start | bytes 196616 | tf_op jit(solution)/shard_map/ppermute | solution.py:406
  93.3 2.3 %collective-permute-start.7 = (f32[128,128]{1,0:T(8,128)S(1)}, f32[128,128]{1,0:T(8,128)S(1)}, u32[]{:S(2)}, u32[]{:S(2)}) collective-permute-start(f32[128,128]{1,0:T(8,128)S(1)} %get-tuple-element.39), channel_id=1, source_target_pairs={{1,2},{2,1},{5,6},{6,5},{9,10},{10,9},{13,14},{14,13},{17,18},{18,... | collective-permute-start | bytes 196616 | tf_op jit(solution)/shard_map/ppermute | solution.py:407
  95.6 0.0 collective-permute-done.6.strip_e
  95.6 3.5 %collective-permute-done.7.strip_o = f32[128,128]{1,0:T(8,128)S(1)} collective-permute-done((f32[128,128]{1,0:T(8,128)S(1)}, f32[128,128]{1,0:T(8,128)S(1)}, u32[]{:S(2)}, u32[]{:S(2)}) %collective-permute-start.7) | collective-permute-done | bytes 65568 | tf_op jit(solution)/shard_map/ppermute | solution.py:407
  99.1 0.8 corners.3
  99.9 0.1 collective-permute-start.10
  100.0 3.8 %collective-permute-start.11 = (f32[64,128]{1,0:T(8,128)S(1)}, f32[64,128]{1,0:T(8,128)S(1)}, u32[]{:S(2)}, u32[]{:S(2)}) collective-permute-start(f32[64,128]{1,0:T(8,128)S(1)} %get-tuple-element.45), channel_id=1, source_target_pairs={{4,8},{8,4},{12,16},{16,12},{20,24},{24,20},{5,9},{9,5},{13,17},{1... | collective-permute-start | bytes 98312 | tf_op jit(solution)/shard_map/ppermute | solution.py:407
  103.8 0.6 dynamic_slice.3
  104.4 1.5 %copy-done.11 = f32[16,240,128]{2,1,0:T(8,128)S(1)} copy-done((f32[16,240,128]{2,1,0:T(8,128)S(1)}, f32[16,240,128]{2,1,0:T(8,128)}, u32[]{:S(2)}) %copy-start.11) | copy-done | bytes 1966104
  105.9 4.7 %gradient_local.1.local_ref = f32[240,16,128]{2,1,0:T(8,128)S(1)} custom-call(f32[16,240,128]{2,1,0:T(8,128)S(1)} %copy-done.11, f32[256,128]{1,0:T(8,128)S(1)} %get-tuple-element.40.refs_1_, bf16[240,240]{1,0:T(8,128)(2,1)S(1)} %copy-done.6, bf16[240,240]{1,0:T(8,128)(2,1)S(1)} %copy-done.7, bf16[256,256]{1,0:T(8,128)(2,1)S(1)} %copy-done, ...), custom_call_target="tpu_custom_call" | custom-call | tf_op jit(solution)/shard_map/gradient_local/pallas_call | solution.py:488
  110.6 0.0 collective-permute-done.8
  110.7 0.0 collective-permute-done.9
  110.7 0.0 collective-permute-done.10.corner_e
  110.8 0.0 collective-permute-done.11.corner_o
  110.8 4.6 %gradient.1 = f32[240,16,128]{2,1,0:T(8,128)} custom-call(s32[2]{0:T(128)S(1)} %pad_add_fusion.par_ref.refs_0_, f32[240,16,128]{2,1,0:T(8,128)S(1)} %gradient_local.1.local_ref, f32[2,128]{1,0:T(2,128)S(1)} %get-tuple-element.41.factor_ref, f32[4,240,128]{2,1,0:T(8,128)S(1)} %convert_element_type.18.got_e, f32[4,240,128]{2,1,0:T(8,128)S(1)} %convert_element_type.20.got_o, ...), custom_call_target="tpu_custom_call" | custom-call | tf_op jit(solution)/shard_map/gradient/pallas_call | solution.py:537
  (22 shorter events, 0.2 us)
Async XLA Ops:
  4.8 26.9 %copy-start.17 = (f32[64]{0:T(128)S(1)}, f32[64]{0:T(128)}, u32[]{:S(2)}) copy-start(f32[64]{0:T(128)} %param.26) | copy-start | bytes 772
  4.8 26.9 %copy-start.18 = (f32[64]{0:T(128)S(1)}, f32[64]{0:T(128)}, u32[]{:S(2)}) copy-start(f32[64]{0:T(128)} %param.25) | copy-start | bytes 772
  4.8 27.0 %copy-start = (bf16[256,256]{1,0:T(8,128)(2,1)S(1)}, bf16[256,256]{1,0:T(8,128)(2,1)}, u32[]{:S(2)}) copy-start(bf16[256,256]{1,0:T(8,128)(2,1)} %constant.53.clone.refs_4_.col_both) | copy-start | bytes 393220
  4.8 27.0 %copy-start.1 = (bf16[128,2048]{1,0:T(8,128)(2,1)S(1)}, bf16[128,2048]{1,0:T(8,128)(2,1)}, u32[]{:S(2)}) copy-start(bf16[128,2048]{1,0:T(8,128)(2,1)} %constant.54.clone.refs_5_) | copy-start | bytes 1572868
  4.8 27.0 %copy-start.2 = (bf16[128,2048]{1,0:T(8,128)(2,1)S(1)}, bf16[128,2048]{1,0:T(8,128)(2,1)}, u32[]{:S(2)}) copy-start(bf16[128,2048]{1,0:T(8,128)(2,1)} %constant.55.clone.refs_6_) | copy-start | bytes 1572868
  4.9 27.0 %copy-start.6 = (bf16[240,240]{1,0:T(8,128)(2,1)S(1)}, bf16[240,240]{1,0:T(8,128)(2,1)}, u32[]{:S(2)}) copy-start(bf16[240,240]{1,0:T(8,128)(2,1)} %constant.51.clone.refs_2_.time_high) | copy-start | bytes 345604
  4.9 27.0 %copy-start.7 = (bf16[240,240]{1,0:T(8,128)(2,1)S(1)}, bf16[240,240]{1,0:T(8,128)(2,1)}, u32[]{:S(2)}) copy-start(bf16[240,240]{1,0:T(8,128)(2,1)} %constant.52.clone.refs_3_.time_low) | copy-start | bytes 345604
  4.9 55.2 %all-to-all-start = ((bf16[32,200,128]{2,1,0:T(8,128)(2,1)}), bf16[32,200,128]{2,1,0:T(8,128)(2,1)S(1)}, u32[]{:S(2)}, u32[]{:S(2)}) async-start(bf16[32,200,128]{2,1,0:T(8,128)(2,1)} %fusion.1), calls=%async_computation | async-start | bytes 3276800 | tf_op jit(solution)/shard_map/all_to_all | solution.py:469
  11.4 1.5 %copy-start.3 = (f32[240,16,128]{2,1,0:T(8,128)S(1)}, f32[240,16,128]{2,1,0:T(8,128)}, u32[]{:S(2)}) copy-start(f32[240,16,128]{2,1,0:T(8,128)} %control_ref.1) | copy-start | bytes 5898244
  15.3 37.1 %collective-permute-start.2 = (f32[4,240,128]{2,1,0:T(8,128)S(1)}, f32[4,240,128]{2,1,0:T(8,128)S(1)}, u32[]{:S(2)}, u32[]{:S(2)}) collective-permute-start(f32[4,240,128]{2,1,0:T(8,128)S(1)} %get-tuple-element.28), channel_id=1, source_target_pairs={{0,4},{4,0},{8,12},{12,8},{16,20},{20,16},{24,28},{28,24},{1,5},{5... | collective-permute-start | bytes 1474568 | tf_op jit(solution)/shard_map/ppermute | solution.py:406
  15.5 37.0 %collective-permute-start.3 = (f32[4,240,128]{2,1,0:T(8,128)S(1)}, f32[4,240,128]{2,1,0:T(8,128)S(1)}, u32[]{:S(2)}, u32[]{:S(2)}) collective-permute-start(f32[4,240,128]{2,1,0:T(8,128)S(1)} %get-tuple-element.29), channel_id=1, source_target_pairs={{4,8},{8,4},{12,16},{16,12},{20,24},{24,20},{5,9},{9,5},{13,17},{1... | collective-permute-start | bytes 1474568 | tf_op jit(solution)/shard_map/ppermute | solution.py:407
  19.7 4.0 %collective-permute-start = (f32[128,128]{1,0:T(8,128)S(1)}, f32[128,128]{1,0:T(8,128)S(1)}, u32[]{:S(2)}, u32[]{:S(2)}) collective-permute-start(f32[128,128]{1,0:T(8,128)S(1)} %get-tuple-element.25), channel_id=1, source_target_pairs={{0,1},{1,0},{2,3},{3,2},{4,5},{5,4},{6,7},{7,6},{8,9},{9,8},{10,11... | collective-permute-start | bytes 196616 | tf_op jit(solution)/shard_map/ppermute | solution.py:406
  20.6 8.1 %collective-permute-start.1 = (f32[128,128]{1,0:T(8,128)S(1)}, f32[128,128]{1,0:T(8,128)S(1)}, u32[]{:S(2)}, u32[]{:S(2)}) collective-permute-start(f32[128,128]{1,0:T(8,128)S(1)} %get-tuple-element.26), channel_id=1, source_target_pairs={{1,2},{2,1},{5,6},{6,5},{9,10},{10,9},{13,14},{14,13},{17,18},{18,... | collective-permute-start | bytes 196616 | tf_op jit(solution)/shard_map/ppermute | solution.py:407
  29.5 22.9 %collective-permute-start.4 = (f32[64,128]{1,0:T(8,128)S(1)}, f32[64,128]{1,0:T(8,128)S(1)}, u32[]{:S(2)}, u32[]{:S(2)}) collective-permute-start(f32[64,128]{1,0:T(8,128)S(1)} %get-tuple-element.30), channel_id=1, source_target_pairs={{0,4},{4,0},{8,12},{12,8},{16,20},{20,16},{24,28},{28,24},{1,5},{5... | collective-permute-start | bytes 98312 | tf_op jit(solution)/shard_map/ppermute | solution.py:406
  29.6 22.8 %collective-permute-start.5 = (f32[64,128]{1,0:T(8,128)S(1)}, f32[64,128]{1,0:T(8,128)S(1)}, u32[]{:S(2)}, u32[]{:S(2)}) collective-permute-start(f32[64,128]{1,0:T(8,128)S(1)} %get-tuple-element.31), channel_id=1, source_target_pairs={{4,8},{8,4},{12,16},{16,12},{20,24},{24,20},{5,9},{9,5},{13,17},{1... | collective-permute-start | bytes 98312 | tf_op jit(solution)/shard_map/ppermute | solution.py:407
  31.8 20.6 %copy-start.12 = (bf16[128,1024]{1,0:T(8,128)(2,1)S(1)}, bf16[128,1024]{1,0:T(8,128)(2,1)}, u32[]{:S(2)}) copy-start(bf16[128,1024]{1,0:T(8,128)(2,1)} %constant.56.clone.corner_high) | copy-start | bytes 786436
  31.9 20.6 %copy-start.13 = (bf16[128,1024]{1,0:T(8,128)(2,1)S(1)}, bf16[128,1024]{1,0:T(8,128)(2,1)}, u32[]{:S(2)}) copy-start(bf16[128,1024]{1,0:T(8,128)(2,1)} %constant.57.clone.corner_low) | copy-start | bytes 786436
  31.9 20.6 %copy-start.15 = (bf16[240,16,128]{2,1,0:T(8,128)(2,1)S(1)}, bf16[240,16,128]{2,1,0:T(8,128)(2,1)}, u32[]{:S(2)}) copy-start(bf16[240,16,128]{2,1,0:T(8,128)(2,1)} %prior_ref.1) | copy-start | bytes 2949124
  31.9 20.6 %copy-start.16 = (bf16[240,16,128]{2,1,0:T(8,128)(2,1)S(1)}, bf16[240,16,128]{2,1,0:T(8,128)(2,1)}, u32[]{:S(2)}) copy-start(bf16[240,16,128]{2,1,0:T(8,128)(2,1)} %scale_ref.1) | copy-start | bytes 2949124
  57.5 1.3 %copy-start.4 = (f32[16,240,128]{2,1,0:T(8,128)}, f32[16,240,128]{2,1,0:T(8,128)S(1)}, u32[]{:S(2)}) copy-start(f32[16,240,128]{2,1,0:T(8,128)S(1)} %get-tuple-element.35.refs_4_) | copy-start | bytes 5898244
  58.8 1.3 %copy-start.8 = (f32[16,240,128]{2,1,0:T(8,128)}, f32[16,240,128]{2,1,0:T(8,128)S(1)}, u32[]{:S(2)}) copy-start(f32[16,240,128]{2,1,0:T(8,128)S(1)} %get-tuple-element.32.refs_1_) | copy-start | bytes 5898244
  60.1 22.8 %copy-start.5 = (f32[16,240,128]{2,1,0:T(8,128)S(1)}, f32[16,240,128]{2,1,0:T(8,128)}, u32[]{:S(2)}) copy-start(f32[16,240,128]{2,1,0:T(8,128)} %copy-done.4) | copy-start | bytes 5898244
  60.1 1.7 %copy-start.9 = (f32[16,240,128]{2,1,0:T(8,128)S(1)}, f32[16,240,128]{2,1,0:T(8,128)}, u32[]{:S(2)}) copy-start(f32[16,240,128]{2,1,0:T(8,128)} %copy-done.8) | copy-start | bytes 5898244
  86.9 1.3 %copy-start.10 = (f32[16,240,128]{2,1,0:T(8,128)}, f32[16,240,128]{2,1,0:T(8,128)S(1)}, u32[]{:S(2)}) copy-start(f32[16,240,128]{2,1,0:T(8,128)S(1)} %get-tuple-element.37.refs_0_) | copy-start | bytes 5898244
  88.2 22.4 %collective-permute-start.8 = (f16[4,240,128]{2,1,0:T(8,128)(2,1)S(1)}, f16[4,240,128]{2,1,0:T(8,128)(2,1)S(1)}, u32[]{:S(2)}, u32[]{:S(2)}) collective-permute-start(f16[4,240,128]{2,1,0:T(8,128)(2,1)S(1)} %convert_element_type.17), channel_id=1, source_target_pairs={{0,4},{4,0},{8,12},{12,8},{16,20},{20,16},{24,28},{28,24},{1,5},{5... | collective-permute-start | bytes 737288 | tf_op jit(solution)/shard_map/ppermute | solution.py:406
  89.8 20.9 %collective-permute-start.9 = (f16[4,240,128]{2,1,0:T(8,128)(2,1)S(1)}, f16[4,240,128]{2,1,0:T(8,128)(2,1)S(1)}, u32[]{:S(2)}, u32[]{:S(2)}) collective-permute-start(f16[4,240,128]{2,1,0:T(8,128)(2,1)S(1)} %convert_element_type.19), channel_id=1, source_target_pairs={{4,8},{8,4},{12,16},{16,12},{20,24},{24,20},{5,9},{9,5},{13,17},{1... | collective-permute-start | bytes 737288 | tf_op jit(solution)/shard_map/ppermute | solution.py:407
  92.1 3.5 %collective-permute-start.6 = (f32[128,128]{1,0:T(8,128)S(1)}, f32[128,128]{1,0:T(8,128)S(1)}, u32[]{:S(2)}, u32[]{:S(2)}) collective-permute-start(f32[128,128]{1,0:T(8,128)S(1)} %get-tuple-element.38), channel_id=1, source_target_pairs={{0,1},{1,0},{2,3},{3,2},{4,5},{5,4},{6,7},{7,6},{8,9},{9,8},{10,11... | collective-permute-start | bytes 196616 | tf_op jit(solution)/shard_map/ppermute | solution.py:406
  93.3 5.9 %collective-permute-start.7 = (f32[128,128]{1,0:T(8,128)S(1)}, f32[128,128]{1,0:T(8,128)S(1)}, u32[]{:S(2)}, u32[]{:S(2)}) collective-permute-start(f32[128,128]{1,0:T(8,128)S(1)} %get-tuple-element.39), channel_id=1, source_target_pairs={{1,2},{2,1},{5,6},{6,5},{9,10},{10,9},{13,14},{14,13},{17,18},{18,... | collective-permute-start | bytes 196616 | tf_op jit(solution)/shard_map/ppermute | solution.py:407
  99.9 10.8 %collective-permute-start.10 = (f32[64,128]{1,0:T(8,128)S(1)}, f32[64,128]{1,0:T(8,128)S(1)}, u32[]{:S(2)}, u32[]{:S(2)}) collective-permute-start(f32[64,128]{1,0:T(8,128)S(1)} %get-tuple-element.44), channel_id=1, source_target_pairs={{0,4},{4,0},{8,12},{12,8},{16,20},{20,16},{24,28},{28,24},{1,5},{5... | collective-permute-start | bytes 98312 | tf_op jit(solution)/shard_map/ppermute | solution.py:406
  100.0 10.8 %collective-permute-start.11 = (f32[64,128]{1,0:T(8,128)S(1)}, f32[64,128]{1,0:T(8,128)S(1)}, u32[]{:S(2)}, u32[]{:S(2)}) collective-permute-start(f32[64,128]{1,0:T(8,128)S(1)} %get-tuple-element.45), channel_id=1, source_target_pairs={{4,8},{8,4},{12,16},{16,12},{20,24},{24,20},{5,9},{9,5},{13,17},{1... | collective-permute-start | bytes 98312 | tf_op jit(solution)/shard_map/ppermute | solution.py:407
  104.4 1.5 %copy-start.11 = (f32[16,240,128]{2,1,0:T(8,128)S(1)}, f32[16,240,128]{2,1,0:T(8,128)}, u32[]{:S(2)}) copy-start(f32[16,240,128]{2,1,0:T(8,128)} %copy-done.10) | copy-start | bytes 5898244
  105.9 4.8 %copy-start.14 = (bf16[128,1024]{1,0:T(8,128)(2,1)S(1)}, bf16[128,1024]{1,0:T(8,128)(2,1)}, u32[]{:S(2)}) copy-start(bf16[128,1024]{1,0:T(8,128)(2,1)} %constant.57.clone.corner_low) | copy-start | bytes 786436

commit v3 on v2

--- a/solution.py
+++ b/solution.py
@@ -12,8 +12,10 @@
 LANES = 128
 SUB = 8
 FOOT_MAX = 0.02
+PIECES = 3
 SCALE_MAX = 2.0
 HALF_TOP = 32768.0
+CONTROL_FACTOR = 4096.0
 F16 = jnp.float16
 VMEM_LIMIT = 12 * 1024 * 1024
 F32 = jnp.float32
@@ -141,8 +143,41 @@
     hours, rows, _ = control_ref.shape
     for row in range(rows):
         field_ref[row] = control_ref[:, row, :]
-    write_rows(par_ref[0], lambda r: field_ref[r], rows, rows_e, rows_o)
+    write_rows(par_ref[0], lambda r: field_ref[r] * CONTROL_FACTOR, rows, rows_e, rows_o)
     fold_hours(pack_strips(lambda r: field_ref[r], par_ref[1], rows), hours, strip_e, strip_o)
+
+
+def strip_kernel(par_ref, field_ref, strip_e, strip_o):
+    rows, hours, _ = field_ref.shape
+    fold_hours(pack_strips(lambda r: field_ref[r], par_ref[1], rows), hours, strip_e, strip_o)
+
+
+def prepare_kernel(
+    foot_ref, start_ref, row_ref, slot_ref, count_ref, out_ref,
+    start_vmem, row_vmem, slot_vmem, count_vmem, notes, sems, *, per,
+):
+    owners, lines, _ = foot_ref.shape
+    slots = start_ref.shape[0]
+    blocks = pltpu.make_async_copy(foot_ref, out_ref.at[:, 0:lines, :], sems.at[0])
+    blocks.start()
+    pairs = ((start_ref, start_vmem), (row_ref, row_vmem), (slot_ref, slot_vmem), (count_ref, count_vmem))
+    small = [pltpu.make_async_copy(a, b, sems.at[1 + i]) for i, (a, b) in enumerate(pairs)]
+    for copy in small:
+        copy.start()
+    for copy in small:
+        copy.wait()
+    start = start_vmem[...]
+    valid = lax.broadcasted_iota(jnp.int32, start.shape, 0) < count_vmem[...]
+    lanes = jnp.concatenate(
+        [start >> 4, start & 15, row_vmem[...], jnp.where(valid, slot_vmem[...], per)], axis=0
+    ).astype(F32)
+    wide = jnp.pad(lanes, ((0, LANES - 4 * slots), (0, LANES - owners)))
+    turned = jnp.transpose(wide)[0:owners]
+    notes[...] = jnp.broadcast_to(turned[:, None, :], notes.shape).astype(BF16)
+    copy = pltpu.make_async_copy(notes, out_ref.at[:, lines : lines + SUB, :], sems.at[5])
+    copy.start()
+    copy.wait()
+    blocks.wait()
 
 
 def corner_kernel(par_ref, strip_e, strip_o, halo_ref, corner_e, corner_o):
@@ -220,17 +255,15 @@
     return total
 
 
-def local_kernel(field_ref, halo_ref, time_high, time_low, col_both, own_high, own_low, out_ref, *, by_hour):
+def local_kernel(field_ref, time_high, time_low, col_both, out_ref, *, by_hour):
     rows, hours, cols = field_ref.shape
     taps = space_taps()
-    halo = halo_parts(halo_ref[0:hours, :])
     for row in range(0, rows, 2):
         pair = [
             column_sums(row_sums(lambda i: field_ref[i], r, 0, rows, taps), col_both[...])
             for r in (row, row + 1)
         ]
-        value = jnp.concatenate(pair, axis=1) + halo_sums(halo, own_high, own_low, row * cols, 2 * cols)
-        both = time_sums(value, time_high[...], time_low[...])
+        both = time_sums(jnp.concatenate(pair, axis=1), time_high[...], time_low[...])
         for k, r in enumerate((row, row + 1)):
             part = both[:, k * cols : (k + 1) * cols]
             if by_hour:
@@ -239,16 +272,30 @@
                 out_ref[r] = part
 
 
+def strips_kernel(local_ref, halo_ref, time_high, time_low, own_high, own_low, out_ref, *, by_hour):
+    if by_hour:
+        hours, rows, cols = local_ref.shape
+    else:
+        rows, hours, cols = local_ref.shape
+    halo = halo_parts(time_sums(halo_ref[0:hours, :], time_high[...], time_low[...]))
+    for row in range(0, rows, 2):
+        both = halo_sums(halo, own_high, own_low, row * cols, 2 * cols)
+        for k, r in enumerate((row, row + 1)):
+            part = both[:, k * cols : (k + 1) * cols]
+            if by_hour:
+                out_ref[:, r, :] = local_ref[:, r, :] + part
+            else:
+                out_ref[r] = local_ref[r] + part
+
+
 def edge_parts(is_even, rows, got_e, got_o, corner_e, corner_o, consts, halo, factor):
     time_high, time_low, col_both, corner_high, corner_low = consts
     hours, cols = halo.shape[1:]
     taps = space_taps()
     for row in range(RAD):
-        even, odd = got_e[row].astype(F32), got_o[row].astype(F32)
-        if factor is not None:
-            even, odd = even * factor, odd * factor
-        halo[row] = choose(is_even, odd, even)
-        halo[RAD + row] = choose(is_even, even, odd)
+        even, odd = got_e[row], got_o[row]
+        halo[row] = choose(is_even, odd, even) * factor
+        halo[RAD + row] = choose(is_even, even, odd) * factor
     corner = halo_parts(corner_strips(is_even, corner_e, corner_o)[0:hours])
     edge = list(range(RAD)) + list(range(rows - RAD, rows))
     for first in range(0, 2 * RAD, 2):
@@ -278,22 +325,34 @@
     wide[...] = prior_ref[...].astype(F32)
     for row in range(RAD, rows - RAD):
         flux_ref[row] = wide[:, row, :] + scale_out[row] * local_ref[row]
-    parts = edge_parts(par_ref[0] == 0, rows, got_e, got_o, corner_e, corner_o, consts, halo, None)
+    parts = edge_parts(par_ref[0] == 0, rows, got_e, got_o, corner_e, corner_o, consts, halo, 1.0 / CONTROL_FACTOR)
     for row, part in parts:
         flux_ref[row] = wide[:, row, :] + scale_out[row] * (local_ref[row] + part)
 
 
 def finish_kernel(
     par_ref, local_ref, factor_ref, got_e, got_o, corner_e, corner_o,
-    time_high, time_low, col_both, corner_high, corner_low, out_ref, halo,
+    time_high, time_low, col_both, corner_high, corner_low, out_ref, halo, edges, total, sems,
 ):
     hours, rows, cols = local_ref.shape
     consts = (time_high, time_low, col_both, corner_high, corner_low)
-    out_ref[...] = local_ref[...]
     factor = factor_ref[1:2, :]
     parts = edge_parts(par_ref[0] == 0, rows, got_e, got_o, corner_e, corner_o, consts, halo, factor)
-    for row, part in parts:
-        out_ref[:, row, :] = out_ref[:, row, :] + part
+    order = []
+    for k, (row, part) in enumerate(parts):
+        edges[k] = part
+        order.append(row)
+    chunk = hours // PIECES
+    copies = []
+    for piece in range(PIECES):
+        here = slice(piece * chunk, (piece + 1) * chunk)
+        total[here] = local_ref[here]
+        for k, row in enumerate(order):
+            total[here, row, :] = total[here, row, :] + edges[k, here, :]
+        copies.append(pltpu.make_async_copy(total.at[here], out_ref.at[here], sems.at[piece]))
+        copies[-1].start()
+    for copy in copies:
+        copy.wait()
 
 
 def blocks_of(foot_ref, source, heights, slots):
@@ -304,10 +363,12 @@
 
 
 def forward_kernel(
-    foot_ref, flux_ref, own_ref, out_ref, table_ref, sums, table_smem, sem,
+    foot_ref, flux_hbm, own_ref, out_ref, table_ref, flux_ref, sums, table_smem, sems,
     *, shift, slots, heights, tiles, per,
 ):
     sources = foot_ref.shape[0]
+    load = pltpu.make_async_copy(flux_hbm, flux_ref, sems.at[0])
+    load.start()
     groups = out_ref.shape[1] - 1
     base = slots * heights
     lane = lane_ids((sources, LANES))
@@ -318,9 +379,10 @@
     receptor = jnp.where(notes < per, source_rec * per + notes, groups * LANES)
     table = jnp.where(lane < slots, offset, receptor)
     table_ref[...] = table
-    copy = pltpu.make_async_copy(table_ref, table_smem, sem)
+    copy = pltpu.make_async_copy(table_ref, table_smem, sems.at[1])
     copy.start()
     copy.wait()
+    load.wait()
 
     def body(source, carry):
         for c, block in blocks_of(foot_ref, source, heights, slots):
@@ -346,16 +408,22 @@
 
 def adjoint_kernel(
     par_ref, table_ref, got_ref, foot_ref, scale_ref,
-    model_ref, factor_ref, field_ref, rows_e, rows_o, strip_e, strip_o,
+    model_ref, factor_ref, field_ref, rows_e, rows_o,
     weight_vmem, weight_smem, sem, *, shift, slots, heights, tiles, per,
 ):
     sources = foot_ref.shape[0]
-    groups = model_ref.shape[0]
+    groups = got_ref.shape[1] - 1
     rows, hours, _ = field_ref.shape
     model = jnp.sum(got_ref[:, 0:groups, :], axis=0)
-    model_ref[...] = model
     packed = LANES // per
     lane = lane_ids((1, LANES))
+    own = jnp.zeros((1, LANES), F32)
+    for q in range(groups):
+        for k in range(packed):
+            line = model[q : q + 1, :]
+            line = line if k == 0 else pltpu.roll(line, LANES - k * per, 1)
+            own = choose(par_ref[2] == q * packed + k, line, own)
+    model_ref[...] = own[:, 0:per]
     weight_vmem[...] = jnp.zeros_like(weight_vmem)
     for q in range(groups):
         observed, error = jnp.zeros((1, LANES), F32), jnp.ones((1, LANES), F32)
@@ -390,7 +458,6 @@
         field_ref[row] = field_ref[row] * scale_ref[row]
     factor = factor_ref[0:1, :]
     write_rows(par_ref[0], lambda r: field_ref[r] * factor, rows, rows_e, rows_o)
-    fold_hours(pack_strips(lambda r: field_ref[r], par_ref[1], rows), hours, strip_e, strip_o)
 
 
 def swap_pairs(count, odd):
@@ -410,15 +477,17 @@
 
 SM = pl.BlockSpec(memory_space=pltpu.SMEM)
 VM = pl.BlockSpec(memory_space=pltpu.VMEM)
-
-
-def call(kernel, out_shape, in_specs, scratch, name):
+HB = pl.BlockSpec(memory_space=pltpu.HBM)
+
+
+def call(kernel, out_shape, in_specs, scratch, name, out_specs=None, alias=None):
     return pl.pallas_call(
         kernel,
         out_shape=out_shape,
         in_specs=in_specs,
-        out_specs=jax.tree.map(lambda _: VM, out_shape),
+        out_specs=jax.tree.map(lambda _: VM, out_shape) if out_specs is None else out_specs,
         scratch_shapes=scratch,
+        input_output_aliases={} if alias is None else alias,
         compiler_params=pltpu.CompilerParams(vmem_limit_bytes=VMEM_LIMIT),
         name=name,
     )
@@ -448,7 +517,7 @@
     groups = per * n_rec // LANES
     shift = (hours - 1).bit_length()
     rec, tile = lax.axis_index("rec"), lax.axis_index("tile")
-    par = jnp.stack([rec % 2, tile % 2]).astype(jnp.int32)
+    par = jnp.stack([rec % 2, tile % 2, rec]).astype(jnp.int32)
     base, own_parts, corner_parts = constants(hours, rows, cols)
     base = [jnp.asarray(c) for c in base]
     own_parts = [jnp.asarray(c) for c in own_parts]
@@ -459,36 +528,59 @@
     field_shape = array(rows, hours, cols)
     halo_scratch = pltpu.VMEM((2 * RAD, hours, cols), F32)
 
-    valid = jnp.arange(slots)[None, :] < slot_count[:, None]
-    notes = jnp.concatenate(
-        [start_hour >> 4, start_hour & 15, grid_row, jnp.where(valid, receptor_slot, per)], axis=1
-    ).astype(BF16)
-    notes = jnp.pad(notes, ((0, 0), (0, LANES - 4 * slots)))[:, None, :]
-    notes = jnp.pad(notes, ((0, 0), (0, SUB - 1), (0, 0)))
-    sent = jnp.concatenate([footprint.reshape(devices, slots * heights, cols), notes], axis=1)
+    def prepare(*refs):
+        prepare_kernel(*refs, per=per)
+
+    numbers = pltpu.VMEM((slots, devices), jnp.int32)
+    sent = call(
+        prepare,
+        jax.ShapeDtypeStruct((devices, slots * heights + SUB, cols), BF16),
+        [HB] * 5,
+        [
+            numbers, numbers, numbers, pltpu.VMEM((1, devices), jnp.int32),
+            pltpu.VMEM((devices, SUB, LANES), BF16), pltpu.SemaphoreType.DMA((6,)),
+        ],
+        "prepare_blocks",
+        out_specs=HB,
+    )(*[
+        pltpu.with_memory_space_constraint(x, pltpu.HBM)
+        for x in (
+            footprint.reshape(devices, slots * heights, cols),
+            start_hour.T, grid_row.T, receptor_slot.T, slot_count[None],
+        )
+    ])
     foot = lax.all_to_all(sent, AXES, split_axis=0, concat_axis=0, tiled=True)
 
     field, rows_e, rows_o, strip_e, strip_o = call(
         pack_kernel, [field_shape, block, block, strip, strip], [SM, VM], [], "pack_control"
     )(par, control)
 
-    def neighbours(rows_e, rows_o, strip_e, strip_o):
-        got_rows = swap("rec", rows_e, rows_o)
+    def neighbours(rows_e, rows_o):
+        return [r.astype(F32) for r in swap("rec", rows_e.astype(F16), rows_o.astype(F16))]
+
+    def sides(strip_e, strip_o):
         got_strips = swap("tile", strip_e, strip_o)
         halo, corner_e, corner_o = call(
             corner_kernel, [array(2 * fold, LANES), corner, corner], [SM, VM, VM], [], "corners"
         )(par, *got_strips)
-        return got_rows, halo, swap("rec", corner_e, corner_o)
-
-    def local_sums(field, halo, by_hour, name):
-        def kernel(*refs):
+        return halo, swap("rec", corner_e, corner_o)
+
+    def inner_sums(field, halo, by_hour, name):
+        def first(*refs):
             local_kernel(*refs, by_hour=by_hour)
 
+        def second(*refs):
+            strips_kernel(*refs, by_hour=by_hour)
+
         shape = array(hours, rows, cols) if by_hour else field_shape
-        return call(kernel, shape, [VM] * 7, [], name)(field, halo, *base, *own_parts)
-
-    got_rows, halo, got_corners = neighbours(rows_e, rows_o, strip_e, strip_o)
-    local = local_sums(field, halo, False, "control_local")
+        local = call(first, shape, [VM] * 4, [], name + "_local")(field, *base)
+        return call(second, shape, [VM] * 6, [], name + "_strips", alias={0: 0})(
+            local, halo, *base[:2], *own_parts
+        )
+
+    got_rows = neighbours(rows_e, rows_o)
+    halo, got_corners = sides(strip_e, strip_o)
+    local = inner_sums(field, halo, False, "control")
     flux, scale = call(
         flux_kernel,
         [field_shape, field_shape],
@@ -506,11 +598,12 @@
     partial, table = call(
         forward,
         [array(devices, groups + 1, LANES), jax.ShapeDtypeStruct((devices, LANES), jnp.int32)],
-        [VM, VM, VM],
+        [VM, HB, VM],
         [
+            pltpu.VMEM((rows, hours, cols), F32),
             pltpu.VMEM((slots, devices, LANES), F32),
             pltpu.SMEM((devices, LANES), jnp.int32),
-            pltpu.SemaphoreType.DMA,
+            pltpu.SemaphoreType.DMA((2,)),
         ],
         "block_values",
     )(foot, flux, own)
@@ -520,9 +613,9 @@
         adjoint_kernel(*refs, **sizes)
 
     weight_rows = -(-(groups + 1) // SUB) * SUB
-    model, factor, field, rows_e, rows_o, strip_e, strip_o = call(
+    model_co2, factor, field, rows_e, rows_o = call(
         adjoint,
-        [array(groups, LANES), array(2, LANES), field_shape, block, block, strip, strip],
+        [array(1, per), array(2, LANES), field_shape, block, block],
         [SM, SM, VM, VM, VM],
         [
             pltpu.VMEM((weight_rows, LANES), F32),
@@ -531,14 +624,24 @@
         ],
         "adjoint_field",
     )(par, table, everyone, foot, scale)
-    got_rows, halo, got_corners = neighbours(rows_e.astype(F16), rows_o.astype(F16), strip_e, strip_o)
-    got_rows = [r.astype(F32) for r in got_rows]
-    local = local_sums(field, halo, True, "gradient_local")
+    got_rows = neighbours(rows_e, rows_o)
+    strips = call(strip_kernel, [strip, strip], [SM, VM], [], "pack_strips")(par, field)
+    halo, got_corners = sides(*strips)
+    local = inner_sums(field, halo, True, "gradient")
     gradient = call(
-        finish_kernel, array(hours, rows, cols), [SM] + [VM] * 11, [halo_scratch], "gradient"
+        finish_kernel,
+        array(hours, rows, cols),
+        [SM] + [VM] * 11,
+        [
+            halo_scratch,
+            halo_scratch,
+            pltpu.VMEM((hours, rows, cols), F32),
+            pltpu.SemaphoreType.DMA((PIECES,)),
+        ],
+        "gradient",
+        out_specs=HB,
     )(par, local, factor, *got_rows, *got_corners, *base, *corner_parts)
-    model_co2 = lax.dynamic_slice_in_dim(model.reshape(-1), rec * per, per)
-    return (model_co2, gradient)
+    return (model_co2.reshape(-1), gradient)
 
 
 def solution(mesh):

time: 116 us -> 157 us (1.35)
  Pallas kernels: 28.3 us -> 82 us
  waiting for transfers between devices: 25.4 us -> 17.1 us
  other arithmetic: 4.39 us -> 0.43 us
  local copies, waits for them, and re-layouts: 9.36 us -> 5.93 us
  blocking collectives: 18.9 us -> 21.8 us
    pallas_call x5 -> x9, Pallas kernels: 14.1 us -> 67.8 us  [the longest x1 48.8 us: per_device(): call(prepare, jax.ShapeDtypeStruct((devices, slots * heights + SUB, cols)...]
    ppermute x6, waiting for transfers between devices: 16.7 us -> 0.02 us  [swap(): lax.ppermute(even, axis, swap_pairs(count, False))]
    ppermute x6, waiting for transfers between devices: 8.63 us -> 17.1 us  [swap(): lax.ppermute(odd, axis, swap_pairs(count, True))]
    all_to_all x1, blocking collectives: 18.9 us -> 21.8 us  [per_device(): lax.all_to_all(partial, AXES, split_axis=0, concat_axis=0, tiled=True)]
    unnamed x38 -> x34, local copies, waits for them, and re-layouts: 8.68 us -> 5.93 us
    concatenate x1 -> x0, other arithmetic: 2.69 us -> none  [per_device(): jnp.concatenate([footprint.reshape(devices, slots * heights, cols), notes...]
  transfers between devices with their start and end apart: 13 -> 13, of which waited for: 3 -> 4; matrix products, arithmetic and copies ran while one was open for 1% -> 0% of each run, Pallas kernels for 15% -> 14%
where the time goes in v3:
time: 157 us
  Pallas kernels  82 us (52%)
  starting transfers between devices  28.1 us (18%)
  blocking collectives  21.8 us (14%)
  waiting for transfers between devices  17.1 us (11%)
  local copies, waits for them, and re-layouts  5.93 us (4%)
    pallas_call x1, Pallas kernels, per_device(): call(prepare, jax.ShapeDtypeStruct((devices, slots * heights + SUB, cols)...  48.8 us
    all_to_all x1, blocking collectives, per_device(): lax.all_to_all(partial, AXES, split_axis=0, concat_axis=0, tiled=True)  21.8 us
    ppermute x6, starting transfers between devices, swap(): lax.ppermute(odd, axis, swap_pairs(count, True))  17.7 us
    ppermute x6, waiting for transfers between devices, swap(): lax.ppermute(odd, axis, swap_pairs(count, True))  17.1 us
    pallas_call x2, Pallas kernels, inner_sums(): call(second, shape, [VM] * 6, [], name + '_strips', alias={0: 0})  6.61 us
    all_to_all x1, starting transfers between devices, per_device(): foot = lax.all_to_all(sent, AXES, split_axis=0, concat_axis=0, tiled=True)  6.42 us
    unnamed x34, local copies, waits for them, and re-layouts  5.93 us
    pallas_call x2, Pallas kernels, inner_sums(): local = call(first, shape, [VM] * 4, [], name + '_local')(field, *base)  5.72 us
  transfers between devices with their start and end apart: 13, of which 4 were waited for; matrix products, arithmetic and copies ran while one was open for 0% of the time, Pallas kernels for 14%

profile of v3, /device:TPU:5, one launch (start us, length us, event | category | flops | bytes accessed | tf_op | source)
XLA Modules:
  0.0 156.5 jit_solution(10503481568975020967)
XLA Ops:
  0.6 48.8 %prepare_blocks.1 = bf16[32,200,128]{2,1,0:T(8,128)(2,1)} custom-call(bf16[32,192,128]{2,1,0:T(8,128)(2,1)} %bitcast.11, s32[8,32]{1,0:T(8,128)} %bitcast.12, s32[8,32]{1,0:T(8,128)} %bitcast.13, s32[8,32]{1,0:T(8,128)} %bitcast.14, s32[1,32]{1,0:T(1,128)} %bitcast.15), custom_call_target="tpu_custom_call" | custom-call | tf_op jit(solution)/shard_map/prepare_blocks/pallas_call | solution.py:535
  49.4 0.0 copy-start.15
  49.5 0.0 copy-start.16
  49.5 6.4 %all-to-all-start = ((bf16[32,200,128]{2,1,0:T(8,128)(2,1)}), bf16[32,200,128]{2,1,0:T(8,128)(2,1)S(1)}, u32[]{:S(2)}, u32[]{:S(2)}) async-start(bf16[32,200,128]{2,1,0:T(8,128)(2,1)} %prepare_blocks.1), calls=%async_computation | async-start | bytes 3276800 | tf_op jit(solution)/shard_map/all_to_all | solution.py:552
  55.9 0.0 copy-start
  55.9 0.0 copy-start.1
  55.9 0.0 copy-start.2
  55.9 0.1 pad_add_fusion.par_ref.refs_0_
  56.0 1.6 %copy-done.5 = f32[240,16,128]{2,1,0:T(8,128)S(1)} copy-done((f32[240,16,128]{2,1,0:T(8,128)S(1)}, f32[240,16,128]{2,1,0:T(8,128)}, u32[]{:S(2)}) %copy-start.5) | copy-done | bytes 1966104
  57.6 2.4 %pack_control.1 = (f32[16,240,128]{2,1,0:T(8,128)S(1)}, f32[4,240,128]{2,1,0:T(8,128)S(1)}, f32[4,240,128]{2,1,0:T(8,128)S(1)}, f32[128,128]{1,0:T(8,128)S(1)}, f32[128,128]{1,0:T(8,128)S(1)}) custom-call(s32[3]{0:T(128)S(1)} %pad_add_fusion.par_ref.refs_0_, f32[240,16,128]{2,1,0:T(8,128)S(1)} %copy-done.5), custom_call_target="tpu_custom_call" | custom-call | tf_op jit(solution)/shard_map/pack_control/pallas_call | solution.py:554
  60.0 0.1 collective-permute-start.2
  60.2 4.2 %collective-permute-start.3 = (f16[4,240,128]{2,1,0:T(8,128)(2,1)S(1)}, f16[4,240,128]{2,1,0:T(8,128)(2,1)S(1)}, u32[]{:S(2)}, u32[]{:S(2)}) collective-permute-start(f16[4,240,128]{2,1,0:T(8,128)(2,1)S(1)} %convert_element_type.26), channel_id=1, source_target_pairs={{4,8},{8,4},{12,16},{16,12},{20,24},{24,20},{5,9},{9,5},{13,17},{1... | collective-permute-start | bytes 737288 | tf_op jit(solution)/shard_map/ppermute | solution.py:474
  64.4 1.0 collective-permute-start
  65.4 3.0 %collective-permute-start.1 = (f32[128,128]{1,0:T(8,128)S(1)}, f32[128,128]{1,0:T(8,128)S(1)}, u32[]{:S(2)}, u32[]{:S(2)}) collective-permute-start(f32[128,128]{1,0:T(8,128)S(1)} %get-tuple-element.26), channel_id=1, source_target_pairs={{1,2},{2,1},{5,6},{6,5},{9,10},{10,9},{13,14},{14,13},{17,18},{18,... | collective-permute-start | bytes 196616 | tf_op jit(solution)/shard_map/ppermute | solution.py:474
  68.4 0.0 collective-permute-done.strip_e
  68.4 5.3 %collective-permute-done.1.strip_o = f32[128,128]{1,0:T(8,128)S(1)} collective-permute-done((f32[128,128]{1,0:T(8,128)S(1)}, f32[128,128]{1,0:T(8,128)S(1)}, u32[]{:S(2)}, u32[]{:S(2)}) %collective-permute-start.1) | collective-permute-done | bytes 65568 | tf_op jit(solution)/shard_map/ppermute | solution.py:474
  73.7 0.8 corners.2
  74.5 0.1 collective-permute-start.4
  74.6 2.1 %collective-permute-start.5 = (f32[64,128]{1,0:T(8,128)S(1)}, f32[64,128]{1,0:T(8,128)S(1)}, u32[]{:S(2)}, u32[]{:S(2)}) collective-permute-start(f32[64,128]{1,0:T(8,128)S(1)} %get-tuple-element.31), channel_id=1, source_target_pairs={{4,8},{8,4},{12,16},{16,12},{20,24},{24,20},{5,9},{9,5},{13,17},{1... | collective-permute-start | bytes 98312 | tf_op jit(solution)/shard_map/ppermute | solution.py:474
  76.7 0.0 copy-done.15
  76.7 0.0 copy-done.16
  76.7 0.1 maximum_bitcast_fusion.refs_2_
  76.8 0.0 copy-done
  76.8 0.0 copy-done.1
  76.8 0.0 copy-start.4
  76.8 2.3 %control_local.1.refs_0_ = f32[16,240,128]{2,1,0:T(8,128)S(1)} custom-call(f32[16,240,128]{2,1,0:T(8,128)S(1)} %get-tuple-element.24.refs_0_, bf16[240,240]{1,0:T(8,128)(2,1)S(1)} %copy-done, bf16[240,240]{1,0:T(8,128)(2,1)S(1)} %copy-done.1, bf16[256,256]{1,0:T(8,128)(2,1)S(1)} %copy-done.2), custom_call_target="tpu_custom_call" | custom-call | tf_op jit(solution)/shard_map/control_local/pallas_call | solution.py:576
  79.1 0.0 copy-start.10
  79.1 0.0 copy-start.11
  79.1 0.0 copy-start.14
  79.2 1.1 control_strips.1.local_ref
  80.3 0.0 copy-start.13
  80.3 0.0 collective-permute-done.2
  80.3 7.8 %collective-permute-done.3 = f16[4,240,128]{2,1,0:T(8,128)(2,1)S(1)} collective-permute-done((f16[4,240,128]{2,1,0:T(8,128)(2,1)S(1)}, f16[4,240,128]{2,1,0:T(8,128)(2,1)S(1)}, u32[]{:S(2)}, u32[]{:S(2)}) %collective-permute-start.3) | collective-permute-done | bytes 245792 | tf_op jit(solution)/shard_map/ppermute | solution.py:474
  88.1 0.0 collective-permute-done.4.corner_e
  88.1 0.7 collective-permute-done.5.corner_o
  88.8 0.0 copy-done.11
  88.8 0.0 copy-done.13
  88.8 4.9 %flux_field.1 = (f32[16,240,128]{2,1,0:T(8,128)S(1)}, f32[16,240,128]{2,1,0:T(8,128)S(1)}) custom-call(s32[3]{0:T(128)S(1)} %pad_add_fusion.par_ref.refs_0_, f32[16,240,128]{2,1,0:T(8,128)S(1)} %control_strips.1.local_ref, bf16[240,16,128]{2,1,0:T(8,128)(2,1)S(1)} %copy-done.13, bf16[240,16,128]{2,1,0:T(8,128)(2,1)S(1)} %copy-done.14, ...), custom_call_target="tpu_custom_call" | custom-call | tf_op jit(solution)/shard_map/flux_field/pallas_call | solution.py:584
  93.8 0.0 copy-start.6
  93.8 1.3 copy-done.6
  95.1 1.3 copy-done.8
  96.3 0.0 all-to-all-done.refs_0_.refs_3_
  96.3 1.7 %copy-done.9 = f32[16,240,128]{2,1,0:T(8,128)S(1)} copy-done((f32[16,240,128]{2,1,0:T(8,128)S(1)}, f32[16,240,128]{2,1,0:T(8,128)}, u32[]{:S(2)}) %copy-start.9) | copy-done | bytes 1966104
  98.0 2.5 %block_values.1 = (f32[32,5,128]{2,1,0:T(8,128)S(1)}, s32[32,128]{1,0:T(8,128)S(1)}) custom-call(bf16[32,200,128]{2,1,0:T(8,128)(2,1)S(1)} %all-to-all-done.refs_0_.refs_3_, f32[16,240,128]{2,1,0:T(8,128)S(1)} %copy-done.9, f32[1,128]{1,0:T(1,128)S(1)} %maximum_bitcast_fusion.refs_2_), custom_call_target="tpu_custom_call" | custom-call | tf_op jit(solution)/shard_map/block_values/pallas_call | solution.py:598
  100.6 21.8 %all_to_all.10.refs_2_ = f32[32,5,128]{2,1,0:T(8,128)S(1)} all-to-all(f32[32,5,128]{2,1,0:T(8,128)S(1)} %get-tuple-element.34), channel_id=1, replica_groups=mesh['rec'=8,'tile'=4] {'rec','tile'}, dimensions={0} | all-to-all | bytes 163840 | tf_op jit(solution)/shard_map/all_to_all | solution.py:610
  122.4 3.8 %adjoint_field.1 = (f32[1,64]{1,0:T(1,128)}, f32[2,128]{1,0:T(2,128)S(1)}, f32[16,240,128]{2,1,0:T(8,128)S(1)}, f32[4,240,128]{2,1,0:T(8,128)S(1)}, f32[4,240,128]{2,1,0:T(8,128)S(1)}) custom-call(s32[3]{0:T(128)S(1)} %pad_add_fusion.par_ref.refs_0_, s32[32,128]{1,0:T(8,128)S(1)} %get-tuple-element.33.refs_1_, f32[32,5,128]{2,1,0:T(8,128)S(1)} %all_to_all.10.refs_2_, ...), custom_call_target="tpu_custom_call" | custom-call | tf_op jit(solution)/shard_map/adjoint_field/pallas_call | solution.py:616
  126.2 1.5 collective-permute-start.8
  127.8 2.1 %collective-permute-start.9 = (f16[4,240,128]{2,1,0:T(8,128)(2,1)S(1)}, f16[4,240,128]{2,1,0:T(8,128)(2,1)S(1)}, u32[]{:S(2)}, u32[]{:S(2)}) collective-permute-start(f16[4,240,128]{2,1,0:T(8,128)(2,1)S(1)} %convert_element_type.30), channel_id=1, source_target_pairs={{4,8},{8,4},{12,16},{16,12},{20,24},{24,20},{5,9},{9,5},{13,17},{1... | collective-permute-start | bytes 737288 | tf_op jit(solution)/shard_map/ppermute | solution.py:474
  129.9 1.3 pack_strips.1
  131.2 1.2 collective-permute-start.6
  132.4 2.5 %collective-permute-start.7 = (f32[128,128]{1,0:T(8,128)S(1)}, f32[128,128]{1,0:T(8,128)S(1)}, u32[]{:S(2)}, u32[]{:S(2)}) collective-permute-start(f32[128,128]{1,0:T(8,128)S(1)} %get-tuple-element.39), channel_id=1, source_target_pairs={{1,2},{2,1},{5,6},{6,5},{9,10},{10,9},{13,14},{14,13},{17,18},{18,... | collective-permute-start | bytes 196616 | tf_op jit(solution)/shard_map/ppermute | solution.py:474
  134.9 0.0 collective-permute-done.6.strip_e
  134.9 3.3 %collective-permute-done.7.strip_o = f32[128,128]{1,0:T(8,128)S(1)} collective-permute-done((f32[128,128]{1,0:T(8,128)S(1)}, f32[128,128]{1,0:T(8,128)S(1)}, u32[]{:S(2)}, u32[]{:S(2)}) %collective-permute-start.7) | collective-permute-done | bytes 65568 | tf_op jit(solution)/shard_map/ppermute | solution.py:474
  138.2 0.8 corners.3
  139.0 0.1 collective-permute-start.10
  139.1 3.8 %collective-permute-start.11 = (f32[64,128]{1,0:T(8,128)S(1)}, f32[64,128]{1,0:T(8,128)S(1)}, u32[]{:S(2)}, u32[]{:S(2)}) collective-permute-start(f32[64,128]{1,0:T(8,128)S(1)} %get-tuple-element.45), channel_id=1, source_target_pairs={{4,8},{8,4},{12,16},{16,12},{20,24},{24,20},{5,9},{9,5},{13,17},{1... | collective-permute-start | bytes 98312 | tf_op jit(solution)/shard_map/ppermute | solution.py:474
  142.9 3.4 %gradient_local.1.refs_0_ = f32[240,16,128]{2,1,0:T(8,128)S(1)} custom-call(f32[16,240,128]{2,1,0:T(8,128)S(1)} %get-tuple-element.37.refs_0_.field_ref, bf16[240,240]{1,0:T(8,128)(2,1)S(1)} %copy-done, bf16[240,240]{1,0:T(8,128)(2,1)S(1)} %copy-done.1, bf16[256,256]{1,0:T(8,128)(2,1)S(1)} %copy-done.2), custom_call_target="tpu_custom_call" | custom-call | tf_op jit(solution)/shard_map/gradient_local/pallas_call | solution.py:576
  146.3 0.0 copy-start.12
  146.3 5.5 %gradient_strips.1.local_ref = f32[240,16,128]{2,1,0:T(8,128)S(1)} custom-call(f32[240,16,128]{2,1,0:T(8,128)S(1)} %gradient_local.1.refs_0_, f32[256,128]{1,0:T(8,128)S(1)} %get-tuple-element.40.refs_1_, bf16[240,240]{1,0:T(8,128)(2,1)S(1)} %copy-done, bf16[240,240]{1,0:T(8,128)(2,1)S(1)} %copy-done.1, ...), custom_call_target="tpu_custom_call", output_to_operand_aliasing={{}: (0, {})} | custom-call | tf_op jit(solution)/shard_map/gradient_strips/pallas_call | solution.py:577
  151.9 0.0 collective-permute-done.8
  151.9 0.0 collective-permute-done.9
  152.0 0.0 collective-permute-done.10.corner_e
  152.0 0.0 collective-permute-done.11.corner_o
  152.0 4.4 %gradient.1 = f32[240,16,128]{2,1,0:T(8,128)} custom-call(s32[3]{0:T(128)S(1)} %pad_add_fusion.par_ref.refs_0_, f32[240,16,128]{2,1,0:T(8,128)S(1)} %gradient_strips.1.local_ref, f32[2,128]{1,0:T(2,128)S(1)} %get-tuple-element.41.factor_ref, f32[4,240,128]{2,1,0:T(8,128)S(1)} %convert_element_type.29.got_e, f32[4,240,128]{2,1,0:T(8,128)S(1)} %convert_element_type.31.got_o, ...), custom_call_target="tpu_custom_call" | custom-call | tf_op jit(solution)/shard_map/gradient/pallas_call | solution.py:631
  (20 shorter events, 0.3 us)
Async XLA Ops:
  49.4 27.2 %copy-start.15 = (f32[64]{0:T(128)S(1)}, f32[64]{0:T(128)}, u32[]{:S(2)}) copy-start(f32[64]{0:T(128)} %param.26) | copy-start | bytes 772
  49.5 27.2 %copy-start.16 = (f32[64]{0:T(128)S(1)}, f32[64]{0:T(128)}, u32[]{:S(2)}) copy-start(f32[64]{0:T(128)} %param.25) | copy-start | bytes 772
  49.5 46.9 %all-to-all-start = ((bf16[32,200,128]{2,1,0:T(8,128)(2,1)}), bf16[32,200,128]{2,1,0:T(8,128)(2,1)S(1)}, u32[]{:S(2)}, u32[]{:S(2)}) async-start(bf16[32,200,128]{2,1,0:T(8,128)(2,1)} %prepare_blocks.1), calls=%async_computation | async-start | bytes 3276800 | tf_op jit(solution)/shard_map/all_to_all | solution.py:552
  55.9 20.9 %copy-start = (bf16[240,240]{1,0:T(8,128)(2,1)S(1)}, bf16[240,240]{1,0:T(8,128)(2,1)}, u32[]{:S(2)}) copy-start(bf16[240,240]{1,0:T(8,128)(2,1)} %constant.40.clone.refs_1_.refs_2_.time_high) | copy-start | bytes 345604
  55.9 20.9 %copy-start.1 = (bf16[240,240]{1,0:T(8,128)(2,1)S(1)}, bf16[240,240]{1,0:T(8,128)(2,1)}, u32[]{:S(2)}) copy-start(bf16[240,240]{1,0:T(8,128)(2,1)} %constant.41.clone.refs_2_.refs_3_.time_low) | copy-start | bytes 345604
  55.9 20.9 %copy-start.2 = (bf16[256,256]{1,0:T(8,128)(2,1)S(1)}, bf16[256,256]{1,0:T(8,128)(2,1)}, u32[]{:S(2)}) copy-start(bf16[256,256]{1,0:T(8,128)(2,1)} %constant.42.clone.refs_3_.col_both) | copy-start | bytes 393220
  56.0 1.6 %copy-start.5 = (f32[240,16,128]{2,1,0:T(8,128)S(1)}, f32[240,16,128]{2,1,0:T(8,128)}, u32[]{:S(2)}) copy-start(f32[240,16,128]{2,1,0:T(8,128)} %control_ref.1) | copy-start | bytes 5898244
  60.0 20.2 %collective-permute-start.2 = (f16[4,240,128]{2,1,0:T(8,128)(2,1)S(1)}, f16[4,240,128]{2,1,0:T(8,128)(2,1)S(1)}, u32[]{:S(2)}, u32[]{:S(2)}) collective-permute-start(f16[4,240,128]{2,1,0:T(8,128)(2,1)S(1)} %convert_element_type.24), channel_id=1, source_target_pairs={{0,4},{4,0},{8,12},{12,8},{16,20},{20,16},{24,28},{28,24},{1,5},{5... | collective-permute-start | bytes 737288 | tf_op jit(solution)/shard_map/ppermute | solution.py:473
  60.2 27.9 %collective-permute-start.3 = (f16[4,240,128]{2,1,0:T(8,128)(2,1)S(1)}, f16[4,240,128]{2,1,0:T(8,128)(2,1)S(1)}, u32[]{:S(2)}, u32[]{:S(2)}) collective-permute-start(f16[4,240,128]{2,1,0:T(8,128)(2,1)S(1)} %convert_element_type.26), channel_id=1, source_target_pairs={{4,8},{8,4},{12,16},{16,12},{20,24},{24,20},{5,9},{9,5},{13,17},{1... | collective-permute-start | bytes 737288 | tf_op jit(solution)/shard_map/ppermute | solution.py:474
  64.4 4.0 %collective-permute-start = (f32[128,128]{1,0:T(8,128)S(1)}, f32[128,128]{1,0:T(8,128)S(1)}, u32[]{:S(2)}, u32[]{:S(2)}) collective-permute-start(f32[128,128]{1,0:T(8,128)S(1)} %get-tuple-element.25), channel_id=1, source_target_pairs={{0,1},{1,0},{2,3},{3,2},{4,5},{5,4},{6,7},{7,6},{8,9},{9,8},{10,11... | collective-permute-start | bytes 196616 | tf_op jit(solution)/shard_map/ppermute | solution.py:473
  65.4 8.3 %collective-permute-start.1 = (f32[128,128]{1,0:T(8,128)S(1)}, f32[128,128]{1,0:T(8,128)S(1)}, u32[]{:S(2)}, u32[]{:S(2)}) collective-permute-start(f32[128,128]{1,0:T(8,128)S(1)} %get-tuple-element.26), channel_id=1, source_target_pairs={{1,2},{2,1},{5,6},{6,5},{9,10},{10,9},{13,14},{14,13},{17,18},{18,... | collective-permute-start | bytes 196616 | tf_op jit(solution)/shard_map/ppermute | solution.py:474
  74.5 13.6 %collective-permute-start.4 = (f32[64,128]{1,0:T(8,128)S(1)}, f32[64,128]{1,0:T(8,128)S(1)}, u32[]{:S(2)}, u32[]{:S(2)}) collective-permute-start(f32[64,128]{1,0:T(8,128)S(1)} %get-tuple-element.30), channel_id=1, source_target_pairs={{0,4},{4,0},{8,12},{12,8},{16,20},{20,16},{24,28},{28,24},{1,5},{5... | collective-permute-start | bytes 98312 | tf_op jit(solution)/shard_map/ppermute | solution.py:473
  74.6 14.2 %collective-permute-start.5 = (f32[64,128]{1,0:T(8,128)S(1)}, f32[64,128]{1,0:T(8,128)S(1)}, u32[]{:S(2)}, u32[]{:S(2)}) collective-permute-start(f32[64,128]{1,0:T(8,128)S(1)} %get-tuple-element.31), channel_id=1, source_target_pairs={{4,8},{8,4},{12,16},{16,12},{20,24},{24,20},{5,9},{9,5},{13,17},{1... | collective-permute-start | bytes 98312 | tf_op jit(solution)/shard_map/ppermute | solution.py:474
  76.8 2.3 %copy-start.3 = (bf16[128,2048]{1,0:T(8,128)(2,1)S(1)}, bf16[128,2048]{1,0:T(8,128)(2,1)}, u32[]{:S(2)}) copy-start(bf16[128,2048]{1,0:T(8,128)(2,1)} %constant.43.clone.refs_4_) | copy-start | bytes 1572868
  76.8 2.3 %copy-start.4 = (bf16[128,2048]{1,0:T(8,128)(2,1)S(1)}, bf16[128,2048]{1,0:T(8,128)(2,1)}, u32[]{:S(2)}) copy-start(bf16[128,2048]{1,0:T(8,128)(2,1)} %constant.44.clone.refs_5_) | copy-start | bytes 1572868
  79.1 9.7 %copy-start.10 = (bf16[128,1024]{1,0:T(8,128)(2,1)S(1)}, bf16[128,1024]{1,0:T(8,128)(2,1)}, u32[]{:S(2)}) copy-start(bf16[128,1024]{1,0:T(8,128)(2,1)} %constant.45.clone.corner_high) | copy-start | bytes 786436
  79.1 9.7 %copy-start.11 = (bf16[128,1024]{1,0:T(8,128)(2,1)S(1)}, bf16[128,1024]{1,0:T(8,128)(2,1)}, u32[]{:S(2)}) copy-start(bf16[128,1024]{1,0:T(8,128)(2,1)} %constant.46.clone.corner_low) | copy-start | bytes 786436
  79.1 9.7 %copy-start.14 = (bf16[240,16,128]{2,1,0:T(8,128)(2,1)S(1)}, bf16[240,16,128]{2,1,0:T(8,128)(2,1)}, u32[]{:S(2)}) copy-start(bf16[240,16,128]{2,1,0:T(8,128)(2,1)} %scale_ref.1) | copy-start | bytes 2949124
  80.3 8.6 %copy-start.13 = (bf16[240,16,128]{2,1,0:T(8,128)(2,1)S(1)}, bf16[240,16,128]{2,1,0:T(8,128)(2,1)}, u32[]{:S(2)}) copy-start(bf16[240,16,128]{2,1,0:T(8,128)(2,1)} %prior_ref.1) | copy-start | bytes 2949124
  93.8 1.3 copy-start.6
  95.1 1.3 copy-start.8
  96.3 26.0 %copy-start.7 = (f32[16,240,128]{2,1,0:T(8,128)S(1)}, f32[16,240,128]{2,1,0:T(8,128)}, u32[]{:S(2)}) copy-start(f32[16,240,128]{2,1,0:T(8,128)} %copy-done.6) | copy-start | bytes 5898244
  96.3 1.7 %copy-start.9 = (f32[16,240,128]{2,1,0:T(8,128)S(1)}, f32[16,240,128]{2,1,0:T(8,128)}, u32[]{:S(2)}) copy-start(f32[16,240,128]{2,1,0:T(8,128)} %copy-done.8) | copy-start | bytes 5898244
  126.2 25.6 %collective-permute-start.8 = (f16[4,240,128]{2,1,0:T(8,128)(2,1)S(1)}, f16[4,240,128]{2,1,0:T(8,128)(2,1)S(1)}, u32[]{:S(2)}, u32[]{:S(2)}) collective-permute-start(f16[4,240,128]{2,1,0:T(8,128)(2,1)S(1)} %convert_element_type.28), channel_id=1, source_target_pairs={{0,4},{4,0},{8,12},{12,8},{16,20},{20,16},{24,28},{28,24},{1,5},{5... | collective-permute-start | bytes 737288 | tf_op jit(solution)/shard_map/ppermute | solution.py:473
  127.8 24.1 %collective-permute-start.9 = (f16[4,240,128]{2,1,0:T(8,128)(2,1)S(1)}, f16[4,240,128]{2,1,0:T(8,128)(2,1)S(1)}, u32[]{:S(2)}, u32[]{:S(2)}) collective-permute-start(f16[4,240,128]{2,1,0:T(8,128)(2,1)S(1)} %convert_element_type.30), channel_id=1, source_target_pairs={{4,8},{8,4},{12,16},{16,12},{20,24},{24,20},{5,9},{9,5},{13,17},{1... | collective-permute-start | bytes 737288 | tf_op jit(solution)/shard_map/ppermute | solution.py:474
  131.2 3.7 %collective-permute-start.6 = (f32[128,128]{1,0:T(8,128)S(1)}, f32[128,128]{1,0:T(8,128)S(1)}, u32[]{:S(2)}, u32[]{:S(2)}) collective-permute-start(f32[128,128]{1,0:T(8,128)S(1)} %get-tuple-element.38), channel_id=1, source_target_pairs={{0,1},{1,0},{2,3},{3,2},{4,5},{5,4},{6,7},{7,6},{8,9},{9,8},{10,11... | collective-permute-start | bytes 196616 | tf_op jit(solution)/shard_map/ppermute | solution.py:473
  132.4 5.9 %collective-permute-start.7 = (f32[128,128]{1,0:T(8,128)S(1)}, f32[128,128]{1,0:T(8,128)S(1)}, u32[]{:S(2)}, u32[]{:S(2)}) collective-permute-start(f32[128,128]{1,0:T(8,128)S(1)} %get-tuple-element.39), channel_id=1, source_target_pairs={{1,2},{2,1},{5,6},{6,5},{9,10},{10,9},{13,14},{14,13},{17,18},{18,... | collective-permute-start | bytes 196616 | tf_op jit(solution)/shard_map/ppermute | solution.py:474
  139.0 13.0 %collective-permute-start.10 = (f32[64,128]{1,0:T(8,128)S(1)}, f32[64,128]{1,0:T(8,128)S(1)}, u32[]{:S(2)}, u32[]{:S(2)}) collective-permute-start(f32[64,128]{1,0:T(8,128)S(1)} %get-tuple-element.44), channel_id=1, source_target_pairs={{0,4},{4,0},{8,12},{12,8},{16,20},{20,16},{24,28},{28,24},{1,5},{5... | collective-permute-start | bytes 98312 | tf_op jit(solution)/shard_map/ppermute | solution.py:473
  139.1 12.9 %collective-permute-start.11 = (f32[64,128]{1,0:T(8,128)S(1)}, f32[64,128]{1,0:T(8,128)S(1)}, u32[]{:S(2)}, u32[]{:S(2)}) collective-permute-start(f32[64,128]{1,0:T(8,128)S(1)} %get-tuple-element.45), channel_id=1, source_target_pairs={{4,8},{8,4},{12,16},{16,12},{20,24},{24,20},{5,9},{9,5},{13,17},{1... | collective-permute-start | bytes 98312 | tf_op jit(solution)/shard_map/ppermute | solution.py:474
  146.3 5.7 %copy-start.12 = (bf16[128,1024]{1,0:T(8,128)(2,1)S(1)}, bf16[128,1024]{1,0:T(8,128)(2,1)}, u32[]{:S(2)}) copy-start(bf16[128,1024]{1,0:T(8,128)(2,1)} %constant.46.clone.corner_low) | copy-start | bytes 786436

commit v4 on v3

--- a/solution.py
+++ b/solution.py
@@ -139,11 +139,15 @@
         send(0, top)
 
 
-def pack_kernel(par_ref, control_ref, field_ref, rows_e, rows_o, strip_e, strip_o):
+def pack_kernel(par_ref, control_ref, rows_e, rows_o):
+    rows = control_ref.shape[1]
+    write_rows(par_ref[0], lambda r: control_ref[:, r, :] * CONTROL_FACTOR, rows, rows_e, rows_o)
+
+
+def turn_kernel(par_ref, after, control_ref, field_ref, strip_e, strip_o):
     hours, rows, _ = control_ref.shape
     for row in range(rows):
         field_ref[row] = control_ref[:, row, :]
-    write_rows(par_ref[0], lambda r: field_ref[r] * CONTROL_FACTOR, rows, rows_e, rows_o)
     fold_hours(pack_strips(lambda r: field_ref[r], par_ref[1], rows), hours, strip_e, strip_o)
 
 
@@ -153,34 +157,27 @@
 
 
 def prepare_kernel(
-    foot_ref, start_ref, row_ref, slot_ref, count_ref, out_ref,
-    start_vmem, row_vmem, slot_vmem, count_vmem, notes, sems, *, per,
+    after_e, after_o, foot_ref, start_ref, row_ref, slot_ref, count_ref, out_ref, notes, sems, *, per,
 ):
     owners, lines, _ = foot_ref.shape
     slots = start_ref.shape[0]
     blocks = pltpu.make_async_copy(foot_ref, out_ref.at[:, 0:lines, :], sems.at[0])
     blocks.start()
-    pairs = ((start_ref, start_vmem), (row_ref, row_vmem), (slot_ref, slot_vmem), (count_ref, count_vmem))
-    small = [pltpu.make_async_copy(a, b, sems.at[1 + i]) for i, (a, b) in enumerate(pairs)]
-    for copy in small:
-        copy.start()
-    for copy in small:
-        copy.wait()
-    start = start_vmem[...]
-    valid = lax.broadcasted_iota(jnp.int32, start.shape, 0) < count_vmem[...]
+    start = start_ref[...]
+    valid = lax.broadcasted_iota(jnp.int32, start.shape, 0) < count_ref[...]
     lanes = jnp.concatenate(
-        [start >> 4, start & 15, row_vmem[...], jnp.where(valid, slot_vmem[...], per)], axis=0
+        [start >> 4, start & 15, row_ref[...], jnp.where(valid, slot_ref[...], per)], axis=0
     ).astype(F32)
     wide = jnp.pad(lanes, ((0, LANES - 4 * slots), (0, LANES - owners)))
     turned = jnp.transpose(wide)[0:owners]
     notes[...] = jnp.broadcast_to(turned[:, None, :], notes.shape).astype(BF16)
-    copy = pltpu.make_async_copy(notes, out_ref.at[:, lines : lines + SUB, :], sems.at[5])
+    copy = pltpu.make_async_copy(notes, out_ref.at[:, lines : lines + SUB, :], sems.at[1])
     copy.start()
     copy.wait()
     blocks.wait()
 
 
-def corner_kernel(par_ref, strip_e, strip_o, halo_ref, corner_e, corner_o):
+def corner_kernel(par_ref, after, strip_e, strip_o, halo_ref, corner_e, corner_o):
     fold = strip_e.shape[0]
     quarter = corner_e.shape[0]
     half = LANES // 2
@@ -255,7 +252,7 @@
     return total
 
 
-def local_kernel(field_ref, time_high, time_low, col_both, out_ref, *, by_hour):
+def local_kernel(after, field_ref, time_high, time_low, col_both, out_ref):
     rows, hours, cols = field_ref.shape
     taps = space_taps()
     for row in range(0, rows, 2):
@@ -265,27 +262,20 @@
         ]
         both = time_sums(jnp.concatenate(pair, axis=1), time_high[...], time_low[...])
         for k, r in enumerate((row, row + 1)):
-            part = both[:, k * cols : (k + 1) * cols]
+            out_ref[r] = both[:, k * cols : (k + 1) * cols]
+
+
+def strips_kernel(local_ref, halo_ref, time_high, time_low, own_high, own_low, out_ref, *, by_hour):
+    rows, hours, cols = local_ref.shape
+    halo = halo_parts(time_sums(halo_ref[0:hours, :], time_high[...], time_low[...]))
+    for row in range(0, rows, 2):
+        both = halo_sums(halo, own_high, own_low, row * cols, 2 * cols)
+        for k, r in enumerate((row, row + 1)):
+            part = local_ref[r] + both[:, k * cols : (k + 1) * cols]
             if by_hour:
                 out_ref[:, r, :] = part
             else:
                 out_ref[r] = part
-
-
-def strips_kernel(local_ref, halo_ref, time_high, time_low, own_high, own_low, out_ref, *, by_hour):
-    if by_hour:
-        hours, rows, cols = local_ref.shape
-    else:
-        rows, hours, cols = local_ref.shape
-    halo = halo_parts(time_sums(halo_ref[0:hours, :], time_high[...], time_low[...]))
-    for row in range(0, rows, 2):
-        both = halo_sums(halo, own_high, own_low, row * cols, 2 * cols)
-        for k, r in enumerate((row, row + 1)):
-            part = both[:, k * cols : (k + 1) * cols]
-            if by_hour:
-                out_ref[:, r, :] = local_ref[:, r, :] + part
-            else:
-                out_ref[r] = local_ref[r] + part
 
 
 def edge_parts(is_even, rows, got_e, got_o, corner_e, corner_o, consts, halo, factor):
@@ -313,21 +303,14 @@
             yield r, both[:, k * cols : (k + 1) * cols]
 
 
-def flux_kernel(
-    par_ref, local_ref, prior_ref, scale_ref, got_e, got_o, corner_e, corner_o,
-    time_high, time_low, col_both, corner_high, corner_low, flux_ref, scale_out, halo, wide,
-):
-    rows, hours, cols = local_ref.shape
-    consts = (time_high, time_low, col_both, corner_high, corner_low)
+def flux_kernel(local_ref, prior_ref, scale_ref, flux_ref, scale_out, wide):
+    rows = local_ref.shape[0]
     wide[...] = scale_ref[...].astype(F32)
     for row in range(rows):
         scale_out[row] = wide[:, row, :]
     wide[...] = prior_ref[...].astype(F32)
-    for row in range(RAD, rows - RAD):
+    for row in range(rows):
         flux_ref[row] = wide[:, row, :] + scale_out[row] * local_ref[row]
-    parts = edge_parts(par_ref[0] == 0, rows, got_e, got_o, corner_e, corner_o, consts, halo, 1.0 / CONTROL_FACTOR)
-    for row, part in parts:
-        flux_ref[row] = wide[:, row, :] + scale_out[row] * (local_ref[row] + part)
 
 
 def finish_kernel(
@@ -338,17 +321,17 @@
     consts = (time_high, time_low, col_both, corner_high, corner_low)
     factor = factor_ref[1:2, :]
     parts = edge_parts(par_ref[0] == 0, rows, got_e, got_o, corner_e, corner_o, consts, halo, factor)
-    order = []
-    for k, (row, part) in enumerate(parts):
-        edges[k] = part
-        order.append(row)
+    for k, (_, part) in enumerate(parts):
+        edges[:, k, :] = part
     chunk = hours // PIECES
+    first = lax.broadcasted_iota(jnp.int32, (chunk, 2 * RAD, cols), 1) < RAD
     copies = []
     for piece in range(PIECES):
         here = slice(piece * chunk, (piece + 1) * chunk)
-        total[here] = local_ref[here]
-        for k, row in enumerate(order):
-            total[here, row, :] = total[here, row, :] + edges[k, here, :]
+        part = edges[here]
+        low, high = slice(0, 2 * RAD), slice(rows - 2 * RAD, rows)
+        total[here, low, :] = local_ref[here, low, :] + jnp.where(first, part, 0.0)
+        total[here, high, :] = local_ref[here, high, :] + jnp.where(first, 0.0, part)
         copies.append(pltpu.make_async_copy(total.at[here], out_ref.at[here], sems.at[piece]))
         copies[-1].start()
     for copy in copies:
@@ -363,12 +346,22 @@
 
 
 def forward_kernel(
-    foot_ref, flux_hbm, own_ref, out_ref, table_ref, flux_ref, sums, table_smem, sems,
-    *, shift, slots, heights, tiles, per,
+    par_ref, foot_ref, own_ref, flux_hbm, scale_hbm, *refs, shift, slots, heights, tiles, per,
 ):
+    far, near = refs[0:9], refs[11:20]
+    out_ref, table_ref = refs[9:11]
+    flux_ref, scale_ref, halo, sums, table_smem, sems = refs[20:]
+    got_e, got_o, corner_e, corner_o = near[0:4]
     sources = foot_ref.shape[0]
-    load = pltpu.make_async_copy(flux_hbm, flux_ref, sems.at[0])
-    load.start()
+    rows = flux_ref.shape[0]
+    pairs = list(zip(far, near)) + [
+        (scale_hbm.at[0:RAD], scale_ref.at[0:RAD]),
+        (scale_hbm.at[rows - RAD : rows], scale_ref.at[RAD : 2 * RAD]),
+        (flux_hbm, flux_ref),
+    ]
+    loads = [pltpu.make_async_copy(a, b, sems.at[i]) for i, (a, b) in enumerate(pairs)]
+    for load in loads:
+        load.start()
     groups = out_ref.shape[1] - 1
     base = slots * heights
     lane = lane_ids((sources, LANES))
@@ -379,10 +372,16 @@
     receptor = jnp.where(notes < per, source_rec * per + notes, groups * LANES)
     table = jnp.where(lane < slots, offset, receptor)
     table_ref[...] = table
-    copy = pltpu.make_async_copy(table_ref, table_smem, sems.at[1])
+    copy = pltpu.make_async_copy(table_ref, table_smem, sems.at[len(loads)])
     copy.start()
+    for load in loads:
+        load.wait()
+    parts = edge_parts(
+        par_ref[0] == 0, rows, got_e, got_o, corner_e, corner_o, near[4:], halo, 1.0 / CONTROL_FACTOR
+    )
+    for k, (row, part) in enumerate(parts):
+        flux_ref[row] = flux_ref[row] + scale_ref[k] * part
     copy.wait()
-    load.wait()
 
     def body(source, carry):
         for c, block in blocks_of(foot_ref, source, heights, slots):
@@ -480,14 +479,13 @@
 HB = pl.BlockSpec(memory_space=pltpu.HBM)
 
 
-def call(kernel, out_shape, in_specs, scratch, name, out_specs=None, alias=None):
+def call(kernel, out_shape, in_specs, scratch, name, out_specs=None):
     return pl.pallas_call(
         kernel,
         out_shape=out_shape,
         in_specs=in_specs,
         out_specs=jax.tree.map(lambda _: VM, out_shape) if out_specs is None else out_specs,
         scratch_shapes=scratch,
-        input_output_aliases={} if alias is None else alias,
         compiler_params=pltpu.CompilerParams(vmem_limit_bytes=VMEM_LIMIT),
         name=name,
     )
@@ -528,66 +526,53 @@
     field_shape = array(rows, hours, cols)
     halo_scratch = pltpu.VMEM((2 * RAD, hours, cols), F32)
 
+    def half(rows_e, rows_o):
+        return rows_e.astype(F16), rows_o.astype(F16)
+
+    def rows_of(rows_e, rows_o):
+        return [r.astype(F32) for r in swap("rec", rows_e, rows_o)]
+
+    def sides(after, strip_e, strip_o):
+        got_strips = swap("tile", strip_e, strip_o)
+        halo, corner_e, corner_o = call(
+            corner_kernel, [array(2 * fold, LANES), corner, corner], [SM, VM, VM, VM], [], "corners"
+        )(par, after, *got_strips)
+        return halo, swap("rec", corner_e, corner_o)
+
+    def inner_sums(field, strip_e, strip_o, by_hour, name):
+        def second(*refs):
+            strips_kernel(*refs, by_hour=by_hour)
+
+        local = call(local_kernel, field_shape, [VM] * 5, [], name + "_local")(strip_e, field, *base)
+        halo, got_corners = sides(local, strip_e, strip_o)
+        shape = array(hours, rows, cols) if by_hour else field_shape
+        local = call(second, shape, [VM] * 6, [], name + "_strips")(local, halo, *base[:2], *own_parts)
+        return local, got_corners
+
     def prepare(*refs):
         prepare_kernel(*refs, per=per)
 
-    numbers = pltpu.VMEM((slots, devices), jnp.int32)
+    rows_e, rows_o = call(pack_kernel, [block, block], [SM, VM], [], "pack_control")(par, control)
     sent = call(
         prepare,
         jax.ShapeDtypeStruct((devices, slots * heights + SUB, cols), BF16),
-        [HB] * 5,
-        [
-            numbers, numbers, numbers, pltpu.VMEM((1, devices), jnp.int32),
-            pltpu.VMEM((devices, SUB, LANES), BF16), pltpu.SemaphoreType.DMA((6,)),
-        ],
+        [VM] * 7,
+        [pltpu.VMEM((devices, SUB, LANES), BF16), pltpu.SemaphoreType.DMA((2,))],
         "prepare_blocks",
         out_specs=HB,
-    )(*[
-        pltpu.with_memory_space_constraint(x, pltpu.HBM)
-        for x in (
-            footprint.reshape(devices, slots * heights, cols),
-            start_hour.T, grid_row.T, receptor_slot.T, slot_count[None],
-        )
-    ])
+    )(
+        rows_e, rows_o, footprint.reshape(devices, slots * heights, cols),
+        start_hour.T, grid_row.T, receptor_slot.T, slot_count[None],
+    )
     foot = lax.all_to_all(sent, AXES, split_axis=0, concat_axis=0, tiled=True)
-
-    field, rows_e, rows_o, strip_e, strip_o = call(
-        pack_kernel, [field_shape, block, block, strip, strip], [SM, VM], [], "pack_control"
-    )(par, control)
-
-    def neighbours(rows_e, rows_o):
-        return [r.astype(F32) for r in swap("rec", rows_e.astype(F16), rows_o.astype(F16))]
-
-    def sides(strip_e, strip_o):
-        got_strips = swap("tile", strip_e, strip_o)
-        halo, corner_e, corner_o = call(
-            corner_kernel, [array(2 * fold, LANES), corner, corner], [SM, VM, VM], [], "corners"
-        )(par, *got_strips)
-        return halo, swap("rec", corner_e, corner_o)
-
-    def inner_sums(field, halo, by_hour, name):
-        def first(*refs):
-            local_kernel(*refs, by_hour=by_hour)
-
-        def second(*refs):
-            strips_kernel(*refs, by_hour=by_hour)
-
-        shape = array(hours, rows, cols) if by_hour else field_shape
-        local = call(first, shape, [VM] * 4, [], name + "_local")(field, *base)
-        return call(second, shape, [VM] * 6, [], name + "_strips", alias={0: 0})(
-            local, halo, *base[:2], *own_parts
-        )
-
-    got_rows = neighbours(rows_e, rows_o)
-    halo, got_corners = sides(strip_e, strip_o)
-    local = inner_sums(field, halo, False, "control")
+    got_rows = rows_of(*half(rows_e, rows_o))
+    field, *strips = call(
+        turn_kernel, [field_shape, strip, strip], [SM, HB, VM], [], "turn_control"
+    )(par, sent, control)
+    local, got_corners = inner_sums(field, *strips, False, "control")
     flux, scale = call(
-        flux_kernel,
-        [field_shape, field_shape],
-        [SM] + [VM] * 12,
-        [halo_scratch, pltpu.VMEM((hours, rows, cols), F32)],
-        "flux_field",
-    )(par, local, prior_flux, flux_scale, *got_rows, *got_corners, *base, *corner_parts)
+        flux_kernel, [field_shape, field_shape], [VM] * 3, [pltpu.VMEM((hours, rows, cols), F32)], "flux_inner"
+    )(local, prior_flux, flux_scale)
 
     own = jnp.concatenate([observed, obs_error, jnp.zeros((LANES - 2 * per,), F32)])[None]
     sizes = dict(shift=shift, slots=slots, heights=heights, tiles=n_tile, per=per)
@@ -595,18 +580,20 @@
     def forward(*refs):
         forward_kernel(*refs, **sizes)
 
+    needed = [*got_rows, *got_corners, *base, *corner_parts]
     partial, table = call(
         forward,
         [array(devices, groups + 1, LANES), jax.ShapeDtypeStruct((devices, LANES), jnp.int32)],
-        [VM, HB, VM],
-        [
-            pltpu.VMEM((rows, hours, cols), F32),
+        [SM, VM, VM] + [HB] * 11,
+        [pltpu.VMEM(x.shape, x.dtype) for x in needed]
+        + [pltpu.VMEM((rows, hours, cols), F32), halo_scratch, halo_scratch]
+        + [
             pltpu.VMEM((slots, devices, LANES), F32),
             pltpu.SMEM((devices, LANES), jnp.int32),
-            pltpu.SemaphoreType.DMA((2,)),
+            pltpu.SemaphoreType.DMA((len(needed) + 4,)),
         ],
         "block_values",
-    )(foot, flux, own)
+    )(par, foot, own, *[pltpu.with_memory_space_constraint(x, pltpu.HBM) for x in (flux, scale, *needed)])
     everyone = lax.all_to_all(partial, AXES, split_axis=0, concat_axis=0, tiled=True)
 
     def adjoint(*refs):
@@ -624,17 +611,16 @@
         ],
         "adjoint_field",
     )(par, table, everyone, foot, scale)
-    got_rows = neighbours(rows_e, rows_o)
+    got_rows = rows_of(*half(rows_e, rows_o))
     strips = call(strip_kernel, [strip, strip], [SM, VM], [], "pack_strips")(par, field)
-    halo, got_corners = sides(*strips)
-    local = inner_sums(field, halo, True, "gradient")
+    local, got_corners = inner_sums(field, *strips, True, "gradient")
     gradient = call(
         finish_kernel,
         array(hours, rows, cols),
         [SM] + [VM] * 11,
         [
             halo_scratch,
-            halo_scratch,
+            pltpu.VMEM((hours, 2 * RAD, cols), F32),
             pltpu.VMEM((hours, rows, cols), F32),
             pltpu.SemaphoreType.DMA((PIECES,)),
         ],

time: 157 us -> 101 us (0.64)
  Pallas kernels: 82 us -> 31.7 us
  waiting for transfers between devices: 17.1 us -> 11.4 us
  blocking collectives: 21.8 us -> 17.4 us
  starting transfers between devices: 28.1 us -> 29.9 us
  other arithmetic: 0.43 us -> 2.01 us
    pallas_call x1, Pallas kernels: 48.8 us -> 1.21 us  [per_device(): call(prepare, jax.ShapeDtypeStruct((devices, slots * heights + SUB, cols)...]
    ppermute x6, waiting for transfers between devices: 17.1 us -> 6.39 us  [swap(): lax.ppermute(odd, axis, swap_pairs(count, True))]
    pallas_call x6 -> x7, Pallas kernels: 19.6 us -> 13.2 us  [the longest x2 4.52 us: inner_sums(): call(local_kernel, field_shape, [VM] * 5, [], name + '_local')]
    all_to_all x1, waiting for transfers between devices: 0.01 us -> 5.04 us  [per_device(): foot = lax.all_to_all(sent, AXES, split_axis=0, concat_axis=0, tiled=True)]
    all_to_all x1, blocking collectives: 21.8 us -> 17.4 us  [per_device(): lax.all_to_all(partial, AXES, split_axis=0, concat_axis=0, tiled=True)]
    pallas_call x1, Pallas kernels: 2.53 us -> 6.44 us  [per_device(): call(forward, [array(devices, groups + 1, LANES), jax.ShapeDtypeStruct((d...]
    ppermute x6, starting transfers between devices: 17.7 us -> 19.6 us  [swap(): lax.ppermute(odd, axis, swap_pairs(count, True))]
    convert_element_type x8, other arithmetic: 0.28 us -> 1.86 us  [the longest x4 1.71 us: rows_of(): return [r.astype(F32) for r in swap('rec', rows_e, rows_o)]]
  transfers between devices with their start and end apart: 13 -> 13, of which waited for: 4 -> 4; matrix products, arithmetic and copies ran while one was open for 0% -> 2% of each run, Pallas kernels for 14% -> 15%
where the time goes in v4:
time: 101 us; the launch traced here: 100 us
  Pallas kernels  31.7 us (31%)
  starting transfers between devices  29.9 us (30%)
  blocking collectives  17.4 us (17%)
  waiting for transfers between devices  11.4 us (11%)
  local copies, waits for them, and re-layouts  6.26 us (6%)
  other arithmetic  2.01 us (2%)
  between operations  1.32 us (1%)
    ppermute x6, starting transfers between devices, swap(): lax.ppermute(odd, axis, swap_pairs(count, True))  19.6 us
    all_to_all x1, blocking collectives, per_device(): lax.all_to_all(partial, AXES, split_axis=0, concat_axis=0, tiled=True)  17.4 us
    pallas_call x1, Pallas kernels, per_device(): call(forward, [array(devices, groups + 1, LANES), jax.ShapeDtypeStruct((d...  6.44 us
    all_to_all x1, starting transfers between devices, per_device(): foot = lax.all_to_all(sent, AXES, split_axis=0, concat_axis=0, tiled=True)  6.42 us
    ppermute x6, waiting for transfers between devices, swap(): lax.ppermute(odd, axis, swap_pairs(count, True))  6.39 us
    unnamed x52, local copies, waits for them, and re-layouts  6.26 us
    all_to_all x1, waiting for transfers between devices, per_device(): foot = lax.all_to_all(sent, AXES, split_axis=0, concat_axis=0, tiled=True)  5.04 us
    pallas_call x2, Pallas kernels, inner_sums(): call(local_kernel, field_shape, [VM] * 5, [], name + '_local')  4.52 us
  transfers between devices with their start and end apart: 13, of which 4 were waited for; matrix products, arithmetic and copies ran while one was open for 2% of the time, Pallas kernels for 15%

profile of v4, /device:TPU:5, one launch (start us, length us, event | category | flops | bytes accessed | tf_op | source)
XLA Modules:
  0.0 100.0 jit_solution(15959457472189018305)
XLA Ops:
  0.7 0.1 pad_add_fusion.par_ref.refs_0_
  0.8 1.5 %copy-done = f32[240,16,128]{2,1,0:T(8,128)S(1)} copy-done((f32[240,16,128]{2,1,0:T(8,128)S(1)}, f32[240,16,128]{2,1,0:T(8,128)}, u32[]{:S(2)}) %copy-start) | copy-done | bytes 1966104
  2.3 1.3 %pack_control.1 = (f32[4,240,128]{2,1,0:T(8,128)S(1)}, f32[4,240,128]{2,1,0:T(8,128)S(1)}) custom-call(s32[3]{0:T(128)S(1)} %pad_add_fusion.par_ref.refs_0_, f32[240,16,128]{2,1,0:T(8,128)S(1)} %copy-done), custom_call_target="tpu_custom_call" | custom-call | tf_op jit(solution)/shard_map/pack_control/pallas_call | solution.py:555
  3.7 0.0 copy-done.13
  3.7 1.2 %prepare_blocks.1.after = bf16[32,200,128]{2,1,0:T(8,128)(2,1)} custom-call(f32[4,240,128]{2,1,0:T(8,128)S(1)} %get-tuple-element.24.refs_0_, f32[4,240,128]{2,1,0:T(8,128)S(1)} %get-tuple-element.25.refs_1_, bf16[32,192,128]{2,1,0:T(8,128)(2,1)S(1)} %bitcast.11, s32[8,32]{1,0:T(8,128)S(1)} %bitcast.12, s32[8,32]{1,0:T(8,128)S(1)} %bitcast.13, ...), custom_call_target="tpu_custom_call" | custom-call | tf_op jit(solution)/shard_map/prepare_blocks/pallas_call | solution.py:556
  4.9 6.4 %all-to-all-start = ((bf16[32,200,128]{2,1,0:T(8,128)(2,1)}), bf16[32,200,128]{2,1,0:T(8,128)(2,1)S(1)}, u32[]{:S(2)}, u32[]{:S(2)}) async-start(bf16[32,200,128]{2,1,0:T(8,128)(2,1)} %prepare_blocks.1.after), calls=%async_computation | async-start | bytes 3276800 | tf_op jit(solution)/shard_map/all_to_all | solution.py:567
  11.4 0.1 collective-permute-start.2
  11.6 4.2 %collective-permute-start.3 = (f16[4,240,128]{2,1,0:T(8,128)(2,1)S(1)}, f16[4,240,128]{2,1,0:T(8,128)(2,1)S(1)}, u32[]{:S(2)}, u32[]{:S(2)}) collective-permute-start(f16[4,240,128]{2,1,0:T(8,128)(2,1)S(1)} %convert_element_type.26), channel_id=1, source_target_pairs={{4,8},{8,4},{12,16},{16,12},{20,24},{24,20},{5,9},{9,5},{13,17},{1... | collective-permute-start | bytes 737288 | tf_op jit(solution)/shard_map/ppermute | solution.py:473
  15.8 0.0 copy-start.1
  15.8 1.5 %copy-done.1 = f32[240,16,128]{2,1,0:T(8,128)S(1)} copy-done((f32[240,16,128]{2,1,0:T(8,128)S(1)}, f32[240,16,128]{2,1,0:T(8,128)}, u32[]{:S(2)}) %copy-start.1) | copy-done | bytes 1966104
  17.4 2.1 %turn_control.1 = (f32[16,240,128]{2,1,0:T(8,128)S(1)}, f32[128,128]{1,0:T(8,128)S(1)}, f32[128,128]{1,0:T(8,128)S(1)}) custom-call(s32[3]{0:T(128)S(1)} %pad_add_fusion.par_ref.refs_0_, bf16[32,200,128]{2,1,0:T(8,128)(2,1)} %prepare_blocks.1.after, f32[240,16,128]{2,1,0:T(8,128)S(1)} %copy-done.1), custom_call_target="tpu_custom_call" | custom-call | tf_op jit(solution)/shard_map/turn_control/pallas_call | solution.py:569
  19.4 1.0 collective-permute-start
  20.4 3.0 %collective-permute-start.1 = (f32[128,128]{1,0:T(8,128)S(1)}, f32[128,128]{1,0:T(8,128)S(1)}, u32[]{:S(2)}, u32[]{:S(2)}) collective-permute-start(f32[128,128]{1,0:T(8,128)S(1)} %get-tuple-element.28), channel_id=1, source_target_pairs={{1,2},{2,1},{5,6},{6,5},{9,10},{10,9},{13,14},{14,13},{17,18},{18,... | collective-permute-start | bytes 196616 | tf_op jit(solution)/shard_map/ppermute | solution.py:473
  23.4 2.3 %control_local.1.after.refs_0_ = f32[16,240,128]{2,1,0:T(8,128)S(1)} custom-call(f32[128,128]{1,0:T(8,128)S(1)} %get-tuple-element.26.after, f32[16,240,128]{2,1,0:T(8,128)S(1)} %get-tuple-element.27.field_ref, bf16[240,240]{1,0:T(8,128)(2,1)S(1)} %copy-done.4, bf16[240,240]{1,0:T(8,128)(2,1)S(1)} %copy-done.6, bf16[256,256]{1,0:T(8,128)(2,1)S(1)} %copy-done.8), custom_call_target="tpu_custom_call" | custom-call | tf_op jit(solution)/shard_map/control_local/pallas_call | solution.py:546
  25.7 0.0 copy-start.24
  25.7 0.0 copy-start.25
  25.7 0.0 copy-start.10
  25.8 0.0 copy-start.11
  25.8 0.0 collective-permute-done.strip_e
  25.8 0.6 collective-permute-done.1.strip_o
  26.3 0.8 corners.2
  27.1 0.1 collective-permute-start.4
  27.2 4.2 %collective-permute-start.5 = (f32[64,128]{1,0:T(8,128)S(1)}, f32[64,128]{1,0:T(8,128)S(1)}, u32[]{:S(2)}, u32[]{:S(2)}) collective-permute-start(f32[64,128]{1,0:T(8,128)S(1)} %get-tuple-element.33), channel_id=1, source_target_pairs={{4,8},{8,4},{12,16},{16,12},{20,24},{24,20},{5,9},{9,5},{13,17},{1... | collective-permute-start | bytes 98312 | tf_op jit(solution)/shard_map/ppermute | solution.py:473
  31.4 0.0 copy-done.24
  31.4 0.0 copy-done.25
  31.4 0.1 maximum_bitcast_fusion.refs_2_
  31.5 1.1 %control_strips.1.local_ref = f32[16,240,128]{2,1,0:T(8,128)S(1)} custom-call(f32[16,240,128]{2,1,0:T(8,128)S(1)} %control_local.1.after.refs_0_, f32[256,128]{1,0:T(8,128)S(1)} %get-tuple-element.29.refs_1_, bf16[240,240]{1,0:T(8,128)(2,1)S(1)} %copy-done.4, bf16[240,240]{1,0:T(8,128)(2,1)S(1)} %copy-done.6, bf16[128,2048]{1,0:T(8,128)(2,1)S(1)} %copy-done.10, ...), custom_call_target="tpu_custom_call" | custom-call | tf_op jit(solution)/shard_map/control_strips/pallas_call | solution.py:549
  32.6 0.1 copy-done.16
  32.7 0.3 copy-done.17
  33.0 2.5 %flux_inner.1 = (f32[16,240,128]{2,1,0:T(8,128)S(1)}, f32[16,240,128]{2,1,0:T(8,128)S(1)}) custom-call(f32[16,240,128]{2,1,0:T(8,128)S(1)} %control_strips.1.local_ref, bf16[240,16,128]{2,1,0:T(8,128)(2,1)S(1)} %copy-done.16, bf16[240,16,128]{2,1,0:T(8,128)(2,1)S(1)} %copy-done.17), custom_call_target="tpu_custom_call" | custom-call | tf_op jit(solution)/shard_map/flux_inner/pallas_call | solution.py:573
  35.5 1.3 %copy-done.2 = f32[16,240,128]{2,1,0:T(8,128)} copy-done((f32[16,240,128]{2,1,0:T(8,128)}, f32[16,240,128]{2,1,0:T(8,128)S(1)}, u32[]{:S(2)}) %copy-start.2) | copy-done | bytes 1966104
  36.9 1.3 %copy-done.12 = f32[16,240,128]{2,1,0:T(8,128)} copy-done((f32[16,240,128]{2,1,0:T(8,128)}, f32[16,240,128]{2,1,0:T(8,128)S(1)}, u32[]{:S(2)}) %copy-start.12) | copy-done | bytes 1966104
  38.1 0.0 collective-permute-done.2
  38.1 0.8 convert_element_type.25.refs_5_
  39.0 4.6 %collective-permute-done.3 = f16[4,240,128]{2,1,0:T(8,128)(2,1)S(1)} collective-permute-done((f16[4,240,128]{2,1,0:T(8,128)(2,1)S(1)}, f16[4,240,128]{2,1,0:T(8,128)(2,1)S(1)}, u32[]{:S(2)}, u32[]{:S(2)}) %collective-permute-start.3) | collective-permute-done | bytes 245792 | tf_op jit(solution)/shard_map/ppermute | solution.py:473
  43.6 0.8 convert_element_type.27.refs_6_
  44.4 0.0 collective-permute-done.4.refs_7_
  44.4 0.0 collective-permute-done.5.refs_8_
  44.4 5.0 %all-to-all-done.refs_1_.refs_3_ = bf16[32,200,128]{2,1,0:T(8,128)(2,1)S(1)} async-done(((bf16[32,200,128]{2,1,0:T(8,128)(2,1)}), bf16[32,200,128]{2,1,0:T(8,128)(2,1)S(1)}, u32[]{:S(2)}, u32[]{:S(2)}) %all-to-all-start) | async-done | bytes 1638432 | tf_op jit(solution)/shard_map/all_to_all | solution.py:567
  49.5 6.4 %block_values.1 = (f32[32,5,128]{2,1,0:T(8,128)S(1)}, s32[32,128]{1,0:T(8,128)S(1)}) custom-call(s32[3]{0:T(128)S(1)} %pad_add_fusion.par_ref.refs_0_, bf16[32,200,128]{2,1,0:T(8,128)(2,1)S(1)} %all-to-all-done.refs_1_.refs_3_, f32[1,128]{1,0:T(1,128)S(1)} %maximum_bitcast_fusion.refs_2_, f32[16,240,128]{2,1,0:T(8,128)} %copy-done.12, ...), custom_call_target="tpu_custom_call" | custom-call | tf_op jit(solution)/shard_map/block_values/pallas_call | solution.py:584
  55.9 17.4 %all_to_all.10.refs_2_ = f32[32,5,128]{2,1,0:T(8,128)S(1)} all-to-all(f32[32,5,128]{2,1,0:T(8,128)S(1)} %get-tuple-element.35), channel_id=1, replica_groups=mesh['rec'=8,'tile'=4] {'rec','tile'}, dimensions={0} | all-to-all | bytes 163840 | tf_op jit(solution)/shard_map/all_to_all | solution.py:597
  73.3 3.9 %adjoint_field.1 = (f32[1,64]{1,0:T(1,128)}, f32[2,128]{1,0:T(2,128)S(1)}, f32[16,240,128]{2,1,0:T(8,128)S(1)}, f32[4,240,128]{2,1,0:T(8,128)S(1)}, f32[4,240,128]{2,1,0:T(8,128)S(1)}) custom-call(s32[3]{0:T(128)S(1)} %pad_add_fusion.par_ref.refs_0_, s32[32,128]{1,0:T(8,128)S(1)} %get-tuple-element.34.refs_1_, f32[32,5,128]{2,1,0:T(8,128)S(1)} %all_to_all.10.refs_2_, ...), custom_call_target="tpu_custom_call" | custom-call | tf_op jit(solution)/shard_map/adjoint_field/pallas_call | solution.py:603
  77.2 0.0 copy-start.5
  77.2 0.0 copy-start.7
  77.2 0.0 copy-start.9
  77.2 1.5 %collective-permute-start.8 = (f16[4,240,128]{2,1,0:T(8,128)(2,1)S(1)}, f16[4,240,128]{2,1,0:T(8,128)(2,1)S(1)}, u32[]{:S(2)}, u32[]{:S(2)}) collective-permute-start(f16[4,240,128]{2,1,0:T(8,128)(2,1)S(1)} %convert_element_type.28), channel_id=1, source_target_pairs={{0,4},{4,0},{8,12},{12,8},{16,20},{20,16},{24,28},{28,24},{1,5},{5... | collective-permute-start | bytes 737288 | tf_op jit(solution)/shard_map/ppermute | solution.py:472
  78.8 2.1 %collective-permute-start.9 = (f16[4,240,128]{2,1,0:T(8,128)(2,1)S(1)}, f16[4,240,128]{2,1,0:T(8,128)(2,1)S(1)}, u32[]{:S(2)}, u32[]{:S(2)}) collective-permute-start(f16[4,240,128]{2,1,0:T(8,128)(2,1)S(1)} %convert_element_type.30), channel_id=1, source_target_pairs={{4,8},{8,4},{12,16},{16,12},{20,24},{24,20},{5,9},{9,5},{13,17},{1... | collective-permute-start | bytes 737288 | tf_op jit(solution)/shard_map/ppermute | solution.py:473
  80.9 1.3 %pack_strips.1 = (f32[128,128]{1,0:T(8,128)S(1)}, f32[128,128]{1,0:T(8,128)S(1)}) custom-call(s32[3]{0:T(128)S(1)} %pad_add_fusion.par_ref.refs_0_, f32[16,240,128]{2,1,0:T(8,128)S(1)} %get-tuple-element.37.field_ref), custom_call_target="tpu_custom_call" | custom-call | tf_op jit(solution)/shard_map/pack_strips/pallas_call | solution.py:615
  82.2 1.2 %collective-permute-start.6 = (f32[128,128]{1,0:T(8,128)S(1)}, f32[128,128]{1,0:T(8,128)S(1)}, u32[]{:S(2)}, u32[]{:S(2)}) collective-permute-start(f32[128,128]{1,0:T(8,128)S(1)} %get-tuple-element.38.after), channel_id=1, source_target_pairs={{0,1},{1,0},{2,3},{3,2},{4,5},{5,4},{6,7},{7,6},{8,9},{9,8},{10,11... | collective-permute-start | bytes 196616 | tf_op jit(solution)/shard_map/ppermute | solution.py:472
  83.4 2.3 %collective-permute-start.7 = (f32[128,128]{1,0:T(8,128)S(1)}, f32[128,128]{1,0:T(8,128)S(1)}, u32[]{:S(2)}, u32[]{:S(2)}) collective-permute-start(f32[128,128]{1,0:T(8,128)S(1)} %get-tuple-element.39), channel_id=1, source_target_pairs={{1,2},{2,1},{5,6},{6,5},{9,10},{10,9},{13,14},{14,13},{17,18},{18,... | collective-permute-start | bytes 196616 | tf_op jit(solution)/shard_map/ppermute | solution.py:473
  85.8 2.3 %gradient_local.1.after.refs_0_ = f32[16,240,128]{2,1,0:T(8,128)S(1)} custom-call(f32[128,128]{1,0:T(8,128)S(1)} %get-tuple-element.38.after, f32[16,240,128]{2,1,0:T(8,128)S(1)} %get-tuple-element.37.field_ref, bf16[240,240]{1,0:T(8,128)(2,1)S(1)} %copy-done.5, bf16[240,240]{1,0:T(8,128)(2,1)S(1)} %copy-done.7, bf16[256,256]{1,0:T(8,128)(2,1)S(1)} %copy-done.9), custom_call_target="tpu_custom_call" | custom-call | tf_op jit(solution)/shard_map/gradient_local/pallas_call | solution.py:546
  88.0 0.0 collective-permute-done.6.strip_e
  88.0 1.2 %collective-permute-done.7.strip_o = f32[128,128]{1,0:T(8,128)S(1)} collective-permute-done((f32[128,128]{1,0:T(8,128)S(1)}, f32[128,128]{1,0:T(8,128)S(1)}, u32[]{:S(2)}, u32[]{:S(2)}) %collective-permute-start.7) | collective-permute-done | bytes 65568 | tf_op jit(solution)/shard_map/ppermute | solution.py:473
  89.2 0.8 corners.3
  90.0 0.1 collective-permute-start.10
  90.1 3.7 %collective-permute-start.11 = (f32[64,128]{1,0:T(8,128)S(1)}, f32[64,128]{1,0:T(8,128)S(1)}, u32[]{:S(2)}, u32[]{:S(2)}) collective-permute-start(f32[64,128]{1,0:T(8,128)S(1)} %get-tuple-element.45), channel_id=1, source_target_pairs={{4,8},{8,4},{12,16},{16,12},{20,24},{24,20},{5,9},{9,5},{13,17},{1... | collective-permute-start | bytes 98312 | tf_op jit(solution)/shard_map/ppermute | solution.py:473
  93.8 0.0 copy-start.14
  93.8 0.0 copy-start.15
  93.8 1.7 %gradient_strips.1.local_ref = f32[240,16,128]{2,1,0:T(8,128)S(1)} custom-call(f32[16,240,128]{2,1,0:T(8,128)S(1)} %gradient_local.1.after.refs_0_, f32[256,128]{1,0:T(8,128)S(1)} %get-tuple-element.40.refs_1_, bf16[240,240]{1,0:T(8,128)(2,1)S(1)} %copy-done.5, bf16[240,240]{1,0:T(8,128)(2,1)S(1)} %copy-done.7, bf16[128,2048]{1,0:T(8,128)(2,1)S(1)} %copy-done.10, ...), custom_call_target="tpu_custom_call" | custom-call | tf_op jit(solution)/shard_map/gradient_strips/pallas_call | solution.py:549
  95.5 0.0 collective-permute-done.8
  95.6 0.0 collective-permute-done.9
  95.6 0.0 collective-permute-done.10.corner_e
  95.7 0.0 collective-permute-done.11.corner_o
  95.7 4.2 %gradient.1 = f32[240,16,128]{2,1,0:T(8,128)} custom-call(s32[3]{0:T(128)S(1)} %pad_add_fusion.par_ref.refs_0_, f32[240,16,128]{2,1,0:T(8,128)S(1)} %gradient_strips.1.local_ref, f32[2,128]{1,0:T(2,128)S(1)} %get-tuple-element.41.factor_ref, f32[4,240,128]{2,1,0:T(8,128)S(1)} %convert_element_type.29.got_e, f32[4,240,128]{2,1,0:T(8,128)S(1)} %convert_element_type.31.got_o, ...), custom_call_target="tpu_custom_call" | custom-call | tf_op jit(solution)/shard_map/gradient/pallas_call | solution.py:617
  (39 shorter events, 0.3 us)
Async XLA Ops:
  0.6 3.0 %copy-start.18 = (s32[32,8]{0,1:T(8,128)S(1)}, s32[32,8]{0,1:T(8,128)}, u32[]{:S(2)}) copy-start(s32[32,8]{0,1:T(8,128)} %param.22) | copy-start | bytes 3076
  0.6 3.0 %copy-start.19 = (s32[32,8]{0,1:T(8,128)S(1)}, s32[32,8]{0,1:T(8,128)}, u32[]{:S(2)}) copy-start(s32[32,8]{0,1:T(8,128)} %param.23) | copy-start | bytes 3076
  0.7 3.0 %copy-start.20 = (s32[32,8]{0,1:T(8,128)S(1)}, s32[32,8]{0,1:T(8,128)}, u32[]{:S(2)}) copy-start(s32[32,8]{0,1:T(8,128)} %param.24) | copy-start | bytes 3076
  0.7 3.0 %copy-start.21 = (s32[32]{0:T(128)S(1)}, s32[32]{0:T(128)}, u32[]{:S(2)}) copy-start(s32[32]{0:T(128)} %param.21) | copy-start | bytes 388
  0.8 1.5 %copy-start = (f32[240,16,128]{2,1,0:T(8,128)S(1)}, f32[240,16,128]{2,1,0:T(8,128)}, u32[]{:S(2)}) copy-start(f32[240,16,128]{2,1,0:T(8,128)} %control_ref.3) | copy-start | bytes 5898244
  2.3 1.4 %copy-start.13 = (bf16[32,8,24,128]{3,2,1,0:T(8,128)(2,1)S(1)}, bf16[32,8,24,128]{3,2,1,0:T(8,128)(2,1)}, u32[]{:S(2)}) copy-start(bf16[32,8,24,128]{3,2,1,0:T(8,128)(2,1)} %param.20) | copy-start | bytes 4718596
  4.9 44.5 %all-to-all-start = ((bf16[32,200,128]{2,1,0:T(8,128)(2,1)}), bf16[32,200,128]{2,1,0:T(8,128)(2,1)S(1)}, u32[]{:S(2)}, u32[]{:S(2)}) async-start(bf16[32,200,128]{2,1,0:T(8,128)(2,1)} %prepare_blocks.1.after), calls=%async_computation | async-start | bytes 3276800 | tf_op jit(solution)/shard_map/all_to_all | solution.py:567
  11.4 26.7 %collective-permute-start.2 = (f16[4,240,128]{2,1,0:T(8,128)(2,1)S(1)}, f16[4,240,128]{2,1,0:T(8,128)(2,1)S(1)}, u32[]{:S(2)}, u32[]{:S(2)}) collective-permute-start(f16[4,240,128]{2,1,0:T(8,128)(2,1)S(1)} %convert_element_type.24), channel_id=1, source_target_pairs={{0,4},{4,0},{8,12},{12,8},{16,20},{20,16},{24,28},{28,24},{1,5},{5... | collective-permute-start | bytes 737288 | tf_op jit(solution)/shard_map/ppermute | solution.py:472
  11.6 32.0 %collective-permute-start.3 = (f16[4,240,128]{2,1,0:T(8,128)(2,1)S(1)}, f16[4,240,128]{2,1,0:T(8,128)(2,1)S(1)}, u32[]{:S(2)}, u32[]{:S(2)}) collective-permute-start(f16[4,240,128]{2,1,0:T(8,128)(2,1)S(1)} %convert_element_type.26), channel_id=1, source_target_pairs={{4,8},{8,4},{12,16},{16,12},{20,24},{24,20},{5,9},{9,5},{13,17},{1... | collective-permute-start | bytes 737288 | tf_op jit(solution)/shard_map/ppermute | solution.py:473
  15.8 1.5 %copy-start.1 = (f32[240,16,128]{2,1,0:T(8,128)S(1)}, f32[240,16,128]{2,1,0:T(8,128)}, u32[]{:S(2)}) copy-start(f32[240,16,128]{2,1,0:T(8,128)} %control_ref.3) | copy-start | bytes 5898244
  17.3 6.1 %copy-start.4 = (bf16[240,240]{1,0:T(8,128)(2,1)S(1)}, bf16[240,240]{1,0:T(8,128)(2,1)}, u32[]{:S(2)}) copy-start(bf16[240,240]{1,0:T(8,128)(2,1)} %constant.40.clone.time_high.refs_2_.refs_9_) | copy-start | bytes 345604
  17.4 6.1 %copy-start.6 = (bf16[240,240]{1,0:T(8,128)(2,1)S(1)}, bf16[240,240]{1,0:T(8,128)(2,1)}, u32[]{:S(2)}) copy-start(bf16[240,240]{1,0:T(8,128)(2,1)} %constant.41.clone.time_low.refs_3_.refs_10_) | copy-start | bytes 345604
  17.4 6.1 %copy-start.8 = (bf16[256,256]{1,0:T(8,128)(2,1)S(1)}, bf16[256,256]{1,0:T(8,128)(2,1)}, u32[]{:S(2)}) copy-start(bf16[256,256]{1,0:T(8,128)(2,1)} %constant.42.clone.col_both.refs_11_) | copy-start | bytes 393220
  19.4 6.3 %collective-permute-start = (f32[128,128]{1,0:T(8,128)S(1)}, f32[128,128]{1,0:T(8,128)S(1)}, u32[]{:S(2)}, u32[]{:S(2)}) collective-permute-start(f32[128,128]{1,0:T(8,128)S(1)} %get-tuple-element.26.after), channel_id=1, source_target_pairs={{0,1},{1,0},{2,3},{3,2},{4,5},{5,4},{6,7},{7,6},{8,9},{9,8},{10,11... | collective-permute-start | bytes 196616 | tf_op jit(solution)/shard_map/ppermute | solution.py:472
  20.4 5.9 %collective-permute-start.1 = (f32[128,128]{1,0:T(8,128)S(1)}, f32[128,128]{1,0:T(8,128)S(1)}, u32[]{:S(2)}, u32[]{:S(2)}) collective-permute-start(f32[128,128]{1,0:T(8,128)S(1)} %get-tuple-element.28), channel_id=1, source_target_pairs={{1,2},{2,1},{5,6},{6,5},{9,10},{10,9},{13,14},{14,13},{17,18},{18,... | collective-permute-start | bytes 196616 | tf_op jit(solution)/shard_map/ppermute | solution.py:473
  25.7 5.7 %copy-start.24 = (f32[64]{0:T(128)S(1)}, f32[64]{0:T(128)}, u32[]{:S(2)}) copy-start(f32[64]{0:T(128)} %param.26) | copy-start | bytes 772
  25.7 5.7 %copy-start.25 = (f32[64]{0:T(128)S(1)}, f32[64]{0:T(128)}, u32[]{:S(2)}) copy-start(f32[64]{0:T(128)} %param.25) | copy-start | bytes 772
  25.7 5.8 %copy-start.10 = (bf16[128,2048]{1,0:T(8,128)(2,1)S(1)}, bf16[128,2048]{1,0:T(8,128)(2,1)}, u32[]{:S(2)}) copy-start(bf16[128,2048]{1,0:T(8,128)(2,1)} %constant.43.clone.refs_4_) | copy-start | bytes 1572868
  25.8 5.8 %copy-start.11 = (bf16[128,2048]{1,0:T(8,128)(2,1)S(1)}, bf16[128,2048]{1,0:T(8,128)(2,1)}, u32[]{:S(2)}) copy-start(bf16[128,2048]{1,0:T(8,128)(2,1)} %constant.44.clone.refs_5_) | copy-start | bytes 1572868
  27.1 17.3 %collective-permute-start.4 = (f32[64,128]{1,0:T(8,128)S(1)}, f32[64,128]{1,0:T(8,128)S(1)}, u32[]{:S(2)}, u32[]{:S(2)}) collective-permute-start(f32[64,128]{1,0:T(8,128)S(1)} %get-tuple-element.32), channel_id=1, source_target_pairs={{0,4},{4,0},{8,12},{12,8},{16,20},{20,16},{24,28},{28,24},{1,5},{5... | collective-permute-start | bytes 98312 | tf_op jit(solution)/shard_map/ppermute | solution.py:472
  27.2 17.2 %collective-permute-start.5 = (f32[64,128]{1,0:T(8,128)S(1)}, f32[64,128]{1,0:T(8,128)S(1)}, u32[]{:S(2)}, u32[]{:S(2)}) collective-permute-start(f32[64,128]{1,0:T(8,128)S(1)} %get-tuple-element.33), channel_id=1, source_target_pairs={{4,8},{8,4},{12,16},{16,12},{20,24},{24,20},{5,9},{9,5},{13,17},{1... | collective-permute-start | bytes 98312 | tf_op jit(solution)/shard_map/ppermute | solution.py:473
  31.5 1.2 %copy-start.16 = (bf16[240,16,128]{2,1,0:T(8,128)(2,1)S(1)}, bf16[240,16,128]{2,1,0:T(8,128)(2,1)}, u32[]{:S(2)}) copy-start(bf16[240,16,128]{2,1,0:T(8,128)(2,1)} %prior_ref.1) | copy-start | bytes 2949124
  31.5 1.5 %copy-start.17 = (bf16[240,16,128]{2,1,0:T(8,128)(2,1)S(1)}, bf16[240,16,128]{2,1,0:T(8,128)(2,1)}, u32[]{:S(2)}) copy-start(bf16[240,16,128]{2,1,0:T(8,128)(2,1)} %scale_ref.1) | copy-start | bytes 2949124
  35.5 1.3 %copy-start.2 = (f32[16,240,128]{2,1,0:T(8,128)}, f32[16,240,128]{2,1,0:T(8,128)S(1)}, u32[]{:S(2)}) copy-start(f32[16,240,128]{2,1,0:T(8,128)S(1)} %get-tuple-element.31.refs_4_) | copy-start | bytes 5898244
  36.9 1.3 %copy-start.12 = (f32[16,240,128]{2,1,0:T(8,128)}, f32[16,240,128]{2,1,0:T(8,128)S(1)}, u32[]{:S(2)}) copy-start(f32[16,240,128]{2,1,0:T(8,128)S(1)} %get-tuple-element.30.refs_3_) | copy-start | bytes 5898244
  44.4 5.1 %copy-start.22 = (f32[64,128]{1,0:T(8,128)}, f32[64,128]{1,0:T(8,128)S(1)}, u32[]{:S(2)}) copy-start(f32[64,128]{1,0:T(8,128)S(1)} %collective-permute-done.4.refs_7_) | copy-start | bytes 98308
  44.4 5.1 %copy-start.23 = (f32[64,128]{1,0:T(8,128)}, f32[64,128]{1,0:T(8,128)S(1)}, u32[]{:S(2)}) copy-start(f32[64,128]{1,0:T(8,128)S(1)} %collective-permute-done.5.refs_8_) | copy-start | bytes 98308
  49.5 23.8 %copy-start.3 = (f32[16,240,128]{2,1,0:T(8,128)S(1)}, f32[16,240,128]{2,1,0:T(8,128)}, u32[]{:S(2)}) copy-start(f32[16,240,128]{2,1,0:T(8,128)} %copy-done.2) | copy-start | bytes 5898244
  77.2 8.6 %copy-start.5 = (bf16[240,240]{1,0:T(8,128)(2,1)S(1)}, bf16[240,240]{1,0:T(8,128)(2,1)}, u32[]{:S(2)}) copy-start(bf16[240,240]{1,0:T(8,128)(2,1)} %constant.40.clone.time_high.refs_2_.refs_9_) | copy-start | bytes 345604
  77.2 8.6 %copy-start.7 = (bf16[240,240]{1,0:T(8,128)(2,1)S(1)}, bf16[240,240]{1,0:T(8,128)(2,1)}, u32[]{:S(2)}) copy-start(bf16[240,240]{1,0:T(8,128)(2,1)} %constant.41.clone.time_low.refs_3_.refs_10_) | copy-start | bytes 345604
  77.2 8.6 %copy-start.9 = (bf16[256,256]{1,0:T(8,128)(2,1)S(1)}, bf16[256,256]{1,0:T(8,128)(2,1)}, u32[]{:S(2)}) copy-start(bf16[256,256]{1,0:T(8,128)(2,1)} %constant.42.clone.col_both.refs_11_) | copy-start | bytes 393220
  77.2 18.3 %collective-permute-start.8 = (f16[4,240,128]{2,1,0:T(8,128)(2,1)S(1)}, f16[4,240,128]{2,1,0:T(8,128)(2,1)S(1)}, u32[]{:S(2)}, u32[]{:S(2)}) collective-permute-start(f16[4,240,128]{2,1,0:T(8,128)(2,1)S(1)} %convert_element_type.28), channel_id=1, source_target_pairs={{0,4},{4,0},{8,12},{12,8},{16,20},{20,16},{24,28},{28,24},{1,5},{5... | collective-permute-start | bytes 737288 | tf_op jit(solution)/shard_map/ppermute | solution.py:472
  78.8 16.8 %collective-permute-start.9 = (f16[4,240,128]{2,1,0:T(8,128)(2,1)S(1)}, f16[4,240,128]{2,1,0:T(8,128)(2,1)S(1)}, u32[]{:S(2)}, u32[]{:S(2)}) collective-permute-start(f16[4,240,128]{2,1,0:T(8,128)(2,1)S(1)} %convert_element_type.30), channel_id=1, source_target_pairs={{4,8},{8,4},{12,16},{16,12},{20,24},{24,20},{5,9},{9,5},{13,17},{1... | collective-permute-start | bytes 737288 | tf_op jit(solution)/shard_map/ppermute | solution.py:473
  82.2 5.8 %collective-permute-start.6 = (f32[128,128]{1,0:T(8,128)S(1)}, f32[128,128]{1,0:T(8,128)S(1)}, u32[]{:S(2)}, u32[]{:S(2)}) collective-permute-start(f32[128,128]{1,0:T(8,128)S(1)} %get-tuple-element.38.after), channel_id=1, source_target_pairs={{0,1},{1,0},{2,3},{3,2},{4,5},{5,4},{6,7},{7,6},{8,9},{9,8},{10,11... | collective-permute-start | bytes 196616 | tf_op jit(solution)/shard_map/ppermute | solution.py:472
  83.4 5.9 %collective-permute-start.7 = (f32[128,128]{1,0:T(8,128)S(1)}, f32[128,128]{1,0:T(8,128)S(1)}, u32[]{:S(2)}, u32[]{:S(2)}) collective-permute-start(f32[128,128]{1,0:T(8,128)S(1)} %get-tuple-element.39), channel_id=1, source_target_pairs={{1,2},{2,1},{5,6},{6,5},{9,10},{10,9},{13,14},{14,13},{17,18},{18,... | collective-permute-start | bytes 196616 | tf_op jit(solution)/shard_map/ppermute | solution.py:473
  90.0 5.6 %collective-permute-start.10 = (f32[64,128]{1,0:T(8,128)S(1)}, f32[64,128]{1,0:T(8,128)S(1)}, u32[]{:S(2)}, u32[]{:S(2)}) collective-permute-start(f32[64,128]{1,0:T(8,128)S(1)} %get-tuple-element.44), channel_id=1, source_target_pairs={{0,4},{4,0},{8,12},{12,8},{16,20},{20,16},{24,28},{28,24},{1,5},{5... | collective-permute-start | bytes 98312 | tf_op jit(solution)/shard_map/ppermute | solution.py:472
  90.1 5.6 %collective-permute-start.11 = (f32[64,128]{1,0:T(8,128)S(1)}, f32[64,128]{1,0:T(8,128)S(1)}, u32[]{:S(2)}, u32[]{:S(2)}) collective-permute-start(f32[64,128]{1,0:T(8,128)S(1)} %get-tuple-element.45), channel_id=1, source_target_pairs={{4,8},{8,4},{12,16},{16,12},{20,24},{24,20},{5,9},{9,5},{13,17},{1... | collective-permute-start | bytes 98312 | tf_op jit(solution)/shard_map/ppermute | solution.py:473
  93.8 1.9 %copy-start.14 = (bf16[128,1024]{1,0:T(8,128)(2,1)S(1)}, bf16[128,1024]{1,0:T(8,128)(2,1)}, u32[]{:S(2)}) copy-start(bf16[128,1024]{1,0:T(8,128)(2,1)} %constant.45.clone.refs_12_.corner_high) | copy-start | bytes 786436
  93.8 1.9 %copy-start.15 = (bf16[128,1024]{1,0:T(8,128)(2,1)S(1)}, bf16[128,1024]{1,0:T(8,128)(2,1)}, u32[]{:S(2)}) copy-start(bf16[128,1024]{1,0:T(8,128)(2,1)} %constant.46.clone.refs_13_.corner_low) | copy-start | bytes 786436

commit v5 on v4

v5 whole, which is shorter than its diff:
```python
import numpy as np
import jax
import jax.numpy as jnp
from jax import lax
from jax.experimental import pallas as pl
from jax.experimental.pallas import tpu as pltpu
from jax.sharding import PartitionSpec as P

RAD = 4
TAPS = 12
AXES = ("rec", "tile")
LANES = 128
SUB = 8
FOOT_MAX = 0.02
PARTS = 4
SCALE_MAX = 2.0
HALF_TOP = 32768.0
CONTROL_FACTOR = 4096.0
F16 = jnp.float16
VMEM_LIMIT = 14 * 1024 * 1024
F32 = jnp.float32
BF16 = jnp.bfloat16


def space_taps():
    offsets = np.arange(-RAD, RAD + 1).astype(np.float64)
    values = np.exp(-2.0 * offsets * offsets / (RAD * RAD))
    return values / np.sqrt(np.sum(values * values))


def time_taps():
    offsets = np.arange(-TAPS, TAPS + 1).astype(np.float64)
    values = np.exp(-2.0 * np.abs(offsets) / TAPS)
    return values / np.sqrt(np.sum(values * values))


def banded(distance, taps, reach):
    inside = np.abs(distance) <= reach
    return np.where(inside, taps[np.clip(distance, -reach, reach) + reach], 0.0)


def two_parts(matrix):
    high = matrix.astype(np.float32).astype(jnp.bfloat16)
    low = (matrix - high.astype(np.float64)).astype(np.float32).astype(jnp.bfloat16)
    return high, low


def constants(hours, rows, cols):
    space = space_taps()
    hour = np.arange(hours)
    time_high, time_low = two_parts(banded(hour[:, None] - hour[None, :], time_taps(), TAPS))
    col = np.arange(cols)
    col_high, col_low = two_parts(banded(col[:, None] - col[None, :], space, RAD))
    col_both = np.block([[col_high, col_low], [col_high, np.zeros_like(col_high)]])
    halo_col = np.concatenate([np.arange(-RAD, 0), np.arange(cols, cols + RAD)])
    edge = banded(halo_col[:, None] - col[None, :], space, RAD)

    def strips(row_of, halo_of, targets):
        by_row = banded(np.array(row_of)[:, None] - np.array(targets)[None, :], space, RAD)
        both = by_row[:, :, None] * edge[np.array(halo_of)][:, None, :]
        return two_parts(both.reshape(len(row_of), -1))

    unused = [(-100, 0)] * (LANES - RAD * rows)
    own = []
    for side in range(2):
        own += [(row, side * RAD + j) for row in range(rows) for j in range(RAD)] + unused
    corner = [], []
    for first, targets in ((rows, rows - 1 - np.arange(RAD)), (-RAD, np.arange(RAD))):
        lanes = [
            (row, side * RAD + j) for side in range(2) for row in range(first, first + RAD) for j in range(RAD)
        ]
        lanes += [(-100, 0)] * (LANES - len(lanes))
        for part, value in zip(corner, strips(*zip(*lanes), targets)):
            part.append(value)
    return (time_high, time_low, col_both), strips(*zip(*own), np.arange(rows)), [np.stack(c) for c in corner]


def split(value):
    high = value.astype(BF16)
    low = (value - high.astype(F32)).astype(BF16)
    return high, low


def dot(a, b):
    return jnp.dot(a, b, preferred_element_type=F32)


def lane_ids(shape):
    return lax.broadcasted_iota(jnp.int32, shape, 1)


def choose(flag, yes, no):
    return jnp.where(flag, yes, no)


def pack_strips(row_value, odd, rows):
    cols = row_value(0).shape[1]
    half = rows * RAD
    source = lax.broadcasted_iota(jnp.int32, (cols, 2 * half), 0)
    lane = lane_ids((cols, 2 * half))
    first = lane < half
    j = lane & (RAD - 1)
    at_first, at_second = choose(odd, j, cols - RAD + j), choose(odd, cols - RAD + j, j)
    wanted = jnp.where(first, at_first, at_second)
    lane_row = jnp.where(first, lane, lane - half) // RAD
    total = None
    for row in range(rows):
        high, low = split(row_value(row))
        pick = jnp.where((source == wanted) & (lane_row == row), 1.0, 0.0).astype(BF16)
        part = dot(jnp.concatenate([high, low], axis=1), jnp.concatenate([pick, pick], axis=0))
        total = part if total is None else total + part
    return total


def fold_corners(odd, strips, corner_e, corner_o):
    quarter = corner_e.shape[0]
    half, part = LANES // 2, RAD * RAD
    lane = lane_ids((quarter, LANES))
    spare = jnp.zeros((4 * quarter - strips.shape[0], LANES), F32)
    whole = jnp.concatenate([strips, spare], axis=0)
    low = high = jnp.zeros((quarter, LANES), F32)
    for q in range(LANES // (2 * part)):
        piece = whole[q * quarter : (q + 1) * quarter]
        for side in range(2):
            to = q * 2 * part + side * part
            here = (lane >= to) & (lane < to + part)
            low = choose(here, pltpu.roll(piece, (to - side * half) % LANES, 1), low)
            high = choose(here, pltpu.roll(piece, (to - side * half - (half - part)) % LANES, 1), high)
    corner_e[...] = choose(odd, low, high)
    corner_o[...] = choose(odd, high, low)


def unfold_corners(value):
    part = 2 * RAD * RAD
    pieces = [value] + [pltpu.roll(value, LANES - q * part, 1) for q in range(1, LANES // part)]
    return jnp.concatenate(pieces, axis=0)


def is_odd(par_ref, axis):
    return par_ref[axis : axis + 1, :] == 1


def write_rows(odd, row_value, rows, rows_e, rows_o):
    for row in range(RAD):
        first, last = row_value(row), row_value(rows - 1 - row)
        rows_e[row] = choose(odd, first, last)
        rows_o[row] = choose(odd, last, first)


def turn_kernel(par_ref, after, control_ref, field_ref, strip_e, strip_o):
    rows = control_ref.shape[1]
    for row in range(rows):
        field_ref[row] = control_ref[:, row, :]
    write_strips(is_odd(par_ref, 1), field_ref, strip_e, strip_o)


def strip_kernel(par_ref, after_e, after_o, field_ref, strip_e, strip_o):
    write_strips(is_odd(par_ref, 1), field_ref, strip_e, strip_o)


def write_strips(odd, field_ref, strip_e, strip_o):
    strips = pack_strips(lambda r: field_ref[r], odd, field_ref.shape[0])
    half = LANES // 2
    left = lane_ids(strips.shape) < half
    strip_e[...] = jnp.where(left, strips, 0.0)
    strip_o[...] = jnp.where(left, pltpu.roll(strips, half, 1), 0.0)


def far_corner_kernel(par_ref, after, strip_e, strip_o, corner_e, corner_o):
    odd = is_odd(par_ref, 1)
    even_swap, odd_swap = strip_e[...], strip_o[...]
    before, after = choose(odd, even_swap, odd_swap), choose(odd, odd_swap, even_swap)
    half = LANES // 2
    both = jnp.where(lane_ids(before.shape) < half, before, pltpu.roll(after, half, 1))
    fold_corners(is_odd(par_ref, 0), both, corner_e, corner_o)


def rows_kernel(par_ref, factor_ref, field_ref, rows_e, rows_o):
    factor = factor_ref[0:1, :]
    write_rows(is_odd(par_ref, 0), lambda r: field_ref[r] * factor, field_ref.shape[0], rows_e, rows_o)


def prepare_kernel(
    foot_ref, start_ref, row_ref, slot_ref, count_ref, out_ref,
    wide_ref, start_vmem, row_vmem, slot_vmem, count_vmem, sems, *, per,
):
    owners, lines, _ = foot_ref.shape
    slots = start_ref.shape[0]
    pairs = ((start_ref, start_vmem), (row_ref, row_vmem), (slot_ref, slot_vmem), (count_ref, count_vmem))
    small = [pltpu.make_async_copy(a, b, sems.at[i]) for i, (a, b) in enumerate(pairs)]
    chunk = owners // PARTS
    parts = [slice(i * chunk, (i + 1) * chunk) for i in range(PARTS)]
    loads = [
        pltpu.make_async_copy(foot_ref.at[here], wide_ref.at[here, 0:lines, :], sems.at[4 + i])
        for i, here in enumerate(parts)
    ]
    for copy in small + loads:
        copy.start()
    for copy in small:
        copy.wait()
    start = start_vmem[...]
    valid = lax.broadcasted_iota(jnp.int32, start.shape, 0) < count_vmem[...]
    lanes = jnp.concatenate(
        [start >> 4, start & 15, row_vmem[...], jnp.where(valid, slot_vmem[...], per)], axis=0
    ).astype(F32)
    wide = jnp.pad(lanes, ((0, LANES - 4 * slots), (0, LANES - owners)))
    turned = jnp.transpose(wide)[0:owners]
    notes = jnp.broadcast_to(turned[:, None, :], (owners, SUB, LANES)).astype(BF16)
    wide_ref[:, lines : lines + SUB, :] = notes
    stores = []
    for i, here in enumerate(parts):
        loads[i].wait()
        stores.append(pltpu.make_async_copy(wide_ref.at[here], out_ref.at[here], sems.at[4 + PARTS + i]))
        stores[-1].start()
    for copy in stores:
        copy.wait()


def halo_sums(parts, high_ref, low_ref, first, width):
    high, low = parts
    weights = high_ref[:, first : first + width]
    return dot(high, weights) + dot(low, weights) + dot(high, low_ref[:, first : first + width])


def column_sums(value, col_both):
    cols = value.shape[1]
    high, low = split(value)
    out = dot(jnp.concatenate([high, low], axis=1), col_both)
    return out[:, :cols] + out[:, cols:]


def time_sums(value, time_high, time_low):
    high, low = split(value)
    return dot(time_high, high) + dot(time_high, low) + dot(time_low, high)


def row_sums(get, row, low, high, taps):
    total = None
    for distance in range(RAD + 1):
        here = [get(r) for r in sorted({row - distance, row + distance}) if low <= r < high]
        if not here:
            continue
        part = here[0] if len(here) == 1 else here[0] + here[1]
        part = float(taps[RAD + distance]) * part
        total = part if total is None else total + part
    return total


def local_kernel(after, field_ref, time_high, time_low, col_both, out_ref):
    rows, hours, cols = field_ref.shape
    taps = space_taps()
    for row in range(0, rows, 2):
        pair = [
            column_sums(row_sums(lambda i: field_ref[i], r, 0, rows, taps), col_both[...])
            for r in (row, row + 1)
        ]
        both = time_sums(jnp.concatenate(pair, axis=1), time_high[...], time_low[...])
        for k, r in enumerate((row, row + 1)):
            out_ref[r] = both[:, k * cols : (k + 1) * cols]


def strips_kernel(par_ref, local_ref, strip_e, strip_o, time_high, time_low, own_high, own_low, out_ref, *, by_hour):
    rows, hours, cols = local_ref.shape
    odd = is_odd(par_ref, 1)
    even_swap, odd_swap = strip_e[...], strip_o[...]
    halo = jnp.concatenate([choose(odd, even_swap, odd_swap), choose(odd, odd_swap, even_swap)], axis=1)
    halo = split(time_sums(halo, time_high[...], time_low[...]))
    for row in range(0, rows, 2):
        both = halo_sums(halo, own_high, own_low, row * cols, 2 * cols)
        for k, r in enumerate((row, row + 1)):
            part = local_ref[r] + both[:, k * cols : (k + 1) * cols]
            if by_hour:
                out_ref[:, r, :] = part
            else:
                out_ref[r] = part


def edge_parts(odd, rows, first, got_e, got_o, consts, halo, factor, corner=None):
    time_high, time_low, col_both = consts
    taps = space_taps()
    for row in range(RAD):
        even, other = got_e[row], got_o[row]
        halo[row] = (choose(odd, even, other) if first else choose(odd, other, even)) * factor
    parts = []
    for k in range(0, RAD, 2):
        pair = []
        for i in (k, k + 1):
            if first:
                summed = row_sums(lambda r: halo[r + RAD], i, -RAD, 0, taps)
            else:
                summed = row_sums(lambda r: halo[r - RAD], i, RAD, 2 * RAD, taps)
            pair.append(column_sums(summed, col_both[...]))
        value = jnp.concatenate(pair, axis=1)
        width = value.shape[1]
        if corner is not None:
            parts_of, high, low = corner
            at = (k if first else RAD + k) * (width // 2)
            value = value + halo_sums(parts_of, high, low, at, width)
        both = time_sums(value, time_high[...], time_low[...])
        half = width // 2
        parts += [both[:, :half], both[:, half:]]
    return parts


def edge_parts(halo, corner, corner_high, corner_low, consts):
    time_high, time_low, col_both = consts
    hours, cols = halo.shape[1:]
    taps = space_taps()
    corner = split(unfold_corners(corner)[0:hours])
    parts = []
    for k in range(0, RAD, 2):
        pair = []
        for i in (k, k + 1):
            summed = None
            for j in range(RAD - i):
                part = float(taps[RAD + i + j + 1]) * halo[j]
                summed = part if summed is None else summed + part
            pair.append(column_sums(summed, col_both[...]))
        value = jnp.concatenate(pair, axis=1) + halo_sums(corner, corner_high, corner_low, k * cols, 2 * cols)
        both = time_sums(value, time_high[...], time_low[...])
        parts += [both[:, :cols], both[:, cols:]]
    return parts


def flux_kernel(
    par_ref, local_ref, prior_ref, scale_ref, got_ref, corner_ref,
    time_high, time_low, col_both, corner_high, corner_low, flux_ref, scale_out, wide, halo,
):
    rows = local_ref.shape[0]
    odd = par_ref[0, 0]
    wide[...] = scale_ref[...].astype(F32)
    for row in range(rows):
        scale_out[row] = wide[:, row, :]
    wide[...] = prior_ref[...].astype(F32)
    for row in range(rows):
        flux_ref[row] = wide[:, row, :] + scale_out[row] * local_ref[row]
    halo[...] = got_ref[...] * (1.0 / CONTROL_FACTOR)
    consts = (time_high, time_low, col_both)
    parts = edge_parts(halo, corner_ref[...], corner_high.at[odd], corner_low.at[odd], consts)
    for k, part in enumerate(parts):
        row = jnp.where(odd == 1, k, rows - 1 - k)
        flux_ref[row] = flux_ref[row] + scale_out[row] * part


def finish_kernel(
    par_ref, local_ref, factor_ref, got_e, got_o, corner_e, corner_o,
    time_high, time_low, col_both, corner_high, corner_low, out_ref, halo, edges, total, sems,
):
    hours, rows, cols = local_ref.shape
    odd = is_odd(par_ref, 0)
    factor = factor_ref[1:2, :]
    consts = (time_high, time_low, col_both)
    inside = lax.broadcasted_iota(jnp.int32, (hours, 2 * RAD, cols), 1)
    copies = []
    for side in range(2):
        before = side == 0
        for k in range(RAD):
            even, other = got_e[k], got_o[k]
            halo[side, k] = (choose(odd, even, other) if before else choose(odd, other, even)) * factor
        even, other = corner_e[...], corner_o[...]
        corner = choose(odd, even, other) if before else choose(odd, other, even)
        which = 1 - side
        parts = edge_parts(halo.at[side], corner, corner_high.at[which], corner_low.at[which], consts)
        for k, part in enumerate(parts):
            edges[:, k if before else 2 * RAD - 1 - k, :] = part
        here = slice(0, 2 * RAD) if before else slice(rows - 2 * RAD, rows)
        mine = inside < RAD if before else inside >= RAD
        total[:, here, :] = local_ref[:, here, :] + jnp.where(mine, edges[...], 0.0)
        copies.append(pltpu.make_async_copy(total.at[:, here, :], out_ref.at[:, here, :], sems.at[side]))
        copies[-1].start()
    for copy in copies:
        copy.wait()


def blocks_of(foot_ref, source, heights, slots):
    for c in range(0, slots, 2):
        both = foot_ref[source, c * heights : (c + 2) * heights, :].astype(F32)
        yield c, both[0:heights]
        yield c + 1, both[heights : 2 * heights]


def forward_kernel(
    par_ref, foot_ref, own_ref, got_ref, flux_hbm, scale_hbm, *refs, shift, slots, heights, tiles, per,
):
    distant, near = refs[0:6], refs[8:14]
    out_ref, table_ref = refs[6:8]
    flux_ref, scale_ref, halo, edges, sums, table_smem, sems = refs[14:]
    corner_ref, *consts, corner_high, corner_low = near
    odd = par_ref[0, 0]
    sources = foot_ref.shape[0]
    rows = flux_ref.shape[0]
    first = (rows - RAD) * odd
    pairs = list(zip(distant, near)) + [(scale_hbm.at[pl.ds(first, RAD)], scale_ref), (flux_hbm, flux_ref)]
    loads = [pltpu.make_async_copy(a, b, sems.at[i]) for i, (a, b) in enumerate(pairs)]
    for load in loads:
        load.start()
    groups = out_ref.shape[1] - 1
    base = slots * heights
    lane = lane_ids((sources, LANES))
    notes = foot_ref[:, base : base + SUB, :].astype(F32)[:, 0, :].astype(jnp.int32)
    start = notes * 16 + pltpu.roll(notes, LANES - slots, 1)
    offset = start + pltpu.roll(notes, LANES - 2 * slots, 1) * (1 << shift)
    source_rec = lax.broadcasted_iota(jnp.int32, (sources, LANES), 0) // tiles
    receptor = jnp.where(notes < per, source_rec * per + notes, groups * LANES)
    table = jnp.where(lane < slots, offset, receptor)
    table_ref[...] = table
    copy = pltpu.make_async_copy(table_ref, table_smem, sems.at[len(loads)])
    copy.start()
    for load in loads[:-2]:
        load.wait()
    halo[...] = got_ref[...] * (1.0 / CONTROL_FACTOR)
    parts = edge_parts(halo, corner_ref[...], corner_high.at[1 - odd], corner_low.at[1 - odd], consts)
    for k, part in enumerate(parts):
        edges[k] = part
    for load in loads[-2:]:
        load.wait()
    for k in range(RAD):
        line = jnp.where(odd == 1, RAD - 1 - k, k)
        flux_ref[first + line] = flux_ref[first + line] + scale_ref[line] * edges[k]
    copy.wait()

    def body(source, carry):
        for c, block in blocks_of(foot_ref, source, heights, slots):
            offset = table_smem[source, c]
            row = lax.shift_right_logical(offset, shift)
            begin = jnp.bitwise_and(offset, (1 << shift) - 1)
            product = flux_ref[row, pl.ds(begin, heights), :] * block
            sums[c, pl.ds(source, 1), :] = jnp.sum(product, axis=0, keepdims=True)
        return carry

    lax.fori_loop(0, sources, body, 0)
    totals = [jnp.zeros((sources, LANES), F32) for _ in range(groups)]
    for c in range(slots):
        value = jnp.sum(sums[c], axis=1, keepdims=True)
        which = table[:, 3 * slots + c : 3 * slots + c + 1]
        for q in range(groups):
            totals[q] = totals[q] + jnp.where(which == lane + q * LANES, value, 0.0)
    for q in range(groups):
        total = jnp.sum(totals[q], axis=0, keepdims=True)
        out_ref[:, q : q + 1, :] = jnp.broadcast_to(total[None], (sources, 1, LANES))
    out_ref[:, groups : groups + 1, :] = jnp.broadcast_to(own_ref[...][None], (sources, 1, LANES))


def adjoint_kernel(
    par_ref, table_vmem, got_ref, foot_ref, scale_ref,
    model_ref, factor_ref, field_ref,
    weight_vmem, weight_smem, table_ref, sems, *, shift, slots, heights, tiles, per,
):
    load = pltpu.make_async_copy(table_vmem, table_ref, sems.at[1])
    load.start()
    sources = foot_ref.shape[0]
    groups = got_ref.shape[1] - 1
    rows, hours, _ = field_ref.shape
    model = jnp.sum(got_ref[:, 0:groups, :], axis=0)
    packed = LANES // per
    lane = lane_ids((1, LANES))
    own = jnp.zeros((1, LANES), F32)
    for q in range(groups):
        for k in range(packed):
            line = model[q : q + 1, :]
            line = line if k == 0 else pltpu.roll(line, LANES - k * per, 1)
            own = choose(par_ref[2:3, :] == q * packed + k, line, own)
    model_ref[...] = own[:, 0:per]
    weight_vmem[...] = jnp.zeros_like(weight_vmem)
    for q in range(groups):
        observed, error = jnp.zeros((1, LANES), F32), jnp.ones((1, LANES), F32)
        for k in range(packed):
            line = got_ref[(q * packed + k) * tiles, groups : groups + 1, :]
            here = (lane >= k * per) & (lane < (k + 1) * per)
            observed = jnp.where(here, line if k == 0 else pltpu.roll(line, k * per, 1), observed)
            turn = (k * per - per) % LANES
            error = jnp.where(here, line if turn == 0 else pltpu.roll(line, turn, 1), error)
        weight_vmem[q : q + 1, :] = (model[q : q + 1, :] - observed) / (error * error)
    copy = pltpu.make_async_copy(weight_vmem, weight_smem, sems.at[0])
    copy.start()
    field_ref[...] = jnp.zeros_like(field_ref)
    top = jnp.max(jnp.abs(weight_vmem[...]), keepdims=True) * (FOOT_MAX * SCALE_MAX * sources * slots)
    top = jnp.maximum(top, 1e-25)
    factor_ref[0:1, :] = jnp.broadcast_to(HALF_TOP / top, (1, LANES))
    factor_ref[1:2, :] = jnp.broadcast_to(top * (1.0 / HALF_TOP), (1, LANES))
    load.wait()
    copy.wait()

    def body(source, carry):
        for c, block in blocks_of(foot_ref, source, heights, slots):
            offset = table_ref[source, c]
            receptor = table_ref[source, 3 * slots + c]
            row = lax.shift_right_logical(offset, shift)
            begin = jnp.bitwise_and(offset, (1 << shift) - 1)
            weight = weight_smem[lax.shift_right_logical(receptor, 7), jnp.bitwise_and(receptor, LANES - 1)]
            field_ref[row, pl.ds(begin, heights), :] += block * weight
        return carry

    lax.fori_loop(0, sources, body, 0)
    for row in range(rows):
        field_ref[row] = field_ref[row] * scale_ref[row]


def swap_pairs(count, odd):
    pairs = []
    for i in range(1 if odd else 0, count - 1, 2):
        pairs += [(i, i + 1), (i + 1, i)]
    return pairs


def swap(axis, even, odd):
    count = lax.axis_size(axis)
    return (
        lax.ppermute(even, axis, swap_pairs(count, False)),
        lax.ppermute(odd, axis, swap_pairs(count, True)),
    )


VM = pl.BlockSpec(memory_space=pltpu.VMEM)
HB = pl.BlockSpec(memory_space=pltpu.HBM)


def call(kernel, out_shape, in_specs, scratch, name, out_specs=None):
    return pl.pallas_call(
        kernel,
        out_shape=out_shape,
        in_specs=in_specs,
        out_specs=jax.tree.map(lambda _: VM, out_shape) if out_specs is None else out_specs,
        scratch_shapes=scratch,
        compiler_params=pltpu.CompilerParams(vmem_limit_bytes=VMEM_LIMIT),
        name=name,
    )


def far(x):
    return pltpu.with_memory_space_constraint(x, pltpu.HBM)


def array(*shape):
    return jax.ShapeDtypeStruct(shape, F32)


def per_device(
    prior_flux,
    flux_scale,
    control,
    footprint,
    slot_count,
    start_hour,
    grid_row,
    receptor_slot,
    observed,
    obs_error,
):
    hours, rows, cols = control.shape
    n_rec, n_tile = lax.axis_size("rec"), lax.axis_size("tile")
    devices = n_rec * n_tile
    slots, heights = footprint.shape[1], footprint.shape[2]
    per = observed.shape[0]
    groups = per * n_rec // LANES
    shift = (hours - 1).bit_length()
    rec, tile = lax.axis_index("rec"), lax.axis_index("tile")
    par = jnp.stack([rec % 2, tile % 2, rec] + [rec * 0] * (SUB - 3)).astype(jnp.int32)
    par = jnp.broadcast_to(par[:, None], (SUB, LANES))
    base, own_parts, corner_parts = constants(hours, rows, cols)
    base = [jnp.asarray(c) for c in base]
    own_parts = [jnp.asarray(c) for c in own_parts]
    corner_parts = [jnp.asarray(c) for c in corner_parts]
    strip = array(hours, LANES)
    corner = array(-(-hours // (4 * SUB)) * SUB, LANES)
    block = array(RAD, hours, cols)
    field_shape = array(rows, hours, cols)
    row_scratch = pltpu.VMEM((RAD, hours, cols), F32)

    def half(rows_e, rows_o):
        return rows_e.astype(F16), rows_o.astype(F16)

    def inner_sums(field, sent, by_hour, name):
        def second(*refs):
            strips_kernel(*refs, by_hour=by_hour)

        got_strips = swap("tile", *sent)
        local = call(local_kernel, field_shape, [VM] * 5, [], name + "_local")(sent[0], field, *base)
        shape = array(hours, rows, cols) if by_hour else field_shape
        corners = call(far_corner_kernel, [corner, corner], [VM] * 4, [], name + "_corners")(par, local, *got_strips)
        got_corners = swap("rec", *corners)
        local = call(second, shape, [VM] * 8, [], name + "_strips")(
            par, local, *got_strips, *base[:2], *own_parts
        )
        return local, got_corners

    def pack_rows(factor, field, name):
        sent = call(rows_kernel, [block, block], [VM] * 3, [], name)(par, factor, field)
        return sent, swap("rec", *half(*sent))

    def prepare(*refs):
        prepare_kernel(*refs, per=per)

    numbers = pltpu.VMEM((slots, devices), jnp.int32)
    lines = slots * heights + SUB
    sent = call(
        prepare,
        jax.ShapeDtypeStruct((devices, lines, cols), BF16),
        [HB] * 5,
        [
            pltpu.VMEM((devices, lines, cols), BF16),
            numbers, numbers, numbers, pltpu.VMEM((1, devices), jnp.int32),
            pltpu.SemaphoreType.DMA((4 + 2 * PARTS,)),
        ],
        "prepare_blocks",
        out_specs=HB,
    )(*[
        far(x)
        for x in (
            footprint.reshape(devices, slots * heights, cols),
            start_hour.T, grid_row.T, receptor_slot.T, slot_count[None],
        )
    ])
    foot = lax.all_to_all(sent, AXES, split_axis=0, concat_axis=0, tiled=True)
    field, *strips = call(
        turn_kernel, [field_shape, strip, strip], [VM, HB, VM], [], "turn_control"
    )(par, sent, control)
    _, got_rows = pack_rows(jnp.full((2, LANES), CONTROL_FACTOR, F32), field, "control_rows")
    local, got_corners = inner_sums(field, strips, False, "control")
    flux, scale = call(
        flux_kernel,
        [field_shape, field_shape],
        [VM] * 11,
        [pltpu.VMEM((hours, rows, cols), F32), row_scratch],
        "flux_field",
    )(par, local, prior_flux, flux_scale, got_rows[0].astype(F32), got_corners[0], *base, *corner_parts)

    own = jnp.concatenate([observed, obs_error, jnp.zeros((LANES - 2 * per,), F32)])[None]
    sizes = dict(shift=shift, slots=slots, heights=heights, tiles=n_tile, per=per)

    def forward(*refs):
        forward_kernel(*refs, **sizes)

    foot, got_odd = lax.optimization_barrier((foot, got_rows[1]))
    needed = [got_corners[1], *base, *corner_parts]
    partial, table = call(
        forward,
        [array(devices, groups + 1, LANES), jax.ShapeDtypeStruct((devices, LANES), jnp.int32)],
        [VM] * 4 + [HB] * 8,
        [pltpu.VMEM(x.shape, x.dtype) for x in needed]
        + [pltpu.VMEM((rows, hours, cols), F32), row_scratch, row_scratch, row_scratch]
        + [
            pltpu.VMEM((slots, devices, LANES), F32),
            pltpu.SMEM((devices, LANES), jnp.int32),
            pltpu.SemaphoreType.DMA((len(needed) + 4,)),
        ],
        "block_values",
    )(par, foot, own, got_odd.astype(F32), *[far(x) for x in (flux, scale, *needed)])
    everyone = lax.all_to_all(partial, AXES, split_axis=0, concat_axis=0, tiled=True)

    def adjoint(*refs):
        adjoint_kernel(*refs, **sizes)

    weight_rows = -(-(groups + 1) // SUB) * SUB
    model_co2, factor, field = call(
        adjoint,
        [array(1, per), array(2, LANES), field_shape],
        [VM] * 5,
        [
            pltpu.VMEM((weight_rows, LANES), F32),
            pltpu.SMEM((weight_rows, LANES), F32),
            pltpu.SMEM((devices, LANES), jnp.int32),
            pltpu.SemaphoreType.DMA((2,)),
        ],
        "adjoint_field",
    )(par, table, everyone, foot, scale)
    sent_rows, got_rows = pack_rows(factor, field, "gradient_rows")
    strips = call(strip_kernel, [strip, strip], [VM] * 4, [], "gradient_pack")(par, *sent_rows, field)
    local, got_corners = inner_sums(field, strips, True, "gradient")
    got_rows = [r.astype(F32) for r in got_rows]
    gradient = call(
        finish_kernel,
        array(hours, rows, cols),
        [VM] * 12,
        [
            pltpu.VMEM((2, RAD, hours, cols), F32),
            pltpu.VMEM((hours, 2 * RAD, cols), F32),
            pltpu.VMEM((hours, rows, cols), F32),
            pltpu.SemaphoreType.DMA((2,)),
        ],
        "gradient",
        out_specs=HB,
    )(par, local, factor, *got_rows, *got_corners, *base, *corner_parts)
    return (model_co2.reshape(-1), gradient)


def solution(mesh):
    return jax.shard_map(
        per_device,
        mesh=mesh,
        in_specs=(
            P(None, "rec", "tile"),
            P(None, "rec", "tile"),
            P(None, "rec", "tile"),
            P(("rec", "tile"), None, None, None),
            P(("rec", "tile")),
            P(("rec", "tile"), None),
            P(("rec", "tile"), None),
            P(("rec", "tile"), None),
            P("rec"),
            P("rec"),
        ),
        out_specs=(P("rec"), P(None, "rec", "tile")),
        check_vma=False,
    )
```

time: 101 us -> 95.1 us (0.942)
  Pallas kernels: 31.7 us -> 26.9 us
  waiting for transfers between devices: 11.4 us -> 15.7 us
  starting transfers between devices: 29.9 us -> 28 us
  blocking collectives: 17.4 us -> 16.1 us
  local copies, waits for them, and re-layouts: 6.26 us -> 4.99 us
    ppermute x6, waiting for transfers between devices: 0.02 us -> 4.51 us  [swap(): lax.ppermute(even, axis, swap_pairs(count, False))]
    pallas_call x11 -> x12, Pallas kernels: 20.8 us -> 18.3 us  [the longest x1 3.37 us: per_device(): call(finish_kernel, array(hours, rows, cols), [VM] * 12, [pltpu.VMEM((2,...]
    pallas_call x1, Pallas kernels: 6.44 us -> 3.99 us  [per_device(): call(forward, [array(devices, groups + 1, LANES), jax.ShapeDtypeStruct((d...]
    ppermute x6, starting transfers between devices: 19.6 us -> 17.7 us  [swap(): lax.ppermute(odd, axis, swap_pairs(count, True))]
    unnamed x52 -> x44, local copies, waits for them, and re-layouts: 6.26 us -> 4.82 us
    all_to_all x1, blocking collectives: 17.4 us -> 16.1 us  [per_device(): lax.all_to_all(partial, AXES, split_axis=0, concat_axis=0, tiled=True)]
    ppermute x6, waiting for transfers between devices: 6.39 us -> 5.32 us  [swap(): lax.ppermute(odd, axis, swap_pairs(count, True))]
  transfers between devices with their start and end apart: 13 -> 13, of which waited for: 4 -> 5; matrix products, arithmetic and copies ran while one was open for 2% -> 2% of each run, Pallas kernels for 15% -> 15%
where the time goes in v5:
time: 95.1 us; the launch traced here: 94.3 us
  starting transfers between devices  28 us (29%)
  Pallas kernels  26.9 us (28%)
  blocking collectives  16.1 us (17%)
  waiting for transfers between devices  15.7 us (17%)
  local copies, waits for them, and re-layouts  4.99 us (5%)
  between operations  1.33 us (1%)
  other arithmetic  1.3 us (1%)
    ppermute x6, starting transfers between devices, swap(): lax.ppermute(odd, axis, swap_pairs(count, True))  17.7 us
    all_to_all x1, blocking collectives, per_device(): lax.all_to_all(partial, AXES, split_axis=0, concat_axis=0, tiled=True)  16.1 us
    all_to_all x1, starting transfers between devices, per_device(): foot = lax.all_to_all(sent, AXES, split_axis=0, concat_axis=0, tiled=True)  6.42 us
    all_to_all x1, waiting for transfers between devices, per_device(): foot = lax.all_to_all(sent, AXES, split_axis=0, concat_axis=0, tiled=True)  5.87 us
    ppermute x6, waiting for transfers between devices, swap(): lax.ppermute(odd, axis, swap_pairs(count, True))  5.32 us
    unnamed x44, local copies, waits for them, and re-layouts  4.82 us
    pallas_call x2, Pallas kernels, inner_sums(): call(local_kernel, field_shape, [VM] * 5, [], name + '_local')  4.62 us
    ppermute x6, waiting for transfers between devices, swap(): lax.ppermute(even, axis, swap_pairs(count, False))  4.51 us
  transfers between devices with their start and end apart: 13, of which 5 were waited for; matrix products, arithmetic and copies ran while one was open for 2% of the time, Pallas kernels for 15%

profile of v5, /device:TPU:5, one launch (start us, length us, event | category | flops | bytes accessed | tf_op | source)
XLA Modules:
  0.0 94.3 jit_solution(3764304820773969009)
XLA Ops:
  0.6 2.3 %prepare_blocks.1.after = bf16[32,200,128]{2,1,0:T(8,128)(2,1)} custom-call(bf16[32,192,128]{2,1,0:T(8,128)(2,1)} %bitcast.11, s32[8,32]{1,0:T(8,128)} %bitcast.12, s32[8,32]{1,0:T(8,128)} %bitcast.13, s32[8,32]{1,0:T(8,128)} %bitcast.14, s32[1,32]{1,0:T(1,128)} %bitcast.15), custom_call_target="tpu_custom_call" | custom-call | tf_op jit(solution)/shard_map/prepare_blocks/pallas_call | solution.py:596
  3.0 6.4 %all-to-all-start = ((bf16[32,200,128]{2,1,0:T(8,128)(2,1)}), bf16[32,200,128]{2,1,0:T(8,128)(2,1)S(1)}, u32[]{:S(2)}, u32[]{:S(2)}) async-start(bf16[32,200,128]{2,1,0:T(8,128)(2,1)} %prepare_blocks.1.after), calls=%async_computation | async-start | bytes 3276800 | tf_op jit(solution)/shard_map/all_to_all | solution.py:614
  9.4 0.1 stack.15
  9.5 0.1 broadcast_in_dim.15.par_ref.refs_0_
  9.6 1.5 %copy-done.15 = f32[240,16,128]{2,1,0:T(8,128)S(1)} copy-done((f32[240,16,128]{2,1,0:T(8,128)S(1)}, f32[240,16,128]{2,1,0:T(8,128)}, u32[]{:S(2)}) %copy-start.15) | copy-done | bytes 1966104
  11.1 1.6 %turn_control.1 = (f32[16,240,128]{2,1,0:T(8,128)S(1)}, f32[240,128]{1,0:T(8,128)S(1)}, f32[240,128]{1,0:T(8,128)S(1)}) custom-call(s32[8,128]{1,0:T(8,128)S(1)} %broadcast_in_dim.15.par_ref.refs_0_, bf16[32,200,128]{2,1,0:T(8,128)(2,1)} %prepare_blocks.1.after, f32[240,16,128]{2,1,0:T(8,128)S(1)} %copy-done.15), custom_call_target="tpu_custom_call" | custom-call | tf_op jit(solution)/shard_map/turn_control/pallas_call | solution.py:615
  12.7 0.0 copy-start.9
  12.8 0.1 control_rows.1
  12.9 0.1 collective-permute-start.3
  13.1 4.2 %collective-permute-start = (f16[4,240,128]{2,1,0:T(8,128)(2,1)S(1)}, f16[4,240,128]{2,1,0:T(8,128)(2,1)}, u32[]{:S(2)}, u32[]{:S(2)}) collective-permute-start(f16[4,240,128]{2,1,0:T(8,128)(2,1)S(1)} %convert_element_type.24), channel_id=1, source_target_pairs={{4,8},{8,4},{12,16},{16,12},{20,24},{24,20},{5,9},{9,5},{13,17},{1... | collective-permute-start | bytes 737288 | tf_op jit(solution)/shard_map/ppermute | solution.py:510
  17.3 1.0 %collective-permute-start.1 = (f32[240,128]{1,0:T(8,128)S(1)}, f32[240,128]{1,0:T(8,128)S(1)}, u32[]{:S(2)}, u32[]{:S(2)}) collective-permute-start(f32[240,128]{1,0:T(8,128)S(1)} %get-tuple-element.28.after), channel_id=1, source_target_pairs={{0,1},{1,0},{2,3},{3,2},{4,5},{5,4},{6,7},{7,6},{8,9},{9,8},{10,11... | collective-permute-start | bytes 368648 | tf_op jit(solution)/shard_map/ppermute | solution.py:509
  18.3 3.0 %collective-permute-start.2 = (f32[240,128]{1,0:T(8,128)S(1)}, f32[240,128]{1,0:T(8,128)S(1)}, u32[]{:S(2)}, u32[]{:S(2)}) collective-permute-start(f32[240,128]{1,0:T(8,128)S(1)} %get-tuple-element.29), channel_id=1, source_target_pairs={{1,2},{2,1},{5,6},{6,5},{9,10},{10,9},{13,14},{14,13},{17,18},{18,... | collective-permute-start | bytes 368648 | tf_op jit(solution)/shard_map/ppermute | solution.py:510
  21.3 2.3 %control_local.1.refs_1_.after = f32[16,240,128]{2,1,0:T(8,128)S(1)} custom-call(f32[240,128]{1,0:T(8,128)S(1)} %get-tuple-element.28.after, f32[16,240,128]{2,1,0:T(8,128)S(1)} %get-tuple-element.24.field_ref, bf16[240,240]{1,0:T(8,128)(2,1)S(1)} %copy-done.2, bf16[240,240]{1,0:T(8,128)(2,1)S(1)} %copy-done.4, bf16[256,256]{1,0:T(8,128)(2,1)S(1)} %copy-done.9), custom_call_target="tpu_custom_call" | custom-call | tf_op jit(solution)/shard_map/control_local/pallas_call | solution.py:578
  23.6 0.0 copy-start.20
  23.6 0.0 copy-start.21
  23.6 0.0 copy-start.6
  23.6 0.0 copy-start.7
  23.7 0.0 collective-permute-done.1.refs_2_.strip_e
  23.7 3.5 %collective-permute-done.2.refs_3_.strip_o = f32[240,128]{1,0:T(8,128)S(1)} collective-permute-done((f32[240,128]{1,0:T(8,128)S(1)}, f32[240,128]{1,0:T(8,128)S(1)}, u32[]{:S(2)}, u32[]{:S(2)}) %collective-permute-start.2) | collective-permute-done | bytes 122912 | tf_op jit(solution)/shard_map/ppermute | solution.py:510
  27.1 0.2 control_corners.1
  27.4 0.1 collective-permute-start.4
  27.5 2.1 %collective-permute-start.5 = (f32[64,128]{1,0:T(8,128)S(1)}, f32[64,128]{1,0:T(8,128)S(1)}, u32[]{:S(2)}, u32[]{:S(2)}) collective-permute-start(f32[64,128]{1,0:T(8,128)S(1)} %get-tuple-element.34), channel_id=1, source_target_pairs={{4,8},{8,4},{12,16},{16,12},{20,24},{24,20},{5,9},{9,5},{13,17},{1... | collective-permute-start | bytes 98312 | tf_op jit(solution)/shard_map/ppermute | solution.py:510
  29.6 0.1 maximum_bitcast_fusion.refs_2_
  29.7 0.0 copy-done.7
  29.7 0.0 copy-start.17
  29.7 0.0 copy-start.18
  29.7 1.1 %control_strips.1.local_ref = f32[16,240,128]{2,1,0:T(8,128)S(1)} custom-call(s32[8,128]{1,0:T(8,128)S(1)} %broadcast_in_dim.15.par_ref.refs_0_, f32[16,240,128]{2,1,0:T(8,128)S(1)} %control_local.1.refs_1_.after, f32[240,128]{1,0:T(8,128)S(1)} %collective-permute-done.1.refs_2_.strip_e, f32[240,128]{1,0:T(8,128)S(1)} %collective-permute-done.2.refs_3_.strip_o, ...), custom_call_target="tpu_custom_call" | custom-call | tf_op jit(solution)/shard_map/control_strips/pallas_call | solution.py:582
  30.8 0.0 collective-permute-done.3
  30.9 4.5 %collective-permute-done.4.corner_ref = f32[64,128]{1,0:T(8,128)S(1)} collective-permute-done((f32[64,128]{1,0:T(8,128)S(1)}, f32[64,128]{1,0:T(8,128)S(1)}, u32[]{:S(2)}, u32[]{:S(2)}) %collective-permute-start.4) | collective-permute-done | bytes 32800 | tf_op jit(solution)/shard_map/ppermute | solution.py:509
  35.4 3.4 %flux_field.1 = (f32[16,240,128]{2,1,0:T(8,128)S(1)}, f32[16,240,128]{2,1,0:T(8,128)S(1)}) custom-call(s32[8,128]{1,0:T(8,128)S(1)} %broadcast_in_dim.15.par_ref.refs_0_, f32[16,240,128]{2,1,0:T(8,128)S(1)} %control_strips.1.local_ref, bf16[240,16,128]{2,1,0:T(8,128)(2,1)S(1)} %copy-done.17, bf16[240,16,128]{2,1,0:T(8,128)(2,1)S(1)} %copy-done.18, ...), custom_call_target="tpu_custom_call" | custom-call | tf_op jit(solution)/shard_map/flux_field/pallas_call | solution.py:620
  38.8 1.3 %copy-done = f32[16,240,128]{2,1,0:T(8,128)} copy-done((f32[16,240,128]{2,1,0:T(8,128)}, f32[16,240,128]{2,1,0:T(8,128)S(1)}, u32[]{:S(2)}) %copy-start) | copy-done | bytes 1966104
  40.1 1.3 %copy-done.16 = f32[16,240,128]{2,1,0:T(8,128)} copy-done((f32[16,240,128]{2,1,0:T(8,128)}, f32[16,240,128]{2,1,0:T(8,128)S(1)}, u32[]{:S(2)}) %copy-start.16) | copy-done | bytes 1966104
  41.3 0.3 collective-permute-done
  41.6 5.9 %all-to-all-done.refs_1_.refs_3_ = bf16[32,200,128]{2,1,0:T(8,128)(2,1)S(1)} async-done(((bf16[32,200,128]{2,1,0:T(8,128)(2,1)}), bf16[32,200,128]{2,1,0:T(8,128)(2,1)S(1)}, u32[]{:S(2)}, u32[]{:S(2)}) %all-to-all-start) | async-done | bytes 1638432 | tf_op jit(solution)/shard_map/all_to_all | solution.py:614
  47.5 1.0 %convert_element_type.25.refs_3_ = f32[4,240,128]{2,1,0:T(8,128)S(1)} convert(f16[4,240,128]{2,1,0:T(8,128)(2,1)} %collective-permute-done) | non-fusion elementwise | flops 122880 | bytes 737280 | tf_op jit(solution)/shard_map/convert_element_type | solution.py:648
  48.5 0.0 collective-permute-done.5.refs_6_
  48.5 0.6 copy-done.19
  49.1 4.0 %block_values.1 = (f32[32,5,128]{2,1,0:T(8,128)S(1)}, s32[32,128]{1,0:T(8,128)S(1)}) custom-call(s32[8,128]{1,0:T(8,128)S(1)} %broadcast_in_dim.15.par_ref.refs_0_, bf16[32,200,128]{2,1,0:T(8,128)(2,1)S(1)} %all-to-all-done.refs_1_.refs_3_, f32[1,128]{1,0:T(1,128)S(1)} %maximum_bitcast_fusion.refs_2_, f32[4,240,128]{2,1,0:T(8,128)S(1)} %convert_element_type.25.refs_3_, ...), custom_call_target="tpu_custom_call" | custom-call | tf_op jit(solution)/shard_map/block_values/pallas_call | solution.py:636
  53.1 16.1 %all_to_all.10.refs_2_ = f32[32,5,128]{2,1,0:T(8,128)S(1)} all-to-all(f32[32,5,128]{2,1,0:T(8,128)S(1)} %get-tuple-element.36), channel_id=1, replica_groups=mesh['rec'=8,'tile'=4] {'rec','tile'}, dimensions={0} | all-to-all | bytes 163840 | tf_op jit(solution)/shard_map/all_to_all | solution.py:649
  69.1 3.1 %adjoint_field.1 = (f32[1,64]{1,0:T(1,128)}, f32[2,128]{1,0:T(2,128)S(1)}, f32[16,240,128]{2,1,0:T(8,128)S(1)}) custom-call(s32[8,128]{1,0:T(8,128)S(1)} %broadcast_in_dim.15.par_ref.refs_0_, s32[32,128]{1,0:T(8,128)S(1)} %get-tuple-element.35.refs_1_, f32[32,5,128]{2,1,0:T(8,128)S(1)} %all_to_all.10.refs_2_, ...), custom_call_target="tpu_custom_call" | custom-call | tf_op jit(solution)/shard_map/adjoint_field/pallas_call | solution.py:655
  72.2 0.1 gradient_rows.1
  72.3 0.0 copy-start.3
  72.4 0.0 copy-start.5
  72.4 0.0 copy-start.10
  72.4 1.5 %collective-permute-start.8 = (f16[4,240,128]{2,1,0:T(8,128)(2,1)S(1)}, f16[4,240,128]{2,1,0:T(8,128)(2,1)S(1)}, u32[]{:S(2)}, u32[]{:S(2)}) collective-permute-start(f16[4,240,128]{2,1,0:T(8,128)(2,1)S(1)} %convert_element_type.28), channel_id=1, source_target_pairs={{0,4},{4,0},{8,12},{12,8},{16,20},{20,16},{24,28},{28,24},{1,5},{5... | collective-permute-start | bytes 737288 | tf_op jit(solution)/shard_map/ppermute | solution.py:509
  73.9 2.1 %collective-permute-start.9 = (f16[4,240,128]{2,1,0:T(8,128)(2,1)S(1)}, f16[4,240,128]{2,1,0:T(8,128)(2,1)S(1)}, u32[]{:S(2)}, u32[]{:S(2)}) collective-permute-start(f16[4,240,128]{2,1,0:T(8,128)(2,1)S(1)} %convert_element_type.30), channel_id=1, source_target_pairs={{4,8},{8,4},{12,16},{16,12},{20,24},{24,20},{5,9},{9,5},{13,17},{1... | collective-permute-start | bytes 737288 | tf_op jit(solution)/shard_map/ppermute | solution.py:510
  76.1 0.8 gradient_pack.1
  76.8 1.2 %collective-permute-start.6 = (f32[240,128]{1,0:T(8,128)S(1)}, f32[240,128]{1,0:T(8,128)S(1)}, u32[]{:S(2)}, u32[]{:S(2)}) collective-permute-start(f32[240,128]{1,0:T(8,128)S(1)} %get-tuple-element.42.after), channel_id=1, source_target_pairs={{0,1},{1,0},{2,3},{3,2},{4,5},{5,4},{6,7},{7,6},{8,9},{9,8},{10,11... | collective-permute-start | bytes 368648 | tf_op jit(solution)/shard_map/ppermute | solution.py:509
  78.0 2.5 %collective-permute-start.7 = (f32[240,128]{1,0:T(8,128)S(1)}, f32[240,128]{1,0:T(8,128)S(1)}, u32[]{:S(2)}, u32[]{:S(2)}) collective-permute-start(f32[240,128]{1,0:T(8,128)S(1)} %get-tuple-element.43), channel_id=1, source_target_pairs={{1,2},{2,1},{5,6},{6,5},{9,10},{10,9},{13,14},{14,13},{17,18},{18,... | collective-permute-start | bytes 368648 | tf_op jit(solution)/shard_map/ppermute | solution.py:510
  80.5 2.3 %gradient_local.1.refs_1_.after = f32[16,240,128]{2,1,0:T(8,128)S(1)} custom-call(f32[240,128]{1,0:T(8,128)S(1)} %get-tuple-element.42.after, f32[16,240,128]{2,1,0:T(8,128)S(1)} %get-tuple-element.39.field_ref, bf16[240,240]{1,0:T(8,128)(2,1)S(1)} %copy-done.3, bf16[240,240]{1,0:T(8,128)(2,1)S(1)} %copy-done.5, bf16[256,256]{1,0:T(8,128)(2,1)S(1)} %copy-done.10), custom_call_target="tpu_custom_call" | custom-call | tf_op jit(solution)/shard_map/gradient_local/pallas_call | solution.py:578
  82.9 0.0 copy-start.8
  82.9 0.0 collective-permute-done.6.refs_2_.strip_e
  82.9 1.6 %collective-permute-done.7.refs_3_.strip_o = f32[240,128]{1,0:T(8,128)S(1)} collective-permute-done((f32[240,128]{1,0:T(8,128)S(1)}, f32[240,128]{1,0:T(8,128)S(1)}, u32[]{:S(2)}, u32[]{:S(2)}) %collective-permute-start.7) | collective-permute-done | bytes 122912 | tf_op jit(solution)/shard_map/ppermute | solution.py:510
  84.5 0.2 gradient_corners.1
  84.7 0.1 collective-permute-start.10
  84.8 0.0 copy-start.12
  84.8 0.0 copy-start.14
  84.8 3.8 %collective-permute-start.11 = (f32[64,128]{1,0:T(8,128)S(1)}, f32[64,128]{1,0:T(8,128)S(1)}, u32[]{:S(2)}, u32[]{:S(2)}) collective-permute-start(f32[64,128]{1,0:T(8,128)S(1)} %get-tuple-element.45), channel_id=1, source_target_pairs={{4,8},{8,4},{12,16},{16,12},{20,24},{24,20},{5,9},{9,5},{13,17},{1... | collective-permute-start | bytes 98312 | tf_op jit(solution)/shard_map/ppermute | solution.py:510
  88.6 2.1 %gradient_strips.1.local_ref = f32[240,16,128]{2,1,0:T(8,128)S(1)} custom-call(s32[8,128]{1,0:T(8,128)S(1)} %broadcast_in_dim.15.par_ref.refs_0_, f32[16,240,128]{2,1,0:T(8,128)S(1)} %gradient_local.1.refs_1_.after, f32[240,128]{1,0:T(8,128)S(1)} %collective-permute-done.6.refs_2_.strip_e, f32[240,128]{1,0:T(8,128)S(1)} %collective-permute-done.7.refs_3_.strip_o, ...), custom_call_target="tpu_custom_call" | custom-call | tf_op jit(solution)/shard_map/gradient_strips/pallas_call | solution.py:582
  90.6 0.0 collective-permute-done.8
  90.7 0.0 collective-permute-done.9
  90.8 0.0 collective-permute-done.10.corner_e
  90.8 0.0 collective-permute-done.11.corner_o
  90.8 3.4 %gradient.1 = f32[240,16,128]{2,1,0:T(8,128)} custom-call(s32[8,128]{1,0:T(8,128)S(1)} %broadcast_in_dim.15.par_ref.refs_0_, f32[240,16,128]{2,1,0:T(8,128)S(1)} %gradient_strips.1.local_ref, f32[2,128]{1,0:T(2,128)S(1)} %get-tuple-element.38.factor_ref, f32[4,240,128]{2,1,0:T(8,128)S(1)} %convert_element_type.29.got_e, ...), custom_call_target="tpu_custom_call" | custom-call | tf_op jit(solution)/shard_map/gradient/pallas_call | solution.py:671
  (35 shorter events, 0.3 us)
Async XLA Ops:
  3.0 44.5 %all-to-all-start = ((bf16[32,200,128]{2,1,0:T(8,128)(2,1)}), bf16[32,200,128]{2,1,0:T(8,128)(2,1)S(1)}, u32[]{:S(2)}, u32[]{:S(2)}) async-start(bf16[32,200,128]{2,1,0:T(8,128)(2,1)} %prepare_blocks.1.after), calls=%async_computation | async-start | bytes 3276800 | tf_op jit(solution)/shard_map/all_to_all | solution.py:614
  9.6 1.5 %copy-start.15 = (f32[240,16,128]{2,1,0:T(8,128)S(1)}, f32[240,16,128]{2,1,0:T(8,128)}, u32[]{:S(2)}) copy-start(f32[240,16,128]{2,1,0:T(8,128)} %control_ref.1) | copy-start | bytes 5898244
  12.7 8.5 %copy-start.2 = (bf16[240,240]{1,0:T(8,128)(2,1)S(1)}, bf16[240,240]{1,0:T(8,128)(2,1)}, u32[]{:S(2)}) copy-start(bf16[240,240]{1,0:T(8,128)(2,1)} %constant.45.clone.time_high.refs_4_.refs_7_) | copy-start | bytes 345604
  12.7 8.5 %copy-start.4 = (bf16[240,240]{1,0:T(8,128)(2,1)S(1)}, bf16[240,240]{1,0:T(8,128)(2,1)}, u32[]{:S(2)}) copy-start(bf16[240,240]{1,0:T(8,128)(2,1)} %constant.46.clone.time_low.refs_5_.refs_8_) | copy-start | bytes 345604
  12.7 8.6 %copy-start.9 = (bf16[256,256]{1,0:T(8,128)(2,1)S(1)}, bf16[256,256]{1,0:T(8,128)(2,1)}, u32[]{:S(2)}) copy-start(bf16[256,256]{1,0:T(8,128)(2,1)} %constant.47.clone.col_both.refs_9_) | copy-start | bytes 393220
  12.9 17.9 %collective-permute-start.3 = (f16[4,240,128]{2,1,0:T(8,128)(2,1)S(1)}, f16[4,240,128]{2,1,0:T(8,128)(2,1)S(1)}, u32[]{:S(2)}, u32[]{:S(2)}) collective-permute-start(f16[4,240,128]{2,1,0:T(8,128)(2,1)S(1)} %convert_element_type.26), channel_id=1, source_target_pairs={{0,4},{4,0},{8,12},{12,8},{16,20},{20,16},{24,28},{28,24},{1,5},{5... | collective-permute-start | bytes 737288 | tf_op jit(solution)/shard_map/ppermute | solution.py:509
  13.1 28.5 %collective-permute-start = (f16[4,240,128]{2,1,0:T(8,128)(2,1)S(1)}, f16[4,240,128]{2,1,0:T(8,128)(2,1)}, u32[]{:S(2)}, u32[]{:S(2)}) collective-permute-start(f16[4,240,128]{2,1,0:T(8,128)(2,1)S(1)} %convert_element_type.24), channel_id=1, source_target_pairs={{4,8},{8,4},{12,16},{16,12},{20,24},{24,20},{5,9},{9,5},{13,17},{1... | collective-permute-start | bytes 737288 | tf_op jit(solution)/shard_map/ppermute | solution.py:510
  17.3 6.4 %collective-permute-start.1 = (f32[240,128]{1,0:T(8,128)S(1)}, f32[240,128]{1,0:T(8,128)S(1)}, u32[]{:S(2)}, u32[]{:S(2)}) collective-permute-start(f32[240,128]{1,0:T(8,128)S(1)} %get-tuple-element.28.after), channel_id=1, source_target_pairs={{0,1},{1,0},{2,3},{3,2},{4,5},{5,4},{6,7},{7,6},{8,9},{9,8},{10,11... | collective-permute-start | bytes 368648 | tf_op jit(solution)/shard_map/ppermute | solution.py:509
  18.3 8.9 %collective-permute-start.2 = (f32[240,128]{1,0:T(8,128)S(1)}, f32[240,128]{1,0:T(8,128)S(1)}, u32[]{:S(2)}, u32[]{:S(2)}) collective-permute-start(f32[240,128]{1,0:T(8,128)S(1)} %get-tuple-element.29), channel_id=1, source_target_pairs={{1,2},{2,1},{5,6},{6,5},{9,10},{10,9},{13,14},{14,13},{17,18},{18,... | collective-permute-start | bytes 368648 | tf_op jit(solution)/shard_map/ppermute | solution.py:510
  23.6 6.0 %copy-start.20 = (f32[64]{0:T(128)S(1)}, f32[64]{0:T(128)}, u32[]{:S(2)}) copy-start(f32[64]{0:T(128)} %param.26) | copy-start | bytes 772
  23.6 6.0 %copy-start.21 = (f32[64]{0:T(128)S(1)}, f32[64]{0:T(128)}, u32[]{:S(2)}) copy-start(f32[64]{0:T(128)} %param.25) | copy-start | bytes 772
  23.6 6.0 %copy-start.6 = (bf16[256,2048]{1,0:T(8,128)(2,1)S(1)}, bf16[256,2048]{1,0:T(8,128)(2,1)}, u32[]{:S(2)}) copy-start(bf16[256,2048]{1,0:T(8,128)(2,1)} %constant.48.clone.refs_6_) | copy-start | bytes 3145732
  23.6 6.0 %copy-start.7 = (bf16[256,2048]{1,0:T(8,128)(2,1)S(1)}, bf16[256,2048]{1,0:T(8,128)(2,1)}, u32[]{:S(2)}) copy-start(bf16[256,2048]{1,0:T(8,128)(2,1)} %constant.49.clone.refs_7_) | copy-start | bytes 3145732
  27.4 8.0 %collective-permute-start.4 = (f32[64,128]{1,0:T(8,128)S(1)}, f32[64,128]{1,0:T(8,128)S(1)}, u32[]{:S(2)}, u32[]{:S(2)}) collective-permute-start(f32[64,128]{1,0:T(8,128)S(1)} %get-tuple-element.31), channel_id=1, source_target_pairs={{0,4},{4,0},{8,12},{12,8},{16,20},{20,16},{24,28},{28,24},{1,5},{5... | collective-permute-start | bytes 98312 | tf_op jit(solution)/shard_map/ppermute | solution.py:509
  27.5 21.0 %collective-permute-start.5 = (f32[64,128]{1,0:T(8,128)S(1)}, f32[64,128]{1,0:T(8,128)S(1)}, u32[]{:S(2)}, u32[]{:S(2)}) collective-permute-start(f32[64,128]{1,0:T(8,128)S(1)} %get-tuple-element.34), channel_id=1, source_target_pairs={{4,8},{8,4},{12,16},{16,12},{20,24},{24,20},{5,9},{9,5},{13,17},{1... | collective-permute-start | bytes 98312 | tf_op jit(solution)/shard_map/ppermute | solution.py:510
  29.7 5.7 %copy-start.11 = (bf16[2,128,512]{2,1,0:T(8,128)(2,1)S(1)}, bf16[2,128,512]{2,1,0:T(8,128)(2,1)}, u32[]{:S(2)}) copy-start(bf16[2,128,512]{2,1,0:T(8,128)(2,1)} %constant.50.clone.corner_high.refs_10_) | copy-start | bytes 786436
  29.7 5.7 %copy-start.13 = (bf16[2,128,512]{2,1,0:T(8,128)(2,1)S(1)}, bf16[2,128,512]{2,1,0:T(8,128)(2,1)}, u32[]{:S(2)}) copy-start(bf16[2,128,512]{2,1,0:T(8,128)(2,1)} %constant.51.clone.corner_low.refs_11_) | copy-start | bytes 786436
  29.7 5.7 %copy-start.17 = (bf16[240,16,128]{2,1,0:T(8,128)(2,1)S(1)}, bf16[240,16,128]{2,1,0:T(8,128)(2,1)}, u32[]{:S(2)}) copy-start(bf16[240,16,128]{2,1,0:T(8,128)(2,1)} %prior_ref.1) | copy-start | bytes 2949124
  29.7 5.7 %copy-start.18 = (bf16[240,16,128]{2,1,0:T(8,128)(2,1)S(1)}, bf16[240,16,128]{2,1,0:T(8,128)(2,1)}, u32[]{:S(2)}) copy-start(bf16[240,16,128]{2,1,0:T(8,128)(2,1)} %scale_ref.1) | copy-start | bytes 2949124
  38.8 1.3 %copy-start = (f32[16,240,128]{2,1,0:T(8,128)}, f32[16,240,128]{2,1,0:T(8,128)S(1)}, u32[]{:S(2)}) copy-start(f32[16,240,128]{2,1,0:T(8,128)S(1)} %get-tuple-element.33.refs_5_.refs_4_) | copy-start | bytes 5898244
  40.1 1.3 %copy-start.16 = (f32[16,240,128]{2,1,0:T(8,128)}, f32[16,240,128]{2,1,0:T(8,128)S(1)}, u32[]{:S(2)}) copy-start(f32[16,240,128]{2,1,0:T(8,128)S(1)} %get-tuple-element.32.refs_4_) | copy-start | bytes 5898244
  48.5 0.6 copy-start.19
  49.1 20.1 %copy-start.1 = (f32[16,240,128]{2,1,0:T(8,128)S(1)}, f32[16,240,128]{2,1,0:T(8,128)}, u32[]{:S(2)}) copy-start(f32[16,240,128]{2,1,0:T(8,128)} %copy-done) | copy-start | bytes 5898244
  72.3 8.2 %copy-start.3 = (bf16[240,240]{1,0:T(8,128)(2,1)S(1)}, bf16[240,240]{1,0:T(8,128)(2,1)}, u32[]{:S(2)}) copy-start(bf16[240,240]{1,0:T(8,128)(2,1)} %constant.45.clone.time_high.refs_4_.refs_7_) | copy-start | bytes 345604
  72.4 8.2 %copy-start.5 = (bf16[240,240]{1,0:T(8,128)(2,1)S(1)}, bf16[240,240]{1,0:T(8,128)(2,1)}, u32[]{:S(2)}) copy-start(bf16[240,240]{1,0:T(8,128)(2,1)} %constant.46.clone.time_low.refs_5_.refs_8_) | copy-start | bytes 345604
  72.4 8.2 %copy-start.10 = (bf16[256,256]{1,0:T(8,128)(2,1)S(1)}, bf16[256,256]{1,0:T(8,128)(2,1)}, u32[]{:S(2)}) copy-start(bf16[256,256]{1,0:T(8,128)(2,1)} %constant.47.clone.col_both.refs_9_) | copy-start | bytes 393220
  72.4 18.3 %collective-permute-start.8 = (f16[4,240,128]{2,1,0:T(8,128)(2,1)S(1)}, f16[4,240,128]{2,1,0:T(8,128)(2,1)S(1)}, u32[]{:S(2)}, u32[]{:S(2)}) collective-permute-start(f16[4,240,128]{2,1,0:T(8,128)(2,1)S(1)} %convert_element_type.28), channel_id=1, source_target_pairs={{0,4},{4,0},{8,12},{12,8},{16,20},{20,16},{24,28},{28,24},{1,5},{5... | collective-permute-start | bytes 737288 | tf_op jit(solution)/shard_map/ppermute | solution.py:509
  73.9 16.8 %collective-permute-start.9 = (f16[4,240,128]{2,1,0:T(8,128)(2,1)S(1)}, f16[4,240,128]{2,1,0:T(8,128)(2,1)S(1)}, u32[]{:S(2)}, u32[]{:S(2)}) collective-permute-start(f16[4,240,128]{2,1,0:T(8,128)(2,1)S(1)} %convert_element_type.30), channel_id=1, source_target_pairs={{4,8},{8,4},{12,16},{16,12},{20,24},{24,20},{5,9},{9,5},{13,17},{1... | collective-permute-start | bytes 737288 | tf_op jit(solution)/shard_map/ppermute | solution.py:510
  76.8 6.1 %collective-permute-start.6 = (f32[240,128]{1,0:T(8,128)S(1)}, f32[240,128]{1,0:T(8,128)S(1)}, u32[]{:S(2)}, u32[]{:S(2)}) collective-permute-start(f32[240,128]{1,0:T(8,128)S(1)} %get-tuple-element.42.after), channel_id=1, source_target_pairs={{0,1},{1,0},{2,3},{3,2},{4,5},{5,4},{6,7},{7,6},{8,9},{9,8},{10,11... | collective-permute-start | bytes 368648 | tf_op jit(solution)/shard_map/ppermute | solution.py:509
  78.0 6.5 %collective-permute-start.7 = (f32[240,128]{1,0:T(8,128)S(1)}, f32[240,128]{1,0:T(8,128)S(1)}, u32[]{:S(2)}, u32[]{:S(2)}) collective-permute-start(f32[240,128]{1,0:T(8,128)S(1)} %get-tuple-element.43), channel_id=1, source_target_pairs={{1,2},{2,1},{5,6},{6,5},{9,10},{10,9},{13,14},{14,13},{17,18},{18,... | collective-permute-start | bytes 368648 | tf_op jit(solution)/shard_map/ppermute | solution.py:510
  82.9 5.7 %copy-start.8 = (bf16[256,2048]{1,0:T(8,128)(2,1)S(1)}, bf16[256,2048]{1,0:T(8,128)(2,1)}, u32[]{:S(2)}) copy-start(bf16[256,2048]{1,0:T(8,128)(2,1)} %constant.49.clone.refs_7_) | copy-start | bytes 3145732
  84.7 6.1 %collective-permute-start.10 = (f32[64,128]{1,0:T(8,128)S(1)}, f32[64,128]{1,0:T(8,128)S(1)}, u32[]{:S(2)}, u32[]{:S(2)}) collective-permute-start(f32[64,128]{1,0:T(8,128)S(1)} %get-tuple-element.44), channel_id=1, source_target_pairs={{0,4},{4,0},{8,12},{12,8},{16,20},{20,16},{24,28},{28,24},{1,5},{5... | collective-permute-start | bytes 98312 | tf_op jit(solution)/shard_map/ppermute | solution.py:509
  84.8 6.0 %copy-start.12 = (bf16[2,128,512]{2,1,0:T(8,128)(2,1)S(1)}, bf16[2,128,512]{2,1,0:T(8,128)(2,1)}, u32[]{:S(2)}) copy-start(bf16[2,128,512]{2,1,0:T(8,128)(2,1)} %constant.50.clone.corner_high.refs_10_) | copy-start | bytes 786436
  84.8 6.0 %copy-start.14 = (bf16[2,128,512]{2,1,0:T(8,128)(2,1)S(1)}, bf16[2,128,512]{2,1,0:T(8,128)(2,1)}, u32[]{:S(2)}) copy-start(bf16[2,128,512]{2,1,0:T(8,128)(2,1)} %constant.51.clone.corner_low.refs_11_) | copy-start | bytes 786436
  84.8 6.0 %collective-permute-start.11 = (f32[64,128]{1,0:T(8,128)S(1)}, f32[64,128]{1,0:T(8,128)S(1)}, u32[]{:S(2)}, u32[]{:S(2)}) collective-permute-start(f32[64,128]{1,0:T(8,128)S(1)} %get-tuple-element.45), channel_id=1, source_target_pairs={{4,8},{8,4},{12,16},{16,12},{20,24},{24,20},{5,9},{9,5},{13,17},{1... | collective-permute-start | bytes 98312 | tf_op jit(solution)/shard_map/ppermute | solution.py:510

commit v6 on v5

--- a/solution.py
+++ b/solution.py
@@ -69,7 +69,6 @@
         lanes = [
             (row, side * RAD + j) for side in range(2) for row in range(first, first + RAD) for j in range(RAD)
         ]
-        lanes += [(-100, 0)] * (LANES - len(lanes))
         for part, value in zip(corner, strips(*zip(*lanes), targets)):
             part.append(value)
     return (time_high, time_low, col_both), strips(*zip(*own), np.arange(rows)), [np.stack(c) for c in corner]
@@ -140,11 +139,13 @@
     return par_ref[axis : axis + 1, :] == 1
 
 
-def write_rows(odd, row_value, rows, rows_e, rows_o):
+def rows_kernel(par_ref, after, factor_ref, field_ref, out_ref, *, even):
+    odd = is_odd(par_ref, 0)
+    factor = factor_ref[0:1, :]
+    rows = field_ref.shape[0]
     for row in range(RAD):
-        first, last = row_value(row), row_value(rows - 1 - row)
-        rows_e[row] = choose(odd, first, last)
-        rows_o[row] = choose(odd, last, first)
+        first, last = field_ref[row], field_ref[rows - 1 - row]
+        out_ref[row] = (choose(odd, first, last) if even else choose(odd, last, first)) * factor
 
 
 def turn_kernel(par_ref, after, control_ref, field_ref, strip_e, strip_o):
@@ -154,7 +155,7 @@
     write_strips(is_odd(par_ref, 1), field_ref, strip_e, strip_o)
 
 
-def strip_kernel(par_ref, after_e, after_o, field_ref, strip_e, strip_o):
+def strip_kernel(par_ref, after, field_ref, strip_e, strip_o):
     write_strips(is_odd(par_ref, 1), field_ref, strip_e, strip_o)
 
 
@@ -175,14 +176,9 @@
     fold_corners(is_odd(par_ref, 0), both, corner_e, corner_o)
 
 
-def rows_kernel(par_ref, factor_ref, field_ref, rows_e, rows_o):
-    factor = factor_ref[0:1, :]
-    write_rows(is_odd(par_ref, 0), lambda r: field_ref[r] * factor, field_ref.shape[0], rows_e, rows_o)
-
-
 def prepare_kernel(
     foot_ref, start_ref, row_ref, slot_ref, count_ref, out_ref,
-    wide_ref, start_vmem, row_vmem, slot_vmem, count_vmem, sems, *, per,
+    blocks_ref, notes_ref, start_vmem, row_vmem, slot_vmem, count_vmem, sems, *, per,
 ):
     owners, lines, _ = foot_ref.shape
     slots = start_ref.shape[0]
@@ -191,11 +187,17 @@
     chunk = owners // PARTS
     parts = [slice(i * chunk, (i + 1) * chunk) for i in range(PARTS)]
     loads = [
-        pltpu.make_async_copy(foot_ref.at[here], wide_ref.at[here, 0:lines, :], sems.at[4 + i])
+        pltpu.make_async_copy(foot_ref.at[here], blocks_ref.at[here], sems.at[4 + i])
         for i, here in enumerate(parts)
     ]
     for copy in small + loads:
         copy.start()
+    stores = []
+    for i, here in enumerate(parts):
+        loads[i].wait()
+        to = out_ref.at[here, 0:lines, :]
+        stores.append(pltpu.make_async_copy(blocks_ref.at[here], to, sems.at[4 + PARTS + i]))
+        stores[-1].start()
     for copy in small:
         copy.wait()
     start = start_vmem[...]
@@ -205,13 +207,9 @@
     ).astype(F32)
     wide = jnp.pad(lanes, ((0, LANES - 4 * slots), (0, LANES - owners)))
     turned = jnp.transpose(wide)[0:owners]
-    notes = jnp.broadcast_to(turned[:, None, :], (owners, SUB, LANES)).astype(BF16)
-    wide_ref[:, lines : lines + SUB, :] = notes
-    stores = []
-    for i, here in enumerate(parts):
-        loads[i].wait()
-        stores.append(pltpu.make_async_copy(wide_ref.at[here], out_ref.at[here], sems.at[4 + PARTS + i]))
-        stores[-1].start()
+    notes_ref[...] = jnp.broadcast_to(turned[:, None, :], notes_ref.shape).astype(BF16)
+    stores.append(pltpu.make_async_copy(notes_ref, out_ref.at[:, lines : lines + SUB, :], sems.at[4 + 2 * PARTS]))
+    stores[-1].start()
     for copy in stores:
         copy.wait()
 
@@ -259,20 +257,42 @@
             out_ref[r] = both[:, k * cols : (k + 1) * cols]
 
 
-def strips_kernel(par_ref, local_ref, strip_e, strip_o, time_high, time_low, own_high, own_low, out_ref, *, by_hour):
-    rows, hours, cols = local_ref.shape
+def strip_halo(par_ref, strip_e, strip_o, time_high, time_low):
     odd = is_odd(par_ref, 1)
     even_swap, odd_swap = strip_e[...], strip_o[...]
     halo = jnp.concatenate([choose(odd, even_swap, odd_swap), choose(odd, odd_swap, even_swap)], axis=1)
-    halo = split(time_sums(halo, time_high[...], time_low[...]))
+    return split(time_sums(halo, time_high[...], time_low[...]))
+
+
+def strips_kernel(par_ref, local_ref, strip_e, strip_o, time_high, time_low, own_high, own_low, out_ref):
+    rows, hours, cols = local_ref.shape
+    halo = strip_halo(par_ref, strip_e, strip_o, time_high, time_low)
     for row in range(0, rows, 2):
         both = halo_sums(halo, own_high, own_low, row * cols, 2 * cols)
         for k, r in enumerate((row, row + 1)):
-            part = local_ref[r] + both[:, k * cols : (k + 1) * cols]
-            if by_hour:
-                out_ref[:, r, :] = part
-            else:
-                out_ref[r] = part
+            out_ref[r] = local_ref[r] + both[:, k * cols : (k + 1) * cols]
+
+
+def sides_kernel(
+    par_ref, local_ref, strip_e, strip_o, factor_ref, got_ref, corner_ref,
+    time_high, time_low, col_both, own_high, own_low, corner_high, corner_low, out_ref, halo,
+):
+    rows, hours, cols = local_ref.shape
+    odd = par_ref[0, 0]
+    halo[...] = got_ref[...] * factor_ref[1:2, :]
+    consts = (time_high, time_low, col_both)
+    parts = edge_parts(halo, corner_ref[...], corner_high.at[odd], corner_low.at[odd], consts)
+    at_first = jnp.where(is_odd(par_ref, 0), 1.0, 0.0)
+    strips = strip_halo(par_ref, strip_e, strip_o, time_high, time_low)
+    for row in range(0, rows, 2):
+        both = halo_sums(strips, own_high, own_low, row * cols, 2 * cols)
+        for k, r in enumerate((row, row + 1)):
+            value = local_ref[r] + both[:, k * cols : (k + 1) * cols]
+            if r < RAD:
+                value = value + parts[r] * at_first
+            if r >= rows - RAD:
+                value = value + parts[rows - 1 - r] * (1.0 - at_first)
+            out_ref[:, r, :] = value
 
 
 def edge_parts(odd, rows, first, got_e, got_o, consts, halo, factor, corner=None):
@@ -306,7 +326,7 @@
     time_high, time_low, col_both = consts
     hours, cols = halo.shape[1:]
     taps = space_taps()
-    corner = split(unfold_corners(corner)[0:hours])
+    corner = split(unfold_corners(corner)[0:hours, 0 : corner_high.shape[0]])
     parts = []
     for k in range(0, RAD, 2):
         pair = []
@@ -343,31 +363,34 @@
 
 
 def finish_kernel(
-    par_ref, local_ref, factor_ref, got_e, got_o, corner_e, corner_o,
-    time_high, time_low, col_both, corner_high, corner_low, out_ref, halo, edges, total, sems,
+    par_ref, model_ref, local_ref, factor_ref, got_ref, corner_ref,
+    time_high, time_low, col_both, corner_high, corner_low,
+    model_out, out_ref, halo, edges, total, model_own, sems,
 ):
     hours, rows, cols = local_ref.shape
-    odd = is_odd(par_ref, 0)
-    factor = factor_ref[1:2, :]
+    half = rows // 2
+    odd = par_ref[0, 0]
+    mine = pl.multiple_of(odd * half, half)
+    rest = pl.multiple_of(half - mine, half)
+    model_own[...] = model_ref[:, 0 : model_own.shape[1]]
+    copies = [
+        pltpu.make_async_copy(model_own, model_out, sems.at[0]),
+        pltpu.make_async_copy(
+            local_ref.at[:, pl.ds(rest, half), :], out_ref.at[:, pl.ds(rest, half), :], sems.at[1]
+        ),
+    ]
+    for copy in copies:
+        copy.start()
+    halo[...] = got_ref[...] * factor_ref[1:2, :]
     consts = (time_high, time_low, col_both)
-    inside = lax.broadcasted_iota(jnp.int32, (hours, 2 * RAD, cols), 1)
-    copies = []
-    for side in range(2):
-        before = side == 0
-        for k in range(RAD):
-            even, other = got_e[k], got_o[k]
-            halo[side, k] = (choose(odd, even, other) if before else choose(odd, other, even)) * factor
-        even, other = corner_e[...], corner_o[...]
-        corner = choose(odd, even, other) if before else choose(odd, other, even)
-        which = 1 - side
-        parts = edge_parts(halo.at[side], corner, corner_high.at[which], corner_low.at[which], consts)
-        for k, part in enumerate(parts):
-            edges[:, k if before else 2 * RAD - 1 - k, :] = part
-        here = slice(0, 2 * RAD) if before else slice(rows - 2 * RAD, rows)
-        mine = inside < RAD if before else inside >= RAD
-        total[:, here, :] = local_ref[:, here, :] + jnp.where(mine, edges[...], 0.0)
-        copies.append(pltpu.make_async_copy(total.at[:, here, :], out_ref.at[:, here, :], sems.at[side]))
-        copies[-1].start()
+    parts = edge_parts(halo, corner_ref[...], corner_high.at[1 - odd], corner_low.at[1 - odd], consts)
+    at_last = jnp.where(is_odd(par_ref, 0), 1.0, 0.0)
+    for k, part in enumerate(parts):
+        edges[:, k, :] = part * (1.0 - at_last)
+        edges[:, half - 1 - k, :] = part * at_last
+    total[...] = local_ref[:, pl.ds(mine, half), :] + edges[...]
+    copies.append(pltpu.make_async_copy(total, out_ref.at[:, pl.ds(mine, half), :], sems.at[2]))
+    copies[-1].start()
     for copy in copies:
         copy.wait()
 
@@ -380,17 +403,19 @@
 
 
 def forward_kernel(
-    par_ref, foot_ref, own_ref, got_ref, flux_hbm, scale_hbm, *refs, shift, slots, heights, tiles, per,
+    par_ref, foot_ref, own_ref, got_ref, corner_ref, flux_hbm, scale_hbm, *refs,
+    shift, slots, heights, tiles, per,
 ):
-    distant, near = refs[0:6], refs[8:14]
-    out_ref, table_ref = refs[6:8]
-    flux_ref, scale_ref, halo, edges, sums, table_smem, sems = refs[14:]
-    corner_ref, *consts, corner_high, corner_low = near
+    distant, near = refs[0:5], refs[7:12]
+    out_ref, table_ref = refs[5:7]
+    flux_ref, scale_ref, halo, edges, sums, table_smem, sems = refs[12:]
+    *consts, corner_high, corner_low = near
     odd = par_ref[0, 0]
     sources = foot_ref.shape[0]
     rows = flux_ref.shape[0]
     first = (rows - RAD) * odd
-    pairs = list(zip(distant, near)) + [(scale_hbm.at[pl.ds(first, RAD)], scale_ref), (flux_hbm, flux_ref)]
+    pairs = list(zip(distant, near)) + [(scale_hbm.at[pl.ds(first, RAD)], scale_ref)]
+    pairs += [(flux_hbm.at[r : r + RAD], flux_ref.at[r : r + RAD]) for r in range(0, rows, RAD)]
     loads = [pltpu.make_async_copy(a, b, sems.at[i]) for i, (a, b) in enumerate(pairs)]
     for load in loads:
         load.start()
@@ -406,13 +431,13 @@
     table_ref[...] = table
     copy = pltpu.make_async_copy(table_ref, table_smem, sems.at[len(loads)])
     copy.start()
-    for load in loads[:-2]:
+    for load in loads[: len(near)]:
         load.wait()
     halo[...] = got_ref[...] * (1.0 / CONTROL_FACTOR)
     parts = edge_parts(halo, corner_ref[...], corner_high.at[1 - odd], corner_low.at[1 - odd], consts)
     for k, part in enumerate(parts):
         edges[k] = part
-    for load in loads[-2:]:
+    for load in loads[len(near) :]:
         load.wait()
     for k in range(RAD):
         line = jnp.where(odd == 1, RAD - 1 - k, k)
@@ -460,7 +485,7 @@
             line = model[q : q + 1, :]
             line = line if k == 0 else pltpu.roll(line, LANES - k * per, 1)
             own = choose(par_ref[2:3, :] == q * packed + k, line, own)
-    model_ref[...] = own[:, 0:per]
+    model_ref[...] = own
     weight_vmem[...] = jnp.zeros_like(weight_vmem)
     for q in range(groups):
         observed, error = jnp.zeros((1, LANES), F32), jnp.ones((1, LANES), F32)
@@ -567,26 +592,17 @@
     field_shape = array(rows, hours, cols)
     row_scratch = pltpu.VMEM((RAD, hours, cols), F32)
 
-    def half(rows_e, rows_o):
-        return rows_e.astype(F16), rows_o.astype(F16)
-
-    def inner_sums(field, sent, by_hour, name):
-        def second(*refs):
-            strips_kernel(*refs, by_hour=by_hour)
-
-        got_strips = swap("tile", *sent)
-        local = call(local_kernel, field_shape, [VM] * 5, [], name + "_local")(sent[0], field, *base)
-        shape = array(hours, rows, cols) if by_hour else field_shape
+    def swaps(after, field, got_strips, name):
+        local = call(local_kernel, field_shape, [VM] * 5, [], name + "_local")(after, field, *base)
         corners = call(far_corner_kernel, [corner, corner], [VM] * 4, [], name + "_corners")(par, local, *got_strips)
-        got_corners = swap("rec", *corners)
-        local = call(second, shape, [VM] * 8, [], name + "_strips")(
-            par, local, *got_strips, *base[:2], *own_parts
-        )
-        return local, got_corners
-
-    def pack_rows(factor, field, name):
-        sent = call(rows_kernel, [block, block], [VM] * 3, [], name)(par, factor, field)
-        return sent, swap("rec", *half(*sent))
+        return local, swap("rec", *corners)
+
+    def swap_rows(even, after, factor, field, name):
+        def kernel(*refs):
+            rows_kernel(*refs, even=even)
+
+        sent = call(kernel, block, [VM] * 4, [], name)(par, after, factor, field)
+        return sent, lax.ppermute(sent.astype(F16), "rec", swap_pairs(n_rec, not even))
 
     def prepare(*refs):
         prepare_kernel(*refs, per=per)
@@ -598,9 +614,10 @@
         jax.ShapeDtypeStruct((devices, lines, cols), BF16),
         [HB] * 5,
         [
-            pltpu.VMEM((devices, lines, cols), BF16),
+            pltpu.VMEM((devices, slots * heights, cols), BF16),
+            pltpu.VMEM((devices, SUB, LANES), BF16),
             numbers, numbers, numbers, pltpu.VMEM((1, devices), jnp.int32),
-            pltpu.SemaphoreType.DMA((4 + 2 * PARTS,)),
+            pltpu.SemaphoreType.DMA((5 + 2 * PARTS,)),
         ],
         "prepare_blocks",
         out_specs=HB,
@@ -615,15 +632,21 @@
     field, *strips = call(
         turn_kernel, [field_shape, strip, strip], [VM, HB, VM], [], "turn_control"
     )(par, sent, control)
-    _, got_rows = pack_rows(jnp.full((2, LANES), CONTROL_FACTOR, F32), field, "control_rows")
-    local, got_corners = inner_sums(field, strips, False, "control")
+    factor = jnp.full((2, LANES), CONTROL_FACTOR, F32)
+    _, got_even = swap_rows(True, strips[0], factor, field, "control_even")
+    _, got_odd = swap_rows(False, strips[0], factor, field, "control_odd")
+    got_strips = swap("tile", *strips)
+    local, got_corners = swaps(strips[0], field, got_strips, "control")
+    local = call(strips_kernel, field_shape, [VM] * 8, [], "control_strips")(
+        par, local, *got_strips, *base[:2], *own_parts
+    )
     flux, scale = call(
         flux_kernel,
         [field_shape, field_shape],
         [VM] * 11,
         [pltpu.VMEM((hours, rows, cols), F32), row_scratch],
         "flux_field",
-    )(par, local, prior_flux, flux_scale, got_rows[0].astype(F32), got_corners[0], *base, *corner_parts)
+    )(par, local, prior_flux, flux_scale, got_even.astype(F32), got_corners[0], *base, *corner_parts)
 
     own = jnp.concatenate([observed, obs_error, jnp.zeros((LANES - 2 * per,), F32)])[None]
     sizes = dict(shift=shift, slots=slots, heights=heights, tiles=n_tile, per=per)
@@ -631,30 +654,30 @@
     def forward(*refs):
         forward_kernel(*refs, **sizes)
 
-    foot, got_odd = lax.optimization_barrier((foot, got_rows[1]))
-    needed = [got_corners[1], *base, *corner_parts]
+    foot, got_odd = lax.optimization_barrier((foot, got_odd))
+    needed = [*base, *corner_parts]
     partial, table = call(
         forward,
         [array(devices, groups + 1, LANES), jax.ShapeDtypeStruct((devices, LANES), jnp.int32)],
-        [VM] * 4 + [HB] * 8,
+        [VM] * 5 + [HB] * 7,
         [pltpu.VMEM(x.shape, x.dtype) for x in needed]
         + [pltpu.VMEM((rows, hours, cols), F32), row_scratch, row_scratch, row_scratch]
         + [
             pltpu.VMEM((slots, devices, LANES), F32),
             pltpu.SMEM((devices, LANES), jnp.int32),
-            pltpu.SemaphoreType.DMA((len(needed) + 4,)),
+            pltpu.SemaphoreType.DMA((len(needed) + rows // RAD + 2,)),
         ],
         "block_values",
-    )(par, foot, own, got_odd.astype(F32), *[far(x) for x in (flux, scale, *needed)])
+    )(par, foot, own, got_odd.astype(F32), got_corners[1], *[far(x) for x in (flux, scale, *needed)])
     everyone = lax.all_to_all(partial, AXES, split_axis=0, concat_axis=0, tiled=True)
 
     def adjoint(*refs):
         adjoint_kernel(*refs, **sizes)
 
     weight_rows = -(-(groups + 1) // SUB) * SUB
-    model_co2, factor, field = call(
+    model, factor, field = call(
         adjoint,
-        [array(1, per), array(2, LANES), field_shape],
+        [array(1, LANES), array(2, LANES), field_shape],
         [VM] * 5,
         [
             pltpu.VMEM((weight_rows, LANES), F32),
@@ -664,23 +687,23 @@
         ],
         "adjoint_field",
     )(par, table, everyone, foot, scale)
-    sent_rows, got_rows = pack_rows(factor, field, "gradient_rows")
-    strips = call(strip_kernel, [strip, strip], [VM] * 4, [], "gradient_pack")(par, *sent_rows, field)
-    local, got_corners = inner_sums(field, strips, True, "gradient")
-    got_rows = [r.astype(F32) for r in got_rows]
-    gradient = call(
+    sent_even, got_even = swap_rows(True, factor, factor, field, "gradient_even")
+    strips = call(strip_kernel, [strip, strip], [VM] * 3, [], "gradient_pack")(par, sent_even, field)
+    got_strips = swap("tile", *strips)
+    sent_odd, got_odd = swap_rows(False, got_strips[0], factor, field, "gradient_odd")
+    local, got_corners = swaps(sent_odd, field, got_strips, "gradient")
+    local = call(sides_kernel, array(hours, rows, cols), [VM] * 14, [row_scratch], "gradient_sides")(
+        par, local, *got_strips, factor, got_even.astype(F32), got_corners[0], *base, *own_parts, *corner_parts
+    )
+    wide = pltpu.VMEM((hours, rows // 2, cols), F32)
+    model_co2, gradient = call(
         finish_kernel,
-        array(hours, rows, cols),
-        [VM] * 12,
-        [
-            pltpu.VMEM((2, RAD, hours, cols), F32),
-            pltpu.VMEM((hours, 2 * RAD, cols), F32),
-            pltpu.VMEM((hours, rows, cols), F32),
-            pltpu.SemaphoreType.DMA((2,)),
-        ],
+        [array(1, per), array(hours, rows, cols)],
+        [VM] * 11,
+        [row_scratch, wide, wide, pltpu.VMEM((1, per), F32), pltpu.SemaphoreType.DMA((3,))],
         "gradient",
-        out_specs=HB,
-    )(par, local, factor, *got_rows, *got_corners, *base, *corner_parts)
+        out_specs=[HB, HB],
+    )(par, model, local, factor, got_odd.astype(F32), got_corners[1], *base, *corner_parts)
     return (model_co2.reshape(-1), gradient)
 
 

time: 95.1 us -> 92.7 us (0.975)
    ppermute x0 -> x4, starting transfers between devices: none -> 8.36 us  [swap_rows(): lax.ppermute(sent.astype(F16), 'rec', swap_pairs(n_rec, not even))]
    ppermute x6 -> x4, starting transfers between devices: 17.7 us -> 11.9 us  [swap(): lax.ppermute(odd, axis, swap_pairs(count, True))]
    ppermute x6 -> x4, starting transfers between devices: 3.92 us -> 0.92 us  [swap(): lax.ppermute(even, axis, swap_pairs(count, False))]
    ppermute x6 -> x4, waiting for transfers between devices: 4.51 us -> 6.84 us  [swap(): lax.ppermute(even, axis, swap_pairs(count, False))]
    all_to_all x1, waiting for transfers between devices: 5.87 us -> 4.56 us  [per_device(): foot = lax.all_to_all(sent, AXES, split_axis=0, concat_axis=0, tiled=True)]
    ppermute x6 -> x4, waiting for transfers between devices: 5.32 us -> 4.4 us  [swap(): lax.ppermute(odd, axis, swap_pairs(count, True))]
    unnamed x44 -> x42, local copies, waits for them, and re-layouts: 4.82 us -> 4.23 us
    pallas_call x11 -> x13, Pallas kernels: 15.6 us -> 15.1 us  [the longest x2 4.61 us: swaps(): call(local_kernel, field_shape, [VM] * 5, [], name + '_local')]
  transfers between devices with their start and end apart: 13 -> 13, of which waited for: 5 -> 4; matrix products, arithmetic and copies ran while one was open for 2% -> 1% of each run, Pallas kernels for 15% -> 15%
where the time goes in v6:
time: 92.7 us; the launch traced here: 92.2 us
  starting transfers between devices  27.6 us (30%)
  Pallas kernels  26.2 us (28%)
  blocking collectives  16.5 us (18%)
  waiting for transfers between devices  15.8 us (17%)
  local copies, waits for them, and re-layouts  4.4 us (5%)
  between operations  1.35 us (1%)
    all_to_all x1, blocking collectives, per_device(): lax.all_to_all(partial, AXES, split_axis=0, concat_axis=0, tiled=True)  16.5 us
    ppermute x4, starting transfers between devices, swap(): lax.ppermute(odd, axis, swap_pairs(count, True))  11.9 us
    ppermute x4, starting transfers between devices, swap_rows(): lax.ppermute(sent.astype(F16), 'rec', swap_pairs(n_rec, not even))  8.36 us
    ppermute x4, waiting for transfers between devices, swap(): lax.ppermute(even, axis, swap_pairs(count, False))  6.84 us
    all_to_all x1, starting transfers between devices, per_device(): foot = lax.all_to_all(sent, AXES, split_axis=0, concat_axis=0, tiled=True)  6.42 us
    pallas_call x2, Pallas kernels, swaps(): call(local_kernel, field_shape, [VM] * 5, [], name + '_local')  4.61 us
    all_to_all x1, waiting for transfers between devices, per_device(): foot = lax.all_to_all(sent, AXES, split_axis=0, concat_axis=0, tiled=True)  4.56 us
    ppermute x4, waiting for transfers between devices, swap(): lax.ppermute(odd, axis, swap_pairs(count, True))  4.4 us
  transfers between devices with their start and end apart: 13, of which 4 were waited for; matrix products, arithmetic and copies ran while one was open for 1% of the time, Pallas kernels for 15%

profile of v6, /device:TPU:5, one launch (start us, length us, event | category | flops | bytes accessed | tf_op | source)
XLA Modules:
  0.0 92.2 jit_solution(14081708279804918511)
XLA Ops:
  0.6 2.4 %prepare_blocks.1.after = bf16[32,200,128]{2,1,0:T(8,128)(2,1)} custom-call(bf16[32,192,128]{2,1,0:T(8,128)(2,1)} %bitcast.11, s32[8,32]{1,0:T(8,128)} %bitcast.12, s32[8,32]{1,0:T(8,128)} %bitcast.13, s32[8,32]{1,0:T(8,128)} %bitcast.14, s32[1,32]{1,0:T(1,128)} %bitcast.15), custom_call_target="tpu_custom_call" | custom-call | tf_op jit(solution)/shard_map/prepare_blocks/pallas_call | solution.py:612
  3.0 6.4 %all-to-all-start = ((bf16[32,200,128]{2,1,0:T(8,128)(2,1)}), bf16[32,200,128]{2,1,0:T(8,128)(2,1)S(1)}, u32[]{:S(2)}, u32[]{:S(2)}) async-start(bf16[32,200,128]{2,1,0:T(8,128)(2,1)} %prepare_blocks.1.after), calls=%async_computation | async-start | bytes 3276800 | tf_op jit(solution)/shard_map/all_to_all | solution.py:631
  9.4 0.1 stack.15
  9.5 0.1 broadcast_in_dim.15.par_ref.refs_0_
  9.6 1.5 %copy-done.11 = f32[240,16,128]{2,1,0:T(8,128)S(1)} copy-done((f32[240,16,128]{2,1,0:T(8,128)S(1)}, f32[240,16,128]{2,1,0:T(8,128)}, u32[]{:S(2)}) %copy-start.11) | copy-done | bytes 1966104
  11.2 1.6 %turn_control.1 = (f32[16,240,128]{2,1,0:T(8,128)S(1)}, f32[240,128]{1,0:T(8,128)S(1)}, f32[240,128]{1,0:T(8,128)S(1)}) custom-call(s32[8,128]{1,0:T(8,128)S(1)} %broadcast_in_dim.15.par_ref.refs_0_, bf16[32,200,128]{2,1,0:T(8,128)(2,1)} %prepare_blocks.1.after, f32[240,16,128]{2,1,0:T(8,128)S(1)} %copy-done.11), custom_call_target="tpu_custom_call" | custom-call | tf_op jit(solution)/shard_map/turn_control/pallas_call | solution.py:632
  12.8 0.1 control_even.1
  12.8 0.0 copy-start.2
  12.8 0.0 copy-start.4
  12.8 0.0 copy-start.6
  12.9 0.1 collective-permute-start.4
  13.0 0.1 control_odd.1
  13.1 4.2 %collective-permute-start = (f16[4,240,128]{2,1,0:T(8,128)(2,1)S(1)}, f16[4,240,128]{2,1,0:T(8,128)(2,1)S(1)}, u32[]{:S(2)}, u32[]{:S(2)}) collective-permute-start(f16[4,240,128]{2,1,0:T(8,128)(2,1)S(1)} %convert_element_type.24), channel_id=1, source_target_pairs={{4,8},{8,4},{12,16},{16,12},{20,24},{24,20},{5,9},{9,5},{13,17},{1... | collective-permute-start | bytes 737288 | tf_op jit(solution)/shard_map/ppermute | solution.py:605
  17.3 3.9 %collective-permute-start.2 = (f32[240,128]{1,0:T(8,128)S(1)}, f32[240,128]{1,0:T(8,128)S(1)}, u32[]{:S(2)}, u32[]{:S(2)}) collective-permute-start(f32[240,128]{1,0:T(8,128)S(1)} %get-tuple-element.26), channel_id=1, source_target_pairs={{1,2},{2,1},{5,6},{6,5},{9,10},{10,9},{13,14},{14,13},{17,18},{18,... | collective-permute-start | bytes 368648 | tf_op jit(solution)/shard_map/ppermute | solution.py:535
  21.3 0.1 collective-permute-start.1
  21.4 2.3 %control_local.1.after.local_ref = f32[16,240,128]{2,1,0:T(8,128)S(1)} custom-call(f32[240,128]{1,0:T(8,128)S(1)} %get-tuple-element.22.refs_1_.after, f32[16,240,128]{2,1,0:T(8,128)S(1)} %get-tuple-element.23.refs_3_.field_ref, bf16[240,240]{1,0:T(8,128)(2,1)S(1)} %copy-done.4, bf16[240,240]{1,0:T(8,128)(2,1)S(1)} %copy-done.2, bf16[256,256]{1,0:T(8,128)(2,1)S(1)} %copy-done.6), custom_call_target="tpu_custom_call" | custom-call | tf_op jit(solution)/shard_map/control_local/pallas_call | solution.py:596
  23.7 0.0 copy-start.19
  23.7 0.0 copy-start.20
  23.7 0.0 copy-start.8
  23.7 0.0 copy-start.9
  23.7 2.9 %collective-permute-done.2.strip_o = f32[240,128]{1,0:T(8,128)S(1)} collective-permute-done((f32[240,128]{1,0:T(8,128)S(1)}, f32[240,128]{1,0:T(8,128)S(1)}, u32[]{:S(2)}, u32[]{:S(2)}) %collective-permute-start.2) | collective-permute-done | bytes 122912 | tf_op jit(solution)/shard_map/ppermute | solution.py:535
  26.6 0.0 collective-permute-done.1.strip_e
  26.6 0.2 control_corners.1
  26.9 1.9 %collective-permute-start.3 = (f32[64,128]{1,0:T(8,128)S(1)}, f32[64,128]{1,0:T(8,128)S(1)}, u32[]{:S(2)}, u32[]{:S(2)}) collective-permute-start(f32[64,128]{1,0:T(8,128)S(1)} %get-tuple-element.27), channel_id=1, source_target_pairs={{4,8},{8,4},{12,16},{16,12},{20,24},{24,20},{5,9},{9,5},{13,17},{1... | collective-permute-start | bytes 98312 | tf_op jit(solution)/shard_map/ppermute | solution.py:535
  28.8 0.1 collective-permute-start.5
  28.9 0.1 maximum_bitcast_fusion.refs_2_
  29.0 0.0 copy-start.17
  29.0 0.0 copy-start.18
  29.0 1.1 %control_strips.1.local_ref = f32[16,240,128]{2,1,0:T(8,128)S(1)} custom-call(s32[8,128]{1,0:T(8,128)S(1)} %broadcast_in_dim.15.par_ref.refs_0_, f32[16,240,128]{2,1,0:T(8,128)S(1)} %control_local.1.after.local_ref, f32[240,128]{1,0:T(8,128)S(1)} %collective-permute-done.1.strip_e, f32[240,128]{1,0:T(8,128)S(1)} %collective-permute-done.2.strip_o, ...), custom_call_target="tpu_custom_call" | custom-call | tf_op jit(solution)/shard_map/control_strips/pallas_call | solution.py:640
  30.1 0.0 collective-permute-done.4
  30.2 6.8 %collective-permute-done.5.corner_ref = f32[64,128]{1,0:T(8,128)S(1)} collective-permute-done((f32[64,128]{1,0:T(8,128)S(1)}, f32[64,128]{1,0:T(8,128)S(1)}, u32[]{:S(2)}, u32[]{:S(2)}) %collective-permute-start.5) | collective-permute-done | bytes 32800 | tf_op jit(solution)/shard_map/ppermute | solution.py:534
  37.1 3.3 %flux_field.1 = (f32[16,240,128]{2,1,0:T(8,128)S(1)}, f32[16,240,128]{2,1,0:T(8,128)S(1)}) custom-call(s32[8,128]{1,0:T(8,128)S(1)} %broadcast_in_dim.15.par_ref.refs_0_, f32[16,240,128]{2,1,0:T(8,128)S(1)} %control_strips.1.local_ref, bf16[240,16,128]{2,1,0:T(8,128)(2,1)S(1)} %copy-done.17, bf16[240,16,128]{2,1,0:T(8,128)(2,1)S(1)} %copy-done.18, ...), custom_call_target="tpu_custom_call" | custom-call | tf_op jit(solution)/shard_map/flux_field/pallas_call | solution.py:643
  40.4 1.3 %copy-done = f32[16,240,128]{2,1,0:T(8,128)} copy-done((f32[16,240,128]{2,1,0:T(8,128)}, f32[16,240,128]{2,1,0:T(8,128)S(1)}, u32[]{:S(2)}) %copy-start) | copy-done | bytes 1966104
  41.7 1.3 %copy-done.12 = f32[16,240,128]{2,1,0:T(8,128)} copy-done((f32[16,240,128]{2,1,0:T(8,128)}, f32[16,240,128]{2,1,0:T(8,128)S(1)}, u32[]{:S(2)}) %copy-start.12) | copy-done | bytes 1966104
  42.9 0.0 collective-permute-done
  42.9 4.6 %all-to-all-done.refs_1_.refs_3_ = bf16[32,200,128]{2,1,0:T(8,128)(2,1)S(1)} async-done(((bf16[32,200,128]{2,1,0:T(8,128)(2,1)}), bf16[32,200,128]{2,1,0:T(8,128)(2,1)S(1)}, u32[]{:S(2)}, u32[]{:S(2)}) %all-to-all-start) | async-done | bytes 1638432 | tf_op jit(solution)/shard_map/all_to_all | solution.py:631
  47.5 0.0 collective-permute-done.3.refs_4_
  47.6 3.8 %block_values.1 = (f32[32,5,128]{2,1,0:T(8,128)S(1)}, s32[32,128]{1,0:T(8,128)S(1)}) custom-call(s32[8,128]{1,0:T(8,128)S(1)} %broadcast_in_dim.15.par_ref.refs_0_, bf16[32,200,128]{2,1,0:T(8,128)(2,1)S(1)} %all-to-all-done.refs_1_.refs_3_, f32[1,128]{1,0:T(1,128)S(1)} %maximum_bitcast_fusion.refs_2_, f32[4,240,128]{2,1,0:T(8,128)S(1)} %convert_element_type.25.refs_3_, ...), custom_call_target="tpu_custom_call" | custom-call | tf_op jit(solution)/shard_map/block_values/pallas_call | solution.py:659
  51.4 16.5 %all_to_all.10.refs_2_ = f32[32,5,128]{2,1,0:T(8,128)S(1)} all-to-all(f32[32,5,128]{2,1,0:T(8,128)S(1)} %get-tuple-element.32), channel_id=1, replica_groups=mesh['rec'=8,'tile'=4] {'rec','tile'}, dimensions={0} | all-to-all | bytes 163840 | tf_op jit(solution)/shard_map/all_to_all | solution.py:672
  67.9 2.5 %adjoint_field.1 = (f32[1,128]{1,0:T(1,128)S(1)}, f32[2,128]{1,0:T(2,128)S(1)}, f32[16,240,128]{2,1,0:T(8,128)S(1)}) custom-call(s32[8,128]{1,0:T(8,128)S(1)} %broadcast_in_dim.15.par_ref.refs_0_, s32[32,128]{1,0:T(8,128)S(1)} %get-tuple-element.31.refs_1_, f32[32,5,128]{2,1,0:T(8,128)S(1)} %all_to_all.10.refs_2_, ...), custom_call_target="tpu_custom_call" | custom-call | tf_op jit(solution)/shard_map/adjoint_field/pallas_call | solution.py:678
  70.5 0.1 gradient_even.1.after
  70.5 0.7 gradient_pack.1
  71.3 0.0 copy-start.3
  71.3 0.0 copy-start.5
  71.3 0.0 copy-start.7
  71.3 0.7 collective-permute-start.6
  72.0 1.2 %collective-permute-start.8 = (f16[4,240,128]{2,1,0:T(8,128)(2,1)S(1)}, f16[4,240,128]{2,1,0:T(8,128)(2,1)S(1)}, u32[]{:S(2)}, u32[]{:S(2)}) collective-permute-start(f16[4,240,128]{2,1,0:T(8,128)(2,1)S(1)} %convert_element_type.28), channel_id=1, source_target_pairs={{0,4},{4,0},{8,12},{12,8},{16,20},{20,16},{24,28},{28,24},{1,5},{5... | collective-permute-start | bytes 737288 | tf_op jit(solution)/shard_map/ppermute | solution.py:605
  73.2 0.0 collective-permute-done.6.refs_1_.strip_e
  73.2 0.1 gradient_odd.1.after
  73.3 2.9 %collective-permute-start.10 = (f16[4,240,128]{2,1,0:T(8,128)(2,1)S(1)}, f16[4,240,128]{2,1,0:T(8,128)(2,1)S(1)}, u32[]{:S(2)}, u32[]{:S(2)}) collective-permute-start(f16[4,240,128]{2,1,0:T(8,128)(2,1)S(1)} %convert_element_type.30), channel_id=1, source_target_pairs={{4,8},{8,4},{12,16},{16,12},{20,24},{24,20},{5,9},{9,5},{13,17},{1... | collective-permute-start | bytes 737288 | tf_op jit(solution)/shard_map/ppermute | solution.py:605
  76.2 2.6 %collective-permute-start.7 = (f32[240,128]{1,0:T(8,128)S(1)}, f32[240,128]{1,0:T(8,128)S(1)}, u32[]{:S(2)}, u32[]{:S(2)}) collective-permute-start(f32[240,128]{1,0:T(8,128)S(1)} %get-tuple-element.37), channel_id=1, source_target_pairs={{1,2},{2,1},{5,6},{6,5},{9,10},{10,9},{13,14},{14,13},{17,18},{18,... | collective-permute-start | bytes 368648 | tf_op jit(solution)/shard_map/ppermute | solution.py:535
  78.8 2.3 %gradient_local.1.after.local_ref = f32[16,240,128]{2,1,0:T(8,128)S(1)} custom-call(f32[4,240,128]{2,1,0:T(8,128)S(1)} %gradient_odd.1.after, f32[16,240,128]{2,1,0:T(8,128)S(1)} %get-tuple-element.35.refs_3_.field_ref, bf16[240,240]{1,0:T(8,128)(2,1)S(1)} %copy-done.5, bf16[240,240]{1,0:T(8,128)(2,1)S(1)} %copy-done.3, bf16[256,256]{1,0:T(8,128)(2,1)S(1)} %copy-done.7), custom_call_target="tpu_custom_call" | custom-call | tf_op jit(solution)/shard_map/gradient_local/pallas_call | solution.py:596
  81.1 0.0 copy-start.10
  81.1 0.0 copy-start.14
  81.1 0.0 copy-start.16
  81.2 1.5 %collective-permute-done.7.strip_o = f32[240,128]{1,0:T(8,128)S(1)} collective-permute-done((f32[240,128]{1,0:T(8,128)S(1)}, f32[240,128]{1,0:T(8,128)S(1)}, u32[]{:S(2)}, u32[]{:S(2)}) %collective-permute-start.7) | collective-permute-done | bytes 122912 | tf_op jit(solution)/shard_map/ppermute | solution.py:535
  82.7 0.2 gradient_corners.1
  82.9 0.1 collective-permute-start.9
  83.0 3.5 %collective-permute-start.11 = (f32[64,128]{1,0:T(8,128)S(1)}, f32[64,128]{1,0:T(8,128)S(1)}, u32[]{:S(2)}, u32[]{:S(2)}) collective-permute-start(f32[64,128]{1,0:T(8,128)S(1)} %get-tuple-element.39), channel_id=1, source_target_pairs={{4,8},{8,4},{12,16},{16,12},{20,24},{24,20},{5,9},{9,5},{13,17},{1... | collective-permute-start | bytes 98312 | tf_op jit(solution)/shard_map/ppermute | solution.py:535
  86.5 0.0 collective-permute-done.8
  86.5 0.0 collective-permute-done.9.corner_ref
  86.6 2.8 %gradient_sides.1.local_ref = f32[240,16,128]{2,1,0:T(8,128)S(1)} custom-call(s32[8,128]{1,0:T(8,128)S(1)} %broadcast_in_dim.15.par_ref.refs_0_, f32[16,240,128]{2,1,0:T(8,128)S(1)} %gradient_local.1.after.local_ref, f32[240,128]{1,0:T(8,128)S(1)} %collective-permute-done.6.refs_1_.strip_e, f32[240,128]{1,0:T(8,128)S(1)} %collective-permute-done.7.strip_o, ...), custom_call_target="tpu_custom_call" | custom-call | tf_op jit(solution)/shard_map/gradient_sides/pallas_call | solution.py:695
  89.4 0.0 collective-permute-done.10
  89.4 2.6 %gradient.1 = (f32[1,64]{1,0:T(1,128)}, f32[240,16,128]{2,1,0:T(8,128)}) custom-call(s32[8,128]{1,0:T(8,128)S(1)} %broadcast_in_dim.15.par_ref.refs_0_, f32[1,128]{1,0:T(1,128)S(1)} %get-tuple-element.33.model_ref, f32[240,16,128]{2,1,0:T(8,128)S(1)} %gradient_sides.1.local_ref, f32[2,128]{1,0:T(2,128)S(1)} %get-tuple-element.34.refs_1_.refs_2_.factor_ref, ...), custom_call_target="tpu_custom_call" | custom-call | tf_op jit(solution)/shard_map/gradient/pallas_call | solution.py:699
  (35 shorter events, 0.3 us)
Async XLA Ops:
  3.0 44.5 %all-to-all-start = ((bf16[32,200,128]{2,1,0:T(8,128)(2,1)}), bf16[32,200,128]{2,1,0:T(8,128)(2,1)S(1)}, u32[]{:S(2)}, u32[]{:S(2)}) async-start(bf16[32,200,128]{2,1,0:T(8,128)(2,1)} %prepare_blocks.1.after), calls=%async_computation | async-start | bytes 3276800 | tf_op jit(solution)/shard_map/all_to_all | solution.py:631
  9.6 1.5 %copy-start.11 = (f32[240,16,128]{2,1,0:T(8,128)S(1)}, f32[240,16,128]{2,1,0:T(8,128)}, u32[]{:S(2)}) copy-start(f32[240,16,128]{2,1,0:T(8,128)} %control_ref.1) | copy-start | bytes 5898244
  12.8 8.5 %copy-start.2 = (bf16[240,240]{1,0:T(8,128)(2,1)S(1)}, bf16[240,240]{1,0:T(8,128)(2,1)}, u32[]{:S(2)}) copy-start(bf16[240,240]{1,0:T(8,128)(2,1)} %constant.46.clone.time_low.refs_8_) | copy-start | bytes 345604
  12.8 8.5 %copy-start.4 = (bf16[240,240]{1,0:T(8,128)(2,1)S(1)}, bf16[240,240]{1,0:T(8,128)(2,1)}, u32[]{:S(2)}) copy-start(bf16[240,240]{1,0:T(8,128)(2,1)} %constant.45.clone.time_high.refs_7_) | copy-start | bytes 345604
  12.8 8.5 %copy-start.6 = (bf16[256,256]{1,0:T(8,128)(2,1)S(1)}, bf16[256,256]{1,0:T(8,128)(2,1)}, u32[]{:S(2)}) copy-start(bf16[256,256]{1,0:T(8,128)(2,1)} %constant.47.clone.col_both.refs_9_) | copy-start | bytes 393220
  12.9 17.3 %collective-permute-start.4 = (f16[4,240,128]{2,1,0:T(8,128)(2,1)S(1)}, f16[4,240,128]{2,1,0:T(8,128)(2,1)S(1)}, u32[]{:S(2)}, u32[]{:S(2)}) collective-permute-start(f16[4,240,128]{2,1,0:T(8,128)(2,1)S(1)} %convert_element_type.26), channel_id=1, source_target_pairs={{0,4},{4,0},{8,12},{12,8},{16,20},{20,16},{24,28},{28,24},{1,5},{5... | collective-permute-start | bytes 737288 | tf_op jit(solution)/shard_map/ppermute | solution.py:605
  13.1 29.8 %collective-permute-start = (f16[4,240,128]{2,1,0:T(8,128)(2,1)S(1)}, f16[4,240,128]{2,1,0:T(8,128)(2,1)S(1)}, u32[]{:S(2)}, u32[]{:S(2)}) collective-permute-start(f16[4,240,128]{2,1,0:T(8,128)(2,1)S(1)} %convert_element_type.24), channel_id=1, source_target_pairs={{4,8},{8,4},{12,16},{16,12},{20,24},{24,20},{5,9},{9,5},{13,17},{1... | collective-permute-start | bytes 737288 | tf_op jit(solution)/shard_map/ppermute | solution.py:605
  17.3 9.3 %collective-permute-start.2 = (f32[240,128]{1,0:T(8,128)S(1)}, f32[240,128]{1,0:T(8,128)S(1)}, u32[]{:S(2)}, u32[]{:S(2)}) collective-permute-start(f32[240,128]{1,0:T(8,128)S(1)} %get-tuple-element.26), channel_id=1, source_target_pairs={{1,2},{2,1},{5,6},{6,5},{9,10},{10,9},{13,14},{14,13},{17,18},{18,... | collective-permute-start | bytes 368648 | tf_op jit(solution)/shard_map/ppermute | solution.py:535
  21.3 5.4 %collective-permute-start.1 = (f32[240,128]{1,0:T(8,128)S(1)}, f32[240,128]{1,0:T(8,128)S(1)}, u32[]{:S(2)}, u32[]{:S(2)}) collective-permute-start(f32[240,128]{1,0:T(8,128)S(1)} %get-tuple-element.22.refs_1_.after), channel_id=1, source_target_pairs={{0,1},{1,0},{2,3},{3,2},{4,5},{5,4},{6,7},{7,6},{8,9},{9,8},{10,11... | collective-permute-start | bytes 368648 | tf_op jit(solution)/shard_map/ppermute | solution.py:534
  23.7 5.2 %copy-start.19 = (f32[64]{0:T(128)S(1)}, f32[64]{0:T(128)}, u32[]{:S(2)}) copy-start(f32[64]{0:T(128)} %param.26) | copy-start | bytes 772
  23.7 5.2 %copy-start.20 = (f32[64]{0:T(128)S(1)}, f32[64]{0:T(128)}, u32[]{:S(2)}) copy-start(f32[64]{0:T(128)} %param.25) | copy-start | bytes 772
  23.7 5.3 %copy-start.8 = (bf16[256,2048]{1,0:T(8,128)(2,1)S(1)}, bf16[256,2048]{1,0:T(8,128)(2,1)}, u32[]{:S(2)}) copy-start(bf16[256,2048]{1,0:T(8,128)(2,1)} %constant.49.clone.own_low) | copy-start | bytes 3145732
  23.7 5.2 %copy-start.9 = (bf16[256,2048]{1,0:T(8,128)(2,1)S(1)}, bf16[256,2048]{1,0:T(8,128)(2,1)}, u32[]{:S(2)}) copy-start(bf16[256,2048]{1,0:T(8,128)(2,1)} %constant.48.clone.own_high) | copy-start | bytes 3145732
  26.9 20.7 %collective-permute-start.3 = (f32[64,128]{1,0:T(8,128)S(1)}, f32[64,128]{1,0:T(8,128)S(1)}, u32[]{:S(2)}, u32[]{:S(2)}) collective-permute-start(f32[64,128]{1,0:T(8,128)S(1)} %get-tuple-element.27), channel_id=1, source_target_pairs={{4,8},{8,4},{12,16},{16,12},{20,24},{24,20},{5,9},{9,5},{13,17},{1... | collective-permute-start | bytes 98312 | tf_op jit(solution)/shard_map/ppermute | solution.py:535
  28.8 8.2 %collective-permute-start.5 = (f32[64,128]{1,0:T(8,128)S(1)}, f32[64,128]{1,0:T(8,128)S(1)}, u32[]{:S(2)}, u32[]{:S(2)}) collective-permute-start(f32[64,128]{1,0:T(8,128)S(1)} %get-tuple-element.28), channel_id=1, source_target_pairs={{0,4},{4,0},{8,12},{12,8},{16,20},{20,16},{24,28},{28,24},{1,5},{5... | collective-permute-start | bytes 98312 | tf_op jit(solution)/shard_map/ppermute | solution.py:534
  29.0 8.1 %copy-start.13 = (bf16[2,32,512]{2,1,0:T(8,128)(2,1)S(1)}, bf16[2,32,512]{2,1,0:T(8,128)(2,1)}, u32[]{:S(2)}) copy-start(bf16[2,32,512]{2,1,0:T(8,128)(2,1)} %constant.51.clone.corner_low.refs_11_) | copy-start | bytes 196612
  29.0 8.1 %copy-start.15 = (bf16[2,32,512]{2,1,0:T(8,128)(2,1)S(1)}, bf16[2,32,512]{2,1,0:T(8,128)(2,1)}, u32[]{:S(2)}) copy-start(bf16[2,32,512]{2,1,0:T(8,128)(2,1)} %constant.50.clone.corner_high.refs_10_) | copy-start | bytes 196612
  29.0 8.1 %copy-start.17 = (bf16[240,16,128]{2,1,0:T(8,128)(2,1)S(1)}, bf16[240,16,128]{2,1,0:T(8,128)(2,1)}, u32[]{:S(2)}) copy-start(bf16[240,16,128]{2,1,0:T(8,128)(2,1)} %prior_ref.1) | copy-start | bytes 2949124
  29.0 8.1 %copy-start.18 = (bf16[240,16,128]{2,1,0:T(8,128)(2,1)S(1)}, bf16[240,16,128]{2,1,0:T(8,128)(2,1)}, u32[]{:S(2)}) copy-start(bf16[240,16,128]{2,1,0:T(8,128)(2,1)} %scale_ref.1) | copy-start | bytes 2949124
  40.4 1.3 %copy-start = (f32[16,240,128]{2,1,0:T(8,128)}, f32[16,240,128]{2,1,0:T(8,128)S(1)}, u32[]{:S(2)}) copy-start(f32[16,240,128]{2,1,0:T(8,128)S(1)} %get-tuple-element.30.refs_6_.refs_4_) | copy-start | bytes 5898244
  41.7 1.3 %copy-start.12 = (f32[16,240,128]{2,1,0:T(8,128)}, f32[16,240,128]{2,1,0:T(8,128)S(1)}, u32[]{:S(2)}) copy-start(f32[16,240,128]{2,1,0:T(8,128)S(1)} %get-tuple-element.29.refs_5_) | copy-start | bytes 5898244
  47.5 20.4 %copy-start.1 = (f32[16,240,128]{2,1,0:T(8,128)S(1)}, f32[16,240,128]{2,1,0:T(8,128)}, u32[]{:S(2)}) copy-start(f32[16,240,128]{2,1,0:T(8,128)} %copy-done) | copy-start | bytes 5898244
  71.3 7.5 %copy-start.3 = (bf16[240,240]{1,0:T(8,128)(2,1)S(1)}, bf16[240,240]{1,0:T(8,128)(2,1)}, u32[]{:S(2)}) copy-start(bf16[240,240]{1,0:T(8,128)(2,1)} %constant.46.clone.time_low.refs_8_) | copy-start | bytes 345604
  71.3 7.5 %copy-start.5 = (bf16[240,240]{1,0:T(8,128)(2,1)S(1)}, bf16[240,240]{1,0:T(8,128)(2,1)}, u32[]{:S(2)}) copy-start(bf16[240,240]{1,0:T(8,128)(2,1)} %constant.45.clone.time_high.refs_7_) | copy-start | bytes 345604
  71.3 7.5 %copy-start.7 = (bf16[256,256]{1,0:T(8,128)(2,1)S(1)}, bf16[256,256]{1,0:T(8,128)(2,1)}, u32[]{:S(2)}) copy-start(bf16[256,256]{1,0:T(8,128)(2,1)} %constant.47.clone.col_both.refs_9_) | copy-start | bytes 393220
  71.3 1.9 %collective-permute-start.6 = (f32[240,128]{1,0:T(8,128)S(1)}, f32[240,128]{1,0:T(8,128)S(1)}, u32[]{:S(2)}, u32[]{:S(2)}) collective-permute-start(f32[240,128]{1,0:T(8,128)S(1)} %get-tuple-element.36), channel_id=1, source_target_pairs={{0,1},{1,0},{2,3},{3,2},{4,5},{5,4},{6,7},{7,6},{8,9},{9,8},{10,11... | collective-permute-start | bytes 368648 | tf_op jit(solution)/shard_map/ppermute | solution.py:534
  72.0 14.4 %collective-permute-start.8 = (f16[4,240,128]{2,1,0:T(8,128)(2,1)S(1)}, f16[4,240,128]{2,1,0:T(8,128)(2,1)S(1)}, u32[]{:S(2)}, u32[]{:S(2)}) collective-permute-start(f16[4,240,128]{2,1,0:T(8,128)(2,1)S(1)} %convert_element_type.28), channel_id=1, source_target_pairs={{0,4},{4,0},{8,12},{12,8},{16,20},{20,16},{24,28},{28,24},{1,5},{5... | collective-permute-start | bytes 737288 | tf_op jit(solution)/shard_map/ppermute | solution.py:605
  73.3 16.1 %collective-permute-start.10 = (f16[4,240,128]{2,1,0:T(8,128)(2,1)S(1)}, f16[4,240,128]{2,1,0:T(8,128)(2,1)S(1)}, u32[]{:S(2)}, u32[]{:S(2)}) collective-permute-start(f16[4,240,128]{2,1,0:T(8,128)(2,1)S(1)} %convert_element_type.30), channel_id=1, source_target_pairs={{4,8},{8,4},{12,16},{16,12},{20,24},{24,20},{5,9},{9,5},{13,17},{1... | collective-permute-start | bytes 737288 | tf_op jit(solution)/shard_map/ppermute | solution.py:605
  76.2 6.5 %collective-permute-start.7 = (f32[240,128]{1,0:T(8,128)S(1)}, f32[240,128]{1,0:T(8,128)S(1)}, u32[]{:S(2)}, u32[]{:S(2)}) collective-permute-start(f32[240,128]{1,0:T(8,128)S(1)} %get-tuple-element.37), channel_id=1, source_target_pairs={{1,2},{2,1},{5,6},{6,5},{9,10},{10,9},{13,14},{14,13},{17,18},{18,... | collective-permute-start | bytes 368648 | tf_op jit(solution)/shard_map/ppermute | solution.py:535
  81.1 5.4 %copy-start.10 = (bf16[256,2048]{1,0:T(8,128)(2,1)S(1)}, bf16[256,2048]{1,0:T(8,128)(2,1)}, u32[]{:S(2)}) copy-start(bf16[256,2048]{1,0:T(8,128)(2,1)} %constant.48.clone.own_high) | copy-start | bytes 3145732
  81.1 5.4 %copy-start.14 = (bf16[2,32,512]{2,1,0:T(8,128)(2,1)S(1)}, bf16[2,32,512]{2,1,0:T(8,128)(2,1)}, u32[]{:S(2)}) copy-start(bf16[2,32,512]{2,1,0:T(8,128)(2,1)} %constant.51.clone.corner_low.refs_11_) | copy-start | bytes 196612
  81.1 5.4 %copy-start.16 = (bf16[2,32,512]{2,1,0:T(8,128)(2,1)S(1)}, bf16[2,32,512]{2,1,0:T(8,128)(2,1)}, u32[]{:S(2)}) copy-start(bf16[2,32,512]{2,1,0:T(8,128)(2,1)} %constant.50.clone.corner_high.refs_10_) | copy-start | bytes 196612
  82.9 3.6 %collective-permute-start.9 = (f32[64,128]{1,0:T(8,128)S(1)}, f32[64,128]{1,0:T(8,128)S(1)}, u32[]{:S(2)}, u32[]{:S(2)}) collective-permute-start(f32[64,128]{1,0:T(8,128)S(1)} %get-tuple-element.38), channel_id=1, source_target_pairs={{0,4},{4,0},{8,12},{12,8},{16,20},{20,16},{24,28},{28,24},{1,5},{5... | collective-permute-start | bytes 98312 | tf_op jit(solution)/shard_map/ppermute | solution.py:534
  83.0 6.5 %collective-permute-start.11 = (f32[64,128]{1,0:T(8,128)S(1)}, f32[64,128]{1,0:T(8,128)S(1)}, u32[]{:S(2)}, u32[]{:S(2)}) collective-permute-start(f32[64,128]{1,0:T(8,128)S(1)} %get-tuple-element.39), channel_id=1, source_target_pairs={{4,8},{8,4},{12,16},{16,12},{20,24},{24,20},{5,9},{9,5},{13,17},{1... | collective-permute-start | bytes 98312 | tf_op jit(solution)/shard_map/ppermute | solution.py:535

commit v7 on v6

--- a/solution.py
+++ b/solution.py
@@ -60,10 +60,7 @@
         both = by_row[:, :, None] * edge[np.array(halo_of)][:, None, :]
         return two_parts(both.reshape(len(row_of), -1))
 
-    unused = [(-100, 0)] * (LANES - RAD * rows)
-    own = []
-    for side in range(2):
-        own += [(row, side * RAD + j) for row in range(rows) for j in range(RAD)] + unused
+    own = [(row, side * RAD + j) for side in range(2) for row in range(rows) for j in range(RAD)]
     corner = [], []
     for first, targets in ((rows, rows - 1 - np.arange(RAD)), (-RAD, np.arange(RAD))):
         lanes = [
@@ -92,15 +89,14 @@
     return jnp.where(flag, yes, no)
 
 
-def pack_strips(row_value, odd, rows):
+def pack_strips(row_value, rows):
     cols = row_value(0).shape[1]
     half = rows * RAD
     source = lax.broadcasted_iota(jnp.int32, (cols, 2 * half), 0)
     lane = lane_ids((cols, 2 * half))
     first = lane < half
     j = lane & (RAD - 1)
-    at_first, at_second = choose(odd, j, cols - RAD + j), choose(odd, cols - RAD + j, j)
-    wanted = jnp.where(first, at_first, at_second)
+    wanted = jnp.where(first, cols - RAD + j, j)
     lane_row = jnp.where(first, lane, lane - half) // RAD
     total = None
     for row in range(rows):
@@ -148,36 +144,44 @@
         out_ref[row] = (choose(odd, first, last) if even else choose(odd, last, first)) * factor
 
 
-def turn_kernel(par_ref, after, control_ref, field_ref, strip_e, strip_o):
+def turn_kernel(after, control_ref, field_ref, last_ref, first_ref):
     rows = control_ref.shape[1]
     for row in range(rows):
         field_ref[row] = control_ref[:, row, :]
-    write_strips(is_odd(par_ref, 1), field_ref, strip_e, strip_o)
-
-
-def strip_kernel(par_ref, after, field_ref, strip_e, strip_o):
-    write_strips(is_odd(par_ref, 1), field_ref, strip_e, strip_o)
-
-
-def write_strips(odd, field_ref, strip_e, strip_o):
-    strips = pack_strips(lambda r: field_ref[r], odd, field_ref.shape[0])
+    write_strips(field_ref, last_ref, first_ref)
+
+
+def strip_kernel(after, field_ref, last_ref, first_ref):
+    write_strips(field_ref, last_ref, first_ref)
+
+
+def write_strips(field_ref, last_ref, first_ref):
+    strips = pack_strips(lambda r: field_ref[r], field_ref.shape[0])
+    fold, half = last_ref.shape[0], LANES // 2
+    early, late = strips[0:fold], strips[fold:]
+    if late.shape[0] < fold:
+        late = jnp.concatenate([late, jnp.zeros((fold - late.shape[0], LANES), F32)], axis=0)
+    left = lane_ids(early.shape) < half
+    last_ref[...] = jnp.where(left, early, pltpu.roll(late, half, 1))
+    first_ref[...] = jnp.where(left, pltpu.roll(early, half, 1), late)
+
+
+def halo_columns(par_ref, before_ref, after_ref):
+    before, after = before_ref[...], after_ref[...]
     half = LANES // 2
-    left = lane_ids(strips.shape) < half
-    strip_e[...] = jnp.where(left, strips, 0.0)
-    strip_o[...] = jnp.where(left, pltpu.roll(strips, half, 1), 0.0)
-
-
-def far_corner_kernel(par_ref, after, strip_e, strip_o, corner_e, corner_o):
-    odd = is_odd(par_ref, 1)
-    even_swap, odd_swap = strip_e[...], strip_o[...]
-    before, after = choose(odd, even_swap, odd_swap), choose(odd, odd_swap, even_swap)
-    half = LANES // 2
-    both = jnp.where(lane_ids(before.shape) < half, before, pltpu.roll(after, half, 1))
-    fold_corners(is_odd(par_ref, 0), both, corner_e, corner_o)
+    left = lane_ids(before.shape) < half
+    early = jnp.where(left, before, pltpu.roll(after, half, 1))
+    late = jnp.where(left, pltpu.roll(before, half, 1), after)
+    outside = jnp.where(lane_ids((1, LANES)) < half, par_ref[3:4, :], par_ref[4:5, :])
+    return jnp.where(outside == 1, 0.0, jnp.concatenate([early, late], axis=0))
+
+
+def far_corner_kernel(par_ref, after, before_ref, after_ref, corner_e, corner_o):
+    fold_corners(is_odd(par_ref, 0), halo_columns(par_ref, before_ref, after_ref), corner_e, corner_o)
 
 
 def prepare_kernel(
-    foot_ref, start_ref, row_ref, slot_ref, count_ref, out_ref,
+    after, foot_ref, start_ref, row_ref, slot_ref, count_ref, out_ref,
     blocks_ref, notes_ref, start_vmem, row_vmem, slot_vmem, count_vmem, sems, *, per,
 ):
     owners, lines, _ = foot_ref.shape
@@ -257,16 +261,14 @@
             out_ref[r] = both[:, k * cols : (k + 1) * cols]
 
 
-def strip_halo(par_ref, strip_e, strip_o, time_high, time_low):
-    odd = is_odd(par_ref, 1)
-    even_swap, odd_swap = strip_e[...], strip_o[...]
-    halo = jnp.concatenate([choose(odd, even_swap, odd_swap), choose(odd, odd_swap, even_swap)], axis=1)
+def strip_halo(par_ref, before_ref, after_ref, time_high, time_low):
+    halo = halo_columns(par_ref, before_ref, after_ref)[0 : time_high.shape[0]]
     return split(time_sums(halo, time_high[...], time_low[...]))
 
 
-def strips_kernel(par_ref, local_ref, strip_e, strip_o, time_high, time_low, own_high, own_low, out_ref):
+def strips_kernel(par_ref, local_ref, before_ref, after_ref, time_high, time_low, own_high, own_low, out_ref):
     rows, hours, cols = local_ref.shape
-    halo = strip_halo(par_ref, strip_e, strip_o, time_high, time_low)
+    halo = strip_halo(par_ref, before_ref, after_ref, time_high, time_low)
     for row in range(0, rows, 2):
         both = halo_sums(halo, own_high, own_low, row * cols, 2 * cols)
         for k, r in enumerate((row, row + 1)):
@@ -274,7 +276,7 @@
 
 
 def sides_kernel(
-    par_ref, local_ref, strip_e, strip_o, factor_ref, got_ref, corner_ref,
+    par_ref, local_ref, before_ref, after_ref, factor_ref, got_ref, corner_ref,
     time_high, time_low, col_both, own_high, own_low, corner_high, corner_low, out_ref, halo,
 ):
     rows, hours, cols = local_ref.shape
@@ -283,7 +285,7 @@
     consts = (time_high, time_low, col_both)
     parts = edge_parts(halo, corner_ref[...], corner_high.at[odd], corner_low.at[odd], consts)
     at_first = jnp.where(is_odd(par_ref, 0), 1.0, 0.0)
-    strips = strip_halo(par_ref, strip_e, strip_o, time_high, time_low)
+    strips = strip_halo(par_ref, before_ref, after_ref, time_high, time_low)
     for row in range(0, rows, 2):
         both = halo_sums(strips, own_high, own_low, row * cols, 2 * cols)
         for k, r in enumerate((row, row + 1)):
@@ -580,17 +582,23 @@
     groups = per * n_rec // LANES
     shift = (hours - 1).bit_length()
     rec, tile = lax.axis_index("rec"), lax.axis_index("tile")
-    par = jnp.stack([rec % 2, tile % 2, rec] + [rec * 0] * (SUB - 3)).astype(jnp.int32)
+    flags = [rec % 2, rec * 0, rec, tile == 0, tile == n_tile - 1] + [rec * 0] * (SUB - 5)
+    par = jnp.stack([flag.astype(jnp.int32) for flag in flags])
     par = jnp.broadcast_to(par[:, None], (SUB, LANES))
     base, own_parts, corner_parts = constants(hours, rows, cols)
     base = [jnp.asarray(c) for c in base]
     own_parts = [jnp.asarray(c) for c in own_parts]
     corner_parts = [jnp.asarray(c) for c in corner_parts]
-    strip = array(hours, LANES)
+    strip = array(-(-hours // (2 * SUB)) * SUB, LANES)
     corner = array(-(-hours // (4 * SUB)) * SUB, LANES)
     block = array(RAD, hours, cols)
     field_shape = array(rows, hours, cols)
     row_scratch = pltpu.VMEM((RAD, hours, cols), F32)
+
+    def pass_strips(last, first):
+        onward = [(i, (i + 1) % n_tile) for i in range(n_tile)]
+        back = [(j, i) for i, j in onward]
+        return lax.ppermute(last, "tile", onward), lax.ppermute(first, "tile", back)
 
     def swaps(after, field, got_strips, name):
         local = call(local_kernel, field_shape, [VM] * 5, [], name + "_local")(after, field, *base)
@@ -612,7 +620,7 @@
     sent = call(
         prepare,
         jax.ShapeDtypeStruct((devices, lines, cols), BF16),
-        [HB] * 5,
+        [VM] + [HB] * 5,
         [
             pltpu.VMEM((devices, slots * heights, cols), BF16),
             pltpu.VMEM((devices, SUB, LANES), BF16),
@@ -621,7 +629,7 @@
         ],
         "prepare_blocks",
         out_specs=HB,
-    )(*[
+    )(par, *[
         far(x)
         for x in (
             footprint.reshape(devices, slots * heights, cols),
@@ -630,12 +638,12 @@
     ])
     foot = lax.all_to_all(sent, AXES, split_axis=0, concat_axis=0, tiled=True)
     field, *strips = call(
-        turn_kernel, [field_shape, strip, strip], [VM, HB, VM], [], "turn_control"
-    )(par, sent, control)
+        turn_kernel, [field_shape, strip, strip], [HB, VM], [], "turn_control"
+    )(sent, control)
     factor = jnp.full((2, LANES), CONTROL_FACTOR, F32)
     _, got_even = swap_rows(True, strips[0], factor, field, "control_even")
     _, got_odd = swap_rows(False, strips[0], factor, field, "control_odd")
-    got_strips = swap("tile", *strips)
+    got_strips = pass_strips(*strips)
     local, got_corners = swaps(strips[0], field, got_strips, "control")
     local = call(strips_kernel, field_shape, [VM] * 8, [], "control_strips")(
         par, local, *got_strips, *base[:2], *own_parts
@@ -688,9 +696,9 @@
         "adjoint_field",
     )(par, table, everyone, foot, scale)
     sent_even, got_even = swap_rows(True, factor, factor, field, "gradient_even")
-    strips = call(strip_kernel, [strip, strip], [VM] * 3, [], "gradient_pack")(par, sent_even, field)
-    got_strips = swap("tile", *strips)
-    sent_odd, got_odd = swap_rows(False, got_strips[0], factor, field, "gradient_odd")
+    strips = call(strip_kernel, [strip, strip], [VM] * 2, [], "gradient_pack")(sent_even, field)
+    got_strips = pass_strips(*strips)
+    sent_odd, got_odd = swap_rows(False, strips[0], factor, field, "gradient_odd")
     local, got_corners = swaps(sent_odd, field, got_strips, "gradient")
     local = call(sides_kernel, array(hours, rows, cols), [VM] * 14, [row_scratch], "gradient_sides")(
         par, local, *got_strips, factor, got_even.astype(F32), got_corners[0], *base, *own_parts, *corner_parts

time: 92.7 us -> 91.8 us (level)
  starting transfers between devices: 27.6 us -> 25.6 us
    ppermute x4, waiting for transfers between devices: 0.01 us -> 8.33 us  [swap_rows(): lax.ppermute(sent.astype(F16), 'rec', swap_pairs(n_rec, not even))]
    ppermute x4 -> x2, waiting for transfers between devices: 6.84 us -> 1.31 us  [swap(): lax.ppermute(even, axis, swap_pairs(count, False))]
    ppermute x4 -> x2, starting transfers between devices: 11.9 us -> 6.97 us  [swap(): lax.ppermute(odd, axis, swap_pairs(count, True))]
    ppermute x4 -> x2, waiting for transfers between devices: 4.4 us -> 0.01 us  [swap(): lax.ppermute(odd, axis, swap_pairs(count, True))]
    ppermute x0 -> x4, starting transfers between devices: none -> 4.08 us  [the longest x2 2.27 us: pass_strips(): lax.ppermute(first, 'tile', back)]
    all_to_all x1, waiting for transfers between devices: 4.56 us -> 5.89 us  [per_device(): foot = lax.all_to_all(sent, AXES, split_axis=0, concat_axis=0, tiled=True)]
    unnamed x42 -> x40, local copies, waits for them, and re-layouts: 4.23 us -> 4.23 us
  transfers between devices with their start and end apart: 13 -> 13, of which waited for: 4 -> 7; matrix products, arithmetic and copies ran while one was open for 1% -> 0% of each run, Pallas kernels for 15% -> 16%
where the time goes in v7:
time: 91.8 us; the launch traced here: 90.4 us
  Pallas kernels  26.3 us (29%)
  starting transfers between devices  25.6 us (28%)
  blocking collectives  16.5 us (18%)
  waiting for transfers between devices  16 us (17%)
  local copies, waits for them, and re-layouts  4.39 us (5%)
  between operations  1.25 us (1%)
    all_to_all x1, blocking collectives, per_device(): lax.all_to_all(partial, AXES, split_axis=0, concat_axis=0, tiled=True)  16.5 us
    ppermute x4, waiting for transfers between devices, swap_rows(): lax.ppermute(sent.astype(F16), 'rec', swap_pairs(n_rec, not even))  8.33 us
    ppermute x4, starting transfers between devices, swap_rows(): lax.ppermute(sent.astype(F16), 'rec', swap_pairs(n_rec, not even))  8 us
    ppermute x2, starting transfers between devices, swap(): lax.ppermute(odd, axis, swap_pairs(count, True))  6.97 us
    all_to_all x1, starting transfers between devices, per_device(): foot = lax.all_to_all(sent, AXES, split_axis=0, concat_axis=0, tiled=True)  6.42 us
    all_to_all x1, waiting for transfers between devices, per_device(): foot = lax.all_to_all(sent, AXES, split_axis=0, concat_axis=0, tiled=True)  5.89 us
    pallas_call x2, Pallas kernels, swaps(): call(local_kernel, field_shape, [VM] * 5, [], name + '_local')  4.62 us
    unnamed x40, local copies, waits for them, and re-layouts  4.23 us
  transfers between devices with their start and end apart: 13, of which 7 were waited for; matrix products, arithmetic and copies ran while one was open for 0% of the time, Pallas kernels for 16%

profile of v7, /device:TPU:5, one launch (start us, length us, event | category | flops | bytes accessed | tf_op | source)
XLA Modules:
  0.0 90.4 jit_solution(13937917336569413971)
XLA Ops:
  0.7 0.1 stack.27
  0.7 0.1 broadcast_in_dim.15.refs_0_.par_ref
  0.8 2.3 %prepare_blocks.1.after = bf16[32,200,128]{2,1,0:T(8,128)(2,1)} custom-call(s32[8,128]{1,0:T(8,128)S(1)} %broadcast_in_dim.15.refs_0_.par_ref, bf16[32,192,128]{2,1,0:T(8,128)(2,1)} %bitcast.12, s32[8,32]{1,0:T(8,128)} %bitcast.13, s32[8,32]{1,0:T(8,128)} %bitcast.14, s32[8,32]{1,0:T(8,128)} %bitcast.15, s32[1,32]{1,0:T(1,128)} %bitcast.16), custom_call_target="tpu_custom_call" | custom-call | tf_op jit(solution)/shard_map/prepare_blocks/pallas_call | solution.py:620
  3.2 6.4 %all-to-all-start = ((bf16[32,200,128]{2,1,0:T(8,128)(2,1)}), bf16[32,200,128]{2,1,0:T(8,128)(2,1)S(1)}, u32[]{:S(2)}, u32[]{:S(2)}) async-start(bf16[32,200,128]{2,1,0:T(8,128)(2,1)} %prepare_blocks.1.after), calls=%async_computation | async-start | bytes 3276800 | tf_op jit(solution)/shard_map/all_to_all | solution.py:639
  9.6 0.0 copy-start.10
  9.6 1.5 %copy-done.10 = f32[240,16,128]{2,1,0:T(8,128)S(1)} copy-done((f32[240,16,128]{2,1,0:T(8,128)S(1)}, f32[240,16,128]{2,1,0:T(8,128)}, u32[]{:S(2)}) %copy-start.10) | copy-done | bytes 1966104
  11.1 1.5 %turn_control.1 = (f32[16,240,128]{2,1,0:T(8,128)S(1)}, f32[120,128]{1,0:T(8,128)S(1)}, f32[120,128]{1,0:T(8,128)S(1)}) custom-call(bf16[32,200,128]{2,1,0:T(8,128)(2,1)} %prepare_blocks.1.after, f32[240,16,128]{2,1,0:T(8,128)S(1)} %copy-done.10), custom_call_target="tpu_custom_call" | custom-call | tf_op jit(solution)/shard_map/turn_control/pallas_call | solution.py:640
  12.6 0.1 control_even.1
  12.7 0.0 copy-start.2
  12.7 0.0 copy-start.4
  12.7 0.0 copy-start.6
  12.7 0.1 collective-permute-start.4
  12.9 0.1 control_odd.1
  13.0 4.2 %collective-permute-start = (f16[4,240,128]{2,1,0:T(8,128)(2,1)S(1)}, f16[4,240,128]{2,1,0:T(8,128)(2,1)S(1)}, u32[]{:S(2)}, u32[]{:S(2)}) collective-permute-start(f16[4,240,128]{2,1,0:T(8,128)(2,1)S(1)} %convert_element_type.26), channel_id=1, source_target_pairs={{4,8},{8,4},{12,16},{16,12},{20,24},{24,20},{5,9},{9,5},{13,17},{1... | collective-permute-start | bytes 737288 | tf_op jit(solution)/shard_map/ppermute | solution.py:613
  17.2 1.0 %collective-permute-start.2 = (f32[120,128]{1,0:T(8,128)S(1)}, f32[120,128]{1,0:T(8,128)S(1)}, u32[]{:S(2)}, u32[]{:S(2)}) collective-permute-start(f32[120,128]{1,0:T(8,128)S(1)} %get-tuple-element.26), channel_id=1, source_target_pairs={{1,0},{2,1},{3,2},{0,3},{5,4},{6,5},{7,6},{4,7},{9,8},{10,9},{11,1... | collective-permute-start | bytes 184328 | tf_op jit(solution)/shard_map/ppermute | solution.py:601
  18.2 1.1 %collective-permute-start.1 = (f32[120,128]{1,0:T(8,128)S(1)}, f32[120,128]{1,0:T(8,128)S(1)}, u32[]{:S(2)}, u32[]{:S(2)}) collective-permute-start(f32[120,128]{1,0:T(8,128)S(1)} %get-tuple-element.22.refs_1_.after), channel_id=1, source_target_pairs={{0,1},{1,2},{2,3},{3,0},{4,5},{5,6},{6,7},{7,4},{8,9},{9,10},{10,1... | collective-permute-start | bytes 184328 | tf_op jit(solution)/shard_map/ppermute | solution.py:601
  19.3 2.3 %control_local.1.after.local_ref = f32[16,240,128]{2,1,0:T(8,128)S(1)} custom-call(f32[120,128]{1,0:T(8,128)S(1)} %get-tuple-element.22.refs_1_.after, f32[16,240,128]{2,1,0:T(8,128)S(1)} %get-tuple-element.23.refs_3_.field_ref, bf16[240,240]{1,0:T(8,128)(2,1)S(1)} %copy-done.4, bf16[240,240]{1,0:T(8,128)(2,1)S(1)} %copy-done.2, bf16[256,256]{1,0:T(8,128)(2,1)S(1)} %copy-done.6), custom_call_target="tpu_custom_call" | custom-call | tf_op jit(solution)/shard_map/control_local/pallas_call | solution.py:604
  21.6 0.0 copy-start.18
  21.6 0.0 copy-start.19
  21.7 0.0 copy-start.8
  21.7 0.0 copy-start.9
  21.7 0.3 collective-permute-done.2.after_ref
  21.9 0.0 collective-permute-done.1.before_ref
  22.0 0.2 control_corners.1
  22.2 2.8 %collective-permute-start.3 = (f32[64,128]{1,0:T(8,128)S(1)}, f32[64,128]{1,0:T(8,128)S(1)}, u32[]{:S(2)}, u32[]{:S(2)}) collective-permute-start(f32[64,128]{1,0:T(8,128)S(1)} %get-tuple-element.27), channel_id=1, source_target_pairs={{4,8},{8,4},{12,16},{16,12},{20,24},{24,20},{5,9},{9,5},{13,17},{1... | collective-permute-start | bytes 98312 | tf_op jit(solution)/shard_map/ppermute | solution.py:537
  25.0 0.1 collective-permute-start.5
  25.1 0.1 maximum_bitcast_fusion.refs_2_
  25.2 0.0 copy-start.16
  25.2 0.0 copy-start.17
  25.2 1.4 %control_strips.1.local_ref = f32[16,240,128]{2,1,0:T(8,128)S(1)} custom-call(s32[8,128]{1,0:T(8,128)S(1)} %broadcast_in_dim.15.refs_0_.par_ref, f32[16,240,128]{2,1,0:T(8,128)S(1)} %control_local.1.after.local_ref, f32[120,128]{1,0:T(8,128)S(1)} %collective-permute-done.1.before_ref, f32[120,128]{1,0:T(8,128)S(1)} %collective-permute-done.2.after_ref, ...), custom_call_target="tpu_custom_call" | custom-call | tf_op jit(solution)/shard_map/control_strips/pallas_call | solution.py:648
  26.6 2.1 %collective-permute-done.4 = f16[4,240,128]{2,1,0:T(8,128)(2,1)S(1)} collective-permute-done((f16[4,240,128]{2,1,0:T(8,128)(2,1)S(1)}, f16[4,240,128]{2,1,0:T(8,128)(2,1)S(1)}, u32[]{:S(2)}, u32[]{:S(2)}) %collective-permute-start.4) | collective-permute-done | bytes 245792 | tf_op jit(solution)/shard_map/ppermute | solution.py:613
  28.8 0.9 collective-permute-done.5.corner_ref
  29.7 3.3 %flux_field.1 = (f32[16,240,128]{2,1,0:T(8,128)S(1)}, f32[16,240,128]{2,1,0:T(8,128)S(1)}) custom-call(s32[8,128]{1,0:T(8,128)S(1)} %broadcast_in_dim.15.refs_0_.par_ref, f32[16,240,128]{2,1,0:T(8,128)S(1)} %control_strips.1.local_ref, bf16[240,16,128]{2,1,0:T(8,128)(2,1)S(1)} %copy-done.16, bf16[240,16,128]{2,1,0:T(8,128)(2,1)S(1)} %copy-done.17, ...), custom_call_target="tpu_custom_call" | custom-call | tf_op jit(solution)/shard_map/flux_field/pallas_call | solution.py:651
  33.0 1.3 %copy-done = f32[16,240,128]{2,1,0:T(8,128)} copy-done((f32[16,240,128]{2,1,0:T(8,128)}, f32[16,240,128]{2,1,0:T(8,128)S(1)}, u32[]{:S(2)}) %copy-start) | copy-done | bytes 1966104
  34.3 1.3 %copy-done.11 = f32[16,240,128]{2,1,0:T(8,128)} copy-done((f32[16,240,128]{2,1,0:T(8,128)}, f32[16,240,128]{2,1,0:T(8,128)S(1)}, u32[]{:S(2)}) %copy-start.11) | copy-done | bytes 1966104
  35.6 6.2 %collective-permute-done = f16[4,240,128]{2,1,0:T(8,128)(2,1)S(1)} collective-permute-done((f16[4,240,128]{2,1,0:T(8,128)(2,1)S(1)}, f16[4,240,128]{2,1,0:T(8,128)(2,1)S(1)}, u32[]{:S(2)}, u32[]{:S(2)}) %collective-permute-start) | collective-permute-done | bytes 245792 | tf_op jit(solution)/shard_map/ppermute | solution.py:613
  41.8 5.9 %all-to-all-done.refs_1_.refs_3_ = bf16[32,200,128]{2,1,0:T(8,128)(2,1)S(1)} async-done(((bf16[32,200,128]{2,1,0:T(8,128)(2,1)}), bf16[32,200,128]{2,1,0:T(8,128)(2,1)S(1)}, u32[]{:S(2)}, u32[]{:S(2)}) %all-to-all-start) | async-done | bytes 1638432 | tf_op jit(solution)/shard_map/all_to_all | solution.py:639
  47.7 0.0 collective-permute-done.3.refs_4_
  47.7 3.8 %block_values.1 = (f32[32,5,128]{2,1,0:T(8,128)S(1)}, s32[32,128]{1,0:T(8,128)S(1)}) custom-call(s32[8,128]{1,0:T(8,128)S(1)} %broadcast_in_dim.15.refs_0_.par_ref, bf16[32,200,128]{2,1,0:T(8,128)(2,1)S(1)} %all-to-all-done.refs_1_.refs_3_, f32[1,128]{1,0:T(1,128)S(1)} %maximum_bitcast_fusion.refs_2_, f32[4,240,128]{2,1,0:T(8,128)S(1)} %convert_element_type.27.refs_3_, ...), custom_call_target="tpu_custom_call" | custom-call | tf_op jit(solution)/shard_map/block_values/pallas_call | solution.py:667
  51.6 16.5 %all_to_all.10.refs_2_ = f32[32,5,128]{2,1,0:T(8,128)S(1)} all-to-all(f32[32,5,128]{2,1,0:T(8,128)S(1)} %get-tuple-element.32), channel_id=1, replica_groups=mesh['rec'=8,'tile'=4] {'rec','tile'}, dimensions={0} | all-to-all | bytes 163840 | tf_op jit(solution)/shard_map/all_to_all | solution.py:680
  68.1 2.5 %adjoint_field.1 = (f32[1,128]{1,0:T(1,128)S(1)}, f32[2,128]{1,0:T(2,128)S(1)}, f32[16,240,128]{2,1,0:T(8,128)S(1)}) custom-call(s32[8,128]{1,0:T(8,128)S(1)} %broadcast_in_dim.15.refs_0_.par_ref, s32[32,128]{1,0:T(8,128)S(1)} %get-tuple-element.31.refs_1_, f32[32,5,128]{2,1,0:T(8,128)S(1)} %all_to_all.10.refs_2_, ...), custom_call_target="tpu_custom_call" | custom-call | tf_op jit(solution)/shard_map/adjoint_field/pallas_call | solution.py:686
  70.6 0.1 gradient_even.1.after
  70.7 0.7 gradient_pack.1
  71.4 0.0 copy-start.3
  71.4 0.0 copy-start.5
  71.5 0.0 copy-start.7
  71.5 1.5 %collective-permute-start.8 = (f16[4,240,128]{2,1,0:T(8,128)(2,1)S(1)}, f16[4,240,128]{2,1,0:T(8,128)(2,1)S(1)}, u32[]{:S(2)}, u32[]{:S(2)}) collective-permute-start(f16[4,240,128]{2,1,0:T(8,128)(2,1)S(1)} %convert_element_type.30), channel_id=1, source_target_pairs={{0,4},{4,0},{8,12},{12,8},{16,20},{20,16},{24,28},{28,24},{1,5},{5... | collective-permute-start | bytes 737288 | tf_op jit(solution)/shard_map/ppermute | solution.py:613
  73.0 0.1 gradient_odd.1.after
  73.1 2.2 %collective-permute-start.10 = (f16[4,240,128]{2,1,0:T(8,128)(2,1)S(1)}, f16[4,240,128]{2,1,0:T(8,128)(2,1)S(1)}, u32[]{:S(2)}, u32[]{:S(2)}) collective-permute-start(f16[4,240,128]{2,1,0:T(8,128)(2,1)S(1)} %convert_element_type.32), channel_id=1, source_target_pairs={{4,8},{8,4},{12,16},{16,12},{20,24},{24,20},{5,9},{9,5},{13,17},{1... | collective-permute-start | bytes 737288 | tf_op jit(solution)/shard_map/ppermute | solution.py:613
  75.3 1.3 %collective-permute-start.7 = (f32[120,128]{1,0:T(8,128)S(1)}, f32[120,128]{1,0:T(8,128)S(1)}, u32[]{:S(2)}, u32[]{:S(2)}) collective-permute-start(f32[120,128]{1,0:T(8,128)S(1)} %get-tuple-element.37), channel_id=1, source_target_pairs={{1,0},{2,1},{3,2},{0,3},{5,4},{6,5},{7,6},{4,7},{9,8},{10,9},{11,1... | collective-permute-start | bytes 184328 | tf_op jit(solution)/shard_map/ppermute | solution.py:601
  76.6 0.7 collective-permute-start.6
  77.3 2.3 %gradient_local.1.after.local_ref = f32[16,240,128]{2,1,0:T(8,128)S(1)} custom-call(f32[4,240,128]{2,1,0:T(8,128)S(1)} %gradient_odd.1.after, f32[16,240,128]{2,1,0:T(8,128)S(1)} %get-tuple-element.35.refs_3_.field_ref, bf16[240,240]{1,0:T(8,128)(2,1)S(1)} %copy-done.5, bf16[240,240]{1,0:T(8,128)(2,1)S(1)} %copy-done.3, bf16[256,256]{1,0:T(8,128)(2,1)S(1)} %copy-done.7), custom_call_target="tpu_custom_call" | custom-call | tf_op jit(solution)/shard_map/gradient_local/pallas_call | solution.py:604
  79.6 0.0 copy-start.13
  79.6 0.0 copy-start.15
  79.6 0.2 collective-permute-done.7.after_ref
  79.7 0.2 gradient_corners.1
  80.0 0.1 collective-permute-start.9
  80.1 4.1 %collective-permute-start.11 = (f32[64,128]{1,0:T(8,128)S(1)}, f32[64,128]{1,0:T(8,128)S(1)}, u32[]{:S(2)}, u32[]{:S(2)}) collective-permute-start(f32[64,128]{1,0:T(8,128)S(1)} %get-tuple-element.39), channel_id=1, source_target_pairs={{4,8},{8,4},{12,16},{16,12},{20,24},{24,20},{5,9},{9,5},{13,17},{1... | collective-permute-start | bytes 98312 | tf_op jit(solution)/shard_map/ppermute | solution.py:537
  84.2 0.0 collective-permute-done.8
  84.3 0.0 collective-permute-done.10
  84.3 0.4 collective-permute-done.9.corner_ref
  84.7 2.9 %gradient_sides.1.local_ref = f32[240,16,128]{2,1,0:T(8,128)S(1)} custom-call(s32[8,128]{1,0:T(8,128)S(1)} %broadcast_in_dim.15.refs_0_.par_ref, f32[16,240,128]{2,1,0:T(8,128)S(1)} %gradient_local.1.after.local_ref, f32[120,128]{1,0:T(8,128)S(1)} %collective-permute-done.6.before_ref, f32[120,128]{1,0:T(8,128)S(1)} %collective-permute-done.7.after_ref, ...), custom_call_target="tpu_custom_call" | custom-call | tf_op jit(solution)/shard_map/gradient_sides/pallas_call | solution.py:703
  87.6 0.0 collective-permute-done.11.corner_ref
  87.6 2.6 %gradient.1 = (f32[1,64]{1,0:T(1,128)}, f32[240,16,128]{2,1,0:T(8,128)}) custom-call(s32[8,128]{1,0:T(8,128)S(1)} %broadcast_in_dim.15.refs_0_.par_ref, f32[1,128]{1,0:T(1,128)S(1)} %get-tuple-element.33.model_ref, f32[240,16,128]{2,1,0:T(8,128)S(1)} %gradient_sides.1.local_ref, f32[2,128]{1,0:T(2,128)S(1)} %get-tuple-element.34.refs_1_.refs_2_.factor_ref, ...), custom_call_target="tpu_custom_call" | custom-call | tf_op jit(solution)/shard_map/gradient/pallas_call | solution.py:707
  (33 shorter events, 0.3 us)
Async XLA Ops:
  3.2 44.5 %all-to-all-start = ((bf16[32,200,128]{2,1,0:T(8,128)(2,1)}), bf16[32,200,128]{2,1,0:T(8,128)(2,1)S(1)}, u32[]{:S(2)}, u32[]{:S(2)}) async-start(bf16[32,200,128]{2,1,0:T(8,128)(2,1)} %prepare_blocks.1.after), calls=%async_computation | async-start | bytes 3276800 | tf_op jit(solution)/shard_map/all_to_all | solution.py:639
  9.6 1.5 %copy-start.10 = (f32[240,16,128]{2,1,0:T(8,128)S(1)}, f32[240,16,128]{2,1,0:T(8,128)}, u32[]{:S(2)}) copy-start(f32[240,16,128]{2,1,0:T(8,128)} %control_ref.1) | copy-start | bytes 5898244
  12.7 6.6 %copy-start.2 = (bf16[240,240]{1,0:T(8,128)(2,1)S(1)}, bf16[240,240]{1,0:T(8,128)(2,1)}, u32[]{:S(2)}) copy-start(bf16[240,240]{1,0:T(8,128)(2,1)} %constant.45.clone.time_low.refs_8_) | copy-start | bytes 345604
  12.7 6.6 %copy-start.4 = (bf16[240,240]{1,0:T(8,128)(2,1)S(1)}, bf16[240,240]{1,0:T(8,128)(2,1)}, u32[]{:S(2)}) copy-start(bf16[240,240]{1,0:T(8,128)(2,1)} %constant.44.clone.time_high.refs_7_) | copy-start | bytes 345604
  12.7 6.6 %copy-start.6 = (bf16[256,256]{1,0:T(8,128)(2,1)S(1)}, bf16[256,256]{1,0:T(8,128)(2,1)}, u32[]{:S(2)}) copy-start(bf16[256,256]{1,0:T(8,128)(2,1)} %constant.46.clone.col_both.refs_9_) | copy-start | bytes 393220
  12.7 16.0 %collective-permute-start.4 = (f16[4,240,128]{2,1,0:T(8,128)(2,1)S(1)}, f16[4,240,128]{2,1,0:T(8,128)(2,1)S(1)}, u32[]{:S(2)}, u32[]{:S(2)}) collective-permute-start(f16[4,240,128]{2,1,0:T(8,128)(2,1)S(1)} %convert_element_type.28), channel_id=1, source_target_pairs={{0,4},{4,0},{8,12},{12,8},{16,20},{20,16},{24,28},{28,24},{1,5},{5... | collective-permute-start | bytes 737288 | tf_op jit(solution)/shard_map/ppermute | solution.py:613
  13.0 28.8 %collective-permute-start = (f16[4,240,128]{2,1,0:T(8,128)(2,1)S(1)}, f16[4,240,128]{2,1,0:T(8,128)(2,1)S(1)}, u32[]{:S(2)}, u32[]{:S(2)}) collective-permute-start(f16[4,240,128]{2,1,0:T(8,128)(2,1)S(1)} %convert_element_type.26), channel_id=1, source_target_pairs={{4,8},{8,4},{12,16},{16,12},{20,24},{24,20},{5,9},{9,5},{13,17},{1... | collective-permute-start | bytes 737288 | tf_op jit(solution)/shard_map/ppermute | solution.py:613
  17.2 4.8 %collective-permute-start.2 = (f32[120,128]{1,0:T(8,128)S(1)}, f32[120,128]{1,0:T(8,128)S(1)}, u32[]{:S(2)}, u32[]{:S(2)}) collective-permute-start(f32[120,128]{1,0:T(8,128)S(1)} %get-tuple-element.26), channel_id=1, source_target_pairs={{1,0},{2,1},{3,2},{0,3},{5,4},{6,5},{7,6},{4,7},{9,8},{10,9},{11,1... | collective-permute-start | bytes 184328 | tf_op jit(solution)/shard_map/ppermute | solution.py:601
  18.2 3.8 %collective-permute-start.1 = (f32[120,128]{1,0:T(8,128)S(1)}, f32[120,128]{1,0:T(8,128)S(1)}, u32[]{:S(2)}, u32[]{:S(2)}) collective-permute-start(f32[120,128]{1,0:T(8,128)S(1)} %get-tuple-element.22.refs_1_.after), channel_id=1, source_target_pairs={{0,1},{1,2},{2,3},{3,0},{4,5},{5,6},{6,7},{7,4},{8,9},{9,10},{10,1... | collective-permute-start | bytes 184328 | tf_op jit(solution)/shard_map/ppermute | solution.py:601
  21.6 3.5 %copy-start.18 = (f32[64]{0:T(128)S(1)}, f32[64]{0:T(128)}, u32[]{:S(2)}) copy-start(f32[64]{0:T(128)} %param.26) | copy-start | bytes 772
  21.6 3.5 %copy-start.19 = (f32[64]{0:T(128)S(1)}, f32[64]{0:T(128)}, u32[]{:S(2)}) copy-start(f32[64]{0:T(128)} %param.25) | copy-start | bytes 772
  21.7 3.5 %copy-start.8 = (bf16[128,2048]{1,0:T(8,128)(2,1)S(1)}, bf16[128,2048]{1,0:T(8,128)(2,1)}, u32[]{:S(2)}) copy-start(bf16[128,2048]{1,0:T(8,128)(2,1)} %constant.48.clone.own_low) | copy-start | bytes 1572868
  21.7 3.5 %copy-start.9 = (bf16[128,2048]{1,0:T(8,128)(2,1)S(1)}, bf16[128,2048]{1,0:T(8,128)(2,1)}, u32[]{:S(2)}) copy-start(bf16[128,2048]{1,0:T(8,128)(2,1)} %constant.47.clone.own_high) | copy-start | bytes 1572868
  22.2 25.5 %collective-permute-start.3 = (f32[64,128]{1,0:T(8,128)S(1)}, f32[64,128]{1,0:T(8,128)S(1)}, u32[]{:S(2)}, u32[]{:S(2)}) collective-permute-start(f32[64,128]{1,0:T(8,128)S(1)} %get-tuple-element.27), channel_id=1, source_target_pairs={{4,8},{8,4},{12,16},{16,12},{20,24},{24,20},{5,9},{9,5},{13,17},{1... | collective-permute-start | bytes 98312 | tf_op jit(solution)/shard_map/ppermute | solution.py:537
  25.0 4.7 %collective-permute-start.5 = (f32[64,128]{1,0:T(8,128)S(1)}, f32[64,128]{1,0:T(8,128)S(1)}, u32[]{:S(2)}, u32[]{:S(2)}) collective-permute-start(f32[64,128]{1,0:T(8,128)S(1)} %get-tuple-element.28), channel_id=1, source_target_pairs={{0,4},{4,0},{8,12},{12,8},{16,20},{20,16},{24,28},{28,24},{1,5},{5... | collective-permute-start | bytes 98312 | tf_op jit(solution)/shard_map/ppermute | solution.py:536
  25.2 4.5 %copy-start.12 = (bf16[2,32,512]{2,1,0:T(8,128)(2,1)S(1)}, bf16[2,32,512]{2,1,0:T(8,128)(2,1)}, u32[]{:S(2)}) copy-start(bf16[2,32,512]{2,1,0:T(8,128)(2,1)} %constant.50.clone.corner_low.refs_11_) | copy-start | bytes 196612
  25.2 4.5 %copy-start.14 = (bf16[2,32,512]{2,1,0:T(8,128)(2,1)S(1)}, bf16[2,32,512]{2,1,0:T(8,128)(2,1)}, u32[]{:S(2)}) copy-start(bf16[2,32,512]{2,1,0:T(8,128)(2,1)} %constant.49.clone.corner_high.refs_10_) | copy-start | bytes 196612
  25.2 4.5 %copy-start.16 = (bf16[240,16,128]{2,1,0:T(8,128)(2,1)S(1)}, bf16[240,16,128]{2,1,0:T(8,128)(2,1)}, u32[]{:S(2)}) copy-start(bf16[240,16,128]{2,1,0:T(8,128)(2,1)} %prior_ref.1) | copy-start | bytes 2949124
  25.2 4.5 %copy-start.17 = (bf16[240,16,128]{2,1,0:T(8,128)(2,1)S(1)}, bf16[240,16,128]{2,1,0:T(8,128)(2,1)}, u32[]{:S(2)}) copy-start(bf16[240,16,128]{2,1,0:T(8,128)(2,1)} %scale_ref.1) | copy-start | bytes 2949124
  33.0 1.3 %copy-start = (f32[16,240,128]{2,1,0:T(8,128)}, f32[16,240,128]{2,1,0:T(8,128)S(1)}, u32[]{:S(2)}) copy-start(f32[16,240,128]{2,1,0:T(8,128)S(1)} %get-tuple-element.30.refs_6_.refs_4_) | copy-start | bytes 5898244
  34.3 1.3 %copy-start.11 = (f32[16,240,128]{2,1,0:T(8,128)}, f32[16,240,128]{2,1,0:T(8,128)S(1)}, u32[]{:S(2)}) copy-start(f32[16,240,128]{2,1,0:T(8,128)S(1)} %get-tuple-element.29.refs_5_) | copy-start | bytes 5898244
  47.7 20.4 %copy-start.1 = (f32[16,240,128]{2,1,0:T(8,128)S(1)}, f32[16,240,128]{2,1,0:T(8,128)}, u32[]{:S(2)}) copy-start(f32[16,240,128]{2,1,0:T(8,128)} %copy-done) | copy-start | bytes 5898244
  71.4 5.8 %copy-start.3 = (bf16[240,240]{1,0:T(8,128)(2,1)S(1)}, bf16[240,240]{1,0:T(8,128)(2,1)}, u32[]{:S(2)}) copy-start(bf16[240,240]{1,0:T(8,128)(2,1)} %constant.45.clone.time_low.refs_8_) | copy-start | bytes 345604
  71.4 5.8 %copy-start.5 = (bf16[240,240]{1,0:T(8,128)(2,1)S(1)}, bf16[240,240]{1,0:T(8,128)(2,1)}, u32[]{:S(2)}) copy-start(bf16[240,240]{1,0:T(8,128)(2,1)} %constant.44.clone.time_high.refs_7_) | copy-start | bytes 345604
  71.5 5.8 %copy-start.7 = (bf16[256,256]{1,0:T(8,128)(2,1)S(1)}, bf16[256,256]{1,0:T(8,128)(2,1)}, u32[]{:S(2)}) copy-start(bf16[256,256]{1,0:T(8,128)(2,1)} %constant.46.clone.col_both.refs_9_) | copy-start | bytes 393220
  71.5 12.7 %collective-permute-start.8 = (f16[4,240,128]{2,1,0:T(8,128)(2,1)S(1)}, f16[4,240,128]{2,1,0:T(8,128)(2,1)S(1)}, u32[]{:S(2)}, u32[]{:S(2)}) collective-permute-start(f16[4,240,128]{2,1,0:T(8,128)(2,1)S(1)} %convert_element_type.30), channel_id=1, source_target_pairs={{0,4},{4,0},{8,12},{12,8},{16,20},{20,16},{24,28},{28,24},{1,5},{5... | collective-permute-start | bytes 737288 | tf_op jit(solution)/shard_map/ppermute | solution.py:613
  73.1 11.2 %collective-permute-start.10 = (f16[4,240,128]{2,1,0:T(8,128)(2,1)S(1)}, f16[4,240,128]{2,1,0:T(8,128)(2,1)S(1)}, u32[]{:S(2)}, u32[]{:S(2)}) collective-permute-start(f16[4,240,128]{2,1,0:T(8,128)(2,1)S(1)} %convert_element_type.32), channel_id=1, source_target_pairs={{4,8},{8,4},{12,16},{16,12},{20,24},{24,20},{5,9},{9,5},{13,17},{1... | collective-permute-start | bytes 737288 | tf_op jit(solution)/shard_map/ppermute | solution.py:613
  75.3 4.5 %collective-permute-start.7 = (f32[120,128]{1,0:T(8,128)S(1)}, f32[120,128]{1,0:T(8,128)S(1)}, u32[]{:S(2)}, u32[]{:S(2)}) collective-permute-start(f32[120,128]{1,0:T(8,128)S(1)} %get-tuple-element.37), channel_id=1, source_target_pairs={{1,0},{2,1},{3,2},{0,3},{5,4},{6,5},{7,6},{4,7},{9,8},{10,9},{11,1... | collective-permute-start | bytes 184328 | tf_op jit(solution)/shard_map/ppermute | solution.py:601
  76.6 3.2 %collective-permute-start.6 = (f32[120,128]{1,0:T(8,128)S(1)}, f32[120,128]{1,0:T(8,128)S(1)}, u32[]{:S(2)}, u32[]{:S(2)}) collective-permute-start(f32[120,128]{1,0:T(8,128)S(1)} %get-tuple-element.36.refs_1_), channel_id=1, source_target_pairs={{0,1},{1,2},{2,3},{3,0},{4,5},{5,6},{6,7},{7,4},{8,9},{9,10},{10,1... | collective-permute-start | bytes 184328 | tf_op jit(solution)/shard_map/ppermute | solution.py:601
  79.6 5.2 %copy-start.13 = (bf16[2,32,512]{2,1,0:T(8,128)(2,1)S(1)}, bf16[2,32,512]{2,1,0:T(8,128)(2,1)}, u32[]{:S(2)}) copy-start(bf16[2,32,512]{2,1,0:T(8,128)(2,1)} %constant.50.clone.corner_low.refs_11_) | copy-start | bytes 196612
  79.6 5.2 %copy-start.15 = (bf16[2,32,512]{2,1,0:T(8,128)(2,1)S(1)}, bf16[2,32,512]{2,1,0:T(8,128)(2,1)}, u32[]{:S(2)}) copy-start(bf16[2,32,512]{2,1,0:T(8,128)(2,1)} %constant.49.clone.corner_high.refs_10_) | copy-start | bytes 196612
  80.0 4.8 %collective-permute-start.9 = (f32[64,128]{1,0:T(8,128)S(1)}, f32[64,128]{1,0:T(8,128)S(1)}, u32[]{:S(2)}, u32[]{:S(2)}) collective-permute-start(f32[64,128]{1,0:T(8,128)S(1)} %get-tuple-element.38), channel_id=1, source_target_pairs={{0,4},{4,0},{8,12},{12,8},{16,20},{20,16},{24,28},{28,24},{1,5},{5... | collective-permute-start | bytes 98312 | tf_op jit(solution)/shard_map/ppermute | solution.py:536
  80.1 7.6 %collective-permute-start.11 = (f32[64,128]{1,0:T(8,128)S(1)}, f32[64,128]{1,0:T(8,128)S(1)}, u32[]{:S(2)}, u32[]{:S(2)}) collective-permute-start(f32[64,128]{1,0:T(8,128)S(1)} %get-tuple-element.39), channel_id=1, source_target_pairs={{4,8},{8,4},{12,16},{16,12},{20,24},{24,20},{5,9},{9,5},{13,17},{1... | collective-permute-start | bytes 98312 | tf_op jit(solution)/shard_map/ppermute | solution.py:537

commit v8 on v7

--- a/solution.py
+++ b/solution.py
@@ -15,7 +15,6 @@
 PARTS = 4
 SCALE_MAX = 2.0
 HALF_TOP = 32768.0
-CONTROL_FACTOR = 4096.0
 F16 = jnp.float16
 VMEM_LIMIT = 14 * 1024 * 1024
 F32 = jnp.float32
@@ -68,7 +67,13 @@
         ]
         for part, value in zip(corner, strips(*zip(*lanes), targets)):
             part.append(value)
-    return (time_high, time_low, col_both), strips(*zip(*own), np.arange(rows)), [np.stack(c) for c in corner]
+    beyond = [strips(*zip(*own), rows + np.arange(RAD)), strips(*zip(*own), -1 - np.arange(RAD))]
+    return (
+        (time_high, time_low, col_both),
+        strips(*zip(*own), np.arange(rows)),
+        [np.stack(c) for c in corner],
+        [np.stack(c) for c in zip(*beyond)],
+    )
 
 
 def split(value):
@@ -297,45 +302,17 @@
             out_ref[:, r, :] = value
 
 
-def edge_parts(odd, rows, first, got_e, got_o, consts, halo, factor, corner=None):
+def beyond_sums(rows, corner, corner_high, corner_low, consts):
     time_high, time_low, col_both = consts
+    cols = col_both.shape[1] // 2
     taps = space_taps()
-    for row in range(RAD):
-        even, other = got_e[row], got_o[row]
-        halo[row] = (choose(odd, even, other) if first else choose(odd, other, even)) * factor
-    parts = []
-    for k in range(0, RAD, 2):
-        pair = []
-        for i in (k, k + 1):
-            if first:
-                summed = row_sums(lambda r: halo[r + RAD], i, -RAD, 0, taps)
-            else:
-                summed = row_sums(lambda r: halo[r - RAD], i, RAD, 2 * RAD, taps)
-            pair.append(column_sums(summed, col_both[...]))
-        value = jnp.concatenate(pair, axis=1)
-        width = value.shape[1]
-        if corner is not None:
-            parts_of, high, low = corner
-            at = (k if first else RAD + k) * (width // 2)
-            value = value + halo_sums(parts_of, high, low, at, width)
-        both = time_sums(value, time_high[...], time_low[...])
-        half = width // 2
-        parts += [both[:, :half], both[:, half:]]
-    return parts
-
-
-def edge_parts(halo, corner, corner_high, corner_low, consts):
-    time_high, time_low, col_both = consts
-    hours, cols = halo.shape[1:]
-    taps = space_taps()
-    corner = split(unfold_corners(corner)[0:hours, 0 : corner_high.shape[0]])
     parts = []
     for k in range(0, RAD, 2):
         pair = []
         for i in (k, k + 1):
             summed = None
             for j in range(RAD - i):
-                part = float(taps[RAD + i + j + 1]) * halo[j]
+                part = float(taps[RAD + i + j + 1]) * rows(j)
                 summed = part if summed is None else summed + part
             pair.append(column_sums(summed, col_both[...]))
         value = jnp.concatenate(pair, axis=1) + halo_sums(corner, corner_high, corner_low, k * cols, 2 * cols)
@@ -344,10 +321,29 @@
     return parts
 
 
-def flux_kernel(
-    par_ref, local_ref, prior_ref, scale_ref, got_ref, corner_ref,
-    time_high, time_low, col_both, corner_high, corner_low, flux_ref, scale_out, wide, halo,
+def edge_parts(halo, corner, corner_high, corner_low, consts):
+    corner = split(unfold_corners(corner)[0 : halo.shape[1], 0 : corner_high.shape[0]])
+    return beyond_sums(lambda j: halo[j], corner, corner_high, corner_low, consts)
+
+
+def beyond_kernel(
+    par_ref, field_ref, before_ref, after_ref, time_high, time_low, col_both, beyond_high, beyond_low,
+    out_even, out_odd,
 ):
+    rows, hours, _ = field_ref.shape
+    odd = is_odd(par_ref, 0)
+    halo = split(halo_columns(par_ref, before_ref, after_ref)[0:hours])
+    consts = (time_high, time_low, col_both)
+    to_after = beyond_sums(
+        lambda j: field_ref[rows - 1 - j], halo, beyond_high.at[0], beyond_low.at[0], consts
+    )
+    to_before = beyond_sums(lambda j: field_ref[j], halo, beyond_high.at[1], beyond_low.at[1], consts)
+    for k in range(RAD):
+        out_even[k] = choose(odd, to_before[k], to_after[k]).astype(BF16)
+        out_odd[k] = choose(odd, to_after[k], to_before[k]).astype(BF16)
+
+
+def flux_kernel(par_ref, local_ref, prior_ref, scale_ref, got_ref, flux_ref, scale_out, wide):
     rows = local_ref.shape[0]
     odd = par_ref[0, 0]
     wide[...] = scale_ref[...].astype(F32)
@@ -356,12 +352,9 @@
     wide[...] = prior_ref[...].astype(F32)
     for row in range(rows):
         flux_ref[row] = wide[:, row, :] + scale_out[row] * local_ref[row]
-    halo[...] = got_ref[...] * (1.0 / CONTROL_FACTOR)
-    consts = (time_high, time_low, col_both)
-    parts = edge_parts(halo, corner_ref[...], corner_high.at[odd], corner_low.at[odd], consts)
-    for k, part in enumerate(parts):
+    for k in range(RAD):
         row = jnp.where(odd == 1, k, rows - 1 - k)
-        flux_ref[row] = flux_ref[row] + scale_out[row] * part
+        flux_ref[row] = flux_ref[row] + scale_out[row] * got_ref[k].astype(F32)
 
 
 def finish_kernel(
@@ -404,46 +397,52 @@
         yield c + 1, both[heights : 2 * heights]
 
 
-def forward_kernel(
-    par_ref, foot_ref, own_ref, got_ref, corner_ref, flux_hbm, scale_hbm, *refs,
-    shift, slots, heights, tiles, per,
+def load_kernel(
+    par_ref, foot_ref, scale_far, *refs, shift, slots, heights, tiles, per, empty
 ):
-    distant, near = refs[0:5], refs[7:12]
-    out_ref, table_ref = refs[5:7]
-    flux_ref, scale_ref, halo, edges, sums, table_smem, sems = refs[12:]
-    *consts, corner_high, corner_low = near
-    odd = par_ref[0, 0]
-    sources = foot_ref.shape[0]
+    count = (len(refs) - 3) // 2
+    distant, (table_ref, scale_ref), near = refs[:count], refs[count : count + 2], refs[count + 2 : -1]
+    sems = refs[-1]
+    flux_far, flux_ref = distant[0], near[0]
     rows = flux_ref.shape[0]
-    first = (rows - RAD) * odd
-    pairs = list(zip(distant, near)) + [(scale_hbm.at[pl.ds(first, RAD)], scale_ref)]
-    pairs += [(flux_hbm.at[r : r + RAD], flux_ref.at[r : r + RAD]) for r in range(0, rows, RAD)]
+    first = (rows - RAD) * par_ref[0, 0]
+    pairs = [(flux_far.at[r : r + RAD], flux_ref.at[r : r + RAD]) for r in range(0, rows, RAD)]
+    pairs += list(zip(distant[1:], near[1:])) + [(scale_far.at[pl.ds(first, RAD)], scale_ref)]
     loads = [pltpu.make_async_copy(a, b, sems.at[i]) for i, (a, b) in enumerate(pairs)]
     for load in loads:
         load.start()
-    groups = out_ref.shape[1] - 1
+    sources = foot_ref.shape[0]
     base = slots * heights
     lane = lane_ids((sources, LANES))
     notes = foot_ref[:, base : base + SUB, :].astype(F32)[:, 0, :].astype(jnp.int32)
     start = notes * 16 + pltpu.roll(notes, LANES - slots, 1)
     offset = start + pltpu.roll(notes, LANES - 2 * slots, 1) * (1 << shift)
     source_rec = lax.broadcasted_iota(jnp.int32, (sources, LANES), 0) // tiles
-    receptor = jnp.where(notes < per, source_rec * per + notes, groups * LANES)
-    table = jnp.where(lane < slots, offset, receptor)
-    table_ref[...] = table
-    copy = pltpu.make_async_copy(table_ref, table_smem, sems.at[len(loads)])
+    receptor = jnp.where(notes < per, source_rec * per + notes, empty)
+    table_ref[...] = jnp.where(lane < slots, offset, receptor)
+    for load in loads:
+        load.wait()
+
+
+def forward_kernel(
+    par_ref, foot_ref, table_ref, own_ref, got_far, flux_in, scale_ref,
+    out_ref, flux_ref, got_ref, sums, table_smem, sems, *, shift, slots, heights, tiles, per,
+):
+    load = pltpu.make_async_copy(got_far, got_ref, sems.at[1])
+    load.start()
+    odd = par_ref[0, 0]
+    sources = foot_ref.shape[0]
+    rows = flux_ref.shape[0]
+    first = (rows - RAD) * odd
+    groups = out_ref.shape[1] - 1
+    lane = lane_ids((sources, LANES))
+    table = table_ref[...]
+    copy = pltpu.make_async_copy(table_ref, table_smem, sems.at[0])
     copy.start()
-    for load in loads[: len(near)]:
-        load.wait()
-    halo[...] = got_ref[...] * (1.0 / CONTROL_FACTOR)
-    parts = edge_parts(halo, corner_ref[...], corner_high.at[1 - odd], corner_low.at[1 - odd], consts)
-    for k, part in enumerate(parts):
-        edges[k] = part
-    for load in loads[len(near) :]:
-        load.wait()
+    load.wait()
     for k in range(RAD):
         line = jnp.where(odd == 1, RAD - 1 - k, k)
-        flux_ref[first + line] = flux_ref[first + line] + scale_ref[line] * edges[k]
+        flux_ref[first + line] = flux_in[first + line] + scale_ref[line] * got_ref[k].astype(F32)
     copy.wait()
 
     def body(source, carry):
@@ -542,13 +541,14 @@
 HB = pl.BlockSpec(memory_space=pltpu.HBM)
 
 
-def call(kernel, out_shape, in_specs, scratch, name, out_specs=None):
+def call(kernel, out_shape, in_specs, scratch, name, out_specs=None, alias=None):
     return pl.pallas_call(
         kernel,
         out_shape=out_shape,
         in_specs=in_specs,
         out_specs=jax.tree.map(lambda _: VM, out_shape) if out_specs is None else out_specs,
         scratch_shapes=scratch,
+        input_output_aliases={} if alias is None else alias,
         compiler_params=pltpu.CompilerParams(vmem_limit_bytes=VMEM_LIMIT),
         name=name,
     )
@@ -585,10 +585,11 @@
     flags = [rec % 2, rec * 0, rec, tile == 0, tile == n_tile - 1] + [rec * 0] * (SUB - 5)
     par = jnp.stack([flag.astype(jnp.int32) for flag in flags])
     par = jnp.broadcast_to(par[:, None], (SUB, LANES))
-    base, own_parts, corner_parts = constants(hours, rows, cols)
+    base, own_parts, corner_parts, beyond_parts = constants(hours, rows, cols)
     base = [jnp.asarray(c) for c in base]
     own_parts = [jnp.asarray(c) for c in own_parts]
     corner_parts = [jnp.asarray(c) for c in corner_parts]
+    beyond_parts = [jnp.asarray(c) for c in beyond_parts]
     strip = array(-(-hours // (2 * SUB)) * SUB, LANES)
     corner = array(-(-hours // (4 * SUB)) * SUB, LANES)
     block = array(RAD, hours, cols)
@@ -640,21 +641,19 @@
     field, *strips = call(
         turn_kernel, [field_shape, strip, strip], [HB, VM], [], "turn_control"
     )(sent, control)
-    factor = jnp.full((2, LANES), CONTROL_FACTOR, F32)
-    _, got_even = swap_rows(True, strips[0], factor, field, "control_even")
-    _, got_odd = swap_rows(False, strips[0], factor, field, "control_odd")
     got_strips = pass_strips(*strips)
-    local, got_corners = swaps(strips[0], field, got_strips, "control")
+    local = call(local_kernel, field_shape, [VM] * 5, [], "control_local")(strips[0], field, *base)
+    small = jax.ShapeDtypeStruct((RAD, hours, cols), BF16)
+    sent_even, sent_odd = call(beyond_kernel, [small, small], [VM] * 9, [], "control_beyond")(
+        par, field, *got_strips, *base, *beyond_parts
+    )
+    got_even, got_odd = swap("rec", sent_even, sent_odd)
     local = call(strips_kernel, field_shape, [VM] * 8, [], "control_strips")(
         par, local, *got_strips, *base[:2], *own_parts
     )
     flux, scale = call(
-        flux_kernel,
-        [field_shape, field_shape],
-        [VM] * 11,
-        [pltpu.VMEM((hours, rows, cols), F32), row_scratch],
-        "flux_field",
-    )(par, local, prior_flux, flux_scale, got_even.astype(F32), got_corners[0], *base, *corner_parts)
+        flux_kernel, [field_shape, field_shape], [VM] * 5, [pltpu.VMEM((hours, rows, cols), F32)], "flux_field"
+    )(par, local, prior_flux, flux_scale, got_even)
 
     own = jnp.concatenate([observed, obs_error, jnp.zeros((LANES - 2 * per,), F32)])[None]
     sizes = dict(shift=shift, slots=slots, heights=heights, tiles=n_tile, per=per)
@@ -662,21 +661,31 @@
     def forward(*refs):
         forward_kernel(*refs, **sizes)
 
-    foot, got_odd = lax.optimization_barrier((foot, got_odd))
-    needed = [*base, *corner_parts]
-    partial, table = call(
+
+    def load(*refs):
+        load_kernel(*refs, empty=groups * LANES, **sizes)
+
+    table, scale_near, flux_near = call(
+        load,
+        [jax.ShapeDtypeStruct((devices, LANES), jnp.int32), block, field_shape],
+        [VM, VM, HB, HB],
+        [pltpu.SemaphoreType.DMA((1 + rows // RAD,))],
+        "load_flux",
+    )(par, foot, far(scale), far(flux))
+    table, got_odd = lax.optimization_barrier((table, got_odd))
+    partial, _ = call(
         forward,
-        [array(devices, groups + 1, LANES), jax.ShapeDtypeStruct((devices, LANES), jnp.int32)],
-        [VM] * 5 + [HB] * 7,
-        [pltpu.VMEM(x.shape, x.dtype) for x in needed]
-        + [pltpu.VMEM((rows, hours, cols), F32), row_scratch, row_scratch, row_scratch]
-        + [
+        [array(devices, groups + 1, LANES), field_shape],
+        [VM] * 4 + [HB] + [VM] * 2,
+        [
+            pltpu.VMEM((RAD, hours, cols), BF16),
             pltpu.VMEM((slots, devices, LANES), F32),
             pltpu.SMEM((devices, LANES), jnp.int32),
-            pltpu.SemaphoreType.DMA((len(needed) + rows // RAD + 2,)),
+            pltpu.SemaphoreType.DMA((2,)),
         ],
         "block_values",
-    )(par, foot, own, got_odd.astype(F32), got_corners[1], *[far(x) for x in (flux, scale, *needed)])
+        alias={5: 1},
+    )(par, foot, table, own, far(got_odd), flux_near, scale_near)
     everyone = lax.all_to_all(partial, AXES, split_axis=0, concat_axis=0, tiled=True)
 
     def adjoint(*refs):

time: 91.8 us -> 90.4 us (0.985)
  starting transfers between devices: 25.6 us -> 22 us
  waiting for transfers between devices: 16 us -> 19 us
  blocking collectives: 16.5 us -> 14.4 us
  Pallas kernels: 26.3 us -> 27.6 us
    ppermute x2, waiting for transfers between devices: 1.31 us -> 9.8 us  [swap(): lax.ppermute(even, axis, swap_pairs(count, False))]
    ppermute x4 -> x2, waiting for transfers between devices: 8.33 us -> 0.01 us  [swap_rows(): lax.ppermute(sent.astype(F16), 'rec', swap_pairs(n_rec, not even))]
    ppermute x2, waiting for transfers between devices: 0.43 us -> 8.27 us  [pass_strips(): lax.ppermute(first, 'tile', back)]
    all_to_all x1, waiting for transfers between devices: 5.89 us -> 0.87 us  [per_device(): foot = lax.all_to_all(sent, AXES, split_axis=0, concat_axis=0, tiled=True)]
    ppermute x4 -> x2, starting transfers between devices: 8 us -> 3.63 us  [swap_rows(): lax.ppermute(sent.astype(F16), 'rec', swap_pairs(n_rec, not even))]
    pallas_call x2 -> x5, Pallas kernels: 7.12 us -> 11 us  [the longest x1 2.64 us: per_device(): call(flux_kernel, [field_shape, field_shape], [VM] * 5, [pltpu.VMEM((hour...]
    pallas_call x2 -> x1, Pallas kernels: 4.62 us -> 2.25 us  [swaps(): call(local_kernel, field_shape, [VM] * 5, [], name + '_local')]
    all_to_all x1, blocking collectives: 16.5 us -> 14.4 us  [per_device(): lax.all_to_all(partial, AXES, split_axis=0, concat_axis=0, tiled=True)]
  transfers between devices with their start and end apart: 13 -> 11, of which waited for: 7 -> 4; matrix products, arithmetic and copies ran while one was open for 0% -> 0% of each run, Pallas kernels for 16% -> 19%
where the time goes in v8:
time: 90.4 us; the launch traced here: 88.6 us
  Pallas kernels  27.6 us (31%)
  starting transfers between devices  22 us (24%)
  waiting for transfers between devices  19 us (21%)
  blocking collectives  14.4 us (16%)
  local copies, waits for them, and re-layouts  4.33 us (5%)
  between operations  1.15 us (1%)
    all_to_all x1, blocking collectives, per_device(): lax.all_to_all(partial, AXES, split_axis=0, concat_axis=0, tiled=True)  14.4 us
    ppermute x2, waiting for transfers between devices, swap(): lax.ppermute(even, axis, swap_pairs(count, False))  9.8 us
    ppermute x2, waiting for transfers between devices, pass_strips(): lax.ppermute(first, 'tile', back)  8.27 us
    ppermute x2, starting transfers between devices, swap(): lax.ppermute(odd, axis, swap_pairs(count, True))  7.01 us
    all_to_all x1, starting transfers between devices, per_device(): foot = lax.all_to_all(sent, AXES, split_axis=0, concat_axis=0, tiled=True)  6.42 us
    unnamed x34, local copies, waits for them, and re-layouts  4.17 us
    ppermute x2, starting transfers between devices, swap_rows(): lax.ppermute(sent.astype(F16), 'rec', swap_pairs(n_rec, not even))  3.63 us
    pallas_call x1, Pallas kernels, per_device(): call(sides_kernel, array(hours, rows, cols), [VM] * 14, [row_scratch], 'g...  2.89 us
  transfers between devices with their start and end apart: 11, of which 4 were waited for; matrix products, arithmetic and copies ran while one was open for 0% of the time, Pallas kernels for 19%

profile of v8, /device:TPU:5, one launch (start us, length us, event | category | flops | bytes accessed | tf_op | source)
XLA Modules:
  0.0 88.6 jit_solution(15728541927359241774)
XLA Ops:
  0.7 0.1 stack.27
  0.7 0.1 broadcast_in_dim.12.refs_0_.par_ref
  0.8 2.3 %prepare_blocks.1.after = bf16[32,200,128]{2,1,0:T(8,128)(2,1)} custom-call(s32[8,128]{1,0:T(8,128)S(1)} %broadcast_in_dim.12.refs_0_.par_ref, bf16[32,192,128]{2,1,0:T(8,128)(2,1)} %bitcast.12, s32[8,32]{1,0:T(8,128)} %bitcast.13, s32[8,32]{1,0:T(8,128)} %bitcast.14, s32[8,32]{1,0:T(8,128)} %bitcast.15, s32[1,32]{1,0:T(1,128)} %bitcast.16), custom_call_target="tpu_custom_call" | custom-call | tf_op jit(solution)/shard_map/prepare_blocks/pallas_call | solution.py:621
  3.2 6.4 %all-to-all-start = ((bf16[32,200,128]{2,1,0:T(8,128)(2,1)}), bf16[32,200,128]{2,1,0:T(8,128)(2,1)S(1)}, u32[]{:S(2)}, u32[]{:S(2)}) async-start(bf16[32,200,128]{2,1,0:T(8,128)(2,1)} %prepare_blocks.1.after), calls=%async_computation | async-start | bytes 3276800 | tf_op jit(solution)/shard_map/all_to_all | solution.py:640
  9.6 0.0 copy-start.7
  9.6 1.5 %copy-done.7 = f32[240,16,128]{2,1,0:T(8,128)S(1)} copy-done((f32[240,16,128]{2,1,0:T(8,128)S(1)}, f32[240,16,128]{2,1,0:T(8,128)}, u32[]{:S(2)}) %copy-start.7) | copy-done | bytes 1966104
  11.1 0.0 copy-start.14
  11.2 1.5 %turn_control.1 = (f32[16,240,128]{2,1,0:T(8,128)S(1)}, f32[120,128]{1,0:T(8,128)S(1)}, f32[120,128]{1,0:T(8,128)S(1)}) custom-call(bf16[32,200,128]{2,1,0:T(8,128)(2,1)} %prepare_blocks.1.after, f32[240,16,128]{2,1,0:T(8,128)S(1)} %copy-done.7), custom_call_target="tpu_custom_call" | custom-call | tf_op jit(solution)/shard_map/turn_control/pallas_call | solution.py:641
  12.6 0.4 collective-permute-start.1
  13.0 1.4 %collective-permute-start = (f32[120,128]{1,0:T(8,128)S(1)}, f32[120,128]{1,0:T(8,128)S(1)}, u32[]{:S(2)}, u32[]{:S(2)}) collective-permute-start(f32[120,128]{1,0:T(8,128)S(1)} %get-tuple-element.24.after), channel_id=1, source_target_pairs={{0,1},{1,2},{2,3},{3,0},{4,5},{5,6},{6,7},{7,4},{8,9},{9,10},{10,1... | collective-permute-start | bytes 184328 | tf_op jit(solution)/shard_map/ppermute | solution.py:602
  14.4 8.3 %collective-permute-done.1.after_ref = f32[120,128]{1,0:T(8,128)S(1)} collective-permute-done((f32[120,128]{1,0:T(8,128)S(1)}, f32[120,128]{1,0:T(8,128)S(1)}, u32[]{:S(2)}, u32[]{:S(2)}) %collective-permute-start.1) | collective-permute-done | bytes 61472 | tf_op jit(solution)/shard_map/ppermute | solution.py:602
  22.7 0.0 collective-permute-done.before_ref
  22.7 0.0 copy-done.2
  22.7 0.0 copy-done.3
  22.7 0.0 copy-done.4
  22.7 0.0 copy-done.13
  22.7 0.0 copy-done.14
  22.7 1.9 %control_beyond.1 = (bf16[4,240,128]{2,1,0:T(8,128)(2,1)S(1)}, bf16[4,240,128]{2,1,0:T(8,128)(2,1)S(1)}) custom-call(s32[8,128]{1,0:T(8,128)S(1)} %broadcast_in_dim.12.refs_0_.par_ref, f32[16,240,128]{2,1,0:T(8,128)S(1)} %get-tuple-element.25.field_ref, f32[120,128]{1,0:T(8,128)S(1)} %collective-permute-done.before_ref, ...), custom_call_target="tpu_custom_call" | custom-call | tf_op jit(solution)/shard_map/control_beyond/pallas_call | solution.py:647
  24.6 1.2 %collective-permute-start.2 = (bf16[4,240,128]{2,1,0:T(8,128)(2,1)S(1)}, bf16[4,240,128]{2,1,0:T(8,128)(2,1)S(1)}, u32[]{:S(2)}, u32[]{:S(2)}) collective-permute-start(bf16[4,240,128]{2,1,0:T(8,128)(2,1)S(1)} %get-tuple-element.27), channel_id=1, source_target_pairs={{0,4},{4,0},{8,12},{12,8},{16,20},{20,16},{24,28},{28,24},{1,5},{5... | collective-permute-start | bytes 737288 | tf_op jit(solution)/shard_map/ppermute | solution.py:535
  25.8 2.8 %collective-permute-start.3 = (bf16[4,240,128]{2,1,0:T(8,128)(2,1)S(1)}, bf16[4,240,128]{2,1,0:T(8,128)(2,1)}, u32[]{:S(2)}, u32[]{:S(2)}) collective-permute-start(bf16[4,240,128]{2,1,0:T(8,128)(2,1)S(1)} %get-tuple-element.31), channel_id=1, source_target_pairs={{4,8},{8,4},{12,16},{16,12},{20,24},{24,20},{5,9},{9,5},{13,17},{1... | collective-permute-start | bytes 737288 | tf_op jit(solution)/shard_map/ppermute | solution.py:536
  28.6 2.3 %control_local.1.local_ref = f32[16,240,128]{2,1,0:T(8,128)S(1)} custom-call(f32[120,128]{1,0:T(8,128)S(1)} %get-tuple-element.24.after, f32[16,240,128]{2,1,0:T(8,128)S(1)} %get-tuple-element.25.field_ref, bf16[240,240]{1,0:T(8,128)(2,1)S(1)} %copy-done.3, bf16[240,240]{1,0:T(8,128)(2,1)S(1)} %copy-done.2, bf16[256,256]{1,0:T(8,128)(2,1)S(1)} %copy-done.4), custom_call_target="tpu_custom_call" | custom-call | tf_op jit(solution)/shard_map/control_local/pallas_call | solution.py:645
  31.0 0.0 copy-done.15
  31.0 0.0 copy-done.16
  31.0 0.1 maximum_bitcast_fusion.refs_3_
  31.0 0.0 copy-done.5
  31.1 0.0 copy-done.6
  31.1 1.4 %control_strips.1.local_ref = f32[16,240,128]{2,1,0:T(8,128)S(1)} custom-call(s32[8,128]{1,0:T(8,128)S(1)} %broadcast_in_dim.12.refs_0_.par_ref, f32[16,240,128]{2,1,0:T(8,128)S(1)} %control_local.1.local_ref, f32[120,128]{1,0:T(8,128)S(1)} %collective-permute-done.before_ref, f32[120,128]{1,0:T(8,128)S(1)} %collective-permute-done.1.after_ref, ...), custom_call_target="tpu_custom_call" | custom-call | tf_op jit(solution)/shard_map/control_strips/pallas_call | solution.py:651
  32.5 9.1 %collective-permute-done.2.got_ref = bf16[4,240,128]{2,1,0:T(8,128)(2,1)S(1)} collective-permute-done((bf16[4,240,128]{2,1,0:T(8,128)(2,1)S(1)}, bf16[4,240,128]{2,1,0:T(8,128)(2,1)S(1)}, u32[]{:S(2)}, u32[]{:S(2)}) %collective-permute-start.2) | collective-permute-done | bytes 245792 | tf_op jit(solution)/shard_map/ppermute | solution.py:535
  41.6 0.0 copy-done.9
  41.6 0.0 copy-done.10
  41.6 2.6 %flux_field.1 = (f32[16,240,128]{2,1,0:T(8,128)S(1)}, f32[16,240,128]{2,1,0:T(8,128)S(1)}) custom-call(s32[8,128]{1,0:T(8,128)S(1)} %broadcast_in_dim.12.refs_0_.par_ref, f32[16,240,128]{2,1,0:T(8,128)S(1)} %control_strips.1.local_ref, bf16[240,16,128]{2,1,0:T(8,128)(2,1)S(1)} %copy-done.9, bf16[240,16,128]{2,1,0:T(8,128)(2,1)S(1)} %copy-done.10, ...), custom_call_target="tpu_custom_call" | custom-call | tf_op jit(solution)/shard_map/flux_field/pallas_call | solution.py:654
  44.2 0.0 copy-start
  44.2 1.3 %copy-done = f32[16,240,128]{2,1,0:T(8,128)} copy-done((f32[16,240,128]{2,1,0:T(8,128)}, f32[16,240,128]{2,1,0:T(8,128)S(1)}, u32[]{:S(2)}) %copy-start) | copy-done | bytes 1966104
  45.5 1.3 %copy-done.8 = f32[16,240,128]{2,1,0:T(8,128)} copy-done((f32[16,240,128]{2,1,0:T(8,128)}, f32[16,240,128]{2,1,0:T(8,128)S(1)}, u32[]{:S(2)}) %copy-start.8) | copy-done | bytes 1966104
  46.8 0.9 all-to-all-done.refs_1_.refs_3_
  47.7 1.7 %load_flux.1 = (s32[32,128]{1,0:T(8,128)S(1)}, f32[4,240,128]{2,1,0:T(8,128)S(1)}, f32[16,240,128]{2,1,0:T(8,128)S(1)}) custom-call(s32[8,128]{1,0:T(8,128)S(1)} %broadcast_in_dim.12.refs_0_.par_ref, bf16[32,200,128]{2,1,0:T(8,128)(2,1)S(1)} %all-to-all-done.refs_1_.refs_3_, f32[16,240,128]{2,1,0:T(8,128)} %copy-done, f32[16,240,128]{2,1,0:T(8,128)} %copy-done.8), custom_call_target="tpu_custom_call" | custom-call | tf_op jit(solution)/shard_map/load_flux/pallas_call | solution.py:668
  49.3 0.0 collective-permute-done.3.refs_4_
  49.4 0.0 copy-start.1
  49.4 2.5 %block_values.1 = (f32[32,5,128]{2,1,0:T(8,128)S(1)}, f32[16,240,128]{2,1,0:T(8,128)S(1)}) custom-call(s32[8,128]{1,0:T(8,128)S(1)} %broadcast_in_dim.12.refs_0_.par_ref, bf16[32,200,128]{2,1,0:T(8,128)(2,1)S(1)} %all-to-all-done.refs_1_.refs_3_, s32[32,128]{1,0:T(8,128)S(1)} %get-tuple-element.32.refs_2_.refs_1_, ...), custom_call_target="tpu_custom_call", output_to_operand_aliasing={{1}: (5, {})} | custom-call | tf_op jit(solution)/shard_map/block_values/pallas_call | solution.py:676
  51.9 14.4 %all_to_all.10.refs_2_ = f32[32,5,128]{2,1,0:T(8,128)S(1)} all-to-all(f32[32,5,128]{2,1,0:T(8,128)S(1)} %get-tuple-element.36), channel_id=1, replica_groups=mesh['rec'=8,'tile'=4] {'rec','tile'}, dimensions={0} | all-to-all | bytes 163840 | tf_op jit(solution)/shard_map/all_to_all | solution.py:689
  66.3 0.0 copy-done.1
  66.3 2.5 %adjoint_field.1 = (f32[1,128]{1,0:T(1,128)S(1)}, f32[2,128]{1,0:T(2,128)S(1)}, f32[16,240,128]{2,1,0:T(8,128)S(1)}) custom-call(s32[8,128]{1,0:T(8,128)S(1)} %broadcast_in_dim.12.refs_0_.par_ref, s32[32,128]{1,0:T(8,128)S(1)} %get-tuple-element.32.refs_2_.refs_1_, f32[32,5,128]{2,1,0:T(8,128)S(1)} %all_to_all.10.refs_2_, ...), custom_call_target="tpu_custom_call" | custom-call | tf_op jit(solution)/shard_map/adjoint_field/pallas_call | solution.py:695
  68.8 0.1 gradient_even.1.after
  68.9 0.7 gradient_pack.1
  69.7 1.5 %collective-permute-start.6 = (f16[4,240,128]{2,1,0:T(8,128)(2,1)S(1)}, f16[4,240,128]{2,1,0:T(8,128)(2,1)S(1)}, u32[]{:S(2)}, u32[]{:S(2)}) collective-permute-start(f16[4,240,128]{2,1,0:T(8,128)(2,1)S(1)} %convert_element_type.14), channel_id=1, source_target_pairs={{0,4},{4,0},{8,12},{12,8},{16,20},{20,16},{24,28},{28,24},{1,5},{5... | collective-permute-start | bytes 737288 | tf_op jit(solution)/shard_map/ppermute | solution.py:614
  71.2 0.1 gradient_odd.1.after
  71.3 2.1 %collective-permute-start.8 = (f16[4,240,128]{2,1,0:T(8,128)(2,1)S(1)}, f16[4,240,128]{2,1,0:T(8,128)(2,1)S(1)}, u32[]{:S(2)}, u32[]{:S(2)}) collective-permute-start(f16[4,240,128]{2,1,0:T(8,128)(2,1)S(1)} %convert_element_type.16), channel_id=1, source_target_pairs={{4,8},{8,4},{12,16},{16,12},{20,24},{24,20},{5,9},{9,5},{13,17},{1... | collective-permute-start | bytes 737288 | tf_op jit(solution)/shard_map/ppermute | solution.py:614
  73.4 1.1 %collective-permute-start.5 = (f32[120,128]{1,0:T(8,128)S(1)}, f32[120,128]{1,0:T(8,128)S(1)}, u32[]{:S(2)}, u32[]{:S(2)}) collective-permute-start(f32[120,128]{1,0:T(8,128)S(1)} %get-tuple-element.41), channel_id=1, source_target_pairs={{1,0},{2,1},{3,2},{0,3},{5,4},{6,5},{7,6},{4,7},{9,8},{10,9},{11,1... | collective-permute-start | bytes 184328 | tf_op jit(solution)/shard_map/ppermute | solution.py:602
  74.6 0.7 collective-permute-start.4
  75.2 2.3 %gradient_local.1.after.local_ref = f32[16,240,128]{2,1,0:T(8,128)S(1)} custom-call(f32[4,240,128]{2,1,0:T(8,128)S(1)} %gradient_odd.1.after, f32[16,240,128]{2,1,0:T(8,128)S(1)} %get-tuple-element.39.refs_3_.field_ref, bf16[240,240]{1,0:T(8,128)(2,1)S(1)} %copy-done.3, bf16[240,240]{1,0:T(8,128)(2,1)S(1)} %copy-done.2, bf16[256,256]{1,0:T(8,128)(2,1)S(1)} %copy-done.4), custom_call_target="tpu_custom_call" | custom-call | tf_op jit(solution)/shard_map/gradient_local/pallas_call | solution.py:605
  77.5 0.0 copy-start.11
  77.5 0.0 copy-start.12
  77.5 0.0 collective-permute-done.5.after_ref
  77.5 0.0 collective-permute-done.4.before_ref
  77.5 0.2 gradient_corners.1
  77.8 0.1 collective-permute-start.7
  77.9 4.3 %collective-permute-start.9 = (f32[64,128]{1,0:T(8,128)S(1)}, f32[64,128]{1,0:T(8,128)S(1)}, u32[]{:S(2)}, u32[]{:S(2)}) collective-permute-start(f32[64,128]{1,0:T(8,128)S(1)} %get-tuple-element.43), channel_id=1, source_target_pairs={{4,8},{8,4},{12,16},{16,12},{20,24},{24,20},{5,9},{9,5},{13,17},{1... | collective-permute-start | bytes 98312 | tf_op jit(solution)/shard_map/ppermute | solution.py:536
  82.1 0.0 collective-permute-done.6
  82.2 0.0 collective-permute-done.8
  82.2 0.7 collective-permute-done.7.corner_ref
  82.9 0.0 copy-done.11
  82.9 2.9 %gradient_sides.1.local_ref = f32[240,16,128]{2,1,0:T(8,128)S(1)} custom-call(s32[8,128]{1,0:T(8,128)S(1)} %broadcast_in_dim.12.refs_0_.par_ref, f32[16,240,128]{2,1,0:T(8,128)S(1)} %gradient_local.1.after.local_ref, f32[120,128]{1,0:T(8,128)S(1)} %collective-permute-done.4.before_ref, f32[120,128]{1,0:T(8,128)S(1)} %collective-permute-done.5.after_ref, ...), custom_call_target="tpu_custom_call" | custom-call | tf_op jit(solution)/shard_map/gradient_sides/pallas_call | solution.py:712
  85.8 0.0 collective-permute-done.9.corner_ref
  85.8 2.6 %gradient.1 = (f32[1,64]{1,0:T(1,128)}, f32[240,16,128]{2,1,0:T(8,128)}) custom-call(s32[8,128]{1,0:T(8,128)S(1)} %broadcast_in_dim.12.refs_0_.par_ref, f32[1,128]{1,0:T(1,128)S(1)} %get-tuple-element.37.model_ref, f32[240,16,128]{2,1,0:T(8,128)S(1)} %gradient_sides.1.local_ref, f32[2,128]{1,0:T(2,128)S(1)} %get-tuple-element.38.refs_1_.refs_2_.factor_ref, ...), custom_call_target="tpu_custom_call" | custom-call | tf_op jit(solution)/shard_map/gradient/pallas_call | solution.py:716
  (17 shorter events, 0.2 us)
Async XLA Ops:
  3.2 44.5 %all-to-all-start = ((bf16[32,200,128]{2,1,0:T(8,128)(2,1)}), bf16[32,200,128]{2,1,0:T(8,128)(2,1)S(1)}, u32[]{:S(2)}, u32[]{:S(2)}) async-start(bf16[32,200,128]{2,1,0:T(8,128)(2,1)} %prepare_blocks.1.after), calls=%async_computation | async-start | bytes 3276800 | tf_op jit(solution)/shard_map/all_to_all | solution.py:640
  9.6 1.5 %copy-start.7 = (f32[240,16,128]{2,1,0:T(8,128)S(1)}, f32[240,16,128]{2,1,0:T(8,128)}, u32[]{:S(2)}) copy-start(f32[240,16,128]{2,1,0:T(8,128)} %control_ref.1) | copy-start | bytes 5898244
  11.1 11.5 %copy-start.2 = (bf16[240,240]{1,0:T(8,128)(2,1)S(1)}, bf16[240,240]{1,0:T(8,128)(2,1)}, u32[]{:S(2)}) copy-start(bf16[240,240]{1,0:T(8,128)(2,1)} %constant.47.clone.time_low) | copy-start | bytes 345604
  11.1 11.5 %copy-start.3 = (bf16[240,240]{1,0:T(8,128)(2,1)S(1)}, bf16[240,240]{1,0:T(8,128)(2,1)}, u32[]{:S(2)}) copy-start(bf16[240,240]{1,0:T(8,128)(2,1)} %constant.46.clone.time_high) | copy-start | bytes 345604
  11.1 11.5 %copy-start.4 = (bf16[256,256]{1,0:T(8,128)(2,1)S(1)}, bf16[256,256]{1,0:T(8,128)(2,1)}, u32[]{:S(2)}) copy-start(bf16[256,256]{1,0:T(8,128)(2,1)} %constant.48.clone.col_both) | copy-start | bytes 393220
  11.1 11.6 %copy-start.13 = (bf16[2,128,512]{2,1,0:T(8,128)(2,1)S(1)}, bf16[2,128,512]{2,1,0:T(8,128)(2,1)}, u32[]{:S(2)}) copy-start(bf16[2,128,512]{2,1,0:T(8,128)(2,1)} %constant.54.clone.beyond_low) | copy-start | bytes 786436
  11.1 11.6 %copy-start.14 = (bf16[2,128,512]{2,1,0:T(8,128)(2,1)S(1)}, bf16[2,128,512]{2,1,0:T(8,128)(2,1)}, u32[]{:S(2)}) copy-start(bf16[2,128,512]{2,1,0:T(8,128)(2,1)} %constant.53.clone.beyond_high) | copy-start | bytes 786436
  12.6 10.1 %collective-permute-start.1 = (f32[120,128]{1,0:T(8,128)S(1)}, f32[120,128]{1,0:T(8,128)S(1)}, u32[]{:S(2)}, u32[]{:S(2)}) collective-permute-start(f32[120,128]{1,0:T(8,128)S(1)} %get-tuple-element.26), channel_id=1, source_target_pairs={{1,0},{2,1},{3,2},{0,3},{5,4},{6,5},{7,6},{4,7},{9,8},{10,9},{11,1... | collective-permute-start | bytes 184328 | tf_op jit(solution)/shard_map/ppermute | solution.py:602
  13.0 9.7 %collective-permute-start = (f32[120,128]{1,0:T(8,128)S(1)}, f32[120,128]{1,0:T(8,128)S(1)}, u32[]{:S(2)}, u32[]{:S(2)}) collective-permute-start(f32[120,128]{1,0:T(8,128)S(1)} %get-tuple-element.24.after), channel_id=1, source_target_pairs={{0,1},{1,2},{2,3},{3,0},{4,5},{5,6},{6,7},{7,4},{8,9},{9,10},{10,1... | collective-permute-start | bytes 184328 | tf_op jit(solution)/shard_map/ppermute | solution.py:602
  24.6 17.0 %collective-permute-start.2 = (bf16[4,240,128]{2,1,0:T(8,128)(2,1)S(1)}, bf16[4,240,128]{2,1,0:T(8,128)(2,1)S(1)}, u32[]{:S(2)}, u32[]{:S(2)}) collective-permute-start(bf16[4,240,128]{2,1,0:T(8,128)(2,1)S(1)} %get-tuple-element.27), channel_id=1, source_target_pairs={{0,4},{4,0},{8,12},{12,8},{16,20},{20,16},{24,28},{28,24},{1,5},{5... | collective-permute-start | bytes 737288 | tf_op jit(solution)/shard_map/ppermute | solution.py:535
  25.8 5.1 %copy-start.15 = (f32[64]{0:T(128)S(1)}, f32[64]{0:T(128)}, u32[]{:S(2)}) copy-start(f32[64]{0:T(128)} %param.28) | copy-start | bytes 772
  25.8 5.1 %copy-start.16 = (f32[64]{0:T(128)S(1)}, f32[64]{0:T(128)}, u32[]{:S(2)}) copy-start(f32[64]{0:T(128)} %param.27) | copy-start | bytes 772
  25.8 5.2 %copy-start.5 = (bf16[128,2048]{1,0:T(8,128)(2,1)S(1)}, bf16[128,2048]{1,0:T(8,128)(2,1)}, u32[]{:S(2)}) copy-start(bf16[128,2048]{1,0:T(8,128)(2,1)} %constant.50.clone.own_low) | copy-start | bytes 1572868
  25.8 5.2 %copy-start.6 = (bf16[128,2048]{1,0:T(8,128)(2,1)S(1)}, bf16[128,2048]{1,0:T(8,128)(2,1)}, u32[]{:S(2)}) copy-start(bf16[128,2048]{1,0:T(8,128)(2,1)} %constant.49.clone.own_high) | copy-start | bytes 1572868
  25.8 23.5 %collective-permute-start.3 = (bf16[4,240,128]{2,1,0:T(8,128)(2,1)S(1)}, bf16[4,240,128]{2,1,0:T(8,128)(2,1)}, u32[]{:S(2)}, u32[]{:S(2)}) collective-permute-start(bf16[4,240,128]{2,1,0:T(8,128)(2,1)S(1)} %get-tuple-element.31), channel_id=1, source_target_pairs={{4,8},{8,4},{12,16},{16,12},{20,24},{24,20},{5,9},{9,5},{13,17},{1... | collective-permute-start | bytes 737288 | tf_op jit(solution)/shard_map/ppermute | solution.py:536
  31.1 10.5 %copy-start.9 = (bf16[240,16,128]{2,1,0:T(8,128)(2,1)S(1)}, bf16[240,16,128]{2,1,0:T(8,128)(2,1)}, u32[]{:S(2)}) copy-start(bf16[240,16,128]{2,1,0:T(8,128)(2,1)} %prior_ref.1) | copy-start | bytes 2949124
  31.1 10.5 %copy-start.10 = (bf16[240,16,128]{2,1,0:T(8,128)(2,1)S(1)}, bf16[240,16,128]{2,1,0:T(8,128)(2,1)}, u32[]{:S(2)}) copy-start(bf16[240,16,128]{2,1,0:T(8,128)(2,1)} %scale_ref.1) | copy-start | bytes 2949124
  44.2 1.3 %copy-start = (f32[16,240,128]{2,1,0:T(8,128)}, f32[16,240,128]{2,1,0:T(8,128)S(1)}, u32[]{:S(2)}) copy-start(f32[16,240,128]{2,1,0:T(8,128)S(1)} %get-tuple-element.28.refs_2_.refs_4_) | copy-start | bytes 5898244
  45.5 1.3 %copy-start.8 = (f32[16,240,128]{2,1,0:T(8,128)}, f32[16,240,128]{2,1,0:T(8,128)S(1)}, u32[]{:S(2)}) copy-start(f32[16,240,128]{2,1,0:T(8,128)S(1)} %get-tuple-element.29.refs_3_) | copy-start | bytes 5898244
  49.4 17.0 %copy-start.1 = (f32[16,240,128]{2,1,0:T(8,128)S(1)}, f32[16,240,128]{2,1,0:T(8,128)}, u32[]{:S(2)}) copy-start(f32[16,240,128]{2,1,0:T(8,128)} %copy-done) | copy-start | bytes 5898244
  69.7 12.4 %collective-permute-start.6 = (f16[4,240,128]{2,1,0:T(8,128)(2,1)S(1)}, f16[4,240,128]{2,1,0:T(8,128)(2,1)S(1)}, u32[]{:S(2)}, u32[]{:S(2)}) collective-permute-start(f16[4,240,128]{2,1,0:T(8,128)(2,1)S(1)} %convert_element_type.14), channel_id=1, source_target_pairs={{0,4},{4,0},{8,12},{12,8},{16,20},{20,16},{24,28},{28,24},{1,5},{5... | collective-permute-start | bytes 737288 | tf_op jit(solution)/shard_map/ppermute | solution.py:614
  71.3 10.9 %collective-permute-start.8 = (f16[4,240,128]{2,1,0:T(8,128)(2,1)S(1)}, f16[4,240,128]{2,1,0:T(8,128)(2,1)S(1)}, u32[]{:S(2)}, u32[]{:S(2)}) collective-permute-start(f16[4,240,128]{2,1,0:T(8,128)(2,1)S(1)} %convert_element_type.16), channel_id=1, source_target_pairs={{4,8},{8,4},{12,16},{16,12},{20,24},{24,20},{5,9},{9,5},{13,17},{1... | collective-permute-start | bytes 737288 | tf_op jit(solution)/shard_map/ppermute | solution.py:614
  73.4 4.1 %collective-permute-start.5 = (f32[120,128]{1,0:T(8,128)S(1)}, f32[120,128]{1,0:T(8,128)S(1)}, u32[]{:S(2)}, u32[]{:S(2)}) collective-permute-start(f32[120,128]{1,0:T(8,128)S(1)} %get-tuple-element.41), channel_id=1, source_target_pairs={{1,0},{2,1},{3,2},{0,3},{5,4},{6,5},{7,6},{4,7},{9,8},{10,9},{11,1... | collective-permute-start | bytes 184328 | tf_op jit(solution)/shard_map/ppermute | solution.py:602
  74.6 3.0 %collective-permute-start.4 = (f32[120,128]{1,0:T(8,128)S(1)}, f32[120,128]{1,0:T(8,128)S(1)}, u32[]{:S(2)}, u32[]{:S(2)}) collective-permute-start(f32[120,128]{1,0:T(8,128)S(1)} %get-tuple-element.40.refs_1_), channel_id=1, source_target_pairs={{0,1},{1,2},{2,3},{3,0},{4,5},{5,6},{6,7},{7,4},{8,9},{9,10},{10,1... | collective-permute-start | bytes 184328 | tf_op jit(solution)/shard_map/ppermute | solution.py:602
  77.5 5.4 %copy-start.11 = (bf16[2,32,512]{2,1,0:T(8,128)(2,1)S(1)}, bf16[2,32,512]{2,1,0:T(8,128)(2,1)}, u32[]{:S(2)}) copy-start(bf16[2,32,512]{2,1,0:T(8,128)(2,1)} %constant.52.clone.corner_low) | copy-start | bytes 196612
  77.5 5.4 %copy-start.12 = (bf16[2,32,512]{2,1,0:T(8,128)(2,1)S(1)}, bf16[2,32,512]{2,1,0:T(8,128)(2,1)}, u32[]{:S(2)}) copy-start(bf16[2,32,512]{2,1,0:T(8,128)(2,1)} %constant.51.clone.corner_high) | copy-start | bytes 196612
  77.8 5.1 %collective-permute-start.7 = (f32[64,128]{1,0:T(8,128)S(1)}, f32[64,128]{1,0:T(8,128)S(1)}, u32[]{:S(2)}, u32[]{:S(2)}) collective-permute-start(f32[64,128]{1,0:T(8,128)S(1)} %get-tuple-element.42), channel_id=1, source_target_pairs={{0,4},{4,0},{8,12},{12,8},{16,20},{20,16},{24,28},{28,24},{1,5},{5... | collective-permute-start | bytes 98312 | tf_op jit(solution)/shard_map/ppermute | solution.py:535
  77.9 8.0 %collective-permute-start.9 = (f32[64,128]{1,0:T(8,128)S(1)}, f32[64,128]{1,0:T(8,128)S(1)}, u32[]{:S(2)}, u32[]{:S(2)}) collective-permute-start(f32[64,128]{1,0:T(8,128)S(1)} %get-tuple-element.43), channel_id=1, source_target_pairs={{4,8},{8,4},{12,16},{16,12},{20,24},{24,20},{5,9},{9,5},{13,17},{1... | collective-permute-start | bytes 98312 | tf_op jit(solution)/shard_map/ppermute | solution.py:536

commit v9 on v8

--- a/solution.py
+++ b/solution.py
@@ -57,22 +57,22 @@
     def strips(row_of, halo_of, targets):
         by_row = banded(np.array(row_of)[:, None] - np.array(targets)[None, :], space, RAD)
         both = by_row[:, :, None] * edge[np.array(halo_of)][:, None, :]
-        return two_parts(both.reshape(len(row_of), -1))
+        high, low = two_parts(both.reshape(len(row_of), -1))
+        return np.concatenate([high, high, low], axis=0)
 
     own = [(row, side * RAD + j) for side in range(2) for row in range(rows) for j in range(RAD)]
-    corner = [], []
+    corner = []
     for first, targets in ((rows, rows - 1 - np.arange(RAD)), (-RAD, np.arange(RAD))):
         lanes = [
             (row, side * RAD + j) for side in range(2) for row in range(first, first + RAD) for j in range(RAD)
         ]
-        for part, value in zip(corner, strips(*zip(*lanes), targets)):
-            part.append(value)
+        corner.append(strips(*zip(*lanes), targets))
     beyond = [strips(*zip(*own), rows + np.arange(RAD)), strips(*zip(*own), -1 - np.arange(RAD))]
     return (
         (time_high, time_low, col_both),
         strips(*zip(*own), np.arange(rows)),
-        [np.stack(c) for c in corner],
-        [np.stack(c) for c in zip(*beyond)],
+        np.stack(corner),
+        np.stack(beyond),
     )
 
 
@@ -186,17 +186,20 @@
 
 
 def prepare_kernel(
-    after, foot_ref, start_ref, row_ref, slot_ref, count_ref, out_ref,
-    blocks_ref, notes_ref, start_vmem, row_vmem, slot_vmem, count_vmem, sems, *, per,
+    after, foot_ref, start_ref, row_ref, slot_ref, count_ref, observed_ref, error_ref, out_ref,
+    blocks_ref, notes_ref, start_vmem, row_vmem, slot_vmem, count_vmem, observed_vmem, error_vmem, sems, *, per,
 ):
     owners, lines, _ = foot_ref.shape
     slots = start_ref.shape[0]
-    pairs = ((start_ref, start_vmem), (row_ref, row_vmem), (slot_ref, slot_vmem), (count_ref, count_vmem))
+    pairs = (
+        (start_ref, start_vmem), (row_ref, row_vmem), (slot_ref, slot_vmem), (count_ref, count_vmem),
+        (observed_ref, observed_vmem), (error_ref, error_vmem),
+    )
     small = [pltpu.make_async_copy(a, b, sems.at[i]) for i, (a, b) in enumerate(pairs)]
     chunk = owners // PARTS
     parts = [slice(i * chunk, (i + 1) * chunk) for i in range(PARTS)]
     loads = [
-        pltpu.make_async_copy(foot_ref.at[here], blocks_ref.at[here], sems.at[4 + i])
+        pltpu.make_async_copy(foot_ref.at[here], blocks_ref.at[here], sems.at[6 + i])
         for i, here in enumerate(parts)
     ]
     for copy in small + loads:
@@ -205,7 +208,7 @@
     for i, here in enumerate(parts):
         loads[i].wait()
         to = out_ref.at[here, 0:lines, :]
-        stores.append(pltpu.make_async_copy(blocks_ref.at[here], to, sems.at[4 + PARTS + i]))
+        stores.append(pltpu.make_async_copy(blocks_ref.at[here], to, sems.at[6 + PARTS + i]))
         stores[-1].start()
     for copy in small:
         copy.wait()
@@ -216,17 +219,33 @@
     ).astype(F32)
     wide = jnp.pad(lanes, ((0, LANES - 4 * slots), (0, LANES - owners)))
     turned = jnp.transpose(wide)[0:owners]
-    notes_ref[...] = jnp.broadcast_to(turned[:, None, :], notes_ref.shape).astype(BF16)
-    stores.append(pltpu.make_async_copy(notes_ref, out_ref.at[:, lines : lines + SUB, :], sems.at[4 + 2 * PARTS]))
+    spare = [jnp.zeros((1, LANES - 2 * per), F32)] if 2 * per < LANES else []
+    own = jnp.concatenate([observed_vmem[...], error_vmem[...]] + spare, axis=1)
+    line = lax.broadcasted_iota(jnp.int32, notes_ref.shape, 1)
+    value = jnp.broadcast_to(turned[:, None, :], notes_ref.shape)
+    for k in range(3):
+        term = own.astype(BF16).astype(F32)
+        own = own - term
+        value = jnp.where(line == 1 + k, term[None], value)
+    notes_ref[...] = value.astype(BF16)
+    stores.append(pltpu.make_async_copy(notes_ref, out_ref.at[:, lines : lines + SUB, :], sems.at[6 + 2 * PARTS]))
     stores[-1].start()
     for copy in stores:
         copy.wait()
 
 
-def halo_sums(parts, high_ref, low_ref, first, width):
-    high, low = parts
-    weights = high_ref[:, first : first + width]
-    return dot(high, weights) + dot(low, weights) + dot(high, low_ref[:, first : first + width])
+def halo_parts(value):
+    high, low = split(value)
+    lanes = [high, low] + ([high] if value.shape[1] < LANES else [])
+    return jnp.concatenate(lanes, axis=1)
+
+
+def halo_sums(both, weights_ref, first, width):
+    used = both.shape[1]
+    out = dot(both, weights_ref[0:used, first : first + width])
+    if used < weights_ref.shape[0]:
+        out = out + dot(both[:, : used // 2], weights_ref[used:, first : first + width])
+    return out
 
 
 def column_sums(value, col_both):
@@ -268,41 +287,25 @@
 
 def strip_halo(par_ref, before_ref, after_ref, time_high, time_low):
     halo = halo_columns(par_ref, before_ref, after_ref)[0 : time_high.shape[0]]
-    return split(time_sums(halo, time_high[...], time_low[...]))
-
-
-def strips_kernel(par_ref, local_ref, before_ref, after_ref, time_high, time_low, own_high, own_low, out_ref):
+    return halo_parts(time_sums(halo, time_high[...], time_low[...]))
+
+
+def strips_kernel(
+    par_ref, local_ref, before_ref, after_ref, time_high, time_low, own_ref, out_ref, *, by_hour
+):
     rows, hours, cols = local_ref.shape
     halo = strip_halo(par_ref, before_ref, after_ref, time_high, time_low)
     for row in range(0, rows, 2):
-        both = halo_sums(halo, own_high, own_low, row * cols, 2 * cols)
-        for k, r in enumerate((row, row + 1)):
-            out_ref[r] = local_ref[r] + both[:, k * cols : (k + 1) * cols]
-
-
-def sides_kernel(
-    par_ref, local_ref, before_ref, after_ref, factor_ref, got_ref, corner_ref,
-    time_high, time_low, col_both, own_high, own_low, corner_high, corner_low, out_ref, halo,
-):
-    rows, hours, cols = local_ref.shape
-    odd = par_ref[0, 0]
-    halo[...] = got_ref[...] * factor_ref[1:2, :]
-    consts = (time_high, time_low, col_both)
-    parts = edge_parts(halo, corner_ref[...], corner_high.at[odd], corner_low.at[odd], consts)
-    at_first = jnp.where(is_odd(par_ref, 0), 1.0, 0.0)
-    strips = strip_halo(par_ref, before_ref, after_ref, time_high, time_low)
-    for row in range(0, rows, 2):
-        both = halo_sums(strips, own_high, own_low, row * cols, 2 * cols)
+        both = halo_sums(halo, own_ref, row * cols, 2 * cols)
         for k, r in enumerate((row, row + 1)):
             value = local_ref[r] + both[:, k * cols : (k + 1) * cols]
-            if r < RAD:
-                value = value + parts[r] * at_first
-            if r >= rows - RAD:
-                value = value + parts[rows - 1 - r] * (1.0 - at_first)
-            out_ref[:, r, :] = value
-
-
-def beyond_sums(rows, corner, corner_high, corner_low, consts):
+            if by_hour:
+                out_ref[:, r, :] = value
+            else:
+                out_ref[r] = value
+
+
+def beyond_sums(rows, corner, corner_weights, consts):
     time_high, time_low, col_both = consts
     cols = col_both.shape[1] // 2
     taps = space_taps()
@@ -315,29 +318,26 @@
                 part = float(taps[RAD + i + j + 1]) * rows(j)
                 summed = part if summed is None else summed + part
             pair.append(column_sums(summed, col_both[...]))
-        value = jnp.concatenate(pair, axis=1) + halo_sums(corner, corner_high, corner_low, k * cols, 2 * cols)
+        value = jnp.concatenate(pair, axis=1) + halo_sums(corner, corner_weights, k * cols, 2 * cols)
         both = time_sums(value, time_high[...], time_low[...])
         parts += [both[:, :cols], both[:, cols:]]
     return parts
 
 
-def edge_parts(halo, corner, corner_high, corner_low, consts):
-    corner = split(unfold_corners(corner)[0 : halo.shape[1], 0 : corner_high.shape[0]])
-    return beyond_sums(lambda j: halo[j], corner, corner_high, corner_low, consts)
+def edge_parts(halo, corner, corner_weights, consts):
+    corner = halo_parts(unfold_corners(corner)[0 : halo.shape[1], 0 : corner_weights.shape[0] // 3])
+    return beyond_sums(lambda j: halo[j], corner, corner_weights, consts)
 
 
 def beyond_kernel(
-    par_ref, field_ref, before_ref, after_ref, time_high, time_low, col_both, beyond_high, beyond_low,
-    out_even, out_odd,
+    par_ref, field_ref, before_ref, after_ref, time_high, time_low, col_both, beyond_ref, out_even, out_odd,
 ):
     rows, hours, _ = field_ref.shape
     odd = is_odd(par_ref, 0)
-    halo = split(halo_columns(par_ref, before_ref, after_ref)[0:hours])
+    halo = halo_parts(halo_columns(par_ref, before_ref, after_ref)[0:hours])
     consts = (time_high, time_low, col_both)
-    to_after = beyond_sums(
-        lambda j: field_ref[rows - 1 - j], halo, beyond_high.at[0], beyond_low.at[0], consts
-    )
-    to_before = beyond_sums(lambda j: field_ref[j], halo, beyond_high.at[1], beyond_low.at[1], consts)
+    to_after = beyond_sums(lambda j: field_ref[rows - 1 - j], halo, beyond_ref.at[0], consts)
+    to_before = beyond_sums(lambda j: field_ref[j], halo, beyond_ref.at[1], consts)
     for k in range(RAD):
         out_even[k] = choose(odd, to_before[k], to_after[k]).astype(BF16)
         out_odd[k] = choose(odd, to_after[k], to_before[k]).astype(BF16)
@@ -358,34 +358,34 @@
 
 
 def finish_kernel(
-    par_ref, model_ref, local_ref, factor_ref, got_ref, corner_ref,
-    time_high, time_low, col_both, corner_high, corner_low,
+    par_ref, model_ref, local_ref, factor_ref, got_e, got_o, corner_e, corner_o,
+    time_high, time_low, col_both, corner_weights,
     model_out, out_ref, halo, edges, total, model_own, sems,
 ):
     hours, rows, cols = local_ref.shape
     half = rows // 2
-    odd = par_ref[0, 0]
-    mine = pl.multiple_of(odd * half, half)
-    rest = pl.multiple_of(half - mine, half)
+    odd = is_odd(par_ref, 0)
+    factor = factor_ref[1:2, :]
+    consts = (time_high, time_low, col_both)
     model_own[...] = model_ref[:, 0 : model_own.shape[1]]
-    copies = [
-        pltpu.make_async_copy(model_own, model_out, sems.at[0]),
-        pltpu.make_async_copy(
-            local_ref.at[:, pl.ds(rest, half), :], out_ref.at[:, pl.ds(rest, half), :], sems.at[1]
-        ),
-    ]
-    for copy in copies:
-        copy.start()
-    halo[...] = got_ref[...] * factor_ref[1:2, :]
-    consts = (time_high, time_low, col_both)
-    parts = edge_parts(halo, corner_ref[...], corner_high.at[1 - odd], corner_low.at[1 - odd], consts)
-    at_last = jnp.where(is_odd(par_ref, 0), 1.0, 0.0)
-    for k, part in enumerate(parts):
-        edges[:, k, :] = part * (1.0 - at_last)
-        edges[:, half - 1 - k, :] = part * at_last
-    total[...] = local_ref[:, pl.ds(mine, half), :] + edges[...]
-    copies.append(pltpu.make_async_copy(total, out_ref.at[:, pl.ds(mine, half), :], sems.at[2]))
-    copies[-1].start()
+    copies = [pltpu.make_async_copy(model_own, model_out, sems.at[2])]
+    copies[0].start()
+    inside = lax.broadcasted_iota(jnp.int32, (hours, half, cols), 1)
+    for side in range(2):
+        before = side == 0
+        for k in range(RAD):
+            even, other = got_e[k], got_o[k]
+            halo[k] = (choose(odd, even, other) if before else choose(odd, other, even)) * factor
+        even, other = corner_e[...], corner_o[...]
+        corner = choose(odd, even, other) if before else choose(odd, other, even)
+        parts = edge_parts(halo, corner, corner_weights.at[1 - side], consts)
+        for k, part in enumerate(parts):
+            edges[:, k if before else half - 1 - k, :] = part
+        here = slice(0, half) if before else slice(rows - half, rows)
+        mine = inside < RAD if before else inside >= half - RAD
+        total[:, here, :] = local_ref[:, here, :] + jnp.where(mine, edges[...], 0.0)
+        copies.append(pltpu.make_async_copy(total.at[:, here, :], out_ref.at[:, here, :], sems.at[side]))
+        copies[-1].start()
     for copy in copies:
         copy.wait()
 
@@ -400,8 +400,9 @@
 def load_kernel(
     par_ref, foot_ref, scale_far, *refs, shift, slots, heights, tiles, per, empty
 ):
-    count = (len(refs) - 3) // 2
-    distant, (table_ref, scale_ref), near = refs[:count], refs[count : count + 2], refs[count + 2 : -1]
+    count = (len(refs) - 4) // 2
+    distant, near = refs[:count], refs[count + 3 : -1]
+    table_ref, seen_ref, scale_ref = refs[count : count + 3]
     sems = refs[-1]
     flux_far, flux_ref = distant[0], near[0]
     rows = flux_ref.shape[0]
@@ -414,7 +415,9 @@
     sources = foot_ref.shape[0]
     base = slots * heights
     lane = lane_ids((sources, LANES))
-    notes = foot_ref[:, base : base + SUB, :].astype(F32)[:, 0, :].astype(jnp.int32)
+    lines = foot_ref[:, base : base + SUB, :].astype(F32)
+    notes = lines[:, 0, :].astype(jnp.int32)
+    seen_ref[...] = lines[:, 1, :] + lines[:, 2, :] + lines[:, 3, :]
     start = notes * 16 + pltpu.roll(notes, LANES - slots, 1)
     offset = start + pltpu.roll(notes, LANES - 2 * slots, 1) * (1 << shift)
     source_rec = lax.broadcasted_iota(jnp.int32, (sources, LANES), 0) // tiles
@@ -425,7 +428,7 @@
 
 
 def forward_kernel(
-    par_ref, foot_ref, table_ref, own_ref, got_far, flux_in, scale_ref,
+    par_ref, foot_ref, table_ref, got_far, flux_in, scale_ref,
     out_ref, flux_ref, got_ref, sums, table_smem, sems, *, shift, slots, heights, tiles, per,
 ):
     load = pltpu.make_async_copy(got_far, got_ref, sems.at[1])
@@ -434,7 +437,7 @@
     sources = foot_ref.shape[0]
     rows = flux_ref.shape[0]
     first = (rows - RAD) * odd
-    groups = out_ref.shape[1] - 1
+    groups = out_ref.shape[1]
     lane = lane_ids((sources, LANES))
     table = table_ref[...]
     copy = pltpu.make_async_copy(table_ref, table_smem, sems.at[0])
@@ -464,18 +467,17 @@
     for q in range(groups):
         total = jnp.sum(totals[q], axis=0, keepdims=True)
         out_ref[:, q : q + 1, :] = jnp.broadcast_to(total[None], (sources, 1, LANES))
-    out_ref[:, groups : groups + 1, :] = jnp.broadcast_to(own_ref[...][None], (sources, 1, LANES))
 
 
 def adjoint_kernel(
-    par_ref, table_vmem, got_ref, foot_ref, scale_ref,
+    par_ref, table_vmem, seen_ref, got_ref, foot_ref, scale_ref,
     model_ref, factor_ref, field_ref,
     weight_vmem, weight_smem, table_ref, sems, *, shift, slots, heights, tiles, per,
 ):
     load = pltpu.make_async_copy(table_vmem, table_ref, sems.at[1])
     load.start()
     sources = foot_ref.shape[0]
-    groups = got_ref.shape[1] - 1
+    groups = got_ref.shape[1]
     rows, hours, _ = field_ref.shape
     model = jnp.sum(got_ref[:, 0:groups, :], axis=0)
     packed = LANES // per
@@ -491,7 +493,8 @@
     for q in range(groups):
         observed, error = jnp.zeros((1, LANES), F32), jnp.ones((1, LANES), F32)
         for k in range(packed):
-            line = got_ref[(q * packed + k) * tiles, groups : groups + 1, :]
+            source = (q * packed + k) * tiles
+            line = seen_ref[source : source + 1, :]
             here = (lane >= k * per) & (lane < (k + 1) * per)
             observed = jnp.where(here, line if k == 0 else pltpu.roll(line, k * per, 1), observed)
             turn = (k * per - per) % LANES
@@ -587,9 +590,9 @@
     par = jnp.broadcast_to(par[:, None], (SUB, LANES))
     base, own_parts, corner_parts, beyond_parts = constants(hours, rows, cols)
     base = [jnp.asarray(c) for c in base]
-    own_parts = [jnp.asarray(c) for c in own_parts]
-    corner_parts = [jnp.asarray(c) for c in corner_parts]
-    beyond_parts = [jnp.asarray(c) for c in beyond_parts]
+    own_parts = jnp.asarray(own_parts)
+    corner_parts = jnp.asarray(corner_parts)
+    beyond_parts = jnp.asarray(beyond_parts)
     strip = array(-(-hours // (2 * SUB)) * SUB, LANES)
     corner = array(-(-hours // (4 * SUB)) * SUB, LANES)
     block = array(RAD, hours, cols)
@@ -606,6 +609,13 @@
         corners = call(far_corner_kernel, [corner, corner], [VM] * 4, [], name + "_corners")(par, local, *got_strips)
         return local, swap("rec", *corners)
 
+    def strip_sums(local, got_strips, by_hour, name):
+        def kernel(*refs):
+            strips_kernel(*refs, by_hour=by_hour)
+
+        shape = array(hours, rows, cols) if by_hour else field_shape
+        return call(kernel, shape, [VM] * 7, [], name)(par, local, *got_strips, *base[:2], own_parts)
+
     def swap_rows(even, after, factor, field, name):
         def kernel(*refs):
             rows_kernel(*refs, even=even)
@@ -621,12 +631,13 @@
     sent = call(
         prepare,
         jax.ShapeDtypeStruct((devices, lines, cols), BF16),
-        [VM] + [HB] * 5,
+        [VM] + [HB] * 7,
         [
             pltpu.VMEM((devices, slots * heights, cols), BF16),
             pltpu.VMEM((devices, SUB, LANES), BF16),
             numbers, numbers, numbers, pltpu.VMEM((1, devices), jnp.int32),
-            pltpu.SemaphoreType.DMA((5 + 2 * PARTS,)),
+            pltpu.VMEM((1, per), F32), pltpu.VMEM((1, per), F32),
+            pltpu.SemaphoreType.DMA((7 + 2 * PARTS,)),
         ],
         "prepare_blocks",
         out_specs=HB,
@@ -634,7 +645,7 @@
         far(x)
         for x in (
             footprint.reshape(devices, slots * heights, cols),
-            start_hour.T, grid_row.T, receptor_slot.T, slot_count[None],
+            start_hour.T, grid_row.T, receptor_slot.T, slot_count[None], observed[None], obs_error[None],
         )
     ])
     foot = lax.all_to_all(sent, AXES, split_axis=0, concat_axis=0, tiled=True)
@@ -644,18 +655,15 @@
     got_strips = pass_strips(*strips)
     local = call(local_kernel, field_shape, [VM] * 5, [], "control_local")(strips[0], field, *base)
     small = jax.ShapeDtypeStruct((RAD, hours, cols), BF16)
-    sent_even, sent_odd = call(beyond_kernel, [small, small], [VM] * 9, [], "control_beyond")(
-        par, field, *got_strips, *base, *beyond_parts
+    sent_even, sent_odd = call(beyond_kernel, [small, small], [VM] * 8, [], "control_beyond")(
+        par, field, *got_strips, *base, beyond_parts
     )
     got_even, got_odd = swap("rec", sent_even, sent_odd)
-    local = call(strips_kernel, field_shape, [VM] * 8, [], "control_strips")(
-        par, local, *got_strips, *base[:2], *own_parts
-    )
+    local = strip_sums(local, got_strips, False, "control_strips")
     flux, scale = call(
         flux_kernel, [field_shape, field_shape], [VM] * 5, [pltpu.VMEM((hours, rows, cols), F32)], "flux_field"
     )(par, local, prior_flux, flux_scale, got_even)
 
-    own = jnp.concatenate([observed, obs_error, jnp.zeros((LANES - 2 * per,), F32)])[None]
     sizes = dict(shift=shift, slots=slots, heights=heights, tiles=n_tile, per=per)
 
     def forward(*refs):
@@ -665,9 +673,9 @@
     def load(*refs):
         load_kernel(*refs, empty=groups * LANES, **sizes)
 
-    table, scale_near, flux_near = call(
+    table, seen, scale_near, flux_near = call(
         load,
-        [jax.ShapeDtypeStruct((devices, LANES), jnp.int32), block, field_shape],
+        [jax.ShapeDtypeStruct((devices, LANES), jnp.int32), array(devices, LANES), block, field_shape],
         [VM, VM, HB, HB],
         [pltpu.SemaphoreType.DMA((1 + rows // RAD,))],
         "load_flux",
@@ -675,8 +683,8 @@
     table, got_odd = lax.optimization_barrier((table, got_odd))
     partial, _ = call(
         forward,
-        [array(devices, groups + 1, LANES), field_shape],
-        [VM] * 4 + [HB] + [VM] * 2,
+        [array(devices, groups, LANES), field_shape],
+        [VM] * 3 + [HB] + [VM] * 2,
         [
             pltpu.VMEM((RAD, hours, cols), BF16),
             pltpu.VMEM((slots, devices, LANES), F32),
@@ -684,8 +692,8 @@
             pltpu.SemaphoreType.DMA((2,)),
         ],
         "block_values",
-        alias={5: 1},
-    )(par, foot, table, own, far(got_odd), flux_near, scale_near)
+        alias={4: 1},
+    )(par, foot, table, far(got_odd), flux_near, scale_near)
     everyone = lax.all_to_all(partial, AXES, split_axis=0, concat_axis=0, tiled=True)
 
     def adjoint(*refs):
@@ -695,7 +703,7 @@
     model, factor, field = call(
         adjoint,
         [array(1, LANES), array(2, LANES), field_shape],
-        [VM] * 5,
+        [VM] * 6,
         [
             pltpu.VMEM((weight_rows, LANES), F32),
             pltpu.SMEM((weight_rows, LANES), F32),
@@ -703,24 +711,27 @@
             pltpu.SemaphoreType.DMA((2,)),
         ],
         "adjoint_field",
-    )(par, table, everyone, foot, scale)
+    )(par, table, seen, everyone, foot, scale)
     sent_even, got_even = swap_rows(True, factor, factor, field, "gradient_even")
     strips = call(strip_kernel, [strip, strip], [VM] * 2, [], "gradient_pack")(sent_even, field)
     got_strips = pass_strips(*strips)
     sent_odd, got_odd = swap_rows(False, strips[0], factor, field, "gradient_odd")
     local, got_corners = swaps(sent_odd, field, got_strips, "gradient")
-    local = call(sides_kernel, array(hours, rows, cols), [VM] * 14, [row_scratch], "gradient_sides")(
-        par, local, *got_strips, factor, got_even.astype(F32), got_corners[0], *base, *own_parts, *corner_parts
-    )
-    wide = pltpu.VMEM((hours, rows // 2, cols), F32)
+    local = strip_sums(local, got_strips, True, "gradient_strips")
     model_co2, gradient = call(
         finish_kernel,
         [array(1, per), array(hours, rows, cols)],
-        [VM] * 11,
-        [row_scratch, wide, wide, pltpu.VMEM((1, per), F32), pltpu.SemaphoreType.DMA((3,))],
+        [VM] * 12,
+        [
+            row_scratch,
+            pltpu.VMEM((hours, rows // 2, cols), F32),
+            pltpu.VMEM((hours, rows, cols), F32),
+            pltpu.VMEM((1, per), F32),
+            pltpu.SemaphoreType.DMA((3,)),
+        ],
         "gradient",
         out_specs=[HB, HB],
-    )(par, model, local, factor, got_odd.astype(F32), got_corners[1], *base, *corner_parts)
+    )(par, model, local, factor, got_even.astype(F32), got_odd.astype(F32), *got_corners, *base, corner_parts)
     return (model_co2.reshape(-1), gradient)
 
 

time: 90.4 us -> 88.7 us (0.981)
  the two profiles are of different devices: /device:TPU:5 before, /device:TPU:12 now
where the time goes in v9:
time: 88.7 us; the launch traced here: 88.3 us
  Pallas kernels  27.1 us (31%)
  waiting for transfers between devices  23.7 us (27%)
  starting transfers between devices  22.4 us (25%)
  blocking collectives  9.57 us (11%)
  local copies, waits for them, and re-layouts  4.31 us (5%)
  between operations  1.09 us (1%)
    all_to_all x1, blocking collectives, per_device(): lax.all_to_all(partial, AXES, split_axis=0, concat_axis=0, tiled=True)  9.57 us
    ppermute x2, starting transfers between devices, swap(): lax.ppermute(odd, axis, swap_pairs(count, True))  8.08 us
    ppermute x2, waiting for transfers between devices, swap(): lax.ppermute(odd, axis, swap_pairs(count, True))  7.23 us
    ppermute x2, waiting for transfers between devices, pass_strips(): lax.ppermute(first, 'tile', back)  6 us
    all_to_all x1, starting transfers between devices, per_device(): foot = lax.all_to_all(sent, AXES, split_axis=0, concat_axis=0, tiled=True)  6 us
    all_to_all x1, waiting for transfers between devices, per_device(): foot = lax.all_to_all(sent, AXES, split_axis=0, concat_axis=0, tiled=True)  4.81 us
    unnamed x26, local copies, waits for them, and re-layouts  4.15 us
    ppermute x2, starting transfers between devices, swap_rows(): lax.ppermute(sent.astype(F16), 'rec', swap_pairs(n_rec, not even))  4.04 us
  transfers between devices with their start and end apart: 11, of which 7 were waited for; matrix products, arithmetic and copies ran while one was open for 0% of the time, Pallas kernels for 18%

profile of v9, /device:TPU:12, one launch (start us, length us, event | category | flops | bytes accessed | tf_op | source)
XLA Modules:
  0.0 88.3 jit_solution(13266938875662452930)
XLA Ops:
  0.7 0.1 stack.27
  0.7 0.1 broadcast_in_dim.15.refs_0_.par_ref
  0.8 2.4 %prepare_blocks.1.after = bf16[32,200,128]{2,1,0:T(8,128)(2,1)} custom-call(s32[8,128]{1,0:T(8,128)S(1)} %broadcast_in_dim.15.refs_0_.par_ref, bf16[32,192,128]{2,1,0:T(8,128)(2,1)} %bitcast.12, s32[8,32]{1,0:T(8,128)} %bitcast.13, s32[8,32]{1,0:T(8,128)} %bitcast.14, s32[8,32]{1,0:T(8,128)} %bitcast.15, s32[1,32]{1,0:T(1,128)} %bitcast.16, ...), custom_call_target="tpu_custom_call" | custom-call | tf_op jit(solution)/shard_map/prepare_blocks/pallas_call | solution.py:631
  3.2 6.0 %all-to-all-start = ((bf16[32,200,128]{2,1,0:T(8,128)(2,1)}), bf16[32,200,128]{2,1,0:T(8,128)(2,1)S(1)}, u32[]{:S(2)}, u32[]{:S(2)}) async-start(bf16[32,200,128]{2,1,0:T(8,128)(2,1)} %prepare_blocks.1.after), calls=%async_computation | async-start | bytes 3276800 | tf_op jit(solution)/shard_map/all_to_all | solution.py:651
  9.2 0.0 copy-start.7
  9.2 1.5 %copy-done.7 = f32[240,16,128]{2,1,0:T(8,128)S(1)} copy-done((f32[240,16,128]{2,1,0:T(8,128)S(1)}, f32[240,16,128]{2,1,0:T(8,128)}, u32[]{:S(2)}) %copy-start.7) | copy-done | bytes 1966104
  10.8 0.0 copy-start.3
  10.8 0.0 copy-start.4
  10.8 0.0 copy-start.5
  10.8 0.0 copy-start.11
  10.8 1.5 %turn_control.1 = (f32[16,240,128]{2,1,0:T(8,128)S(1)}, f32[120,128]{1,0:T(8,128)S(1)}, f32[120,128]{1,0:T(8,128)S(1)}) custom-call(bf16[32,200,128]{2,1,0:T(8,128)(2,1)} %prepare_blocks.1.after, f32[240,16,128]{2,1,0:T(8,128)S(1)} %copy-done.7), custom_call_target="tpu_custom_call" | custom-call | tf_op jit(solution)/shard_map/turn_control/pallas_call | solution.py:652
  12.2 1.3 %collective-permute-start.1 = (f32[120,128]{1,0:T(8,128)S(1)}, f32[120,128]{1,0:T(8,128)S(1)}, u32[]{:S(2)}, u32[]{:S(2)}) collective-permute-start(f32[120,128]{1,0:T(8,128)S(1)} %get-tuple-element.27), channel_id=1, source_target_pairs={{1,0},{2,1},{3,2},{0,3},{5,4},{6,5},{7,6},{4,7},{9,8},{10,9},{11,1... | collective-permute-start | bytes 184328 | tf_op jit(solution)/shard_map/ppermute | solution.py:605
  13.5 0.0 collective-permute-start
  13.5 6.0 %collective-permute-done.1.refs_3_.after_ref = f32[120,128]{1,0:T(8,128)S(1)} collective-permute-done((f32[120,128]{1,0:T(8,128)S(1)}, f32[120,128]{1,0:T(8,128)S(1)}, u32[]{:S(2)}, u32[]{:S(2)}) %collective-permute-start.1) | collective-permute-done | bytes 61472 | tf_op jit(solution)/shard_map/ppermute | solution.py:605
  19.5 1.8 %collective-permute-done.refs_2_.before_ref = f32[120,128]{1,0:T(8,128)S(1)} collective-permute-done((f32[120,128]{1,0:T(8,128)S(1)}, f32[120,128]{1,0:T(8,128)S(1)}, u32[]{:S(2)}, u32[]{:S(2)}) %collective-permute-start) | collective-permute-done | bytes 61472 | tf_op jit(solution)/shard_map/ppermute | solution.py:605
  21.3 0.0 copy-done.3
  21.3 0.0 copy-done.4
  21.3 0.0 copy-done.5
  21.3 0.0 copy-done.11
  21.3 2.7 %control_beyond.1 = (bf16[4,240,128]{2,1,0:T(8,128)(2,1)S(1)}, bf16[4,240,128]{2,1,0:T(8,128)(2,1)}) custom-call(s32[8,128]{1,0:T(8,128)S(1)} %broadcast_in_dim.15.refs_0_.par_ref, f32[16,240,128]{2,1,0:T(8,128)S(1)} %get-tuple-element.26.field_ref, f32[120,128]{1,0:T(8,128)S(1)} %collective-permute-done.refs_2_.before_ref, ...), custom_call_target="tpu_custom_call" | custom-call | tf_op jit(solution)/shard_map/control_beyond/pallas_call | solution.py:658
  24.0 0.1 collective-permute-start.2
  24.1 0.0 copy-start.2
  24.1 6.0 %collective-permute-start.3 = (bf16[4,240,128]{2,1,0:T(8,128)(2,1)}, bf16[4,240,128]{2,1,0:T(8,128)(2,1)}, u32[]{:S(2)}, u32[]{:S(2)}) collective-permute-start(bf16[4,240,128]{2,1,0:T(8,128)(2,1)} %get-tuple-element.32), channel_id=1, source_target_pairs={{4,8},{8,4},{12,16},{16,12},{20,24},{24,20},{5,9},{9,5},{13,17},{1... | collective-permute-start | bytes 737288 | tf_op jit(solution)/shard_map/ppermute | solution.py:539
  30.1 2.3 %control_local.1.refs_1_ = f32[16,240,128]{2,1,0:T(8,128)S(1)} custom-call(f32[120,128]{1,0:T(8,128)S(1)} %get-tuple-element.25.after, f32[16,240,128]{2,1,0:T(8,128)S(1)} %get-tuple-element.26.field_ref, bf16[240,240]{1,0:T(8,128)(2,1)S(1)} %copy-done.4, bf16[240,240]{1,0:T(8,128)(2,1)S(1)} %copy-done.3, bf16[256,256]{1,0:T(8,128)(2,1)S(1)} %copy-done.5), custom_call_target="tpu_custom_call" | custom-call | tf_op jit(solution)/shard_map/control_local/pallas_call | solution.py:656
  32.5 0.0 copy-done.2
  32.5 0.0 copy-start.9
  32.5 0.0 copy-start.10
  32.5 1.1 %control_strips.1.local_ref = f32[16,240,128]{2,1,0:T(8,128)S(1)} custom-call(s32[8,128]{1,0:T(8,128)S(1)} %broadcast_in_dim.15.refs_0_.par_ref, f32[16,240,128]{2,1,0:T(8,128)S(1)} %control_local.1.refs_1_, f32[120,128]{1,0:T(8,128)S(1)} %collective-permute-done.refs_2_.before_ref, f32[120,128]{1,0:T(8,128)S(1)} %collective-permute-done.1.refs_3_.after_ref, ...), custom_call_target="tpu_custom_call" | custom-call | tf_op jit(solution)/shard_map/control_strips/pallas_call | solution.py:617
  33.6 2.7 %collective-permute-done.2.got_ref = bf16[4,240,128]{2,1,0:T(8,128)(2,1)S(1)} collective-permute-done((bf16[4,240,128]{2,1,0:T(8,128)(2,1)S(1)}, bf16[4,240,128]{2,1,0:T(8,128)(2,1)S(1)}, u32[]{:S(2)}, u32[]{:S(2)}) %collective-permute-start.2) | collective-permute-done | bytes 245792 | tf_op jit(solution)/shard_map/ppermute | solution.py:538
  36.3 0.0 copy-done.9
  36.3 0.0 copy-done.10
  36.3 2.6 %flux_field.1 = (f32[16,240,128]{2,1,0:T(8,128)S(1)}, f32[16,240,128]{2,1,0:T(8,128)S(1)}) custom-call(s32[8,128]{1,0:T(8,128)S(1)} %broadcast_in_dim.15.refs_0_.par_ref, f32[16,240,128]{2,1,0:T(8,128)S(1)} %control_strips.1.local_ref, bf16[240,16,128]{2,1,0:T(8,128)(2,1)S(1)} %copy-done.9, bf16[240,16,128]{2,1,0:T(8,128)(2,1)S(1)} %copy-done.10, ...), custom_call_target="tpu_custom_call" | custom-call | tf_op jit(solution)/shard_map/flux_field/pallas_call | solution.py:663
  38.9 0.0 copy-start
  38.9 1.3 %copy-done = f32[16,240,128]{2,1,0:T(8,128)} copy-done((f32[16,240,128]{2,1,0:T(8,128)}, f32[16,240,128]{2,1,0:T(8,128)S(1)}, u32[]{:S(2)}) %copy-start) | copy-done | bytes 1966104
  40.2 1.3 %copy-done.8 = f32[16,240,128]{2,1,0:T(8,128)} copy-done((f32[16,240,128]{2,1,0:T(8,128)}, f32[16,240,128]{2,1,0:T(8,128)S(1)}, u32[]{:S(2)}) %copy-start.8) | copy-done | bytes 1966104
  41.5 4.8 %all-to-all-done.refs_1_.refs_4_ = bf16[32,200,128]{2,1,0:T(8,128)(2,1)S(1)} async-done(((bf16[32,200,128]{2,1,0:T(8,128)(2,1)}), bf16[32,200,128]{2,1,0:T(8,128)(2,1)S(1)}, u32[]{:S(2)}, u32[]{:S(2)}) %all-to-all-start) | async-done | bytes 1638432 | tf_op jit(solution)/shard_map/all_to_all | solution.py:651
  46.3 1.7 %load_flux.1 = (s32[32,128]{1,0:T(8,128)S(1)}, f32[32,128]{1,0:T(8,128)S(1)}, f32[4,240,128]{2,1,0:T(8,128)S(1)}, f32[16,240,128]{2,1,0:T(8,128)S(1)}) custom-call(s32[8,128]{1,0:T(8,128)S(1)} %broadcast_in_dim.15.refs_0_.par_ref, bf16[32,200,128]{2,1,0:T(8,128)(2,1)S(1)} %all-to-all-done.refs_1_.refs_4_, f32[16,240,128]{2,1,0:T(8,128)} %copy-done, ...), custom_call_target="tpu_custom_call" | custom-call | tf_op jit(solution)/shard_map/load_flux/pallas_call | solution.py:676
  48.0 4.4 %collective-permute-done.3.refs_3_ = bf16[4,240,128]{2,1,0:T(8,128)(2,1)} collective-permute-done((bf16[4,240,128]{2,1,0:T(8,128)(2,1)}, bf16[4,240,128]{2,1,0:T(8,128)(2,1)}, u32[]{:S(2)}, u32[]{:S(2)}) %collective-permute-start.3) | collective-permute-done | bytes 245792 | tf_op jit(solution)/shard_map/ppermute | solution.py:539
  52.4 2.5 %block_values.1 = (f32[32,4,128]{2,1,0:T(4,128)S(1)}, f32[16,240,128]{2,1,0:T(8,128)S(1)}) custom-call(s32[8,128]{1,0:T(8,128)S(1)} %broadcast_in_dim.15.refs_0_.par_ref, bf16[32,200,128]{2,1,0:T(8,128)(2,1)S(1)} %all-to-all-done.refs_1_.refs_4_, s32[32,128]{1,0:T(8,128)S(1)} %get-tuple-element.33.refs_2_.refs_1_, ...), custom_call_target="tpu_custom_call", output_to_operand_aliasing={{1}: (4, {})} | custom-call | tf_op jit(solution)/shard_map/block_values/pallas_call | solution.py:684
  54.8 9.6 %all_to_all.10.refs_3_ = f32[32,4,128]{2,1,0:T(4,128)S(1)} all-to-all(f32[32,4,128]{2,1,0:T(4,128)S(1)} %get-tuple-element.38), channel_id=1, replica_groups=mesh['rec'=8,'tile'=4] {'rec','tile'}, dimensions={0} | all-to-all | bytes 131072 | tf_op jit(solution)/shard_map/all_to_all | solution.py:697
  64.4 0.0 copy-done.1
  64.4 2.5 %adjoint_field.1 = (f32[1,128]{1,0:T(1,128)S(1)}, f32[2,128]{1,0:T(2,128)S(1)}, f32[16,240,128]{2,1,0:T(8,128)S(1)}) custom-call(s32[8,128]{1,0:T(8,128)S(1)} %broadcast_in_dim.15.refs_0_.par_ref, s32[32,128]{1,0:T(8,128)S(1)} %get-tuple-element.33.refs_2_.refs_1_, f32[32,128]{1,0:T(8,128)S(1)} %get-tuple-element.34.refs_2_, ...), custom_call_target="tpu_custom_call" | custom-call | tf_op jit(solution)/shard_map/adjoint_field/pallas_call | solution.py:703
  67.0 0.1 gradient_even.1.after
  67.0 0.7 gradient_pack.1
  67.8 0.0 copy-start.6
  67.8 1.5 %collective-permute-start.6 = (f16[4,240,128]{2,1,0:T(8,128)(2,1)S(1)}, f16[4,240,128]{2,1,0:T(8,128)(2,1)S(1)}, u32[]{:S(2)}, u32[]{:S(2)}) collective-permute-start(f16[4,240,128]{2,1,0:T(8,128)(2,1)S(1)} %convert_element_type.14), channel_id=1, source_target_pairs={{0,4},{4,0},{8,12},{12,8},{16,20},{20,16},{24,28},{28,24},{1,5},{5... | collective-permute-start | bytes 737288 | tf_op jit(solution)/shard_map/ppermute | solution.py:624
  69.3 0.1 gradient_odd.1.after
  69.4 2.5 %collective-permute-start.7 = (f16[4,240,128]{2,1,0:T(8,128)(2,1)S(1)}, f16[4,240,128]{2,1,0:T(8,128)(2,1)S(1)}, u32[]{:S(2)}, u32[]{:S(2)}) collective-permute-start(f16[4,240,128]{2,1,0:T(8,128)(2,1)S(1)} %convert_element_type.16), channel_id=1, source_target_pairs={{4,8},{8,4},{12,16},{16,12},{20,24},{24,20},{5,9},{9,5},{13,17},{1... | collective-permute-start | bytes 737288 | tf_op jit(solution)/shard_map/ppermute | solution.py:624
  72.0 0.1 collective-permute-start.5
  72.0 0.5 collective-permute-start.4
  72.5 0.0 copy-done.6
  72.5 2.3 %gradient_local.1.refs_1_.after = f32[16,240,128]{2,1,0:T(8,128)S(1)} custom-call(f32[4,240,128]{2,1,0:T(8,128)S(1)} %gradient_odd.1.after, f32[16,240,128]{2,1,0:T(8,128)S(1)} %get-tuple-element.41.refs_3_.field_ref, bf16[240,240]{1,0:T(8,128)(2,1)S(1)} %copy-done.4, bf16[240,240]{1,0:T(8,128)(2,1)S(1)} %copy-done.3, bf16[256,256]{1,0:T(8,128)(2,1)S(1)} %copy-done.6), custom_call_target="tpu_custom_call" | custom-call | tf_op jit(solution)/shard_map/gradient_local/pallas_call | solution.py:608
  74.8 0.0 collective-permute-done.5.refs_3_.after_ref
  74.8 1.2 %collective-permute-done.4.refs_2_.before_ref = f32[120,128]{1,0:T(8,128)S(1)} collective-permute-done((f32[120,128]{1,0:T(8,128)S(1)}, f32[120,128]{1,0:T(8,128)S(1)}, u32[]{:S(2)}, u32[]{:S(2)}) %collective-permute-start.4) | collective-permute-done | bytes 61472 | tf_op jit(solution)/shard_map/ppermute | solution.py:605
  76.0 0.2 gradient_corners.1
  76.2 2.4 %collective-permute-start.8 = (f32[64,128]{1,0:T(8,128)S(1)}, f32[64,128]{1,0:T(8,128)S(1)}, u32[]{:S(2)}, u32[]{:S(2)}) collective-permute-start(f32[64,128]{1,0:T(8,128)S(1)} %get-tuple-element.44), channel_id=1, source_target_pairs={{0,4},{4,0},{8,12},{12,8},{16,20},{20,16},{24,28},{28,24},{1,5},{5... | collective-permute-start | bytes 98312 | tf_op jit(solution)/shard_map/ppermute | solution.py:538
  78.6 2.0 %collective-permute-start.9 = (f32[64,128]{1,0:T(8,128)S(1)}, f32[64,128]{1,0:T(8,128)S(1)}, u32[]{:S(2)}, u32[]{:S(2)}) collective-permute-start(f32[64,128]{1,0:T(8,128)S(1)} %get-tuple-element.45), channel_id=1, source_target_pairs={{4,8},{8,4},{12,16},{16,12},{20,24},{24,20},{5,9},{9,5},{13,17},{1... | collective-permute-start | bytes 98312 | tf_op jit(solution)/shard_map/ppermute | solution.py:539
  80.7 1.8 %gradient_strips.1.local_ref = f32[240,16,128]{2,1,0:T(8,128)S(1)} custom-call(s32[8,128]{1,0:T(8,128)S(1)} %broadcast_in_dim.15.refs_0_.par_ref, f32[16,240,128]{2,1,0:T(8,128)S(1)} %gradient_local.1.refs_1_.after, f32[120,128]{1,0:T(8,128)S(1)} %collective-permute-done.4.refs_2_.before_ref, f32[120,128]{1,0:T(8,128)S(1)} %collective-permute-done.5.refs_3_.after_ref, ...), custom_call_target="tpu_custom_call" | custom-call | tf_op jit(solution)/shard_map/gradient_strips/pallas_call | solution.py:617
  82.5 0.0 collective-permute-done.6
  82.5 0.0 collective-permute-done.7
  82.6 0.0 collective-permute-done.8.corner_e
  82.6 2.9 %collective-permute-done.9.corner_o = f32[64,128]{1,0:T(8,128)S(1)} collective-permute-done((f32[64,128]{1,0:T(8,128)S(1)}, f32[64,128]{1,0:T(8,128)S(1)}, u32[]{:S(2)}, u32[]{:S(2)}) %collective-permute-start.9) | collective-permute-done | bytes 32800 | tf_op jit(solution)/shard_map/ppermute | solution.py:539
  85.4 0.0 copy-done.12
  85.4 2.7 %gradient.1 = (f32[1,64]{1,0:T(1,128)}, f32[240,16,128]{2,1,0:T(8,128)}) custom-call(s32[8,128]{1,0:T(8,128)S(1)} %broadcast_in_dim.15.refs_0_.par_ref, f32[1,128]{1,0:T(1,128)S(1)} %get-tuple-element.39.model_ref, f32[240,16,128]{2,1,0:T(8,128)S(1)} %gradient_strips.1.local_ref, f32[2,128]{1,0:T(2,128)S(1)} %get-tuple-element.40.refs_1_.refs_2_.factor_ref, ...), custom_call_target="tpu_custom_call" | custom-call | tf_op jit(solution)/shard_map/gradient/pallas_call | solution.py:721
  (8 shorter events, 0.1 us)
Async XLA Ops:
  3.2 43.1 %all-to-all-start = ((bf16[32,200,128]{2,1,0:T(8,128)(2,1)}), bf16[32,200,128]{2,1,0:T(8,128)(2,1)S(1)}, u32[]{:S(2)}, u32[]{:S(2)}) async-start(bf16[32,200,128]{2,1,0:T(8,128)(2,1)} %prepare_blocks.1.after), calls=%async_computation | async-start | bytes 3276800 | tf_op jit(solution)/shard_map/all_to_all | solution.py:651
  9.2 1.5 %copy-start.7 = (f32[240,16,128]{2,1,0:T(8,128)S(1)}, f32[240,16,128]{2,1,0:T(8,128)}, u32[]{:S(2)}) copy-start(f32[240,16,128]{2,1,0:T(8,128)} %control_ref.1) | copy-start | bytes 5898244
  10.8 10.6 %copy-start.3 = (bf16[240,240]{1,0:T(8,128)(2,1)S(1)}, bf16[240,240]{1,0:T(8,128)(2,1)}, u32[]{:S(2)}) copy-start(bf16[240,240]{1,0:T(8,128)(2,1)} %constant.41.clone.time_low.refs_5_) | copy-start | bytes 345604
  10.8 10.6 %copy-start.4 = (bf16[240,240]{1,0:T(8,128)(2,1)S(1)}, bf16[240,240]{1,0:T(8,128)(2,1)}, u32[]{:S(2)}) copy-start(bf16[240,240]{1,0:T(8,128)(2,1)} %constant.40.clone.time_high.refs_4_) | copy-start | bytes 345604
  10.8 10.6 %copy-start.5 = (bf16[256,256]{1,0:T(8,128)(2,1)S(1)}, bf16[256,256]{1,0:T(8,128)(2,1)}, u32[]{:S(2)}) copy-start(bf16[256,256]{1,0:T(8,128)(2,1)} %constant.42.clone.col_both) | copy-start | bytes 393220
  10.8 10.6 %copy-start.11 = (bf16[2,384,512]{2,1,0:T(8,128)(2,1)S(1)}, bf16[2,384,512]{2,1,0:T(8,128)(2,1)}, u32[]{:S(2)}) copy-start(bf16[2,384,512]{2,1,0:T(8,128)(2,1)} %constant.45.clone.beyond_ref) | copy-start | bytes 2359300
  12.2 7.3 %collective-permute-start.1 = (f32[120,128]{1,0:T(8,128)S(1)}, f32[120,128]{1,0:T(8,128)S(1)}, u32[]{:S(2)}, u32[]{:S(2)}) collective-permute-start(f32[120,128]{1,0:T(8,128)S(1)} %get-tuple-element.27), channel_id=1, source_target_pairs={{1,0},{2,1},{3,2},{0,3},{5,4},{6,5},{7,6},{4,7},{9,8},{10,9},{11,1... | collective-permute-start | bytes 184328 | tf_op jit(solution)/shard_map/ppermute | solution.py:605
  13.5 7.8 %collective-permute-start = (f32[120,128]{1,0:T(8,128)S(1)}, f32[120,128]{1,0:T(8,128)S(1)}, u32[]{:S(2)}, u32[]{:S(2)}) collective-permute-start(f32[120,128]{1,0:T(8,128)S(1)} %get-tuple-element.25.after), channel_id=1, source_target_pairs={{0,1},{1,2},{2,3},{3,0},{4,5},{5,6},{6,7},{7,4},{8,9},{9,10},{10,1... | collective-permute-start | bytes 184328 | tf_op jit(solution)/shard_map/ppermute | solution.py:605
  24.0 12.3 %collective-permute-start.2 = (bf16[4,240,128]{2,1,0:T(8,128)(2,1)S(1)}, bf16[4,240,128]{2,1,0:T(8,128)(2,1)S(1)}, u32[]{:S(2)}, u32[]{:S(2)}) collective-permute-start(bf16[4,240,128]{2,1,0:T(8,128)(2,1)S(1)} %get-tuple-element.28), channel_id=1, source_target_pairs={{0,4},{4,0},{8,12},{12,8},{16,20},{20,16},{24,28},{28,24},{1,5},{5... | collective-permute-start | bytes 737288 | tf_op jit(solution)/shard_map/ppermute | solution.py:538
  24.1 8.4 %copy-start.2 = (bf16[384,2048]{1,0:T(8,128)(2,1)S(1)}, bf16[384,2048]{1,0:T(8,128)(2,1)}, u32[]{:S(2)}) copy-start(bf16[384,2048]{1,0:T(8,128)(2,1)} %constant.43.clone.refs_6_) | copy-start | bytes 4718596
  24.1 28.3 %collective-permute-start.3 = (bf16[4,240,128]{2,1,0:T(8,128)(2,1)}, bf16[4,240,128]{2,1,0:T(8,128)(2,1)}, u32[]{:S(2)}, u32[]{:S(2)}) collective-permute-start(bf16[4,240,128]{2,1,0:T(8,128)(2,1)} %get-tuple-element.32), channel_id=1, source_target_pairs={{4,8},{8,4},{12,16},{16,12},{20,24},{24,20},{5,9},{9,5},{13,17},{1... | collective-permute-start | bytes 737288 | tf_op jit(solution)/shard_map/ppermute | solution.py:539
  32.5 3.8 %copy-start.9 = (bf16[240,16,128]{2,1,0:T(8,128)(2,1)S(1)}, bf16[240,16,128]{2,1,0:T(8,128)(2,1)}, u32[]{:S(2)}) copy-start(bf16[240,16,128]{2,1,0:T(8,128)(2,1)} %prior_ref.1) | copy-start | bytes 2949124
  32.5 3.8 %copy-start.10 = (bf16[240,16,128]{2,1,0:T(8,128)(2,1)S(1)}, bf16[240,16,128]{2,1,0:T(8,128)(2,1)}, u32[]{:S(2)}) copy-start(bf16[240,16,128]{2,1,0:T(8,128)(2,1)} %scale_ref.1) | copy-start | bytes 2949124
  38.9 1.3 %copy-start = (f32[16,240,128]{2,1,0:T(8,128)}, f32[16,240,128]{2,1,0:T(8,128)S(1)}, u32[]{:S(2)}) copy-start(f32[16,240,128]{2,1,0:T(8,128)S(1)} %get-tuple-element.29.refs_2_.refs_5_) | copy-start | bytes 5898244
  40.2 1.3 %copy-start.8 = (f32[16,240,128]{2,1,0:T(8,128)}, f32[16,240,128]{2,1,0:T(8,128)S(1)}, u32[]{:S(2)}) copy-start(f32[16,240,128]{2,1,0:T(8,128)S(1)} %get-tuple-element.30.refs_3_) | copy-start | bytes 5898244
  52.4 12.1 %copy-start.1 = (f32[16,240,128]{2,1,0:T(8,128)S(1)}, f32[16,240,128]{2,1,0:T(8,128)}, u32[]{:S(2)}) copy-start(f32[16,240,128]{2,1,0:T(8,128)} %copy-done) | copy-start | bytes 5898244
  67.8 4.8 %copy-start.6 = (bf16[256,256]{1,0:T(8,128)(2,1)S(1)}, bf16[256,256]{1,0:T(8,128)(2,1)}, u32[]{:S(2)}) copy-start(bf16[256,256]{1,0:T(8,128)(2,1)} %constant.42.clone.col_both) | copy-start | bytes 393220
  67.8 14.6 %collective-permute-start.6 = (f16[4,240,128]{2,1,0:T(8,128)(2,1)S(1)}, f16[4,240,128]{2,1,0:T(8,128)(2,1)S(1)}, u32[]{:S(2)}, u32[]{:S(2)}) collective-permute-start(f16[4,240,128]{2,1,0:T(8,128)(2,1)S(1)} %convert_element_type.14), channel_id=1, source_target_pairs={{0,4},{4,0},{8,12},{12,8},{16,20},{20,16},{24,28},{28,24},{1,5},{5... | collective-permute-start | bytes 737288 | tf_op jit(solution)/shard_map/ppermute | solution.py:624
  69.4 13.1 %collective-permute-start.7 = (f16[4,240,128]{2,1,0:T(8,128)(2,1)S(1)}, f16[4,240,128]{2,1,0:T(8,128)(2,1)S(1)}, u32[]{:S(2)}, u32[]{:S(2)}) collective-permute-start(f16[4,240,128]{2,1,0:T(8,128)(2,1)S(1)} %convert_element_type.16), channel_id=1, source_target_pairs={{4,8},{8,4},{12,16},{16,12},{20,24},{24,20},{5,9},{9,5},{13,17},{1... | collective-permute-start | bytes 737288 | tf_op jit(solution)/shard_map/ppermute | solution.py:624
  72.0 2.9 %collective-permute-start.5 = (f32[120,128]{1,0:T(8,128)S(1)}, f32[120,128]{1,0:T(8,128)S(1)}, u32[]{:S(2)}, u32[]{:S(2)}) collective-permute-start(f32[120,128]{1,0:T(8,128)S(1)} %get-tuple-element.43), channel_id=1, source_target_pairs={{1,0},{2,1},{3,2},{0,3},{5,4},{6,5},{7,6},{4,7},{9,8},{10,9},{11,1... | collective-permute-start | bytes 184328 | tf_op jit(solution)/shard_map/ppermute | solution.py:605
  72.0 4.0 %collective-permute-start.4 = (f32[120,128]{1,0:T(8,128)S(1)}, f32[120,128]{1,0:T(8,128)S(1)}, u32[]{:S(2)}, u32[]{:S(2)}) collective-permute-start(f32[120,128]{1,0:T(8,128)S(1)} %get-tuple-element.42.refs_1_), channel_id=1, source_target_pairs={{0,1},{1,2},{2,3},{3,0},{4,5},{5,6},{6,7},{7,4},{8,9},{9,10},{10,1... | collective-permute-start | bytes 184328 | tf_op jit(solution)/shard_map/ppermute | solution.py:605
  76.2 6.3 %collective-permute-start.8 = (f32[64,128]{1,0:T(8,128)S(1)}, f32[64,128]{1,0:T(8,128)S(1)}, u32[]{:S(2)}, u32[]{:S(2)}) collective-permute-start(f32[64,128]{1,0:T(8,128)S(1)} %get-tuple-element.44), channel_id=1, source_target_pairs={{0,4},{4,0},{8,12},{12,8},{16,20},{20,16},{24,28},{28,24},{1,5},{5... | collective-permute-start | bytes 98312 | tf_op jit(solution)/shard_map/ppermute | solution.py:538
  78.6 6.8 %copy-start.12 = (bf16[2,96,512]{2,1,0:T(8,128)(2,1)S(1)}, bf16[2,96,512]{2,1,0:T(8,128)(2,1)}, u32[]{:S(2)}) copy-start(bf16[2,96,512]{2,1,0:T(8,128)(2,1)} %constant.44.clone.corner_weights) | copy-start | bytes 589828
  78.6 6.8 %collective-permute-start.9 = (f32[64,128]{1,0:T(8,128)S(1)}, f32[64,128]{1,0:T(8,128)S(1)}, u32[]{:S(2)}, u32[]{:S(2)}) collective-permute-start(f32[64,128]{1,0:T(8,128)S(1)} %get-tuple-element.45), channel_id=1, source_target_pairs={{4,8},{8,4},{12,16},{16,12},{20,24},{24,20},{5,9},{9,5},{13,17},{1... | collective-permute-start | bytes 98312 | tf_op jit(solution)/shard_map/ppermute | solution.py:539

commit v10 on v9

--- a/solution.py
+++ b/solution.py
@@ -357,35 +357,51 @@
         flux_ref[row] = flux_ref[row] + scale_out[row] * got_ref[k].astype(F32)
 
 
+def even_kernel(
+    par_ref, local_ref, factor_ref, got_ref, corner_ref, time_high, time_low, col_both, corner_weights,
+    out_ref, halo,
+):
+    rows, hours, cols = local_ref.shape
+    odd = par_ref[0, 0]
+    for row in range(RAD, rows - RAD):
+        out_ref[:, row, :] = local_ref[row]
+    halo[...] = got_ref[...] * factor_ref[1:2, :]
+    consts = (time_high, time_low, col_both)
+    parts = edge_parts(halo, corner_ref[...], corner_weights.at[odd], consts)
+    at_first = jnp.where(is_odd(par_ref, 0), 1.0, 0.0)
+    for k, part in enumerate(parts):
+        out_ref[:, k, :] = local_ref[k] + part * at_first
+        out_ref[:, rows - 1 - k, :] = local_ref[rows - 1 - k] + part * (1.0 - at_first)
+
+
 def finish_kernel(
-    par_ref, model_ref, local_ref, factor_ref, got_e, got_o, corner_e, corner_o,
+    par_ref, model_ref, local_ref, factor_ref, got_ref, corner_ref,
     time_high, time_low, col_both, corner_weights,
     model_out, out_ref, halo, edges, total, model_own, sems,
 ):
     hours, rows, cols = local_ref.shape
     half = rows // 2
-    odd = is_odd(par_ref, 0)
-    factor = factor_ref[1:2, :]
+    odd = par_ref[0, 0]
+    mine = pl.multiple_of(odd * half, half)
+    rest = pl.multiple_of(half - mine, half)
+    model_own[...] = model_ref[:, 0 : model_own.shape[1]]
+    copies = [
+        pltpu.make_async_copy(model_own, model_out, sems.at[0]),
+        pltpu.make_async_copy(
+            local_ref.at[:, pl.ds(rest, half), :], out_ref.at[:, pl.ds(rest, half), :], sems.at[1]
+        ),
+    ]
+    for copy in copies:
+        copy.start()
+    halo[...] = got_ref[...] * factor_ref[1:2, :]
     consts = (time_high, time_low, col_both)
-    model_own[...] = model_ref[:, 0 : model_own.shape[1]]
-    copies = [pltpu.make_async_copy(model_own, model_out, sems.at[2])]
-    copies[0].start()
-    inside = lax.broadcasted_iota(jnp.int32, (hours, half, cols), 1)
-    for side in range(2):
-        before = side == 0
-        for k in range(RAD):
-            even, other = got_e[k], got_o[k]
-            halo[k] = (choose(odd, even, other) if before else choose(odd, other, even)) * factor
-        even, other = corner_e[...], corner_o[...]
-        corner = choose(odd, even, other) if before else choose(odd, other, even)
-        parts = edge_parts(halo, corner, corner_weights.at[1 - side], consts)
-        for k, part in enumerate(parts):
-            edges[:, k if before else half - 1 - k, :] = part
-        here = slice(0, half) if before else slice(rows - half, rows)
-        mine = inside < RAD if before else inside >= half - RAD
-        total[:, here, :] = local_ref[:, here, :] + jnp.where(mine, edges[...], 0.0)
-        copies.append(pltpu.make_async_copy(total.at[:, here, :], out_ref.at[:, here, :], sems.at[side]))
-        copies[-1].start()
+    parts = edge_parts(halo, corner_ref[...], corner_weights.at[1 - odd], consts)
+    for k, part in enumerate(parts):
+        edges[:, jnp.where(odd == 1, half - 1 - k, k), :] = part
+    inside = lax.broadcasted_iota(jnp.int32, edges.shape, 1) // RAD
+    total[...] = local_ref[:, pl.ds(mine, half), :] + jnp.where(inside == odd, edges[...], 0.0)
+    copies.append(pltpu.make_async_copy(total, out_ref.at[:, pl.ds(mine, half), :], sems.at[2]))
+    copies[-1].start()
     for copy in copies:
         copy.wait()
 
@@ -471,10 +487,10 @@
 
 def adjoint_kernel(
     par_ref, table_vmem, seen_ref, got_ref, foot_ref, scale_ref,
-    model_ref, factor_ref, field_ref,
-    weight_vmem, weight_smem, table_ref, sems, *, shift, slots, heights, tiles, per,
-):
-    load = pltpu.make_async_copy(table_vmem, table_ref, sems.at[1])
+    model_ref, factor_ref, field_ref, rows_even, last_ref, first_ref,
+    weight_rows, table_ref, sem, *, shift, slots, heights, tiles, per,
+):
+    load = pltpu.make_async_copy(table_vmem, table_ref, sem)
     load.start()
     sources = foot_ref.shape[0]
     groups = got_ref.shape[1]
@@ -489,7 +505,7 @@
             line = line if k == 0 else pltpu.roll(line, LANES - k * per, 1)
             own = choose(par_ref[2:3, :] == q * packed + k, line, own)
     model_ref[...] = own
-    weight_vmem[...] = jnp.zeros_like(weight_vmem)
+    weights = []
     for q in range(groups):
         observed, error = jnp.zeros((1, LANES), F32), jnp.ones((1, LANES), F32)
         for k in range(packed):
@@ -499,30 +515,39 @@
             observed = jnp.where(here, line if k == 0 else pltpu.roll(line, k * per, 1), observed)
             turn = (k * per - per) % LANES
             error = jnp.where(here, line if turn == 0 else pltpu.roll(line, turn, 1), error)
-        weight_vmem[q : q + 1, :] = (model[q : q + 1, :] - observed) / (error * error)
-    copy = pltpu.make_async_copy(weight_vmem, weight_smem, sems.at[0])
-    copy.start()
+        weights.append((model[q : q + 1, :] - observed) / (error * error))
+    lanes = lane_ids((sources, LANES))
+    table = table_vmem[...]
+    for c in range(slots):
+        which = table[:, 3 * slots + c : 3 * slots + c + 1]
+        found = jnp.zeros((sources, LANES), F32)
+        for q in range(groups):
+            found = jnp.where(which == lanes + q * LANES, weights[q], found)
+        weight_rows[c] = jnp.broadcast_to(jnp.sum(found, axis=1, keepdims=True), (sources, LANES))
     field_ref[...] = jnp.zeros_like(field_ref)
-    top = jnp.max(jnp.abs(weight_vmem[...]), keepdims=True) * (FOOT_MAX * SCALE_MAX * sources * slots)
+    largest = jnp.abs(weights[0])
+    for weight in weights[1:]:
+        largest = jnp.maximum(largest, jnp.abs(weight))
+    top = jnp.max(largest, keepdims=True) * (FOOT_MAX * SCALE_MAX * sources * slots)
     top = jnp.maximum(top, 1e-25)
     factor_ref[0:1, :] = jnp.broadcast_to(HALF_TOP / top, (1, LANES))
     factor_ref[1:2, :] = jnp.broadcast_to(top * (1.0 / HALF_TOP), (1, LANES))
     load.wait()
-    copy.wait()
 
     def body(source, carry):
         for c, block in blocks_of(foot_ref, source, heights, slots):
             offset = table_ref[source, c]
-            receptor = table_ref[source, 3 * slots + c]
             row = lax.shift_right_logical(offset, shift)
             begin = jnp.bitwise_and(offset, (1 << shift) - 1)
-            weight = weight_smem[lax.shift_right_logical(receptor, 7), jnp.bitwise_and(receptor, LANES - 1)]
+            weight = weight_rows[c, pl.ds(source, 1), :]
             field_ref[row, pl.ds(begin, heights), :] += block * weight
         return carry
 
     lax.fori_loop(0, sources, body, 0)
     for row in range(rows):
         field_ref[row] = field_ref[row] * scale_ref[row]
+    rows_kernel(par_ref, None, factor_ref, field_ref, rows_even, even=True)
+    write_strips(field_ref, last_ref, first_ref)
 
 
 def swap_pairs(count, odd):
@@ -699,39 +724,34 @@
     def adjoint(*refs):
         adjoint_kernel(*refs, **sizes)
 
-    weight_rows = -(-(groups + 1) // SUB) * SUB
-    model, factor, field = call(
+    model, factor, field, sent_even, *strips = call(
         adjoint,
-        [array(1, LANES), array(2, LANES), field_shape],
+        [array(1, LANES), array(2, LANES), field_shape, block, strip, strip],
         [VM] * 6,
         [
-            pltpu.VMEM((weight_rows, LANES), F32),
-            pltpu.SMEM((weight_rows, LANES), F32),
+            pltpu.VMEM((slots, devices, LANES), F32),
             pltpu.SMEM((devices, LANES), jnp.int32),
-            pltpu.SemaphoreType.DMA((2,)),
+            pltpu.SemaphoreType.DMA,
         ],
         "adjoint_field",
     )(par, table, seen, everyone, foot, scale)
-    sent_even, got_even = swap_rows(True, factor, factor, field, "gradient_even")
-    strips = call(strip_kernel, [strip, strip], [VM] * 2, [], "gradient_pack")(sent_even, field)
+    got_even = lax.ppermute(sent_even.astype(F16), "rec", swap_pairs(n_rec, False))
     got_strips = pass_strips(*strips)
     sent_odd, got_odd = swap_rows(False, strips[0], factor, field, "gradient_odd")
     local, got_corners = swaps(sent_odd, field, got_strips, "gradient")
-    local = strip_sums(local, got_strips, True, "gradient_strips")
+    local = strip_sums(local, got_strips, False, "gradient_strips")
+    local = call(even_kernel, array(hours, rows, cols), [VM] * 9, [row_scratch], "gradient_with_even")(
+        par, local, factor, got_even.astype(F32), got_corners[0], *base, corner_parts
+    )
+    wide = pltpu.VMEM((hours, rows // 2, cols), F32)
     model_co2, gradient = call(
         finish_kernel,
         [array(1, per), array(hours, rows, cols)],
-        [VM] * 12,
-        [
-            row_scratch,
-            pltpu.VMEM((hours, rows // 2, cols), F32),
-            pltpu.VMEM((hours, rows, cols), F32),
-            pltpu.VMEM((1, per), F32),
-            pltpu.SemaphoreType.DMA((3,)),
-        ],
+        [VM] * 10,
+        [row_scratch, wide, wide, pltpu.VMEM((1, per), F32), pltpu.SemaphoreType.DMA((3,))],
         "gradient",
         out_specs=[HB, HB],
-    )(par, model, local, factor, got_even.astype(F32), got_odd.astype(F32), *got_corners, *base, corner_parts)
+    )(par, model, local, factor, got_odd.astype(F32), got_corners[1], *base, corner_parts)
     return (model_co2.reshape(-1), gradient)
 
 

time: 88.7 us -> 87.9 us (level)
  the two profiles are of different devices: /device:TPU:12 before, /device:TPU:5 now
where the time goes in v10:
time: 87.9 us; the launch traced here: 86.3 us
  Pallas kernels  27.4 us (31%)
  starting transfers between devices  21.7 us (25%)
  waiting for transfers between devices  18 us (20%)
  blocking collectives  13.7 us (16%)
  local copies, waits for them, and re-layouts  4.32 us (5%)
  between operations  1.12 us (1%)
    all_to_all x1, blocking collectives, per_device(): lax.all_to_all(partial, AXES, split_axis=0, concat_axis=0, tiled=True)  13.7 us
    ppermute x2, waiting for transfers between devices, swap(): lax.ppermute(even, axis, swap_pairs(count, False))  9.32 us
    ppermute x2, waiting for transfers between devices, pass_strips(): lax.ppermute(first, 'tile', back)  8.33 us
    ppermute x2, starting transfers between devices, swap(): lax.ppermute(odd, axis, swap_pairs(count, True))  6.9 us
    all_to_all x1, starting transfers between devices, per_device(): foot = lax.all_to_all(sent, AXES, split_axis=0, concat_axis=0, tiled=True)  6.42 us
    unnamed x26, local copies, waits for them, and re-layouts  4.16 us
    pallas_call x1, Pallas kernels, per_device(): call(adjoint, [array(1, LANES), array(2, LANES), field_shape, block, stri...  2.82 us
    pallas_call x1, Pallas kernels, per_device(): call(beyond_kernel, [small, small], [VM] * 8, [], 'control_beyond')  2.67 us
  transfers between devices with their start and end apart: 11, of which 4 were waited for; matrix products, arithmetic and copies ran while one was open for 0% of the time, Pallas kernels for 20%

profile of v10, /device:TPU:5, one launch (start us, length us, event | category | flops | bytes accessed | tf_op | source)
XLA Modules:
  0.0 86.3 jit_solution(1569807975789428458)
XLA Ops:
  0.7 0.1 stack.27
  0.7 0.1 broadcast_in_dim.15.refs_0_.par_ref
  0.8 2.4 %prepare_blocks.1.after = bf16[32,200,128]{2,1,0:T(8,128)(2,1)} custom-call(s32[8,128]{1,0:T(8,128)S(1)} %broadcast_in_dim.15.refs_0_.par_ref, bf16[32,192,128]{2,1,0:T(8,128)(2,1)} %bitcast.12, s32[8,32]{1,0:T(8,128)} %bitcast.13, s32[8,32]{1,0:T(8,128)} %bitcast.14, s32[8,32]{1,0:T(8,128)} %bitcast.15, s32[1,32]{1,0:T(1,128)} %bitcast.16, ...), custom_call_target="tpu_custom_call" | custom-call | tf_op jit(solution)/shard_map/prepare_blocks/pallas_call | solution.py:656
  3.2 6.4 %all-to-all-start = ((bf16[32,200,128]{2,1,0:T(8,128)(2,1)}), bf16[32,200,128]{2,1,0:T(8,128)(2,1)S(1)}, u32[]{:S(2)}, u32[]{:S(2)}) async-start(bf16[32,200,128]{2,1,0:T(8,128)(2,1)} %prepare_blocks.1.after), calls=%async_computation | async-start | bytes 3276800 | tf_op jit(solution)/shard_map/all_to_all | solution.py:676
  9.6 0.0 copy-start.7
  9.7 1.5 %copy-done.7 = f32[240,16,128]{2,1,0:T(8,128)S(1)} copy-done((f32[240,16,128]{2,1,0:T(8,128)S(1)}, f32[240,16,128]{2,1,0:T(8,128)}, u32[]{:S(2)}) %copy-start.7) | copy-done | bytes 1966104
  11.2 0.0 copy-start.3
  11.2 0.0 copy-start.4
  11.2 0.0 copy-start.5
  11.2 0.0 copy-start.12
  11.2 1.5 %turn_control.1 = (f32[16,240,128]{2,1,0:T(8,128)S(1)}, f32[120,128]{1,0:T(8,128)S(1)}, f32[120,128]{1,0:T(8,128)S(1)}) custom-call(bf16[32,200,128]{2,1,0:T(8,128)(2,1)} %prepare_blocks.1.after, f32[240,16,128]{2,1,0:T(8,128)S(1)} %copy-done.7), custom_call_target="tpu_custom_call" | custom-call | tf_op jit(solution)/shard_map/turn_control/pallas_call | solution.py:677
  12.7 0.4 collective-permute-start.1
  13.1 1.4 %collective-permute-start = (f32[120,128]{1,0:T(8,128)S(1)}, f32[120,128]{1,0:T(8,128)S(1)}, u32[]{:S(2)}, u32[]{:S(2)}) collective-permute-start(f32[120,128]{1,0:T(8,128)S(1)} %get-tuple-element.26.after), channel_id=1, source_target_pairs={{0,1},{1,2},{2,3},{3,0},{4,5},{5,6},{6,7},{7,4},{8,9},{9,10},{10,1... | collective-permute-start | bytes 184328 | tf_op jit(solution)/shard_map/ppermute | solution.py:630
  14.5 8.3 %collective-permute-done.1.refs_3_.after_ref = f32[120,128]{1,0:T(8,128)S(1)} collective-permute-done((f32[120,128]{1,0:T(8,128)S(1)}, f32[120,128]{1,0:T(8,128)S(1)}, u32[]{:S(2)}, u32[]{:S(2)}) %collective-permute-start.1) | collective-permute-done | bytes 61472 | tf_op jit(solution)/shard_map/ppermute | solution.py:630
  22.7 0.0 collective-permute-done.refs_2_.before_ref
  22.7 0.0 copy-done.3
  22.7 0.0 copy-done.4
  22.7 0.0 copy-done.5
  22.8 0.0 copy-done.12
  22.8 2.7 %control_beyond.1 = (bf16[4,240,128]{2,1,0:T(8,128)(2,1)S(1)}, bf16[4,240,128]{2,1,0:T(8,128)(2,1)}) custom-call(s32[8,128]{1,0:T(8,128)S(1)} %broadcast_in_dim.15.refs_0_.par_ref, f32[16,240,128]{2,1,0:T(8,128)S(1)} %get-tuple-element.27.field_ref, f32[120,128]{1,0:T(8,128)S(1)} %collective-permute-done.refs_2_.before_ref, ...), custom_call_target="tpu_custom_call" | custom-call | tf_op jit(solution)/shard_map/control_beyond/pallas_call | solution.py:683
  25.4 1.2 %collective-permute-start.2 = (bf16[4,240,128]{2,1,0:T(8,128)(2,1)S(1)}, bf16[4,240,128]{2,1,0:T(8,128)(2,1)S(1)}, u32[]{:S(2)}, u32[]{:S(2)}) collective-permute-start(bf16[4,240,128]{2,1,0:T(8,128)(2,1)S(1)} %get-tuple-element.29), channel_id=1, source_target_pairs={{0,4},{4,0},{8,12},{12,8},{16,20},{20,16},{24,28},{28,24},{1,5},{5... | collective-permute-start | bytes 737288 | tf_op jit(solution)/shard_map/ppermute | solution.py:563
  26.6 2.8 %collective-permute-start.3 = (bf16[4,240,128]{2,1,0:T(8,128)(2,1)}, bf16[4,240,128]{2,1,0:T(8,128)(2,1)}, u32[]{:S(2)}, u32[]{:S(2)}) collective-permute-start(bf16[4,240,128]{2,1,0:T(8,128)(2,1)} %get-tuple-element.33), channel_id=1, source_target_pairs={{4,8},{8,4},{12,16},{16,12},{20,24},{24,20},{5,9},{9,5},{13,17},{1... | collective-permute-start | bytes 737288 | tf_op jit(solution)/shard_map/ppermute | solution.py:564
  29.4 2.3 %control_local.1.refs_1_ = f32[16,240,128]{2,1,0:T(8,128)S(1)} custom-call(f32[120,128]{1,0:T(8,128)S(1)} %get-tuple-element.26.after, f32[16,240,128]{2,1,0:T(8,128)S(1)} %get-tuple-element.27.field_ref, bf16[240,240]{1,0:T(8,128)(2,1)S(1)} %copy-done.4, bf16[240,240]{1,0:T(8,128)(2,1)S(1)} %copy-done.3, bf16[256,256]{1,0:T(8,128)(2,1)S(1)} %copy-done.5), custom_call_target="tpu_custom_call" | custom-call | tf_op jit(solution)/shard_map/control_local/pallas_call | solution.py:681
  31.7 0.0 copy-done.2
  31.7 0.0 copy-start.9
  31.7 0.0 copy-start.10
  31.7 1.1 %control_strips.1.local_ref = f32[16,240,128]{2,1,0:T(8,128)S(1)} custom-call(s32[8,128]{1,0:T(8,128)S(1)} %broadcast_in_dim.15.refs_0_.par_ref, f32[16,240,128]{2,1,0:T(8,128)S(1)} %control_local.1.refs_1_, f32[120,128]{1,0:T(8,128)S(1)} %collective-permute-done.refs_2_.before_ref, f32[120,128]{1,0:T(8,128)S(1)} %collective-permute-done.1.refs_3_.after_ref, ...), custom_call_target="tpu_custom_call" | custom-call | tf_op jit(solution)/shard_map/control_strips/pallas_call | solution.py:642
  32.9 9.3 %collective-permute-done.2.got_ref = bf16[4,240,128]{2,1,0:T(8,128)(2,1)S(1)} collective-permute-done((bf16[4,240,128]{2,1,0:T(8,128)(2,1)S(1)}, bf16[4,240,128]{2,1,0:T(8,128)(2,1)S(1)}, u32[]{:S(2)}, u32[]{:S(2)}) %collective-permute-start.2) | collective-permute-done | bytes 245792 | tf_op jit(solution)/shard_map/ppermute | solution.py:563
  42.2 0.0 copy-done.9
  42.2 0.0 copy-done.10
  42.2 2.6 %flux_field.1 = (f32[16,240,128]{2,1,0:T(8,128)S(1)}, f32[16,240,128]{2,1,0:T(8,128)S(1)}) custom-call(s32[8,128]{1,0:T(8,128)S(1)} %broadcast_in_dim.15.refs_0_.par_ref, f32[16,240,128]{2,1,0:T(8,128)S(1)} %control_strips.1.local_ref, bf16[240,16,128]{2,1,0:T(8,128)(2,1)S(1)} %copy-done.9, bf16[240,16,128]{2,1,0:T(8,128)(2,1)S(1)} %copy-done.10, ...), custom_call_target="tpu_custom_call" | custom-call | tf_op jit(solution)/shard_map/flux_field/pallas_call | solution.py:688
  44.8 0.0 copy-start
  44.8 1.3 %copy-done = f32[16,240,128]{2,1,0:T(8,128)} copy-done((f32[16,240,128]{2,1,0:T(8,128)}, f32[16,240,128]{2,1,0:T(8,128)S(1)}, u32[]{:S(2)}) %copy-start) | copy-done | bytes 1966104
  46.1 1.3 %copy-done.8 = f32[16,240,128]{2,1,0:T(8,128)} copy-done((f32[16,240,128]{2,1,0:T(8,128)}, f32[16,240,128]{2,1,0:T(8,128)S(1)}, u32[]{:S(2)}) %copy-start.8) | copy-done | bytes 1966104
  47.4 0.3 all-to-all-done.refs_1_.refs_4_
  47.7 1.7 %load_flux.1 = (s32[32,128]{1,0:T(8,128)S(1)}, f32[32,128]{1,0:T(8,128)S(1)}, f32[4,240,128]{2,1,0:T(8,128)S(1)}, f32[16,240,128]{2,1,0:T(8,128)S(1)}) custom-call(s32[8,128]{1,0:T(8,128)S(1)} %broadcast_in_dim.15.refs_0_.par_ref, bf16[32,200,128]{2,1,0:T(8,128)(2,1)S(1)} %all-to-all-done.refs_1_.refs_4_, f32[16,240,128]{2,1,0:T(8,128)} %copy-done, ...), custom_call_target="tpu_custom_call" | custom-call | tf_op jit(solution)/shard_map/load_flux/pallas_call | solution.py:701
  49.4 0.0 collective-permute-done.3.refs_3_
  49.4 0.0 copy-start.1
  49.4 2.5 %block_values.1 = (f32[32,4,128]{2,1,0:T(4,128)S(1)}, f32[16,240,128]{2,1,0:T(8,128)S(1)}) custom-call(s32[8,128]{1,0:T(8,128)S(1)} %broadcast_in_dim.15.refs_0_.par_ref, bf16[32,200,128]{2,1,0:T(8,128)(2,1)S(1)} %all-to-all-done.refs_1_.refs_4_, s32[32,128]{1,0:T(8,128)S(1)} %get-tuple-element.34.refs_2_.refs_1_, ...), custom_call_target="tpu_custom_call", output_to_operand_aliasing={{1}: (4, {})} | custom-call | tf_op jit(solution)/shard_map/block_values/pallas_call | solution.py:709
  51.9 13.7 %all_to_all.10.refs_3_ = f32[32,4,128]{2,1,0:T(4,128)S(1)} all-to-all(f32[32,4,128]{2,1,0:T(4,128)S(1)} %get-tuple-element.39), channel_id=1, replica_groups=mesh['rec'=8,'tile'=4] {'rec','tile'}, dimensions={0} | all-to-all | bytes 131072 | tf_op jit(solution)/shard_map/all_to_all | solution.py:722
  65.6 0.0 copy-done.1
  65.6 2.8 %adjoint_field.1 = (f32[1,128]{1,0:T(1,128)S(1)}, f32[2,128]{1,0:T(2,128)S(1)}, f32[16,240,128]{2,1,0:T(8,128)S(1)}, f32[4,240,128]{2,1,0:T(8,128)S(1)}, f32[120,128]{1,0:T(8,128)S(1)}, /*index=5*/f32[120,128]{1,0:T(8,128)S(1)}) custom-call(s32[8,128]{1,0:T(8,128)S(1)} %broadcast_in_dim.15.refs_0_.par_ref, s32[32,128]{1,0:T(8,128)S(1)} %get-tuple-element.34.refs_2_.refs_1_, ...), custom_call_target="tpu_custom_call" | custom-call | tf_op jit(solution)/shard_map/adjoint_field/pallas_call | solution.py:727
  68.4 0.0 copy-start.6
  68.5 1.3 %collective-permute-start.6 = (f16[4,240,128]{2,1,0:T(8,128)(2,1)S(1)}, f16[4,240,128]{2,1,0:T(8,128)(2,1)S(1)}, u32[]{:S(2)}, u32[]{:S(2)}) collective-permute-start(f16[4,240,128]{2,1,0:T(8,128)(2,1)S(1)} %convert_element_type.14), channel_id=1, source_target_pairs={{0,4},{4,0},{8,12},{12,8},{16,20},{20,16},{24,28},{28,24},{1,5},{5... | collective-permute-start | bytes 737288 | tf_op jit(solution)/shard_map/ppermute | solution.py:738
  69.8 0.1 gradient_odd.1.after
  69.9 2.2 %collective-permute-start.8 = (f16[4,240,128]{2,1,0:T(8,128)(2,1)S(1)}, f16[4,240,128]{2,1,0:T(8,128)(2,1)S(1)}, u32[]{:S(2)}, u32[]{:S(2)}) collective-permute-start(f16[4,240,128]{2,1,0:T(8,128)(2,1)S(1)} %convert_element_type.16), channel_id=1, source_target_pairs={{4,8},{8,4},{12,16},{16,12},{20,24},{24,20},{5,9},{9,5},{13,17},{1... | collective-permute-start | bytes 737288 | tf_op jit(solution)/shard_map/ppermute | solution.py:649
  72.1 1.1 %collective-permute-start.5 = (f32[120,128]{1,0:T(8,128)S(1)}, f32[120,128]{1,0:T(8,128)S(1)}, u32[]{:S(2)}, u32[]{:S(2)}) collective-permute-start(f32[120,128]{1,0:T(8,128)S(1)} %get-tuple-element.44), channel_id=1, source_target_pairs={{1,0},{2,1},{3,2},{0,3},{5,4},{6,5},{7,6},{4,7},{9,8},{10,9},{11,1... | collective-permute-start | bytes 184328 | tf_op jit(solution)/shard_map/ppermute | solution.py:630
  73.2 0.7 collective-permute-start.4
  73.9 0.0 copy-done.6
  73.9 2.3 %gradient_local.1.refs_1_.after = f32[16,240,128]{2,1,0:T(8,128)S(1)} custom-call(f32[4,240,128]{2,1,0:T(8,128)S(1)} %gradient_odd.1.after, f32[16,240,128]{2,1,0:T(8,128)S(1)} %get-tuple-element.43.refs_3_.field_ref, bf16[240,240]{1,0:T(8,128)(2,1)S(1)} %copy-done.4, bf16[240,240]{1,0:T(8,128)(2,1)S(1)} %copy-done.3, bf16[256,256]{1,0:T(8,128)(2,1)S(1)} %copy-done.6), custom_call_target="tpu_custom_call" | custom-call | tf_op jit(solution)/shard_map/gradient_local/pallas_call | solution.py:633
  76.2 0.1 collective-permute-done.5.refs_3_.after_ref
  76.3 0.0 collective-permute-done.4.refs_2_.before_ref
  76.3 0.2 gradient_corners.1
  76.5 0.1 collective-permute-start.7
  76.6 0.0 copy-start.11
  76.6 4.2 %collective-permute-start.9 = (f32[64,128]{1,0:T(8,128)S(1)}, f32[64,128]{1,0:T(8,128)S(1)}, u32[]{:S(2)}, u32[]{:S(2)}) collective-permute-start(f32[64,128]{1,0:T(8,128)S(1)} %get-tuple-element.47), channel_id=1, source_target_pairs={{4,8},{8,4},{12,16},{16,12},{20,24},{24,20},{5,9},{9,5},{13,17},{1... | collective-permute-start | bytes 98312 | tf_op jit(solution)/shard_map/ppermute | solution.py:564
  80.7 1.1 %gradient_strips.1.local_ref = f32[16,240,128]{2,1,0:T(8,128)S(1)} custom-call(s32[8,128]{1,0:T(8,128)S(1)} %broadcast_in_dim.15.refs_0_.par_ref, f32[16,240,128]{2,1,0:T(8,128)S(1)} %gradient_local.1.refs_1_.after, f32[120,128]{1,0:T(8,128)S(1)} %collective-permute-done.4.refs_2_.before_ref, f32[120,128]{1,0:T(8,128)S(1)} %collective-permute-done.5.refs_3_.after_ref, ...), custom_call_target="tpu_custom_call" | custom-call | tf_op jit(solution)/shard_map/gradient_strips/pallas_call | solution.py:642
  81.9 0.0 collective-permute-done.6
  81.9 0.0 collective-permute-done.8
  82.0 0.0 collective-permute-done.7.corner_ref
  82.0 0.0 copy-done.11
  82.0 1.7 %gradient_with_even.1.local_ref = f32[240,16,128]{2,1,0:T(8,128)S(1)} custom-call(s32[8,128]{1,0:T(8,128)S(1)} %broadcast_in_dim.15.refs_0_.par_ref, f32[16,240,128]{2,1,0:T(8,128)S(1)} %gradient_strips.1.local_ref, f32[2,128]{1,0:T(2,128)S(1)} %get-tuple-element.42.refs_2_.factor_ref, f32[4,240,128]{2,1,0:T(8,128)S(1)} %convert_element_type.15.got_ref, ...), custom_call_target="tpu_custom_call" | custom-call | tf_op jit(solution)/shard_map/gradient_with_even/pallas_call | solution.py:743
  83.8 0.0 collective-permute-done.9.corner_ref
  83.8 2.4 %gradient.1 = (f32[1,64]{1,0:T(1,128)}, f32[240,16,128]{2,1,0:T(8,128)}) custom-call(s32[8,128]{1,0:T(8,128)S(1)} %broadcast_in_dim.15.refs_0_.par_ref, f32[1,128]{1,0:T(1,128)S(1)} %get-tuple-element.40.model_ref, f32[240,16,128]{2,1,0:T(8,128)S(1)} %gradient_with_even.1.local_ref, f32[2,128]{1,0:T(2,128)S(1)} %get-tuple-element.42.refs_2_.factor_ref, ...), custom_call_target="tpu_custom_call" | custom-call | tf_op jit(solution)/shard_map/gradient/pallas_call | solution.py:747
  (7 shorter events, 0.1 us)
Async XLA Ops:
  3.2 44.5 %all-to-all-start = ((bf16[32,200,128]{2,1,0:T(8,128)(2,1)}), bf16[32,200,128]{2,1,0:T(8,128)(2,1)S(1)}, u32[]{:S(2)}, u32[]{:S(2)}) async-start(bf16[32,200,128]{2,1,0:T(8,128)(2,1)} %prepare_blocks.1.after), calls=%async_computation | async-start | bytes 3276800 | tf_op jit(solution)/shard_map/all_to_all | solution.py:676
  9.6 1.5 %copy-start.7 = (f32[240,16,128]{2,1,0:T(8,128)S(1)}, f32[240,16,128]{2,1,0:T(8,128)}, u32[]{:S(2)}) copy-start(f32[240,16,128]{2,1,0:T(8,128)} %control_ref.1) | copy-start | bytes 5898244
  11.2 11.5 %copy-start.3 = (bf16[240,240]{1,0:T(8,128)(2,1)S(1)}, bf16[240,240]{1,0:T(8,128)(2,1)}, u32[]{:S(2)}) copy-start(bf16[240,240]{1,0:T(8,128)(2,1)} %constant.41.clone.time_low.refs_5_) | copy-start | bytes 345604
  11.2 11.5 %copy-start.4 = (bf16[240,240]{1,0:T(8,128)(2,1)S(1)}, bf16[240,240]{1,0:T(8,128)(2,1)}, u32[]{:S(2)}) copy-start(bf16[240,240]{1,0:T(8,128)(2,1)} %constant.40.clone.time_high.refs_4_) | copy-start | bytes 345604
  11.2 11.5 %copy-start.5 = (bf16[256,256]{1,0:T(8,128)(2,1)S(1)}, bf16[256,256]{1,0:T(8,128)(2,1)}, u32[]{:S(2)}) copy-start(bf16[256,256]{1,0:T(8,128)(2,1)} %constant.42.clone.col_both) | copy-start | bytes 393220
  11.2 11.6 %copy-start.12 = (bf16[2,384,512]{2,1,0:T(8,128)(2,1)S(1)}, bf16[2,384,512]{2,1,0:T(8,128)(2,1)}, u32[]{:S(2)}) copy-start(bf16[2,384,512]{2,1,0:T(8,128)(2,1)} %constant.45.clone.beyond_ref) | copy-start | bytes 2359300
  12.7 10.1 %collective-permute-start.1 = (f32[120,128]{1,0:T(8,128)S(1)}, f32[120,128]{1,0:T(8,128)S(1)}, u32[]{:S(2)}, u32[]{:S(2)}) collective-permute-start(f32[120,128]{1,0:T(8,128)S(1)} %get-tuple-element.28), channel_id=1, source_target_pairs={{1,0},{2,1},{3,2},{0,3},{5,4},{6,5},{7,6},{4,7},{9,8},{10,9},{11,1... | collective-permute-start | bytes 184328 | tf_op jit(solution)/shard_map/ppermute | solution.py:630
  13.1 9.7 %collective-permute-start = (f32[120,128]{1,0:T(8,128)S(1)}, f32[120,128]{1,0:T(8,128)S(1)}, u32[]{:S(2)}, u32[]{:S(2)}) collective-permute-start(f32[120,128]{1,0:T(8,128)S(1)} %get-tuple-element.26.after), channel_id=1, source_target_pairs={{0,1},{1,2},{2,3},{3,0},{4,5},{5,6},{6,7},{7,4},{8,9},{9,10},{10,1... | collective-permute-start | bytes 184328 | tf_op jit(solution)/shard_map/ppermute | solution.py:630
  25.4 16.7 %collective-permute-start.2 = (bf16[4,240,128]{2,1,0:T(8,128)(2,1)S(1)}, bf16[4,240,128]{2,1,0:T(8,128)(2,1)S(1)}, u32[]{:S(2)}, u32[]{:S(2)}) collective-permute-start(bf16[4,240,128]{2,1,0:T(8,128)(2,1)S(1)} %get-tuple-element.29), channel_id=1, source_target_pairs={{0,4},{4,0},{8,12},{12,8},{16,20},{20,16},{24,28},{28,24},{1,5},{5... | collective-permute-start | bytes 737288 | tf_op jit(solution)/shard_map/ppermute | solution.py:563
  26.6 5.1 %copy-start.2 = (bf16[384,2048]{1,0:T(8,128)(2,1)S(1)}, bf16[384,2048]{1,0:T(8,128)(2,1)}, u32[]{:S(2)}) copy-start(bf16[384,2048]{1,0:T(8,128)(2,1)} %constant.43.clone.refs_6_) | copy-start | bytes 4718596
  26.6 22.8 %collective-permute-start.3 = (bf16[4,240,128]{2,1,0:T(8,128)(2,1)}, bf16[4,240,128]{2,1,0:T(8,128)(2,1)}, u32[]{:S(2)}, u32[]{:S(2)}) collective-permute-start(bf16[4,240,128]{2,1,0:T(8,128)(2,1)} %get-tuple-element.33), channel_id=1, source_target_pairs={{4,8},{8,4},{12,16},{16,12},{20,24},{24,20},{5,9},{9,5},{13,17},{1... | collective-permute-start | bytes 737288 | tf_op jit(solution)/shard_map/ppermute | solution.py:564
  31.7 10.5 %copy-start.9 = (bf16[240,16,128]{2,1,0:T(8,128)(2,1)S(1)}, bf16[240,16,128]{2,1,0:T(8,128)(2,1)}, u32[]{:S(2)}) copy-start(bf16[240,16,128]{2,1,0:T(8,128)(2,1)} %prior_ref.1) | copy-start | bytes 2949124
  31.7 10.5 %copy-start.10 = (bf16[240,16,128]{2,1,0:T(8,128)(2,1)S(1)}, bf16[240,16,128]{2,1,0:T(8,128)(2,1)}, u32[]{:S(2)}) copy-start(bf16[240,16,128]{2,1,0:T(8,128)(2,1)} %scale_ref.1) | copy-start | bytes 2949124
  44.8 1.3 %copy-start = (f32[16,240,128]{2,1,0:T(8,128)}, f32[16,240,128]{2,1,0:T(8,128)S(1)}, u32[]{:S(2)}) copy-start(f32[16,240,128]{2,1,0:T(8,128)S(1)} %get-tuple-element.30.refs_2_.refs_5_) | copy-start | bytes 5898244
  46.1 1.3 %copy-start.8 = (f32[16,240,128]{2,1,0:T(8,128)}, f32[16,240,128]{2,1,0:T(8,128)S(1)}, u32[]{:S(2)}) copy-start(f32[16,240,128]{2,1,0:T(8,128)S(1)} %get-tuple-element.31.refs_3_) | copy-start | bytes 5898244
  49.4 16.2 %copy-start.1 = (f32[16,240,128]{2,1,0:T(8,128)S(1)}, f32[16,240,128]{2,1,0:T(8,128)}, u32[]{:S(2)}) copy-start(f32[16,240,128]{2,1,0:T(8,128)} %copy-done) | copy-start | bytes 5898244
  68.4 5.5 %copy-start.6 = (bf16[256,256]{1,0:T(8,128)(2,1)S(1)}, bf16[256,256]{1,0:T(8,128)(2,1)}, u32[]{:S(2)}) copy-start(bf16[256,256]{1,0:T(8,128)(2,1)} %constant.42.clone.col_both) | copy-start | bytes 393220
  68.5 13.4 %collective-permute-start.6 = (f16[4,240,128]{2,1,0:T(8,128)(2,1)S(1)}, f16[4,240,128]{2,1,0:T(8,128)(2,1)S(1)}, u32[]{:S(2)}, u32[]{:S(2)}) collective-permute-start(f16[4,240,128]{2,1,0:T(8,128)(2,1)S(1)} %convert_element_type.14), channel_id=1, source_target_pairs={{0,4},{4,0},{8,12},{12,8},{16,20},{20,16},{24,28},{28,24},{1,5},{5... | collective-permute-start | bytes 737288 | tf_op jit(solution)/shard_map/ppermute | solution.py:738
  69.9 12.1 %collective-permute-start.8 = (f16[4,240,128]{2,1,0:T(8,128)(2,1)S(1)}, f16[4,240,128]{2,1,0:T(8,128)(2,1)S(1)}, u32[]{:S(2)}, u32[]{:S(2)}) collective-permute-start(f16[4,240,128]{2,1,0:T(8,128)(2,1)S(1)} %convert_element_type.16), channel_id=1, source_target_pairs={{4,8},{8,4},{12,16},{16,12},{20,24},{24,20},{5,9},{9,5},{13,17},{1... | collective-permute-start | bytes 737288 | tf_op jit(solution)/shard_map/ppermute | solution.py:649
  72.1 4.2 %collective-permute-start.5 = (f32[120,128]{1,0:T(8,128)S(1)}, f32[120,128]{1,0:T(8,128)S(1)}, u32[]{:S(2)}, u32[]{:S(2)}) collective-permute-start(f32[120,128]{1,0:T(8,128)S(1)} %get-tuple-element.44), channel_id=1, source_target_pairs={{1,0},{2,1},{3,2},{0,3},{5,4},{6,5},{7,6},{4,7},{9,8},{10,9},{11,1... | collective-permute-start | bytes 184328 | tf_op jit(solution)/shard_map/ppermute | solution.py:630
  73.2 3.1 %collective-permute-start.4 = (f32[120,128]{1,0:T(8,128)S(1)}, f32[120,128]{1,0:T(8,128)S(1)}, u32[]{:S(2)}, u32[]{:S(2)}) collective-permute-start(f32[120,128]{1,0:T(8,128)S(1)} %get-tuple-element.41.refs_1_), channel_id=1, source_target_pairs={{0,1},{1,2},{2,3},{3,0},{4,5},{5,6},{6,7},{7,4},{8,9},{9,10},{10,1... | collective-permute-start | bytes 184328 | tf_op jit(solution)/shard_map/ppermute | solution.py:630
  76.5 5.5 %collective-permute-start.7 = (f32[64,128]{1,0:T(8,128)S(1)}, f32[64,128]{1,0:T(8,128)S(1)}, u32[]{:S(2)}, u32[]{:S(2)}) collective-permute-start(f32[64,128]{1,0:T(8,128)S(1)} %get-tuple-element.46), channel_id=1, source_target_pairs={{0,4},{4,0},{8,12},{12,8},{16,20},{20,16},{24,28},{28,24},{1,5},{5... | collective-permute-start | bytes 98312 | tf_op jit(solution)/shard_map/ppermute | solution.py:563
  76.6 5.4 %copy-start.11 = (bf16[2,96,512]{2,1,0:T(8,128)(2,1)S(1)}, bf16[2,96,512]{2,1,0:T(8,128)(2,1)}, u32[]{:S(2)}) copy-start(bf16[2,96,512]{2,1,0:T(8,128)(2,1)} %constant.44.clone.corner_weights) | copy-start | bytes 589828
  76.6 7.2 %collective-permute-start.9 = (f32[64,128]{1,0:T(8,128)S(1)}, f32[64,128]{1,0:T(8,128)S(1)}, u32[]{:S(2)}, u32[]{:S(2)}) collective-permute-start(f32[64,128]{1,0:T(8,128)S(1)} %get-tuple-element.47), channel_id=1, source_target_pairs={{4,8},{8,4},{12,16},{16,12},{20,24},{24,20},{5,9},{9,5},{13,17},{1... | collective-permute-start | bytes 98312 | tf_op jit(solution)/shard_map/ppermute | solution.py:564

commit v11 on v9

--- a/solution.py
+++ b/solution.py
@@ -112,8 +112,8 @@
     return total
 
 
-def fold_corners(odd, strips, corner_e, corner_o):
-    quarter = corner_e.shape[0]
+def fold_corners(strips, last_ref, first_ref):
+    quarter = last_ref.shape[0]
     half, part = LANES // 2, RAD * RAD
     lane = lane_ids((quarter, LANES))
     spare = jnp.zeros((4 * quarter - strips.shape[0], LANES), F32)
@@ -126,8 +126,8 @@
             here = (lane >= to) & (lane < to + part)
             low = choose(here, pltpu.roll(piece, (to - side * half) % LANES, 1), low)
             high = choose(here, pltpu.roll(piece, (to - side * half - (half - part)) % LANES, 1), high)
-    corner_e[...] = choose(odd, low, high)
-    corner_o[...] = choose(odd, high, low)
+    last_ref[...] = high
+    first_ref[...] = low
 
 
 def unfold_corners(value):
@@ -181,8 +181,8 @@
     return jnp.where(outside == 1, 0.0, jnp.concatenate([early, late], axis=0))
 
 
-def far_corner_kernel(par_ref, after, before_ref, after_ref, corner_e, corner_o):
-    fold_corners(is_odd(par_ref, 0), halo_columns(par_ref, before_ref, after_ref), corner_e, corner_o)
+def far_corner_kernel(par_ref, after, before_ref, after_ref, last_ref, first_ref):
+    fold_corners(halo_columns(par_ref, before_ref, after_ref), last_ref, first_ref)
 
 
 def prepare_kernel(
@@ -358,7 +358,7 @@
 
 
 def finish_kernel(
-    par_ref, model_ref, local_ref, factor_ref, got_e, got_o, corner_e, corner_o,
+    par_ref, model_ref, local_ref, factor_ref, got_e, got_o, corner_before, corner_after,
     time_high, time_low, col_both, corner_weights,
     model_out, out_ref, halo, edges, total, model_own, sems,
 ):
@@ -376,8 +376,8 @@
         for k in range(RAD):
             even, other = got_e[k], got_o[k]
             halo[k] = (choose(odd, even, other) if before else choose(odd, other, even)) * factor
-        even, other = corner_e[...], corner_o[...]
-        corner = choose(odd, even, other) if before else choose(odd, other, even)
+        corner = corner_before[...] if before else corner_after[...]
+        corner = jnp.where(par_ref[5 + side : 6 + side, :] == 1, 0.0, corner)
         parts = edge_parts(halo, corner, corner_weights.at[1 - side], consts)
         for k, part in enumerate(parts):
             edges[:, k if before else half - 1 - k, :] = part
@@ -471,10 +471,10 @@
 
 def adjoint_kernel(
     par_ref, table_vmem, seen_ref, got_ref, foot_ref, scale_ref,
-    model_ref, factor_ref, field_ref,
-    weight_vmem, weight_smem, table_ref, sems, *, shift, slots, heights, tiles, per,
+    model_ref, factor_ref, field_ref, rows_even, last_ref, first_ref,
+    weight_rows, table_ref, sem, *, shift, slots, heights, tiles, per,
 ):
-    load = pltpu.make_async_copy(table_vmem, table_ref, sems.at[1])
+    load = pltpu.make_async_copy(table_vmem, table_ref, sem)
     load.start()
     sources = foot_ref.shape[0]
     groups = got_ref.shape[1]
@@ -489,7 +489,7 @@
             line = line if k == 0 else pltpu.roll(line, LANES - k * per, 1)
             own = choose(par_ref[2:3, :] == q * packed + k, line, own)
     model_ref[...] = own
-    weight_vmem[...] = jnp.zeros_like(weight_vmem)
+    weights = []
     for q in range(groups):
         observed, error = jnp.zeros((1, LANES), F32), jnp.ones((1, LANES), F32)
         for k in range(packed):
@@ -499,30 +499,39 @@
             observed = jnp.where(here, line if k == 0 else pltpu.roll(line, k * per, 1), observed)
             turn = (k * per - per) % LANES
             error = jnp.where(here, line if turn == 0 else pltpu.roll(line, turn, 1), error)
-        weight_vmem[q : q + 1, :] = (model[q : q + 1, :] - observed) / (error * error)
-    copy = pltpu.make_async_copy(weight_vmem, weight_smem, sems.at[0])
-    copy.start()
+        weights.append((model[q : q + 1, :] - observed) / (error * error))
+    lanes = lane_ids((sources, LANES))
+    table = table_vmem[...]
+    for c in range(slots):
+        which = table[:, 3 * slots + c : 3 * slots + c + 1]
+        found = jnp.zeros((sources, LANES), F32)
+        for q in range(groups):
+            found = jnp.where(which == lanes + q * LANES, weights[q], found)
+        weight_rows[c] = jnp.broadcast_to(jnp.sum(found, axis=1, keepdims=True), (sources, LANES))
     field_ref[...] = jnp.zeros_like(field_ref)
-    top = jnp.max(jnp.abs(weight_vmem[...]), keepdims=True) * (FOOT_MAX * SCALE_MAX * sources * slots)
+    largest = jnp.abs(weights[0])
+    for weight in weights[1:]:
+        largest = jnp.maximum(largest, jnp.abs(weight))
+    top = jnp.max(largest, keepdims=True) * (FOOT_MAX * SCALE_MAX * sources * slots)
     top = jnp.maximum(top, 1e-25)
     factor_ref[0:1, :] = jnp.broadcast_to(HALF_TOP / top, (1, LANES))
     factor_ref[1:2, :] = jnp.broadcast_to(top * (1.0 / HALF_TOP), (1, LANES))
     load.wait()
-    copy.wait()
 
     def body(source, carry):
         for c, block in blocks_of(foot_ref, source, heights, slots):
             offset = table_ref[source, c]
-            receptor = table_ref[source, 3 * slots + c]
             row = lax.shift_right_logical(offset, shift)
             begin = jnp.bitwise_and(offset, (1 << shift) - 1)
-            weight = weight_smem[lax.shift_right_logical(receptor, 7), jnp.bitwise_and(receptor, LANES - 1)]
+            weight = weight_rows[c, pl.ds(source, 1), :]
             field_ref[row, pl.ds(begin, heights), :] += block * weight
         return carry
 
     lax.fori_loop(0, sources, body, 0)
     for row in range(rows):
         field_ref[row] = field_ref[row] * scale_ref[row]
+    rows_kernel(par_ref, None, factor_ref, field_ref, rows_even, even=True)
+    write_strips(field_ref, last_ref, first_ref)
 
 
 def swap_pairs(count, odd):
@@ -585,7 +594,8 @@
     groups = per * n_rec // LANES
     shift = (hours - 1).bit_length()
     rec, tile = lax.axis_index("rec"), lax.axis_index("tile")
-    flags = [rec % 2, rec * 0, rec, tile == 0, tile == n_tile - 1] + [rec * 0] * (SUB - 5)
+    flags = [rec % 2, rec * 0, rec, tile == 0, tile == n_tile - 1, rec == 0, rec == n_rec - 1]
+    flags += [rec * 0] * (SUB - len(flags))
     par = jnp.stack([flag.astype(jnp.int32) for flag in flags])
     par = jnp.broadcast_to(par[:, None], (SUB, LANES))
     base, own_parts, corner_parts, beyond_parts = constants(hours, rows, cols)
@@ -599,15 +609,16 @@
     field_shape = array(rows, hours, cols)
     row_scratch = pltpu.VMEM((RAD, hours, cols), F32)
 
-    def pass_strips(last, first):
-        onward = [(i, (i + 1) % n_tile) for i in range(n_tile)]
+    def pass_on(axis, last, first):
+        count = lax.axis_size(axis)
+        onward = [(i, (i + 1) % count) for i in range(count)]
         back = [(j, i) for i, j in onward]
-        return lax.ppermute(last, "tile", onward), lax.ppermute(first, "tile", back)
+        return lax.ppermute(last, axis, onward), lax.ppermute(first, axis, back)
 
     def swaps(after, field, got_strips, name):
         local = call(local_kernel, field_shape, [VM] * 5, [], name + "_local")(after, field, *base)
         corners = call(far_corner_kernel, [corner, corner], [VM] * 4, [], name + "_corners")(par, local, *got_strips)
-        return local, swap("rec", *corners)
+        return local, pass_on("rec", *corners)
 
     def strip_sums(local, got_strips, by_hour, name):
         def kernel(*refs):
@@ -652,7 +663,7 @@
     field, *strips = call(
         turn_kernel, [field_shape, strip, strip], [HB, VM], [], "turn_control"
     )(sent, control)
-    got_strips = pass_strips(*strips)
+    got_strips = pass_on("tile", *strips)
     local = call(local_kernel, field_shape, [VM] * 5, [], "control_local")(strips[0], field, *base)
     small = jax.ShapeDtypeStruct((RAD, hours, cols), BF16)
     sent_even, sent_odd = call(beyond_kernel, [small, small], [VM] * 8, [], "control_beyond")(
@@ -699,22 +710,19 @@
     def adjoint(*refs):
         adjoint_kernel(*refs, **sizes)
 
-    weight_rows = -(-(groups + 1) // SUB) * SUB
-    model, factor, field = call(
+    model, factor, field, sent_even, *strips = call(
         adjoint,
-        [array(1, LANES), array(2, LANES), field_shape],
+        [array(1, LANES), array(2, LANES), field_shape, block, strip, strip],
         [VM] * 6,
         [
-            pltpu.VMEM((weight_rows, LANES), F32),
-            pltpu.SMEM((weight_rows, LANES), F32),
+            pltpu.VMEM((slots, devices, LANES), F32),
             pltpu.SMEM((devices, LANES), jnp.int32),
-            pltpu.SemaphoreType.DMA((2,)),
+            pltpu.SemaphoreType.DMA,
         ],
         "adjoint_field",
     )(par, table, seen, everyone, foot, scale)
-    sent_even, got_even = swap_rows(True, factor, factor, field, "gradient_even")
-    strips = call(strip_kernel, [strip, strip], [VM] * 2, [], "gradient_pack")(sent_even, field)
-    got_strips = pass_strips(*strips)
+    got_even = lax.ppermute(sent_even.astype(F16), "rec", swap_pairs(n_rec, False))
+    got_strips = pass_on("tile", *strips)
     sent_odd, got_odd = swap_rows(False, strips[0], factor, field, "gradient_odd")
     local, got_corners = swaps(sent_odd, field, got_strips, "gradient")
     local = strip_sums(local, got_strips, True, "gradient_strips")

time: 88.7 us -> 87.2 us (0.983)
  the two profiles are of different devices: /device:TPU:12 before, /device:TPU:0 now
where the time goes in v11:
time: 87.2 us; the launch traced here: 86.8 us
  Pallas kernels  26.7 us (31%)
  waiting for transfers between devices  24.1 us (28%)
  starting transfers between devices  17 us (19%)
  blocking collectives  13.6 us (16%)
  local copies, waits for them, and re-layouts  4.31 us (5%)
  between operations  1.07 us (1%)
    all_to_all x1, blocking collectives, per_device(): lax.all_to_all(partial, AXES, split_axis=0, concat_axis=0, tiled=True)  13.6 us
    ppermute x6, waiting for transfers between devices, pass_on(): return (lax.ppermute(last, axis, onward), lax.ppermute(first, axis, back))  11.8 us
    ppermute x1, waiting for transfers between devices, swap(): lax.ppermute(even, axis, swap_pairs(count, False))  9.98 us
    all_to_all x1, starting transfers between devices, per_device(): foot = lax.all_to_all(sent, AXES, split_axis=0, concat_axis=0, tiled=True)  7.3 us
    ppermute x6, starting transfers between devices, pass_on(): return (lax.ppermute(last, axis, onward), lax.ppermute(first, axis, back))  6.9 us
    unnamed x26, local copies, waits for them, and re-layouts  4.15 us
    pallas_call x2, Pallas kernels, strip_sums(): call(kernel, shape, [VM] * 7, [], name)  2.93 us
    pallas_call x1, Pallas kernels, per_device(): call(adjoint, [array(1, LANES), array(2, LANES), field_shape, block, stri...  2.83 us
  transfers between devices with their start and end apart: 11, of which 6 were waited for; matrix products, arithmetic and copies ran while one was open for 0% of the time, Pallas kernels for 19%

profile of v11, /device:TPU:0, one launch (start us, length us, event | category | flops | bytes accessed | tf_op | source)
XLA Modules:
  0.0 86.8 jit_solution(10153953031515876476)
XLA Ops:
  0.6 0.1 stack.43
  0.7 0.1 broadcast_in_dim.15.refs_0_.par_ref
  0.8 2.4 %prepare_blocks.1.after = bf16[32,200,128]{2,1,0:T(8,128)(2,1)} custom-call(s32[8,128]{1,0:T(8,128)S(1)} %broadcast_in_dim.15.refs_0_.par_ref, bf16[32,192,128]{2,1,0:T(8,128)(2,1)} %bitcast.14, s32[8,32]{1,0:T(8,128)} %bitcast.15, s32[8,32]{1,0:T(8,128)} %bitcast.16, s32[8,32]{1,0:T(8,128)} %bitcast.17, s32[1,32]{1,0:T(1,128)} %bitcast.18, ...), custom_call_target="tpu_custom_call" | custom-call | tf_op jit(solution)/shard_map/prepare_blocks/pallas_call | solution.py:642
  3.2 7.3 %all-to-all-start = ((bf16[32,200,128]{2,1,0:T(8,128)(2,1)}), bf16[32,200,128]{2,1,0:T(8,128)(2,1)S(1)}, u32[]{:S(2)}, u32[]{:S(2)}) async-start(bf16[32,200,128]{2,1,0:T(8,128)(2,1)} %prepare_blocks.1.after), calls=%async_computation | async-start | bytes 3276800 | tf_op jit(solution)/shard_map/all_to_all | solution.py:662
  10.5 0.0 copy-start.7
  10.5 1.5 %copy-done.7 = f32[240,16,128]{2,1,0:T(8,128)S(1)} copy-done((f32[240,16,128]{2,1,0:T(8,128)S(1)}, f32[240,16,128]{2,1,0:T(8,128)}, u32[]{:S(2)}) %copy-start.7) | copy-done | bytes 1966104
  12.1 0.0 copy-start.3
  12.1 0.0 copy-start.4
  12.1 0.0 copy-start.5
  12.1 0.0 copy-start.11
  12.1 1.5 %turn_control.1 = (f32[16,240,128]{2,1,0:T(8,128)S(1)}, f32[120,128]{1,0:T(8,128)S(1)}, f32[120,128]{1,0:T(8,128)S(1)}) custom-call(bf16[32,200,128]{2,1,0:T(8,128)(2,1)} %prepare_blocks.1.after, f32[240,16,128]{2,1,0:T(8,128)S(1)} %copy-done.7), custom_call_target="tpu_custom_call" | custom-call | tf_op jit(solution)/shard_map/turn_control/pallas_call | solution.py:663
  13.5 1.6 %collective-permute-start.1 = (f32[120,128]{1,0:T(8,128)S(1)}, f32[120,128]{1,0:T(8,128)S(1)}, u32[]{:S(2)}, u32[]{:S(2)}) collective-permute-start(f32[120,128]{1,0:T(8,128)S(1)} %get-tuple-element.28), channel_id=1, source_target_pairs={{1,0},{2,1},{3,2},{0,3},{5,4},{6,5},{7,6},{4,7},{9,8},{10,9},{11,1... | collective-permute-start | bytes 184328 | tf_op jit(solution)/shard_map/ppermute | solution.py:616
  15.1 0.0 collective-permute-start
  15.1 7.5 %collective-permute-done.1.refs_3_.after_ref = f32[120,128]{1,0:T(8,128)S(1)} collective-permute-done((f32[120,128]{1,0:T(8,128)S(1)}, f32[120,128]{1,0:T(8,128)S(1)}, u32[]{:S(2)}, u32[]{:S(2)}) %collective-permute-start.1) | collective-permute-done | bytes 61472 | tf_op jit(solution)/shard_map/ppermute | solution.py:616
  22.6 2.3 %collective-permute-done.refs_2_.before_ref = f32[120,128]{1,0:T(8,128)S(1)} collective-permute-done((f32[120,128]{1,0:T(8,128)S(1)}, f32[120,128]{1,0:T(8,128)S(1)}, u32[]{:S(2)}, u32[]{:S(2)}) %collective-permute-start) | collective-permute-done | bytes 61472 | tf_op jit(solution)/shard_map/ppermute | solution.py:616
  24.9 0.0 copy-done.3
  24.9 0.0 copy-done.4
  24.9 0.0 copy-done.5
  24.9 0.0 copy-done.11
  24.9 2.7 %control_beyond.1 = (bf16[4,240,128]{2,1,0:T(8,128)(2,1)S(1)}, bf16[4,240,128]{2,1,0:T(8,128)(2,1)}) custom-call(s32[8,128]{1,0:T(8,128)S(1)} %broadcast_in_dim.15.refs_0_.par_ref, f32[16,240,128]{2,1,0:T(8,128)S(1)} %get-tuple-element.27.field_ref, f32[120,128]{1,0:T(8,128)S(1)} %collective-permute-done.refs_2_.before_ref, ...), custom_call_target="tpu_custom_call" | custom-call | tf_op jit(solution)/shard_map/control_beyond/pallas_call | solution.py:669
  27.6 0.0 collective-permute-start.2
  27.6 0.0 copy-start.2
  27.6 1.5 %collective-permute-start.3 = (bf16[4,240,128]{2,1,0:T(8,128)(2,1)}, bf16[4,240,128]{2,1,0:T(8,128)(2,1)}, u32[]{:S(2)}, u32[]{:S(2)}) collective-permute-start(bf16[4,240,128]{2,1,0:T(8,128)(2,1)} %get-tuple-element.33), channel_id=1, source_target_pairs={{4,8},{8,4},{12,16},{16,12},{20,24},{24,20},{5,9},{9,5},{13,17},{1... | collective-permute-start | bytes 737288 | tf_op jit(solution)/shard_map/ppermute | solution.py:548
  29.1 2.3 %control_local.1.refs_1_ = f32[16,240,128]{2,1,0:T(8,128)S(1)} custom-call(f32[120,128]{1,0:T(8,128)S(1)} %get-tuple-element.26.after, f32[16,240,128]{2,1,0:T(8,128)S(1)} %get-tuple-element.27.field_ref, bf16[240,240]{1,0:T(8,128)(2,1)S(1)} %copy-done.4, bf16[240,240]{1,0:T(8,128)(2,1)S(1)} %copy-done.3, bf16[256,256]{1,0:T(8,128)(2,1)S(1)} %copy-done.5), custom_call_target="tpu_custom_call" | custom-call | tf_op jit(solution)/shard_map/control_local/pallas_call | solution.py:667
  31.4 0.0 copy-done.2
  31.4 0.0 copy-start.9
  31.4 0.0 copy-start.10
  31.4 1.1 %control_strips.1.local_ref = f32[16,240,128]{2,1,0:T(8,128)S(1)} custom-call(s32[8,128]{1,0:T(8,128)S(1)} %broadcast_in_dim.15.refs_0_.par_ref, f32[16,240,128]{2,1,0:T(8,128)S(1)} %control_local.1.refs_1_, f32[120,128]{1,0:T(8,128)S(1)} %collective-permute-done.refs_2_.before_ref, f32[120,128]{1,0:T(8,128)S(1)} %collective-permute-done.1.refs_3_.after_ref, ...), custom_call_target="tpu_custom_call" | custom-call | tf_op jit(solution)/shard_map/control_strips/pallas_call | solution.py:628
  32.6 10.0 %collective-permute-done.2.got_ref = bf16[4,240,128]{2,1,0:T(8,128)(2,1)S(1)} collective-permute-done((bf16[4,240,128]{2,1,0:T(8,128)(2,1)S(1)}, bf16[4,240,128]{2,1,0:T(8,128)(2,1)S(1)}, u32[]{:S(2)}, u32[]{:S(2)}) %collective-permute-start.2) | collective-permute-done | bytes 245792 | tf_op jit(solution)/shard_map/ppermute | solution.py:547
  42.5 0.0 copy-done.9
  42.5 0.0 copy-done.10
  42.5 2.6 %flux_field.1 = (f32[16,240,128]{2,1,0:T(8,128)S(1)}, f32[16,240,128]{2,1,0:T(8,128)S(1)}) custom-call(s32[8,128]{1,0:T(8,128)S(1)} %broadcast_in_dim.15.refs_0_.par_ref, f32[16,240,128]{2,1,0:T(8,128)S(1)} %control_strips.1.local_ref, bf16[240,16,128]{2,1,0:T(8,128)(2,1)S(1)} %copy-done.9, bf16[240,16,128]{2,1,0:T(8,128)(2,1)S(1)} %copy-done.10, ...), custom_call_target="tpu_custom_call" | custom-call | tf_op jit(solution)/shard_map/flux_field/pallas_call | solution.py:674
  45.2 0.0 copy-start
  45.2 1.3 %copy-done = f32[16,240,128]{2,1,0:T(8,128)} copy-done((f32[16,240,128]{2,1,0:T(8,128)}, f32[16,240,128]{2,1,0:T(8,128)S(1)}, u32[]{:S(2)}) %copy-start) | copy-done | bytes 1966104
  46.4 0.0 copy-start.8
  46.4 1.3 %copy-done.8 = f32[16,240,128]{2,1,0:T(8,128)} copy-done((f32[16,240,128]{2,1,0:T(8,128)}, f32[16,240,128]{2,1,0:T(8,128)S(1)}, u32[]{:S(2)}) %copy-start.8) | copy-done | bytes 1966104
  47.7 2.2 %all-to-all-done.refs_1_.refs_4_ = bf16[32,200,128]{2,1,0:T(8,128)(2,1)S(1)} async-done(((bf16[32,200,128]{2,1,0:T(8,128)(2,1)}), bf16[32,200,128]{2,1,0:T(8,128)(2,1)S(1)}, u32[]{:S(2)}, u32[]{:S(2)}) %all-to-all-start) | async-done | bytes 1638432 | tf_op jit(solution)/shard_map/all_to_all | solution.py:662
  50.0 1.7 %load_flux.1 = (s32[32,128]{1,0:T(8,128)S(1)}, f32[32,128]{1,0:T(8,128)S(1)}, f32[4,240,128]{2,1,0:T(8,128)S(1)}, f32[16,240,128]{2,1,0:T(8,128)S(1)}) custom-call(s32[8,128]{1,0:T(8,128)S(1)} %broadcast_in_dim.15.refs_0_.par_ref, bf16[32,200,128]{2,1,0:T(8,128)(2,1)S(1)} %all-to-all-done.refs_1_.refs_4_, f32[16,240,128]{2,1,0:T(8,128)} %copy-done, ...), custom_call_target="tpu_custom_call" | custom-call | tf_op jit(solution)/shard_map/load_flux/pallas_call | solution.py:687
  51.7 0.0 collective-permute-done.3.refs_3_
  51.7 0.0 copy-start.1
  51.7 2.5 %block_values.1 = (f32[32,4,128]{2,1,0:T(4,128)S(1)}, f32[16,240,128]{2,1,0:T(8,128)S(1)}) custom-call(s32[8,128]{1,0:T(8,128)S(1)} %broadcast_in_dim.15.refs_0_.par_ref, bf16[32,200,128]{2,1,0:T(8,128)(2,1)S(1)} %all-to-all-done.refs_1_.refs_4_, s32[32,128]{1,0:T(8,128)S(1)} %get-tuple-element.34.refs_2_.refs_1_, ...), custom_call_target="tpu_custom_call", output_to_operand_aliasing={{1}: (4, {})} | custom-call | tf_op jit(solution)/shard_map/block_values/pallas_call | solution.py:695
  54.2 13.6 %all_to_all.10.refs_3_ = f32[32,4,128]{2,1,0:T(4,128)S(1)} all-to-all(f32[32,4,128]{2,1,0:T(4,128)S(1)} %get-tuple-element.39), channel_id=1, replica_groups=mesh['rec'=8,'tile'=4] {'rec','tile'}, dimensions={0} | all-to-all | bytes 131072 | tf_op jit(solution)/shard_map/all_to_all | solution.py:708
  67.8 0.0 copy-done.1
  67.8 2.8 %adjoint_field.1 = (f32[1,128]{1,0:T(1,128)S(1)}, f32[2,128]{1,0:T(2,128)S(1)}, f32[16,240,128]{2,1,0:T(8,128)S(1)}, f32[4,240,128]{2,1,0:T(8,128)S(1)}, f32[120,128]{1,0:T(8,128)S(1)}, /*index=5*/f32[120,128]{1,0:T(8,128)S(1)}) custom-call(s32[8,128]{1,0:T(8,128)S(1)} %broadcast_in_dim.15.refs_0_.par_ref, s32[32,128]{1,0:T(8,128)S(1)} %get-tuple-element.34.refs_2_.refs_1_, ...), custom_call_target="tpu_custom_call" | custom-call | tf_op jit(solution)/shard_map/adjoint_field/pallas_call | solution.py:713
  70.6 0.0 copy-start.6
  70.7 0.7 collective-permute-start.6
  71.3 0.1 gradient_odd.1.after
  71.4 0.7 collective-permute-start.7
  72.1 0.1 collective-permute-start.5
  72.2 0.5 collective-permute-start.4
  72.7 0.0 copy-done.6
  72.7 2.3 %gradient_local.1.refs_1_.after = f32[16,240,128]{2,1,0:T(8,128)S(1)} custom-call(f32[4,240,128]{2,1,0:T(8,128)S(1)} %gradient_odd.1.after, f32[16,240,128]{2,1,0:T(8,128)S(1)} %get-tuple-element.43.refs_3_.field_ref, bf16[240,240]{1,0:T(8,128)(2,1)S(1)} %copy-done.4, bf16[240,240]{1,0:T(8,128)(2,1)S(1)} %copy-done.3, bf16[256,256]{1,0:T(8,128)(2,1)S(1)} %copy-done.6), custom_call_target="tpu_custom_call" | custom-call | tf_op jit(solution)/shard_map/gradient_local/pallas_call | solution.py:619
  75.0 0.0 collective-permute-done.5.refs_3_.after_ref
  75.0 1.4 %collective-permute-done.4.refs_2_.before_ref = f32[120,128]{1,0:T(8,128)S(1)} collective-permute-done((f32[120,128]{1,0:T(8,128)S(1)}, f32[120,128]{1,0:T(8,128)S(1)}, u32[]{:S(2)}, u32[]{:S(2)}) %collective-permute-start.4) | collective-permute-done | bytes 61472 | tf_op jit(solution)/shard_map/ppermute | solution.py:616
  76.4 0.2 gradient_corners.1
  76.6 3.1 %collective-permute-start.8 = (f32[64,128]{1,0:T(8,128)S(1)}, f32[64,128]{1,0:T(8,128)S(1)}, u32[]{:S(2)}, u32[]{:S(2)}) collective-permute-start(f32[64,128]{1,0:T(8,128)S(1)} %get-tuple-element.46), channel_id=1, source_target_pairs={{0,4},{4,8},{8,12},{12,16},{16,20},{20,24},{24,28},{28,0},{1,5},{5... | collective-permute-start | bytes 98312 | tf_op jit(solution)/shard_map/ppermute | solution.py:616
  79.7 1.7 %collective-permute-start.9 = (f32[64,128]{1,0:T(8,128)S(1)}, f32[64,128]{1,0:T(8,128)S(1)}, u32[]{:S(2)}, u32[]{:S(2)}) collective-permute-start(f32[64,128]{1,0:T(8,128)S(1)} %get-tuple-element.47), channel_id=1, source_target_pairs={{4,0},{8,4},{12,8},{16,12},{20,16},{24,20},{28,24},{0,28},{5,1},{9... | collective-permute-start | bytes 98312 | tf_op jit(solution)/shard_map/ppermute | solution.py:616
  81.4 1.8 %gradient_strips.1.local_ref = f32[240,16,128]{2,1,0:T(8,128)S(1)} custom-call(s32[8,128]{1,0:T(8,128)S(1)} %broadcast_in_dim.15.refs_0_.par_ref, f32[16,240,128]{2,1,0:T(8,128)S(1)} %gradient_local.1.refs_1_.after, f32[120,128]{1,0:T(8,128)S(1)} %collective-permute-done.4.refs_2_.before_ref, f32[120,128]{1,0:T(8,128)S(1)} %collective-permute-done.5.refs_3_.after_ref, ...), custom_call_target="tpu_custom_call" | custom-call | tf_op jit(solution)/shard_map/gradient_strips/pallas_call | solution.py:628
  83.2 0.0 collective-permute-done.6
  83.3 0.0 collective-permute-done.7
  83.3 0.0 collective-permute-done.8.corner_before
  83.3 0.6 collective-permute-done.9.corner_after
  84.0 0.0 copy-done.12
  84.0 2.7 %gradient.1 = (f32[1,64]{1,0:T(1,128)}, f32[240,16,128]{2,1,0:T(8,128)}) custom-call(s32[8,128]{1,0:T(8,128)S(1)} %broadcast_in_dim.15.refs_0_.par_ref, f32[1,128]{1,0:T(1,128)S(1)} %get-tuple-element.40.model_ref, f32[240,16,128]{2,1,0:T(8,128)S(1)} %gradient_strips.1.local_ref, f32[2,128]{1,0:T(2,128)S(1)} %get-tuple-element.42.refs_2_.factor_ref, ...), custom_call_target="tpu_custom_call" | custom-call | tf_op jit(solution)/shard_map/gradient/pallas_call | solution.py:729
  (5 shorter events, 0.1 us)
Async XLA Ops:
  3.2 46.8 %all-to-all-start = ((bf16[32,200,128]{2,1,0:T(8,128)(2,1)}), bf16[32,200,128]{2,1,0:T(8,128)(2,1)S(1)}, u32[]{:S(2)}, u32[]{:S(2)}) async-start(bf16[32,200,128]{2,1,0:T(8,128)(2,1)} %prepare_blocks.1.after), calls=%async_computation | async-start | bytes 3276800 | tf_op jit(solution)/shard_map/all_to_all | solution.py:662
  10.5 1.5 %copy-start.7 = (f32[240,16,128]{2,1,0:T(8,128)S(1)}, f32[240,16,128]{2,1,0:T(8,128)}, u32[]{:S(2)}) copy-start(f32[240,16,128]{2,1,0:T(8,128)} %control_ref.1) | copy-start | bytes 5898244
  12.1 12.8 %copy-start.3 = (bf16[240,240]{1,0:T(8,128)(2,1)S(1)}, bf16[240,240]{1,0:T(8,128)(2,1)}, u32[]{:S(2)}) copy-start(bf16[240,240]{1,0:T(8,128)(2,1)} %constant.42.clone.time_low.refs_5_) | copy-start | bytes 345604
  12.1 12.8 %copy-start.4 = (bf16[240,240]{1,0:T(8,128)(2,1)S(1)}, bf16[240,240]{1,0:T(8,128)(2,1)}, u32[]{:S(2)}) copy-start(bf16[240,240]{1,0:T(8,128)(2,1)} %constant.41.clone.time_high.refs_4_) | copy-start | bytes 345604
  12.1 12.8 %copy-start.5 = (bf16[256,256]{1,0:T(8,128)(2,1)S(1)}, bf16[256,256]{1,0:T(8,128)(2,1)}, u32[]{:S(2)}) copy-start(bf16[256,256]{1,0:T(8,128)(2,1)} %constant.43.clone.col_both) | copy-start | bytes 393220
  12.1 12.8 %copy-start.11 = (bf16[2,384,512]{2,1,0:T(8,128)(2,1)S(1)}, bf16[2,384,512]{2,1,0:T(8,128)(2,1)}, u32[]{:S(2)}) copy-start(bf16[2,384,512]{2,1,0:T(8,128)(2,1)} %constant.46.clone.beyond_ref) | copy-start | bytes 2359300
  13.5 9.1 %collective-permute-start.1 = (f32[120,128]{1,0:T(8,128)S(1)}, f32[120,128]{1,0:T(8,128)S(1)}, u32[]{:S(2)}, u32[]{:S(2)}) collective-permute-start(f32[120,128]{1,0:T(8,128)S(1)} %get-tuple-element.28), channel_id=1, source_target_pairs={{1,0},{2,1},{3,2},{0,3},{5,4},{6,5},{7,6},{4,7},{9,8},{10,9},{11,1... | collective-permute-start | bytes 184328 | tf_op jit(solution)/shard_map/ppermute | solution.py:616
  15.1 9.8 %collective-permute-start = (f32[120,128]{1,0:T(8,128)S(1)}, f32[120,128]{1,0:T(8,128)S(1)}, u32[]{:S(2)}, u32[]{:S(2)}) collective-permute-start(f32[120,128]{1,0:T(8,128)S(1)} %get-tuple-element.26.after), channel_id=1, source_target_pairs={{0,1},{1,2},{2,3},{3,0},{4,5},{5,6},{6,7},{7,4},{8,9},{9,10},{10,1... | collective-permute-start | bytes 184328 | tf_op jit(solution)/shard_map/ppermute | solution.py:616
  27.6 14.9 %collective-permute-start.2 = (bf16[4,240,128]{2,1,0:T(8,128)(2,1)S(1)}, bf16[4,240,128]{2,1,0:T(8,128)(2,1)S(1)}, u32[]{:S(2)}, u32[]{:S(2)}) collective-permute-start(bf16[4,240,128]{2,1,0:T(8,128)(2,1)S(1)} %get-tuple-element.29), channel_id=1, source_target_pairs={{0,4},{4,0},{8,12},{12,8},{16,20},{20,16},{24,28},{28,24},{1,5},{5... | collective-permute-start | bytes 737288 | tf_op jit(solution)/shard_map/ppermute | solution.py:547
  27.6 3.8 %copy-start.2 = (bf16[384,2048]{1,0:T(8,128)(2,1)S(1)}, bf16[384,2048]{1,0:T(8,128)(2,1)}, u32[]{:S(2)}) copy-start(bf16[384,2048]{1,0:T(8,128)(2,1)} %constant.44.clone.refs_6_) | copy-start | bytes 4718596
  27.6 24.1 %collective-permute-start.3 = (bf16[4,240,128]{2,1,0:T(8,128)(2,1)}, bf16[4,240,128]{2,1,0:T(8,128)(2,1)}, u32[]{:S(2)}, u32[]{:S(2)}) collective-permute-start(bf16[4,240,128]{2,1,0:T(8,128)(2,1)} %get-tuple-element.33), channel_id=1, source_target_pairs={{4,8},{8,4},{12,16},{16,12},{20,24},{24,20},{5,9},{9,5},{13,17},{1... | collective-permute-start | bytes 737288 | tf_op jit(solution)/shard_map/ppermute | solution.py:548
  31.4 11.1 %copy-start.9 = (bf16[240,16,128]{2,1,0:T(8,128)(2,1)S(1)}, bf16[240,16,128]{2,1,0:T(8,128)(2,1)}, u32[]{:S(2)}) copy-start(bf16[240,16,128]{2,1,0:T(8,128)(2,1)} %prior_ref.1) | copy-start | bytes 2949124
  31.4 11.1 %copy-start.10 = (bf16[240,16,128]{2,1,0:T(8,128)(2,1)S(1)}, bf16[240,16,128]{2,1,0:T(8,128)(2,1)}, u32[]{:S(2)}) copy-start(bf16[240,16,128]{2,1,0:T(8,128)(2,1)} %scale_ref.1) | copy-start | bytes 2949124
  45.2 1.3 %copy-start = (f32[16,240,128]{2,1,0:T(8,128)}, f32[16,240,128]{2,1,0:T(8,128)S(1)}, u32[]{:S(2)}) copy-start(f32[16,240,128]{2,1,0:T(8,128)S(1)} %get-tuple-element.30.refs_2_.refs_5_) | copy-start | bytes 5898244
  46.4 1.3 %copy-start.8 = (f32[16,240,128]{2,1,0:T(8,128)}, f32[16,240,128]{2,1,0:T(8,128)S(1)}, u32[]{:S(2)}) copy-start(f32[16,240,128]{2,1,0:T(8,128)S(1)} %get-tuple-element.31.refs_3_) | copy-start | bytes 5898244
  51.7 16.1 %copy-start.1 = (f32[16,240,128]{2,1,0:T(8,128)S(1)}, f32[16,240,128]{2,1,0:T(8,128)}, u32[]{:S(2)}) copy-start(f32[16,240,128]{2,1,0:T(8,128)} %copy-done) | copy-start | bytes 5898244
  70.6 2.1 %copy-start.6 = (bf16[256,256]{1,0:T(8,128)(2,1)S(1)}, bf16[256,256]{1,0:T(8,128)(2,1)}, u32[]{:S(2)}) copy-start(bf16[256,256]{1,0:T(8,128)(2,1)} %constant.43.clone.col_both) | copy-start | bytes 393220
  70.7 12.6 %collective-permute-start.6 = (f16[4,240,128]{2,1,0:T(8,128)(2,1)S(1)}, f16[4,240,128]{2,1,0:T(8,128)(2,1)S(1)}, u32[]{:S(2)}, u32[]{:S(2)}) collective-permute-start(f16[4,240,128]{2,1,0:T(8,128)(2,1)S(1)} %convert_element_type.16), channel_id=1, source_target_pairs={{0,4},{4,0},{8,12},{12,8},{16,20},{20,16},{24,28},{28,24},{1,5},{5... | collective-permute-start | bytes 737288 | tf_op jit(solution)/shard_map/ppermute | solution.py:724
  71.4 11.9 %collective-permute-start.7 = (f16[4,240,128]{2,1,0:T(8,128)(2,1)S(1)}, f16[4,240,128]{2,1,0:T(8,128)(2,1)S(1)}, u32[]{:S(2)}, u32[]{:S(2)}) collective-permute-start(f16[4,240,128]{2,1,0:T(8,128)(2,1)S(1)} %convert_element_type.18), channel_id=1, source_target_pairs={{4,8},{8,4},{12,16},{16,12},{20,24},{24,20},{5,9},{9,5},{13,17},{1... | collective-permute-start | bytes 737288 | tf_op jit(solution)/shard_map/ppermute | solution.py:635
  72.1 2.9 %collective-permute-start.5 = (f32[120,128]{1,0:T(8,128)S(1)}, f32[120,128]{1,0:T(8,128)S(1)}, u32[]{:S(2)}, u32[]{:S(2)}) collective-permute-start(f32[120,128]{1,0:T(8,128)S(1)} %get-tuple-element.44), channel_id=1, source_target_pairs={{1,0},{2,1},{3,2},{0,3},{5,4},{6,5},{7,6},{4,7},{9,8},{10,9},{11,1... | collective-permute-start | bytes 184328 | tf_op jit(solution)/shard_map/ppermute | solution.py:616
  72.2 4.2 %collective-permute-start.4 = (f32[120,128]{1,0:T(8,128)S(1)}, f32[120,128]{1,0:T(8,128)S(1)}, u32[]{:S(2)}, u32[]{:S(2)}) collective-permute-start(f32[120,128]{1,0:T(8,128)S(1)} %get-tuple-element.41.refs_1_), channel_id=1, source_target_pairs={{0,1},{1,2},{2,3},{3,0},{4,5},{5,6},{6,7},{7,4},{8,9},{9,10},{10,1... | collective-permute-start | bytes 184328 | tf_op jit(solution)/shard_map/ppermute | solution.py:616
  76.6 6.7 %collective-permute-start.8 = (f32[64,128]{1,0:T(8,128)S(1)}, f32[64,128]{1,0:T(8,128)S(1)}, u32[]{:S(2)}, u32[]{:S(2)}) collective-permute-start(f32[64,128]{1,0:T(8,128)S(1)} %get-tuple-element.46), channel_id=1, source_target_pairs={{0,4},{4,8},{8,12},{12,16},{16,20},{20,24},{24,28},{28,0},{1,5},{5... | collective-permute-start | bytes 98312 | tf_op jit(solution)/shard_map/ppermute | solution.py:616
  79.7 4.2 %copy-start.12 = (bf16[2,96,512]{2,1,0:T(8,128)(2,1)S(1)}, bf16[2,96,512]{2,1,0:T(8,128)(2,1)}, u32[]{:S(2)}) copy-start(bf16[2,96,512]{2,1,0:T(8,128)(2,1)} %constant.45.clone.corner_weights) | copy-start | bytes 589828
  79.7 4.2 %collective-permute-start.9 = (f32[64,128]{1,0:T(8,128)S(1)}, f32[64,128]{1,0:T(8,128)S(1)}, u32[]{:S(2)}, u32[]{:S(2)}) collective-permute-start(f32[64,128]{1,0:T(8,128)S(1)} %get-tuple-element.47), channel_id=1, source_target_pairs={{4,0},{8,4},{12,8},{16,12},{20,16},{24,20},{28,24},{0,28},{5,1},{9... | collective-permute-start | bytes 98312 | tf_op jit(solution)/shard_map/ppermute | solution.py:616

commit v12 on v11

--- a/solution.py
+++ b/solution.py
@@ -13,6 +13,7 @@
 SUB = 8
 FOOT_MAX = 0.02
 PARTS = 4
+PIECES = 3
 SCALE_MAX = 2.0
 HALF_TOP = 32768.0
 F16 = jnp.float16
@@ -149,7 +150,17 @@
         out_ref[row] = (choose(odd, first, last) if even else choose(odd, last, first)) * factor
 
 
-def turn_kernel(after, control_ref, field_ref, last_ref, first_ref):
+def turn_kernel(after, control_ref, field_ref, last_ref, first_ref, flags_ref, *, n_rec, n_tile):
+    rec, tile = lax.axis_index("rec"), lax.axis_index("tile")
+    flags = [
+        rec % 2, rec * 0, rec, jnp.where(tile == 0, 1, 0), jnp.where(tile == n_tile - 1, 1, 0),
+        jnp.where(rec == 0, 1, 0), jnp.where(rec == n_rec - 1, 1, 0),
+    ]
+    line = lax.broadcasted_iota(jnp.int32, flags_ref.shape, 0)
+    value = jnp.zeros(flags_ref.shape, jnp.int32)
+    for k, flag in enumerate(flags):
+        value = jnp.where(line == k, flag.astype(jnp.int32), value)
+    flags_ref[...] = value
     rows = control_ref.shape[1]
     for row in range(rows):
         field_ref[row] = control_ref[:, row, :]
@@ -186,7 +197,7 @@
 
 
 def prepare_kernel(
-    after, foot_ref, start_ref, row_ref, slot_ref, count_ref, observed_ref, error_ref, out_ref,
+    foot_ref, start_ref, row_ref, slot_ref, count_ref, observed_ref, error_ref, out_ref,
     blocks_ref, notes_ref, start_vmem, row_vmem, slot_vmem, count_vmem, observed_vmem, error_vmem, sems, *, per,
 ):
     owners, lines, _ = foot_ref.shape
@@ -368,9 +379,9 @@
     factor = factor_ref[1:2, :]
     consts = (time_high, time_low, col_both)
     model_own[...] = model_ref[:, 0 : model_own.shape[1]]
-    copies = [pltpu.make_async_copy(model_own, model_out, sems.at[2])]
+    copies = [pltpu.make_async_copy(model_own, model_out, sems.at[2 * PIECES])]
     copies[0].start()
-    inside = lax.broadcasted_iota(jnp.int32, (hours, half, cols), 1)
+    inside = lax.broadcasted_iota(jnp.int32, (hours // PIECES, half, cols), 1)
     for side in range(2):
         before = side == 0
         for k in range(RAD):
@@ -382,10 +393,15 @@
         for k, part in enumerate(parts):
             edges[:, k if before else half - 1 - k, :] = part
         here = slice(0, half) if before else slice(rows - half, rows)
-        mine = inside < RAD if before else inside >= half - RAD
-        total[:, here, :] = local_ref[:, here, :] + jnp.where(mine, edges[...], 0.0)
-        copies.append(pltpu.make_async_copy(total.at[:, here, :], out_ref.at[:, here, :], sems.at[side]))
-        copies[-1].start()
+        for piece in range(PIECES):
+            span = slice(piece * hours // PIECES, (piece + 1) * hours // PIECES)
+            mine = inside < RAD if before else inside >= half - RAD
+            total[span, here, :] = local_ref[span, here, :] + jnp.where(mine, edges[span], 0.0)
+            copy = pltpu.make_async_copy(
+                total.at[span, here, :], out_ref.at[span, here, :], sems.at[side * PIECES + piece]
+            )
+            copy.start()
+            copies.append(copy)
     for copy in copies:
         copy.wait()
 
@@ -593,11 +609,6 @@
     per = observed.shape[0]
     groups = per * n_rec // LANES
     shift = (hours - 1).bit_length()
-    rec, tile = lax.axis_index("rec"), lax.axis_index("tile")
-    flags = [rec % 2, rec * 0, rec, tile == 0, tile == n_tile - 1, rec == 0, rec == n_rec - 1]
-    flags += [rec * 0] * (SUB - len(flags))
-    par = jnp.stack([flag.astype(jnp.int32) for flag in flags])
-    par = jnp.broadcast_to(par[:, None], (SUB, LANES))
     base, own_parts, corner_parts, beyond_parts = constants(hours, rows, cols)
     base = [jnp.asarray(c) for c in base]
     own_parts = jnp.asarray(own_parts)
@@ -642,7 +653,7 @@
     sent = call(
         prepare,
         jax.ShapeDtypeStruct((devices, lines, cols), BF16),
-        [VM] + [HB] * 7,
+        [HB] * 7,
         [
             pltpu.VMEM((devices, slots * heights, cols), BF16),
             pltpu.VMEM((devices, SUB, LANES), BF16),
@@ -652,7 +663,7 @@
         ],
         "prepare_blocks",
         out_specs=HB,
-    )(par, *[
+    )(*[
         far(x)
         for x in (
             footprint.reshape(devices, slots * heights, cols),
@@ -660,8 +671,15 @@
         )
     ])
     foot = lax.all_to_all(sent, AXES, split_axis=0, concat_axis=0, tiled=True)
-    field, *strips = call(
-        turn_kernel, [field_shape, strip, strip], [HB, VM], [], "turn_control"
+    def turn(*refs):
+        turn_kernel(*refs, n_rec=n_rec, n_tile=n_tile)
+
+    field, *strips, par = call(
+        turn,
+        [field_shape, strip, strip, jax.ShapeDtypeStruct((SUB, LANES), jnp.int32)],
+        [HB, VM],
+        [],
+        "turn_control",
     )(sent, control)
     got_strips = pass_on("tile", *strips)
     local = call(local_kernel, field_shape, [VM] * 5, [], "control_local")(strips[0], field, *base)
@@ -735,7 +753,7 @@
             pltpu.VMEM((hours, rows // 2, cols), F32),
             pltpu.VMEM((hours, rows, cols), F32),
             pltpu.VMEM((1, per), F32),
-            pltpu.SemaphoreType.DMA((3,)),
+            pltpu.SemaphoreType.DMA((2 * PIECES + 1,)),
         ],
         "gradient",
         out_specs=[HB, HB],

time: 87.2 us -> 86.9 us (level)
  no operation moved by 1% of the time
where the time goes in v12:
time: 86.9 us; the launch traced here: 86.5 us
  Pallas kernels  26.5 us (30%)
  waiting for transfers between devices  24.1 us (28%)
  starting transfers between devices  17 us (20%)
  blocking collectives  13.6 us (16%)
  local copies, waits for them, and re-layouts  4.15 us (5%)
  between operations  1.05 us (1%)
    all_to_all x1, blocking collectives, per_device(): lax.all_to_all(partial, AXES, split_axis=0, concat_axis=0, tiled=True)  13.6 us
    ppermute x6, waiting for transfers between devices, pass_on(): return (lax.ppermute(last, axis, onward), lax.ppermute(first, axis, back))  11.8 us
    ppermute x1, waiting for transfers between devices, swap(): lax.ppermute(even, axis, swap_pairs(count, False))  10 us
    all_to_all x1, starting transfers between devices, per_device(): foot = lax.all_to_all(sent, AXES, split_axis=0, concat_axis=0, tiled=True)  7.3 us
    ppermute x6, starting transfers between devices, pass_on(): return (lax.ppermute(last, axis, onward), lax.ppermute(first, axis, back))  6.9 us
    unnamed x26, local copies, waits for them, and re-layouts  4.15 us
    pallas_call x2, Pallas kernels, strip_sums(): call(kernel, shape, [VM] * 7, [], name)  2.93 us
    pallas_call x1, Pallas kernels, per_device(): call(adjoint, [array(1, LANES), array(2, LANES), field_shape, block, stri...  2.83 us
  transfers between devices with their start and end apart: 11, of which 6 were waited for; matrix products, arithmetic and copies ran while one was open for 0% of the time, Pallas kernels for 19%

profile of v12, /device:TPU:0, one launch (start us, length us, event | category | flops | bytes accessed | tf_op | source)
XLA Modules:
  0.0 86.5 jit_solution(1357859025329705160)
XLA Ops:
  0.6 2.4 %prepare_blocks.1.refs_0_ = bf16[32,200,128]{2,1,0:T(8,128)(2,1)} custom-call(bf16[32,192,128]{2,1,0:T(8,128)(2,1)} %bitcast.8, s32[8,32]{1,0:T(8,128)} %bitcast.9, s32[8,32]{1,0:T(8,128)} %bitcast.10, s32[8,32]{1,0:T(8,128)} %bitcast.11, s32[1,32]{1,0:T(1,128)} %bitcast.12, f32[1,64]{1,0:T(1,128)} %bitcast.13, f32[1,64]{1,0:T(1,128)} %bitcast.14), custom_call_target="tpu_custom_call" | custom-call | tf_op jit(solution)/shard_map/prepare_blocks/pallas_call | solution.py:653
  3.0 7.3 %all-to-all-start = ((bf16[32,200,128]{2,1,0:T(8,128)(2,1)}), bf16[32,200,128]{2,1,0:T(8,128)(2,1)S(1)}, u32[]{:S(2)}, u32[]{:S(2)}) async-start(bf16[32,200,128]{2,1,0:T(8,128)(2,1)} %prepare_blocks.1.refs_0_), calls=%async_computation | async-start | bytes 3276800 | tf_op jit(solution)/shard_map/all_to_all | solution.py:673
  10.3 0.0 copy-start.7
  10.4 1.5 %copy-done.7 = f32[240,16,128]{2,1,0:T(8,128)S(1)} copy-done((f32[240,16,128]{2,1,0:T(8,128)S(1)}, f32[240,16,128]{2,1,0:T(8,128)}, u32[]{:S(2)}) %copy-start.7) | copy-done | bytes 1966104
  11.9 0.0 copy-start.3
  11.9 0.0 copy-start.4
  11.9 0.0 copy-start.5
  11.9 0.0 copy-start.11
  11.9 1.5 %turn_control.1 = (f32[16,240,128]{2,1,0:T(8,128)S(1)}, f32[120,128]{1,0:T(8,128)S(1)}, f32[120,128]{1,0:T(8,128)S(1)}, s32[8,128]{1,0:T(8,128)S(1)}) custom-call(bf16[32,200,128]{2,1,0:T(8,128)(2,1)} %prepare_blocks.1.refs_0_, f32[240,16,128]{2,1,0:T(8,128)S(1)} %copy-done.7), custom_call_target="tpu_custom_call" | custom-call | tf_op jit(solution)/shard_map/turn_control/pallas_call | solution.py:677
  13.4 1.6 %collective-permute-start.1 = (f32[120,128]{1,0:T(8,128)S(1)}, f32[120,128]{1,0:T(8,128)S(1)}, u32[]{:S(2)}, u32[]{:S(2)}) collective-permute-start(f32[120,128]{1,0:T(8,128)S(1)} %get-tuple-element.30), channel_id=1, source_target_pairs={{1,0},{2,1},{3,2},{0,3},{5,4},{6,5},{7,6},{4,7},{9,8},{10,9},{11,1... | collective-permute-start | bytes 184328 | tf_op jit(solution)/shard_map/ppermute | solution.py:627
  14.9 0.0 collective-permute-start
  14.9 7.5 %collective-permute-done.1.refs_3_.after_ref = f32[120,128]{1,0:T(8,128)S(1)} collective-permute-done((f32[120,128]{1,0:T(8,128)S(1)}, f32[120,128]{1,0:T(8,128)S(1)}, u32[]{:S(2)}, u32[]{:S(2)}) %collective-permute-start.1) | collective-permute-done | bytes 61472 | tf_op jit(solution)/shard_map/ppermute | solution.py:627
  22.4 2.3 %collective-permute-done.refs_2_.before_ref = f32[120,128]{1,0:T(8,128)S(1)} collective-permute-done((f32[120,128]{1,0:T(8,128)S(1)}, f32[120,128]{1,0:T(8,128)S(1)}, u32[]{:S(2)}, u32[]{:S(2)}) %collective-permute-start) | collective-permute-done | bytes 61472 | tf_op jit(solution)/shard_map/ppermute | solution.py:627
  24.7 0.0 copy-done.3
  24.7 0.0 copy-done.4
  24.7 0.0 copy-done.5
  24.7 0.0 copy-done.11
  24.7 2.7 %control_beyond.1 = (bf16[4,240,128]{2,1,0:T(8,128)(2,1)S(1)}, bf16[4,240,128]{2,1,0:T(8,128)(2,1)}) custom-call(s32[8,128]{1,0:T(8,128)S(1)} %get-tuple-element.27.refs_0_.par_ref, f32[16,240,128]{2,1,0:T(8,128)S(1)} %get-tuple-element.29.field_ref, f32[120,128]{1,0:T(8,128)S(1)} %collective-permute-done.refs_2_.before_ref, ...), custom_call_target="tpu_custom_call" | custom-call | tf_op jit(solution)/shard_map/control_beyond/pallas_call | solution.py:687
  27.4 0.0 collective-permute-start.2
  27.4 0.0 copy-start.2
  27.4 1.5 %collective-permute-start.3 = (bf16[4,240,128]{2,1,0:T(8,128)(2,1)}, bf16[4,240,128]{2,1,0:T(8,128)(2,1)}, u32[]{:S(2)}, u32[]{:S(2)}) collective-permute-start(bf16[4,240,128]{2,1,0:T(8,128)(2,1)} %get-tuple-element.35), channel_id=1, source_target_pairs={{4,8},{8,4},{12,16},{16,12},{20,24},{24,20},{5,9},{9,5},{13,17},{1... | collective-permute-start | bytes 737288 | tf_op jit(solution)/shard_map/ppermute | solution.py:564
  28.9 2.3 %control_local.1.refs_1_ = f32[16,240,128]{2,1,0:T(8,128)S(1)} custom-call(f32[120,128]{1,0:T(8,128)S(1)} %get-tuple-element.28.after, f32[16,240,128]{2,1,0:T(8,128)S(1)} %get-tuple-element.29.field_ref, bf16[240,240]{1,0:T(8,128)(2,1)S(1)} %copy-done.4, bf16[240,240]{1,0:T(8,128)(2,1)S(1)} %copy-done.3, bf16[256,256]{1,0:T(8,128)(2,1)S(1)} %copy-done.5), custom_call_target="tpu_custom_call" | custom-call | tf_op jit(solution)/shard_map/control_local/pallas_call | solution.py:685
  31.2 0.0 copy-done.2
  31.2 0.0 copy-start.9
  31.2 0.0 copy-start.10
  31.2 1.1 %control_strips.1.local_ref = f32[16,240,128]{2,1,0:T(8,128)S(1)} custom-call(s32[8,128]{1,0:T(8,128)S(1)} %get-tuple-element.27.refs_0_.par_ref, f32[16,240,128]{2,1,0:T(8,128)S(1)} %control_local.1.refs_1_, f32[120,128]{1,0:T(8,128)S(1)} %collective-permute-done.refs_2_.before_ref, f32[120,128]{1,0:T(8,128)S(1)} %collective-permute-done.1.refs_3_.after_ref, ...), custom_call_target="tpu_custom_call" | custom-call | tf_op jit(solution)/shard_map/control_strips/pallas_call | solution.py:639
  32.3 10.0 %collective-permute-done.2.got_ref = bf16[4,240,128]{2,1,0:T(8,128)(2,1)S(1)} collective-permute-done((bf16[4,240,128]{2,1,0:T(8,128)(2,1)S(1)}, bf16[4,240,128]{2,1,0:T(8,128)(2,1)S(1)}, u32[]{:S(2)}, u32[]{:S(2)}) %collective-permute-start.2) | collective-permute-done | bytes 245792 | tf_op jit(solution)/shard_map/ppermute | solution.py:563
  42.3 0.0 copy-done.9
  42.4 0.0 copy-done.10
  42.4 2.6 %flux_field.1 = (f32[16,240,128]{2,1,0:T(8,128)S(1)}, f32[16,240,128]{2,1,0:T(8,128)S(1)}) custom-call(s32[8,128]{1,0:T(8,128)S(1)} %get-tuple-element.27.refs_0_.par_ref, f32[16,240,128]{2,1,0:T(8,128)S(1)} %control_strips.1.local_ref, bf16[240,16,128]{2,1,0:T(8,128)(2,1)S(1)} %copy-done.9, bf16[240,16,128]{2,1,0:T(8,128)(2,1)S(1)} %copy-done.10, ...), custom_call_target="tpu_custom_call" | custom-call | tf_op jit(solution)/shard_map/flux_field/pallas_call | solution.py:692
  45.0 0.0 copy-start
  45.0 1.3 %copy-done = f32[16,240,128]{2,1,0:T(8,128)} copy-done((f32[16,240,128]{2,1,0:T(8,128)}, f32[16,240,128]{2,1,0:T(8,128)S(1)}, u32[]{:S(2)}) %copy-start) | copy-done | bytes 1966104
  46.3 0.0 copy-start.8
  46.3 1.3 %copy-done.8 = f32[16,240,128]{2,1,0:T(8,128)} copy-done((f32[16,240,128]{2,1,0:T(8,128)}, f32[16,240,128]{2,1,0:T(8,128)S(1)}, u32[]{:S(2)}) %copy-start.8) | copy-done | bytes 1966104
  47.6 2.2 %all-to-all-done.refs_1_.refs_4_ = bf16[32,200,128]{2,1,0:T(8,128)(2,1)S(1)} async-done(((bf16[32,200,128]{2,1,0:T(8,128)(2,1)}), bf16[32,200,128]{2,1,0:T(8,128)(2,1)S(1)}, u32[]{:S(2)}, u32[]{:S(2)}) %all-to-all-start) | async-done | bytes 1638432 | tf_op jit(solution)/shard_map/all_to_all | solution.py:673
  49.8 1.7 %load_flux.1 = (s32[32,128]{1,0:T(8,128)S(1)}, f32[32,128]{1,0:T(8,128)S(1)}, f32[4,240,128]{2,1,0:T(8,128)S(1)}, f32[16,240,128]{2,1,0:T(8,128)S(1)}) custom-call(s32[8,128]{1,0:T(8,128)S(1)} %get-tuple-element.27.refs_0_.par_ref, bf16[32,200,128]{2,1,0:T(8,128)(2,1)S(1)} %all-to-all-done.refs_1_.refs_4_, f32[16,240,128]{2,1,0:T(8,128)} %copy-done, ...), custom_call_target="tpu_custom_call" | custom-call | tf_op jit(solution)/shard_map/load_flux/pallas_call | solution.py:705
  51.5 0.0 collective-permute-done.3.refs_3_
  51.5 0.0 copy-start.1
  51.5 2.5 %block_values.1 = (f32[32,4,128]{2,1,0:T(4,128)S(1)}, f32[16,240,128]{2,1,0:T(8,128)S(1)}) custom-call(s32[8,128]{1,0:T(8,128)S(1)} %get-tuple-element.27.refs_0_.par_ref, bf16[32,200,128]{2,1,0:T(8,128)(2,1)S(1)} %all-to-all-done.refs_1_.refs_4_, s32[32,128]{1,0:T(8,128)S(1)} %get-tuple-element.36.refs_2_.refs_1_, ...), custom_call_target="tpu_custom_call", output_to_operand_aliasing={{1}: (4, {})} | custom-call | tf_op jit(solution)/shard_map/block_values/pallas_call | solution.py:713
  54.0 13.6 %all_to_all.10.refs_3_ = f32[32,4,128]{2,1,0:T(4,128)S(1)} all-to-all(f32[32,4,128]{2,1,0:T(4,128)S(1)} %get-tuple-element.41), channel_id=1, replica_groups=mesh['rec'=8,'tile'=4] {'rec','tile'}, dimensions={0} | all-to-all | bytes 131072 | tf_op jit(solution)/shard_map/all_to_all | solution.py:726
  67.6 0.0 copy-done.1
  67.6 2.8 %adjoint_field.1 = (f32[1,128]{1,0:T(1,128)S(1)}, f32[2,128]{1,0:T(2,128)S(1)}, f32[16,240,128]{2,1,0:T(8,128)S(1)}, f32[4,240,128]{2,1,0:T(8,128)S(1)}, f32[120,128]{1,0:T(8,128)S(1)}, /*index=5*/f32[120,128]{1,0:T(8,128)S(1)}) custom-call(s32[8,128]{1,0:T(8,128)S(1)} %get-tuple-element.27.refs_0_.par_ref, s32[32,128]{1,0:T(8,128)S(1)} %get-tuple-element.36.refs_2_.refs_1_, ...), custom_call_target="tpu_custom_call" | custom-call | tf_op jit(solution)/shard_map/adjoint_field/pallas_call | solution.py:731
  70.4 0.0 copy-start.6
  70.5 0.7 collective-permute-start.6
  71.1 0.1 gradient_odd.1.after
  71.2 0.7 collective-permute-start.7
  71.9 0.1 collective-permute-start.5
  72.0 0.5 collective-permute-start.4
  72.5 0.0 copy-done.6
  72.5 2.3 %gradient_local.1.refs_1_.after = f32[16,240,128]{2,1,0:T(8,128)S(1)} custom-call(f32[4,240,128]{2,1,0:T(8,128)S(1)} %gradient_odd.1.after, f32[16,240,128]{2,1,0:T(8,128)S(1)} %get-tuple-element.45.refs_3_.field_ref, bf16[240,240]{1,0:T(8,128)(2,1)S(1)} %copy-done.4, bf16[240,240]{1,0:T(8,128)(2,1)S(1)} %copy-done.3, bf16[256,256]{1,0:T(8,128)(2,1)S(1)} %copy-done.6), custom_call_target="tpu_custom_call" | custom-call | tf_op jit(solution)/shard_map/gradient_local/pallas_call | solution.py:630
  74.8 0.0 collective-permute-done.5.refs_3_.after_ref
  74.8 1.4 %collective-permute-done.4.refs_2_.before_ref = f32[120,128]{1,0:T(8,128)S(1)} collective-permute-done((f32[120,128]{1,0:T(8,128)S(1)}, f32[120,128]{1,0:T(8,128)S(1)}, u32[]{:S(2)}, u32[]{:S(2)}) %collective-permute-start.4) | collective-permute-done | bytes 61472 | tf_op jit(solution)/shard_map/ppermute | solution.py:627
  76.2 0.2 gradient_corners.1
  76.4 3.1 %collective-permute-start.8 = (f32[64,128]{1,0:T(8,128)S(1)}, f32[64,128]{1,0:T(8,128)S(1)}, u32[]{:S(2)}, u32[]{:S(2)}) collective-permute-start(f32[64,128]{1,0:T(8,128)S(1)} %get-tuple-element.48), channel_id=1, source_target_pairs={{0,4},{4,8},{8,12},{12,16},{16,20},{20,24},{24,28},{28,0},{1,5},{5... | collective-permute-start | bytes 98312 | tf_op jit(solution)/shard_map/ppermute | solution.py:627
  79.5 0.0 copy-start.12
  79.5 1.7 %collective-permute-start.9 = (f32[64,128]{1,0:T(8,128)S(1)}, f32[64,128]{1,0:T(8,128)S(1)}, u32[]{:S(2)}, u32[]{:S(2)}) collective-permute-start(f32[64,128]{1,0:T(8,128)S(1)} %get-tuple-element.49), channel_id=1, source_target_pairs={{4,0},{8,4},{12,8},{16,12},{20,16},{24,20},{28,24},{0,28},{5,1},{9... | collective-permute-start | bytes 98312 | tf_op jit(solution)/shard_map/ppermute | solution.py:627
  81.2 1.8 %gradient_strips.1.local_ref = f32[240,16,128]{2,1,0:T(8,128)S(1)} custom-call(s32[8,128]{1,0:T(8,128)S(1)} %get-tuple-element.27.refs_0_.par_ref, f32[16,240,128]{2,1,0:T(8,128)S(1)} %gradient_local.1.refs_1_.after, f32[120,128]{1,0:T(8,128)S(1)} %collective-permute-done.4.refs_2_.before_ref, f32[120,128]{1,0:T(8,128)S(1)} %collective-permute-done.5.refs_3_.after_ref, ...), custom_call_target="tpu_custom_call" | custom-call | tf_op jit(solution)/shard_map/gradient_strips/pallas_call | solution.py:639
  83.0 0.0 collective-permute-done.6
  83.1 0.0 collective-permute-done.7
  83.1 0.0 collective-permute-done.8.corner_before
  83.2 0.6 collective-permute-done.9.corner_after
  83.8 0.0 copy-done.12
  83.8 2.6 %gradient.1 = (f32[1,64]{1,0:T(1,128)}, f32[240,16,128]{2,1,0:T(8,128)}) custom-call(s32[8,128]{1,0:T(8,128)S(1)} %get-tuple-element.27.refs_0_.par_ref, f32[1,128]{1,0:T(1,128)S(1)} %get-tuple-element.42.model_ref, f32[240,16,128]{2,1,0:T(8,128)S(1)} %gradient_strips.1.local_ref, f32[2,128]{1,0:T(2,128)S(1)} %get-tuple-element.44.refs_2_.factor_ref, ...), custom_call_target="tpu_custom_call" | custom-call | tf_op jit(solution)/shard_map/gradient/pallas_call | solution.py:747
  (4 shorter events, 0.1 us)
Async XLA Ops:
  3.0 46.8 %all-to-all-start = ((bf16[32,200,128]{2,1,0:T(8,128)(2,1)}), bf16[32,200,128]{2,1,0:T(8,128)(2,1)S(1)}, u32[]{:S(2)}, u32[]{:S(2)}) async-start(bf16[32,200,128]{2,1,0:T(8,128)(2,1)} %prepare_blocks.1.refs_0_), calls=%async_computation | async-start | bytes 3276800 | tf_op jit(solution)/shard_map/all_to_all | solution.py:673
  10.3 1.5 %copy-start.7 = (f32[240,16,128]{2,1,0:T(8,128)S(1)}, f32[240,16,128]{2,1,0:T(8,128)}, u32[]{:S(2)}) copy-start(f32[240,16,128]{2,1,0:T(8,128)} %refs_1_.1) | copy-start | bytes 5898244
  11.9 12.8 %copy-start.3 = (bf16[240,240]{1,0:T(8,128)(2,1)S(1)}, bf16[240,240]{1,0:T(8,128)(2,1)}, u32[]{:S(2)}) copy-start(bf16[240,240]{1,0:T(8,128)(2,1)} %constant.13.clone.time_low.refs_5_) | copy-start | bytes 345604
  11.9 12.8 %copy-start.4 = (bf16[240,240]{1,0:T(8,128)(2,1)S(1)}, bf16[240,240]{1,0:T(8,128)(2,1)}, u32[]{:S(2)}) copy-start(bf16[240,240]{1,0:T(8,128)(2,1)} %constant.12.clone.time_high.refs_4_) | copy-start | bytes 345604
  11.9 12.8 %copy-start.5 = (bf16[256,256]{1,0:T(8,128)(2,1)S(1)}, bf16[256,256]{1,0:T(8,128)(2,1)}, u32[]{:S(2)}) copy-start(bf16[256,256]{1,0:T(8,128)(2,1)} %constant.14.clone.col_both) | copy-start | bytes 393220
  11.9 12.8 %copy-start.11 = (bf16[2,384,512]{2,1,0:T(8,128)(2,1)S(1)}, bf16[2,384,512]{2,1,0:T(8,128)(2,1)}, u32[]{:S(2)}) copy-start(bf16[2,384,512]{2,1,0:T(8,128)(2,1)} %constant.17.clone.beyond_ref) | copy-start | bytes 2359300
  13.4 9.1 %collective-permute-start.1 = (f32[120,128]{1,0:T(8,128)S(1)}, f32[120,128]{1,0:T(8,128)S(1)}, u32[]{:S(2)}, u32[]{:S(2)}) collective-permute-start(f32[120,128]{1,0:T(8,128)S(1)} %get-tuple-element.30), channel_id=1, source_target_pairs={{1,0},{2,1},{3,2},{0,3},{5,4},{6,5},{7,6},{4,7},{9,8},{10,9},{11,1... | collective-permute-start | bytes 184328 | tf_op jit(solution)/shard_map/ppermute | solution.py:627
  14.9 9.8 %collective-permute-start = (f32[120,128]{1,0:T(8,128)S(1)}, f32[120,128]{1,0:T(8,128)S(1)}, u32[]{:S(2)}, u32[]{:S(2)}) collective-permute-start(f32[120,128]{1,0:T(8,128)S(1)} %get-tuple-element.28.after), channel_id=1, source_target_pairs={{0,1},{1,2},{2,3},{3,0},{4,5},{5,6},{6,7},{7,4},{8,9},{9,10},{10,1... | collective-permute-start | bytes 184328 | tf_op jit(solution)/shard_map/ppermute | solution.py:627
  27.4 15.0 %collective-permute-start.2 = (bf16[4,240,128]{2,1,0:T(8,128)(2,1)S(1)}, bf16[4,240,128]{2,1,0:T(8,128)(2,1)S(1)}, u32[]{:S(2)}, u32[]{:S(2)}) collective-permute-start(bf16[4,240,128]{2,1,0:T(8,128)(2,1)S(1)} %get-tuple-element.31), channel_id=1, source_target_pairs={{0,4},{4,0},{8,12},{12,8},{16,20},{20,16},{24,28},{28,24},{1,5},{5... | collective-permute-start | bytes 737288 | tf_op jit(solution)/shard_map/ppermute | solution.py:563
  27.4 3.8 %copy-start.2 = (bf16[384,2048]{1,0:T(8,128)(2,1)S(1)}, bf16[384,2048]{1,0:T(8,128)(2,1)}, u32[]{:S(2)}) copy-start(bf16[384,2048]{1,0:T(8,128)(2,1)} %constant.15.clone.refs_6_) | copy-start | bytes 4718596
  27.4 24.1 %collective-permute-start.3 = (bf16[4,240,128]{2,1,0:T(8,128)(2,1)}, bf16[4,240,128]{2,1,0:T(8,128)(2,1)}, u32[]{:S(2)}, u32[]{:S(2)}) collective-permute-start(bf16[4,240,128]{2,1,0:T(8,128)(2,1)} %get-tuple-element.35), channel_id=1, source_target_pairs={{4,8},{8,4},{12,16},{16,12},{20,24},{24,20},{5,9},{9,5},{13,17},{1... | collective-permute-start | bytes 737288 | tf_op jit(solution)/shard_map/ppermute | solution.py:564
  31.2 11.2 %copy-start.9 = (bf16[240,16,128]{2,1,0:T(8,128)(2,1)S(1)}, bf16[240,16,128]{2,1,0:T(8,128)(2,1)}, u32[]{:S(2)}) copy-start(bf16[240,16,128]{2,1,0:T(8,128)(2,1)} %prior_ref.1) | copy-start | bytes 2949124
  31.2 11.2 %copy-start.10 = (bf16[240,16,128]{2,1,0:T(8,128)(2,1)S(1)}, bf16[240,16,128]{2,1,0:T(8,128)(2,1)}, u32[]{:S(2)}) copy-start(bf16[240,16,128]{2,1,0:T(8,128)(2,1)} %scale_ref.1) | copy-start | bytes 2949124
  45.0 1.3 %copy-start = (f32[16,240,128]{2,1,0:T(8,128)}, f32[16,240,128]{2,1,0:T(8,128)S(1)}, u32[]{:S(2)}) copy-start(f32[16,240,128]{2,1,0:T(8,128)S(1)} %get-tuple-element.32.refs_2_.refs_5_) | copy-start | bytes 5898244
  46.3 1.3 %copy-start.8 = (f32[16,240,128]{2,1,0:T(8,128)}, f32[16,240,128]{2,1,0:T(8,128)S(1)}, u32[]{:S(2)}) copy-start(f32[16,240,128]{2,1,0:T(8,128)S(1)} %get-tuple-element.33.refs_3_) | copy-start | bytes 5898244
  51.5 16.1 %copy-start.1 = (f32[16,240,128]{2,1,0:T(8,128)S(1)}, f32[16,240,128]{2,1,0:T(8,128)}, u32[]{:S(2)}) copy-start(f32[16,240,128]{2,1,0:T(8,128)} %copy-done) | copy-start | bytes 5898244
  70.4 2.1 %copy-start.6 = (bf16[256,256]{1,0:T(8,128)(2,1)S(1)}, bf16[256,256]{1,0:T(8,128)(2,1)}, u32[]{:S(2)}) copy-start(bf16[256,256]{1,0:T(8,128)(2,1)} %constant.14.clone.col_both) | copy-start | bytes 393220
  70.5 12.6 %collective-permute-start.6 = (f16[4,240,128]{2,1,0:T(8,128)(2,1)S(1)}, f16[4,240,128]{2,1,0:T(8,128)(2,1)S(1)}, u32[]{:S(2)}, u32[]{:S(2)}) collective-permute-start(f16[4,240,128]{2,1,0:T(8,128)(2,1)S(1)} %convert_element_type.12), channel_id=1, source_target_pairs={{0,4},{4,0},{8,12},{12,8},{16,20},{20,16},{24,28},{28,24},{1,5},{5... | collective-permute-start | bytes 737288 | tf_op jit(solution)/shard_map/ppermute | solution.py:742
  71.2 11.9 %collective-permute-start.7 = (f16[4,240,128]{2,1,0:T(8,128)(2,1)S(1)}, f16[4,240,128]{2,1,0:T(8,128)(2,1)S(1)}, u32[]{:S(2)}, u32[]{:S(2)}) collective-permute-start(f16[4,240,128]{2,1,0:T(8,128)(2,1)S(1)} %convert_element_type.14), channel_id=1, source_target_pairs={{4,8},{8,4},{12,16},{16,12},{20,24},{24,20},{5,9},{9,5},{13,17},{1... | collective-permute-start | bytes 737288 | tf_op jit(solution)/shard_map/ppermute | solution.py:646
  71.9 2.9 %collective-permute-start.5 = (f32[120,128]{1,0:T(8,128)S(1)}, f32[120,128]{1,0:T(8,128)S(1)}, u32[]{:S(2)}, u32[]{:S(2)}) collective-permute-start(f32[120,128]{1,0:T(8,128)S(1)} %get-tuple-element.46), channel_id=1, source_target_pairs={{1,0},{2,1},{3,2},{0,3},{5,4},{6,5},{7,6},{4,7},{9,8},{10,9},{11,1... | collective-permute-start | bytes 184328 | tf_op jit(solution)/shard_map/ppermute | solution.py:627
  72.0 4.2 %collective-permute-start.4 = (f32[120,128]{1,0:T(8,128)S(1)}, f32[120,128]{1,0:T(8,128)S(1)}, u32[]{:S(2)}, u32[]{:S(2)}) collective-permute-start(f32[120,128]{1,0:T(8,128)S(1)} %get-tuple-element.43.refs_1_), channel_id=1, source_target_pairs={{0,1},{1,2},{2,3},{3,0},{4,5},{5,6},{6,7},{7,4},{8,9},{9,10},{10,1... | collective-permute-start | bytes 184328 | tf_op jit(solution)/shard_map/ppermute | solution.py:627
  76.4 6.7 %collective-permute-start.8 = (f32[64,128]{1,0:T(8,128)S(1)}, f32[64,128]{1,0:T(8,128)S(1)}, u32[]{:S(2)}, u32[]{:S(2)}) collective-permute-start(f32[64,128]{1,0:T(8,128)S(1)} %get-tuple-element.48), channel_id=1, source_target_pairs={{0,4},{4,8},{8,12},{12,16},{16,20},{20,24},{24,28},{28,0},{1,5},{5... | collective-permute-start | bytes 98312 | tf_op jit(solution)/shard_map/ppermute | solution.py:627
  79.5 4.2 %copy-start.12 = (bf16[2,96,512]{2,1,0:T(8,128)(2,1)S(1)}, bf16[2,96,512]{2,1,0:T(8,128)(2,1)}, u32[]{:S(2)}) copy-start(bf16[2,96,512]{2,1,0:T(8,128)(2,1)} %constant.16.clone.corner_weights) | copy-start | bytes 589828
  79.5 4.2 %collective-permute-start.9 = (f32[64,128]{1,0:T(8,128)S(1)}, f32[64,128]{1,0:T(8,128)S(1)}, u32[]{:S(2)}, u32[]{:S(2)}) collective-permute-start(f32[64,128]{1,0:T(8,128)S(1)} %get-tuple-element.49), channel_id=1, source_target_pairs={{4,0},{8,4},{12,8},{16,12},{20,16},{24,20},{28,24},{0,28},{5,1},{9... | collective-permute-start | bytes 98312 | tf_op jit(solution)/shard_map/ppermute | solution.py:627

commit v13 on v12

--- a/solution.py
+++ b/solution.py
@@ -386,17 +386,17 @@
         before = side == 0
         for k in range(RAD):
             even, other = got_e[k], got_o[k]
-            halo[k] = (choose(odd, even, other) if before else choose(odd, other, even)) * factor
+            halo[side, k] = (choose(odd, even, other) if before else choose(odd, other, even)) * factor
         corner = corner_before[...] if before else corner_after[...]
         corner = jnp.where(par_ref[5 + side : 6 + side, :] == 1, 0.0, corner)
-        parts = edge_parts(halo, corner, corner_weights.at[1 - side], consts)
+        parts = edge_parts(halo.at[side], corner, corner_weights.at[1 - side], consts)
         for k, part in enumerate(parts):
-            edges[:, k if before else half - 1 - k, :] = part
+            edges[side, :, k if before else half - 1 - k, :] = part
         here = slice(0, half) if before else slice(rows - half, rows)
         for piece in range(PIECES):
             span = slice(piece * hours // PIECES, (piece + 1) * hours // PIECES)
             mine = inside < RAD if before else inside >= half - RAD
-            total[span, here, :] = local_ref[span, here, :] + jnp.where(mine, edges[span], 0.0)
+            total[span, here, :] = local_ref[span, here, :] + jnp.where(mine, edges[side, span], 0.0)
             copy = pltpu.make_async_copy(
                 total.at[span, here, :], out_ref.at[span, here, :], sems.at[side * PIECES + piece]
             )
@@ -749,8 +749,8 @@
         [array(1, per), array(hours, rows, cols)],
         [VM] * 12,
         [
-            row_scratch,
-            pltpu.VMEM((hours, rows // 2, cols), F32),
+            pltpu.VMEM((2, RAD, hours, cols), F32),
+            pltpu.VMEM((2, hours, rows // 2, cols), F32),
             pltpu.VMEM((hours, rows, cols), F32),
             pltpu.VMEM((1, per), F32),
             pltpu.SemaphoreType.DMA((2 * PIECES + 1,)),

time: 86.9 us -> 86.9 us (level)
  no operation moved by 1% of the time
where the time goes in v13:
time: 86.9 us; the launch traced here: 86.6 us
  Pallas kernels  26.5 us (30%)
  waiting for transfers between devices  24.1 us (28%)
  starting transfers between devices  17 us (20%)
  blocking collectives  13.6 us (16%)
  local copies, waits for them, and re-layouts  4.15 us (5%)
  between operations  1.05 us (1%)
    all_to_all x1, blocking collectives, per_device(): lax.all_to_all(partial, AXES, split_axis=0, concat_axis=0, tiled=True)  13.6 us
    ppermute x6, waiting for transfers between devices, pass_on(): return (lax.ppermute(last, axis, onward), lax.ppermute(first, axis, back))  11.8 us
    ppermute x1, waiting for transfers between devices, swap(): lax.ppermute(even, axis, swap_pairs(count, False))  10 us
    all_to_all x1, starting transfers between devices, per_device(): foot = lax.all_to_all(sent, AXES, split_axis=0, concat_axis=0, tiled=True)  7.3 us
    ppermute x6, starting transfers between devices, pass_on(): return (lax.ppermute(last, axis, onward), lax.ppermute(first, axis, back))  6.9 us
    unnamed x26, local copies, waits for them, and re-layouts  4.15 us
    pallas_call x2, Pallas kernels, strip_sums(): call(kernel, shape, [VM] * 7, [], name)  2.93 us
    pallas_call x1, Pallas kernels, per_device(): call(adjoint, [array(1, LANES), array(2, LANES), field_shape, block, stri...  2.83 us
  transfers between devices with their start and end apart: 11, of which 6 were waited for; matrix products, arithmetic and copies ran while one was open for 0% of the time, Pallas kernels for 19%

profile of v13, /device:TPU:0, one launch (start us, length us, event | category | flops | bytes accessed | tf_op | source)
XLA Modules:
  0.0 86.6 jit_solution(5673977587893585511)
XLA Ops:
  0.6 2.4 %prepare_blocks.1.refs_0_ = bf16[32,200,128]{2,1,0:T(8,128)(2,1)} custom-call(bf16[32,192,128]{2,1,0:T(8,128)(2,1)} %bitcast.8, s32[8,32]{1,0:T(8,128)} %bitcast.9, s32[8,32]{1,0:T(8,128)} %bitcast.10, s32[8,32]{1,0:T(8,128)} %bitcast.11, s32[1,32]{1,0:T(1,128)} %bitcast.12, f32[1,64]{1,0:T(1,128)} %bitcast.13, f32[1,64]{1,0:T(1,128)} %bitcast.14), custom_call_target="tpu_custom_call" | custom-call | tf_op jit(solution)/shard_map/prepare_blocks/pallas_call | solution.py:653
  3.0 7.3 %all-to-all-start = ((bf16[32,200,128]{2,1,0:T(8,128)(2,1)}), bf16[32,200,128]{2,1,0:T(8,128)(2,1)S(1)}, u32[]{:S(2)}, u32[]{:S(2)}) async-start(bf16[32,200,128]{2,1,0:T(8,128)(2,1)} %prepare_blocks.1.refs_0_), calls=%async_computation | async-start | bytes 3276800 | tf_op jit(solution)/shard_map/all_to_all | solution.py:673
  10.3 0.0 copy-start.7
  10.4 1.5 %copy-done.7 = f32[240,16,128]{2,1,0:T(8,128)S(1)} copy-done((f32[240,16,128]{2,1,0:T(8,128)S(1)}, f32[240,16,128]{2,1,0:T(8,128)}, u32[]{:S(2)}) %copy-start.7) | copy-done | bytes 1966104
  11.9 0.0 copy-start.3
  11.9 0.0 copy-start.4
  11.9 0.0 copy-start.5
  11.9 0.0 copy-start.11
  11.9 1.5 %turn_control.1 = (f32[16,240,128]{2,1,0:T(8,128)S(1)}, f32[120,128]{1,0:T(8,128)S(1)}, f32[120,128]{1,0:T(8,128)S(1)}, s32[8,128]{1,0:T(8,128)S(1)}) custom-call(bf16[32,200,128]{2,1,0:T(8,128)(2,1)} %prepare_blocks.1.refs_0_, f32[240,16,128]{2,1,0:T(8,128)S(1)} %copy-done.7), custom_call_target="tpu_custom_call" | custom-call | tf_op jit(solution)/shard_map/turn_control/pallas_call | solution.py:677
  13.4 1.6 %collective-permute-start.1 = (f32[120,128]{1,0:T(8,128)S(1)}, f32[120,128]{1,0:T(8,128)S(1)}, u32[]{:S(2)}, u32[]{:S(2)}) collective-permute-start(f32[120,128]{1,0:T(8,128)S(1)} %get-tuple-element.30), channel_id=1, source_target_pairs={{1,0},{2,1},{3,2},{0,3},{5,4},{6,5},{7,6},{4,7},{9,8},{10,9},{11,1... | collective-permute-start | bytes 184328 | tf_op jit(solution)/shard_map/ppermute | solution.py:627
  14.9 0.0 collective-permute-start
  14.9 7.5 %collective-permute-done.1.refs_3_.after_ref = f32[120,128]{1,0:T(8,128)S(1)} collective-permute-done((f32[120,128]{1,0:T(8,128)S(1)}, f32[120,128]{1,0:T(8,128)S(1)}, u32[]{:S(2)}, u32[]{:S(2)}) %collective-permute-start.1) | collective-permute-done | bytes 61472 | tf_op jit(solution)/shard_map/ppermute | solution.py:627
  22.4 2.3 %collective-permute-done.refs_2_.before_ref = f32[120,128]{1,0:T(8,128)S(1)} collective-permute-done((f32[120,128]{1,0:T(8,128)S(1)}, f32[120,128]{1,0:T(8,128)S(1)}, u32[]{:S(2)}, u32[]{:S(2)}) %collective-permute-start) | collective-permute-done | bytes 61472 | tf_op jit(solution)/shard_map/ppermute | solution.py:627
  24.7 0.0 copy-done.3
  24.7 0.0 copy-done.4
  24.7 0.0 copy-done.5
  24.7 0.0 copy-done.11
  24.7 2.7 %control_beyond.1 = (bf16[4,240,128]{2,1,0:T(8,128)(2,1)S(1)}, bf16[4,240,128]{2,1,0:T(8,128)(2,1)}) custom-call(s32[8,128]{1,0:T(8,128)S(1)} %get-tuple-element.27.refs_0_.par_ref, f32[16,240,128]{2,1,0:T(8,128)S(1)} %get-tuple-element.29.field_ref, f32[120,128]{1,0:T(8,128)S(1)} %collective-permute-done.refs_2_.before_ref, ...), custom_call_target="tpu_custom_call" | custom-call | tf_op jit(solution)/shard_map/control_beyond/pallas_call | solution.py:687
  27.4 0.0 collective-permute-start.2
  27.4 0.0 copy-start.2
  27.4 1.5 %collective-permute-start.3 = (bf16[4,240,128]{2,1,0:T(8,128)(2,1)}, bf16[4,240,128]{2,1,0:T(8,128)(2,1)}, u32[]{:S(2)}, u32[]{:S(2)}) collective-permute-start(bf16[4,240,128]{2,1,0:T(8,128)(2,1)} %get-tuple-element.35), channel_id=1, source_target_pairs={{4,8},{8,4},{12,16},{16,12},{20,24},{24,20},{5,9},{9,5},{13,17},{1... | collective-permute-start | bytes 737288 | tf_op jit(solution)/shard_map/ppermute | solution.py:564
  28.9 2.3 %control_local.1.refs_1_ = f32[16,240,128]{2,1,0:T(8,128)S(1)} custom-call(f32[120,128]{1,0:T(8,128)S(1)} %get-tuple-element.28.after, f32[16,240,128]{2,1,0:T(8,128)S(1)} %get-tuple-element.29.field_ref, bf16[240,240]{1,0:T(8,128)(2,1)S(1)} %copy-done.4, bf16[240,240]{1,0:T(8,128)(2,1)S(1)} %copy-done.3, bf16[256,256]{1,0:T(8,128)(2,1)S(1)} %copy-done.5), custom_call_target="tpu_custom_call" | custom-call | tf_op jit(solution)/shard_map/control_local/pallas_call | solution.py:685
  31.2 0.0 copy-done.2
  31.2 0.0 copy-start.9
  31.2 0.0 copy-start.10
  31.2 1.1 %control_strips.1.local_ref = f32[16,240,128]{2,1,0:T(8,128)S(1)} custom-call(s32[8,128]{1,0:T(8,128)S(1)} %get-tuple-element.27.refs_0_.par_ref, f32[16,240,128]{2,1,0:T(8,128)S(1)} %control_local.1.refs_1_, f32[120,128]{1,0:T(8,128)S(1)} %collective-permute-done.refs_2_.before_ref, f32[120,128]{1,0:T(8,128)S(1)} %collective-permute-done.1.refs_3_.after_ref, ...), custom_call_target="tpu_custom_call" | custom-call | tf_op jit(solution)/shard_map/control_strips/pallas_call | solution.py:639
  32.3 10.0 %collective-permute-done.2.got_ref = bf16[4,240,128]{2,1,0:T(8,128)(2,1)S(1)} collective-permute-done((bf16[4,240,128]{2,1,0:T(8,128)(2,1)S(1)}, bf16[4,240,128]{2,1,0:T(8,128)(2,1)S(1)}, u32[]{:S(2)}, u32[]{:S(2)}) %collective-permute-start.2) | collective-permute-done | bytes 245792 | tf_op jit(solution)/shard_map/ppermute | solution.py:563
  42.3 0.0 copy-done.9
  42.4 0.0 copy-done.10
  42.4 2.6 %flux_field.1 = (f32[16,240,128]{2,1,0:T(8,128)S(1)}, f32[16,240,128]{2,1,0:T(8,128)S(1)}) custom-call(s32[8,128]{1,0:T(8,128)S(1)} %get-tuple-element.27.refs_0_.par_ref, f32[16,240,128]{2,1,0:T(8,128)S(1)} %control_strips.1.local_ref, bf16[240,16,128]{2,1,0:T(8,128)(2,1)S(1)} %copy-done.9, bf16[240,16,128]{2,1,0:T(8,128)(2,1)S(1)} %copy-done.10, ...), custom_call_target="tpu_custom_call" | custom-call | tf_op jit(solution)/shard_map/flux_field/pallas_call | solution.py:692
  45.0 0.0 copy-start
  45.0 1.3 %copy-done = f32[16,240,128]{2,1,0:T(8,128)} copy-done((f32[16,240,128]{2,1,0:T(8,128)}, f32[16,240,128]{2,1,0:T(8,128)S(1)}, u32[]{:S(2)}) %copy-start) | copy-done | bytes 1966104
  46.3 0.0 copy-start.8
  46.3 1.3 %copy-done.8 = f32[16,240,128]{2,1,0:T(8,128)} copy-done((f32[16,240,128]{2,1,0:T(8,128)}, f32[16,240,128]{2,1,0:T(8,128)S(1)}, u32[]{:S(2)}) %copy-start.8) | copy-done | bytes 1966104
  47.6 2.2 %all-to-all-done.refs_1_.refs_4_ = bf16[32,200,128]{2,1,0:T(8,128)(2,1)S(1)} async-done(((bf16[32,200,128]{2,1,0:T(8,128)(2,1)}), bf16[32,200,128]{2,1,0:T(8,128)(2,1)S(1)}, u32[]{:S(2)}, u32[]{:S(2)}) %all-to-all-start) | async-done | bytes 1638432 | tf_op jit(solution)/shard_map/all_to_all | solution.py:673
  49.8 1.7 %load_flux.1 = (s32[32,128]{1,0:T(8,128)S(1)}, f32[32,128]{1,0:T(8,128)S(1)}, f32[4,240,128]{2,1,0:T(8,128)S(1)}, f32[16,240,128]{2,1,0:T(8,128)S(1)}) custom-call(s32[8,128]{1,0:T(8,128)S(1)} %get-tuple-element.27.refs_0_.par_ref, bf16[32,200,128]{2,1,0:T(8,128)(2,1)S(1)} %all-to-all-done.refs_1_.refs_4_, f32[16,240,128]{2,1,0:T(8,128)} %copy-done, ...), custom_call_target="tpu_custom_call" | custom-call | tf_op jit(solution)/shard_map/load_flux/pallas_call | solution.py:705
  51.5 0.0 collective-permute-done.3.refs_3_
  51.5 0.0 copy-start.1
  51.5 2.5 %block_values.1 = (f32[32,4,128]{2,1,0:T(4,128)S(1)}, f32[16,240,128]{2,1,0:T(8,128)S(1)}) custom-call(s32[8,128]{1,0:T(8,128)S(1)} %get-tuple-element.27.refs_0_.par_ref, bf16[32,200,128]{2,1,0:T(8,128)(2,1)S(1)} %all-to-all-done.refs_1_.refs_4_, s32[32,128]{1,0:T(8,128)S(1)} %get-tuple-element.36.refs_2_.refs_1_, ...), custom_call_target="tpu_custom_call", output_to_operand_aliasing={{1}: (4, {})} | custom-call | tf_op jit(solution)/shard_map/block_values/pallas_call | solution.py:713
  54.0 13.6 %all_to_all.10.refs_3_ = f32[32,4,128]{2,1,0:T(4,128)S(1)} all-to-all(f32[32,4,128]{2,1,0:T(4,128)S(1)} %get-tuple-element.41), channel_id=1, replica_groups=mesh['rec'=8,'tile'=4] {'rec','tile'}, dimensions={0} | all-to-all | bytes 131072 | tf_op jit(solution)/shard_map/all_to_all | solution.py:726
  67.6 0.0 copy-done.1
  67.6 2.8 %adjoint_field.1 = (f32[1,128]{1,0:T(1,128)S(1)}, f32[2,128]{1,0:T(2,128)S(1)}, f32[16,240,128]{2,1,0:T(8,128)S(1)}, f32[4,240,128]{2,1,0:T(8,128)S(1)}, f32[120,128]{1,0:T(8,128)S(1)}, /*index=5*/f32[120,128]{1,0:T(8,128)S(1)}) custom-call(s32[8,128]{1,0:T(8,128)S(1)} %get-tuple-element.27.refs_0_.par_ref, s32[32,128]{1,0:T(8,128)S(1)} %get-tuple-element.36.refs_2_.refs_1_, ...), custom_call_target="tpu_custom_call" | custom-call | tf_op jit(solution)/shard_map/adjoint_field/pallas_call | solution.py:731
  70.4 0.0 copy-start.6
  70.5 0.7 collective-permute-start.6
  71.1 0.1 gradient_odd.1.after
  71.2 0.7 collective-permute-start.7
  71.9 0.1 collective-permute-start.5
  72.0 0.5 collective-permute-start.4
  72.5 0.0 copy-done.6
  72.5 2.3 %gradient_local.1.refs_1_.after = f32[16,240,128]{2,1,0:T(8,128)S(1)} custom-call(f32[4,240,128]{2,1,0:T(8,128)S(1)} %gradient_odd.1.after, f32[16,240,128]{2,1,0:T(8,128)S(1)} %get-tuple-element.45.refs_3_.field_ref, bf16[240,240]{1,0:T(8,128)(2,1)S(1)} %copy-done.4, bf16[240,240]{1,0:T(8,128)(2,1)S(1)} %copy-done.3, bf16[256,256]{1,0:T(8,128)(2,1)S(1)} %copy-done.6), custom_call_target="tpu_custom_call" | custom-call | tf_op jit(solution)/shard_map/gradient_local/pallas_call | solution.py:630
  74.8 0.0 collective-permute-done.5.refs_3_.after_ref
  74.8 1.4 %collective-permute-done.4.refs_2_.before_ref = f32[120,128]{1,0:T(8,128)S(1)} collective-permute-done((f32[120,128]{1,0:T(8,128)S(1)}, f32[120,128]{1,0:T(8,128)S(1)}, u32[]{:S(2)}, u32[]{:S(2)}) %collective-permute-start.4) | collective-permute-done | bytes 61472 | tf_op jit(solution)/shard_map/ppermute | solution.py:627
  76.2 0.2 gradient_corners.1
  76.4 3.1 %collective-permute-start.8 = (f32[64,128]{1,0:T(8,128)S(1)}, f32[64,128]{1,0:T(8,128)S(1)}, u32[]{:S(2)}, u32[]{:S(2)}) collective-permute-start(f32[64,128]{1,0:T(8,128)S(1)} %get-tuple-element.48), channel_id=1, source_target_pairs={{0,4},{4,8},{8,12},{12,16},{16,20},{20,24},{24,28},{28,0},{1,5},{5... | collective-permute-start | bytes 98312 | tf_op jit(solution)/shard_map/ppermute | solution.py:627
  79.5 0.0 copy-start.12
  79.5 1.7 %collective-permute-start.9 = (f32[64,128]{1,0:T(8,128)S(1)}, f32[64,128]{1,0:T(8,128)S(1)}, u32[]{:S(2)}, u32[]{:S(2)}) collective-permute-start(f32[64,128]{1,0:T(8,128)S(1)} %get-tuple-element.49), channel_id=1, source_target_pairs={{4,0},{8,4},{12,8},{16,12},{20,16},{24,20},{28,24},{0,28},{5,1},{9... | collective-permute-start | bytes 98312 | tf_op jit(solution)/shard_map/ppermute | solution.py:627
  81.2 1.8 %gradient_strips.1.local_ref = f32[240,16,128]{2,1,0:T(8,128)S(1)} custom-call(s32[8,128]{1,0:T(8,128)S(1)} %get-tuple-element.27.refs_0_.par_ref, f32[16,240,128]{2,1,0:T(8,128)S(1)} %gradient_local.1.refs_1_.after, f32[120,128]{1,0:T(8,128)S(1)} %collective-permute-done.4.refs_2_.before_ref, f32[120,128]{1,0:T(8,128)S(1)} %collective-permute-done.5.refs_3_.after_ref, ...), custom_call_target="tpu_custom_call" | custom-call | tf_op jit(solution)/shard_map/gradient_strips/pallas_call | solution.py:639
  83.0 0.0 collective-permute-done.6
  83.1 0.0 collective-permute-done.7
  83.1 0.0 collective-permute-done.8.corner_before
  83.2 0.6 collective-permute-done.9.corner_after
  83.8 0.0 copy-done.12
  83.8 2.6 %gradient.1 = (f32[1,64]{1,0:T(1,128)}, f32[240,16,128]{2,1,0:T(8,128)}) custom-call(s32[8,128]{1,0:T(8,128)S(1)} %get-tuple-element.27.refs_0_.par_ref, f32[1,128]{1,0:T(1,128)S(1)} %get-tuple-element.42.model_ref, f32[240,16,128]{2,1,0:T(8,128)S(1)} %gradient_strips.1.local_ref, f32[2,128]{1,0:T(2,128)S(1)} %get-tuple-element.44.refs_2_.factor_ref, ...), custom_call_target="tpu_custom_call" | custom-call | tf_op jit(solution)/shard_map/gradient/pallas_call | solution.py:747
  (4 shorter events, 0.1 us)
Async XLA Ops:
  3.0 46.8 %all-to-all-start = ((bf16[32,200,128]{2,1,0:T(8,128)(2,1)}), bf16[32,200,128]{2,1,0:T(8,128)(2,1)S(1)}, u32[]{:S(2)}, u32[]{:S(2)}) async-start(bf16[32,200,128]{2,1,0:T(8,128)(2,1)} %prepare_blocks.1.refs_0_), calls=%async_computation | async-start | bytes 3276800 | tf_op jit(solution)/shard_map/all_to_all | solution.py:673
  10.3 1.5 %copy-start.7 = (f32[240,16,128]{2,1,0:T(8,128)S(1)}, f32[240,16,128]{2,1,0:T(8,128)}, u32[]{:S(2)}) copy-start(f32[240,16,128]{2,1,0:T(8,128)} %refs_1_.1) | copy-start | bytes 5898244
  11.9 12.8 %copy-start.3 = (bf16[240,240]{1,0:T(8,128)(2,1)S(1)}, bf16[240,240]{1,0:T(8,128)(2,1)}, u32[]{:S(2)}) copy-start(bf16[240,240]{1,0:T(8,128)(2,1)} %constant.13.clone.time_low.refs_5_) | copy-start | bytes 345604
  11.9 12.8 %copy-start.4 = (bf16[240,240]{1,0:T(8,128)(2,1)S(1)}, bf16[240,240]{1,0:T(8,128)(2,1)}, u32[]{:S(2)}) copy-start(bf16[240,240]{1,0:T(8,128)(2,1)} %constant.12.clone.time_high.refs_4_) | copy-start | bytes 345604
  11.9 12.8 %copy-start.5 = (bf16[256,256]{1,0:T(8,128)(2,1)S(1)}, bf16[256,256]{1,0:T(8,128)(2,1)}, u32[]{:S(2)}) copy-start(bf16[256,256]{1,0:T(8,128)(2,1)} %constant.14.clone.col_both) | copy-start | bytes 393220
  11.9 12.8 %copy-start.11 = (bf16[2,384,512]{2,1,0:T(8,128)(2,1)S(1)}, bf16[2,384,512]{2,1,0:T(8,128)(2,1)}, u32[]{:S(2)}) copy-start(bf16[2,384,512]{2,1,0:T(8,128)(2,1)} %constant.17.clone.beyond_ref) | copy-start | bytes 2359300
  13.4 9.1 %collective-permute-start.1 = (f32[120,128]{1,0:T(8,128)S(1)}, f32[120,128]{1,0:T(8,128)S(1)}, u32[]{:S(2)}, u32[]{:S(2)}) collective-permute-start(f32[120,128]{1,0:T(8,128)S(1)} %get-tuple-element.30), channel_id=1, source_target_pairs={{1,0},{2,1},{3,2},{0,3},{5,4},{6,5},{7,6},{4,7},{9,8},{10,9},{11,1... | collective-permute-start | bytes 184328 | tf_op jit(solution)/shard_map/ppermute | solution.py:627
  14.9 9.8 %collective-permute-start = (f32[120,128]{1,0:T(8,128)S(1)}, f32[120,128]{1,0:T(8,128)S(1)}, u32[]{:S(2)}, u32[]{:S(2)}) collective-permute-start(f32[120,128]{1,0:T(8,128)S(1)} %get-tuple-element.28.after), channel_id=1, source_target_pairs={{0,1},{1,2},{2,3},{3,0},{4,5},{5,6},{6,7},{7,4},{8,9},{9,10},{10,1... | collective-permute-start | bytes 184328 | tf_op jit(solution)/shard_map/ppermute | solution.py:627
  27.4 15.0 %collective-permute-start.2 = (bf16[4,240,128]{2,1,0:T(8,128)(2,1)S(1)}, bf16[4,240,128]{2,1,0:T(8,128)(2,1)S(1)}, u32[]{:S(2)}, u32[]{:S(2)}) collective-permute-start(bf16[4,240,128]{2,1,0:T(8,128)(2,1)S(1)} %get-tuple-element.31), channel_id=1, source_target_pairs={{0,4},{4,0},{8,12},{12,8},{16,20},{20,16},{24,28},{28,24},{1,5},{5... | collective-permute-start | bytes 737288 | tf_op jit(solution)/shard_map/ppermute | solution.py:563
  27.4 3.8 %copy-start.2 = (bf16[384,2048]{1,0:T(8,128)(2,1)S(1)}, bf16[384,2048]{1,0:T(8,128)(2,1)}, u32[]{:S(2)}) copy-start(bf16[384,2048]{1,0:T(8,128)(2,1)} %constant.15.clone.refs_6_) | copy-start | bytes 4718596
  27.4 24.1 %collective-permute-start.3 = (bf16[4,240,128]{2,1,0:T(8,128)(2,1)}, bf16[4,240,128]{2,1,0:T(8,128)(2,1)}, u32[]{:S(2)}, u32[]{:S(2)}) collective-permute-start(bf16[4,240,128]{2,1,0:T(8,128)(2,1)} %get-tuple-element.35), channel_id=1, source_target_pairs={{4,8},{8,4},{12,16},{16,12},{20,24},{24,20},{5,9},{9,5},{13,17},{1... | collective-permute-start | bytes 737288 | tf_op jit(solution)/shard_map/ppermute | solution.py:564
  31.2 11.2 %copy-start.9 = (bf16[240,16,128]{2,1,0:T(8,128)(2,1)S(1)}, bf16[240,16,128]{2,1,0:T(8,128)(2,1)}, u32[]{:S(2)}) copy-start(bf16[240,16,128]{2,1,0:T(8,128)(2,1)} %prior_ref.1) | copy-start | bytes 2949124
  31.2 11.2 %copy-start.10 = (bf16[240,16,128]{2,1,0:T(8,128)(2,1)S(1)}, bf16[240,16,128]{2,1,0:T(8,128)(2,1)}, u32[]{:S(2)}) copy-start(bf16[240,16,128]{2,1,0:T(8,128)(2,1)} %scale_ref.1) | copy-start | bytes 2949124
  45.0 1.3 %copy-start = (f32[16,240,128]{2,1,0:T(8,128)}, f32[16,240,128]{2,1,0:T(8,128)S(1)}, u32[]{:S(2)}) copy-start(f32[16,240,128]{2,1,0:T(8,128)S(1)} %get-tuple-element.32.refs_2_.refs_5_) | copy-start | bytes 5898244
  46.3 1.3 %copy-start.8 = (f32[16,240,128]{2,1,0:T(8,128)}, f32[16,240,128]{2,1,0:T(8,128)S(1)}, u32[]{:S(2)}) copy-start(f32[16,240,128]{2,1,0:T(8,128)S(1)} %get-tuple-element.33.refs_3_) | copy-start | bytes 5898244
  51.5 16.1 %copy-start.1 = (f32[16,240,128]{2,1,0:T(8,128)S(1)}, f32[16,240,128]{2,1,0:T(8,128)}, u32[]{:S(2)}) copy-start(f32[16,240,128]{2,1,0:T(8,128)} %copy-done) | copy-start | bytes 5898244
  70.4 2.1 %copy-start.6 = (bf16[256,256]{1,0:T(8,128)(2,1)S(1)}, bf16[256,256]{1,0:T(8,128)(2,1)}, u32[]{:S(2)}) copy-start(bf16[256,256]{1,0:T(8,128)(2,1)} %constant.14.clone.col_both) | copy-start | bytes 393220
  70.5 12.6 %collective-permute-start.6 = (f16[4,240,128]{2,1,0:T(8,128)(2,1)S(1)}, f16[4,240,128]{2,1,0:T(8,128)(2,1)S(1)}, u32[]{:S(2)}, u32[]{:S(2)}) collective-permute-start(f16[4,240,128]{2,1,0:T(8,128)(2,1)S(1)} %convert_element_type.12), channel_id=1, source_target_pairs={{0,4},{4,0},{8,12},{12,8},{16,20},{20,16},{24,28},{28,24},{1,5},{5... | collective-permute-start | bytes 737288 | tf_op jit(solution)/shard_map/ppermute | solution.py:742
  71.2 11.9 %collective-permute-start.7 = (f16[4,240,128]{2,1,0:T(8,128)(2,1)S(1)}, f16[4,240,128]{2,1,0:T(8,128)(2,1)S(1)}, u32[]{:S(2)}, u32[]{:S(2)}) collective-permute-start(f16[4,240,128]{2,1,0:T(8,128)(2,1)S(1)} %convert_element_type.14), channel_id=1, source_target_pairs={{4,8},{8,4},{12,16},{16,12},{20,24},{24,20},{5,9},{9,5},{13,17},{1... | collective-permute-start | bytes 737288 | tf_op jit(solution)/shard_map/ppermute | solution.py:646
  71.9 2.9 %collective-permute-start.5 = (f32[120,128]{1,0:T(8,128)S(1)}, f32[120,128]{1,0:T(8,128)S(1)}, u32[]{:S(2)}, u32[]{:S(2)}) collective-permute-start(f32[120,128]{1,0:T(8,128)S(1)} %get-tuple-element.46), channel_id=1, source_target_pairs={{1,0},{2,1},{3,2},{0,3},{5,4},{6,5},{7,6},{4,7},{9,8},{10,9},{11,1... | collective-permute-start | bytes 184328 | tf_op jit(solution)/shard_map/ppermute | solution.py:627
  72.0 4.2 %collective-permute-start.4 = (f32[120,128]{1,0:T(8,128)S(1)}, f32[120,128]{1,0:T(8,128)S(1)}, u32[]{:S(2)}, u32[]{:S(2)}) collective-permute-start(f32[120,128]{1,0:T(8,128)S(1)} %get-tuple-element.43.refs_1_), channel_id=1, source_target_pairs={{0,1},{1,2},{2,3},{3,0},{4,5},{5,6},{6,7},{7,4},{8,9},{9,10},{10,1... | collective-permute-start | bytes 184328 | tf_op jit(solution)/shard_map/ppermute | solution.py:627
  76.4 6.7 %collective-permute-start.8 = (f32[64,128]{1,0:T(8,128)S(1)}, f32[64,128]{1,0:T(8,128)S(1)}, u32[]{:S(2)}, u32[]{:S(2)}) collective-permute-start(f32[64,128]{1,0:T(8,128)S(1)} %get-tuple-element.48), channel_id=1, source_target_pairs={{0,4},{4,8},{8,12},{12,16},{16,20},{20,24},{24,28},{28,0},{1,5},{5... | collective-permute-start | bytes 98312 | tf_op jit(solution)/shard_map/ppermute | solution.py:627
  79.5 4.2 %copy-start.12 = (bf16[2,96,512]{2,1,0:T(8,128)(2,1)S(1)}, bf16[2,96,512]{2,1,0:T(8,128)(2,1)}, u32[]{:S(2)}) copy-start(bf16[2,96,512]{2,1,0:T(8,128)(2,1)} %constant.16.clone.corner_weights) | copy-start | bytes 589828
  79.5 4.2 %collective-permute-start.9 = (f32[64,128]{1,0:T(8,128)S(1)}, f32[64,128]{1,0:T(8,128)S(1)}, u32[]{:S(2)}, u32[]{:S(2)}) collective-permute-start(f32[64,128]{1,0:T(8,128)S(1)} %get-tuple-element.49), channel_id=1, source_target_pairs={{4,0},{8,4},{12,8},{16,12},{20,16},{24,20},{28,24},{0,28},{5,1},{9... | collective-permute-start | bytes 98312 | tf_op jit(solution)/shard_map/ppermute | solution.py:627
